TPU v7x, 32 devices: a whole 2x2x4 slice. The times are simulated.
32 devices in a mesh: depth: 4 (over y, x), row: 2 (over core), col: 4 (over z).
Axes of the slice: x: 2, y: 2, z: 4, core: 2. Of those that a mesh axis runs over, the one named last changes fastest.
Arguments:
- tokens: float32 [1024, 8192], P(('depth', 'col'), 'row'), may hold values from -16 to 16
- w_query: float32 [8192, 4096], P('row', 'col'), may hold values from -0.0625 to 0.0625
- w_key: float32 [8192, 512], P('row', 'col'), may hold values from -0.0625 to 0.0625
- w_value: float32 [8192, 512], P('row', 'col'), may hold values from -0.0625 to 0.0625
- w_out: float32 [4096, 8192], P('col', 'row'), may hold values from -0.09375 to 0.09375
Outputs:
- mixed: float32 [1024, 8192], P(('depth', 'col'), 'row')
All inputs are finite; a program needn't handle non-finite values.
Results may differ from a plain program's by a relative error of at most 0.0003.
Values sent between devices are 32-bit elements; how exact they have to be, the bound alone decides.
No kernel may reach another device: no remote copies, remote signals or barrier semaphores. Data moves between devices by JAX's collectives and lax.ppermute only.
A program may use at most 128 MiB of HBM per device.

v0:
```python
import math

import jax
import jax.numpy as jnp
from jax import lax
from jax.sharding import PartitionSpec as P

QUERY_HEADS = 32
KEY_VALUE_HEADS = 4
HEAD_SIZE_DIM = 128


def start_state(query_rows, kv_width):
    count_of_heads = kv_width // HEAD_SIZE_DIM
    queries_per_group = QUERY_HEADS // KEY_VALUE_HEADS
    count_of_rows = query_rows.shape[0]
    running_max = jnp.full((count_of_heads, queries_per_group, count_of_rows), -1e30, jnp.float32)
    running_sum = jnp.zeros((count_of_heads, queries_per_group, count_of_rows), jnp.float32)
    weighted = jnp.zeros(
        (count_of_heads, queries_per_group, count_of_rows, HEAD_SIZE_DIM), jnp.float32
    )
    return (running_max, running_sum, weighted)


def fold_keys(query_rows, state_now, block_pair):
    highest = lax.Precision.HIGHEST
    running_max, running_sum, weighted = state_now
    key_block, value_block = block_pair
    count_of_heads = key_block.shape[1] // HEAD_SIZE_DIM
    count_of_rows = query_rows.shape[0]
    query_head_rows = query_rows.reshape(
        count_of_rows, count_of_heads, QUERY_HEADS // KEY_VALUE_HEADS, HEAD_SIZE_DIM
    )
    key_head_rows = key_block.reshape(-1, count_of_heads, HEAD_SIZE_DIM)
    value_head_rows = value_block.reshape(-1, count_of_heads, HEAD_SIZE_DIM)
    scores = jnp.einsum("rkgd,nkd->kgrn", query_head_rows, key_head_rows, precision=highest) * (
        1.0 / math.sqrt(HEAD_SIZE_DIM)
    )
    newest = jnp.maximum(running_max, jnp.max(scores, axis=-1))
    weights = jnp.exp(scores - newest[..., None])
    running_sum = jnp.sum(weights, axis=-1)
    weighted = jnp.einsum("kgrn,nkd->kgrd", weights, value_head_rows, precision=highest)
    return (newest, running_sum, weighted)


def finish(state_now):
    running_max, running_sum, weighted = state_now
    attention_output = weighted / running_sum[..., None]
    count_of_heads, queries_per_group, count_of_rows, head_size = attention_output.shape
    return attention_output.transpose(2, 0, 1, 3).reshape(
        count_of_rows, count_of_heads * queries_per_group * head_size
    )


def on_device(tokens, w_query, w_key, w_value, w_out):
    highest = lax.Precision.HIGHEST
    gathered = lax.all_gather(tokens, "col", axis=0, tiled=True)
    q_width = w_query.shape[1]
    kv_width = w_key.shape[1]

    def product(weight):
        return jnp.dot(gathered, weight, preferred_element_type=jnp.float32, precision=highest)

    joined = lax.psum_scatter(
        jnp.concatenate([product(w_query), product(w_key), product(w_value)], axis=1),
        "row",
        scatter_dimension=0,
        tiled=True,
    )
    query_rows = joined[:, :q_width]
    local_keys = joined[:, q_width : q_width + kv_width]
    local_values = joined[:, q_width + kv_width :]
    state_end = fold_keys(
        query_rows,
        start_state(query_rows, kv_width),
        (
            lax.all_gather(local_keys, "row", axis=0, tiled=True),
            lax.all_gather(local_values, "row", axis=0, tiled=True),
        ),
    )
    attention_output = finish(state_end)
    set_attended = lax.all_gather(attention_output, "row", axis=0, tiled=True)
    return lax.psum_scatter(
        jnp.dot(set_attended, w_out, preferred_element_type=jnp.float32, precision=highest),
        "col",
        scatter_dimension=0,
        tiled=True,
    )


def solution(mesh):
    placed = (
        P(("depth", "col"), "row"),
        P("row", "col"),
        P("row", "col"),
        P("row", "col"),
        P("col", "row"),
    )
    return jax.shard_map(
        on_device, mesh=mesh, in_specs=placed, out_specs=P(("depth", "col"), "row"), check_vma=False
    )
```

profile of v0, /device:TPU:0, one launch (start us, length us, event | category | flops | bytes accessed | tf_op | source)
XLA Modules:
  0.0 249.7 jit_solution(1448447206593735178)
XLA Ops:
  6.5 0.0 copy-start
  6.5 0.0 all-gather.3.cloned.1.call-start
  6.5 0.7 all-gather.3.cloned.1.call-update
  7.3 0.0 reduce-scatter.3.cloned.1.call-start
  7.3 85.1 %all-gather.3.cloned.1.call-done = f32[256,4096]{1,0:T(8,128)} async-done(((f32[64,4096]{1,0:T(8,128)}), f32[256,4096]{1,0:T(8,128)}) %all-gather.3.cloned.1.call-update) | async-done | bytes 4194320 | tf_op jit(solution)/shard_map/all_gather | solution.py:57
  92.4 0.0 copy-done
  92.4 0.0 copy-start.1
  92.4 0.0 copy-start.2
  92.4 6.1 %fusion.12 = f32[256,128]{1,0:T(8,128)S(1)} fusion(f32[256,4096]{1,0:T(8,128)} %all-gather.3.cloned.1.call-done, f32[4096,128]{1,0:T(8,128)S(1)} %copy-done), kind=kOutput, calls=%fused_computation.18 | convolution fusion | flops 1610612736 | bytes 6422528 | tf_op jit(solution)/shard_map/dot_general | solution.py:62
  98.5 0.0 copy-done.1
  98.5 0.0 copy-done.2
  98.6 3.5 %fusion.11 = f32[256,128]{1,0:T(8,128)S(1)} fusion(f32[256,4096]{1,0:T(8,128)S(1)} %copy-done.1, f32[4096,128]{1,0:T(8,128)S(1)} %copy-done.2), kind=kOutput, calls=%fused_computation.17 | convolution fusion | flops 1610612736 | bytes 6422528 | tf_op jit(solution)/shard_map/dot_general | solution.py:62
  102.0 17.2 %fusion.10 = f32[256,1024]{1,0:T(8,128)S(1)} fusion(f32[256,4096]{1,0:T(8,128)S(1)} %copy-done.1, f32[4096,1024]{1,0:T(8,128)} %param.6), kind=kOutput, calls=%fused_computation.16 | convolution fusion | flops 12884901888 | bytes 22020096 | tf_op jit(solution)/shard_map/dot_general | solution.py:62
  119.2 1.2 pad_maximum_fusion
  120.4 0.0 reduce-scatter.3.cloned.1.call-update
  120.4 0.0 all-gather.5.cloned.1.call-start
  120.5 7.4 %reduce-scatter.3.cloned.1.call-done = f32[128,1280]{1,0:T(8,128)} async-done(((f32[256,1280]{1,0:T(8,128)}), f32[128,1280]{1,0:T(8,128)}) %reduce-scatter.3.cloned.1.call-update) | async-done | bytes 655376 | tf_op jit(solution)/shard_map/reduce_scatter | solution.py:64
  127.9 0.9 fusion.8
  128.8 1.9 all_gather.14
  130.7 2.1 all_gather.13
  132.7 2.1 fusion.9
  134.8 0.2 fusion.2
  135.0 1.6 convolution_divide_fusion
  136.6 0.0 all-gather.5.cloned.1.call-update
  136.6 0.0 reduce-scatter.5.cloned.1.call-start
  136.7 10.3 %all-gather.5.cloned.1.call-done = f32[256,1024]{0,1:T(8,128)} async-done(((f32[128,1024]{0,1:T(8,128)}), f32[256,1024]{0,1:T(8,128)}) %all-gather.5.cloned.1.call-update) | async-done | bytes 1048592 | tf_op jit(solution)/shard_map/all_gather | solution.py:82
  147.0 18.0 %fusion.13 = f32[256,4096]{1,0:T(8,128)} fusion(f32[256,1024]{0,1:T(8,128)} %all-gather.5.cloned.1.call-done, f32[1024,4096]{1,0:T(8,128)} %param.9), kind=kOutput, calls=%fused_computation.19 | convolution fusion | flops 12884901888 | bytes 22020096 | tf_op jit(solution)/shard_map/dot_general | solution.py:84
  165.0 0.0 reduce-scatter.5.cloned.1.call-update
  165.0 78.1 %reduce-scatter.5.cloned.1.call-done = f32[64,4096]{1,0:T(8,128)} async-done(((f32[256,4096]{1,0:T(8,128)}), f32[64,4096]{1,0:T(8,128)}) %reduce-scatter.5.cloned.1.call-update) | async-done | bytes 1048592 | tf_op jit(solution)/shard_map/reduce_scatter | solution.py:83
  (1 shorter events, 0.0 us)
Async XLA Ops:
  6.5 85.9 %copy-start = (f32[4096,128]{1,0:T(8,128)S(1)}, f32[4096,128]{1,0:T(8,128)}, u32[]{:S(2)}) copy-start(f32[4096,128]{1,0:T(8,128)} %param.8) | copy-start | bytes 6291460
  6.5 85.9 %all-gather.3.cloned.1.call-start = ((), (), s32[]{:S(2)}) async-start(), calls=%async_computation.2 | async-start | bytes 5242880 | tf_op jit(solution)/shard_map/all_gather | solution.py:57
  7.3 120.6 %reduce-scatter.3.cloned.1.call-start = ((), (), s32[]{:S(2)}) async-start(), calls=%async_computation.3 | async-start | bytes 1966080 | tf_op jit(solution)/shard_map/reduce_scatter | solution.py:64
  92.4 6.1 %copy-start.1 = (f32[256,4096]{1,0:T(8,128)S(1)}, f32[256,4096]{1,0:T(8,128)}, u32[]{:S(2)}) copy-start(f32[256,4096]{1,0:T(8,128)} %all-gather.3.cloned.1.call-done) | copy-start | bytes 12582916
  92.4 6.1 %copy-start.2 = (f32[4096,128]{1,0:T(8,128)S(1)}, f32[4096,128]{1,0:T(8,128)}, u32[]{:S(2)}) copy-start(f32[4096,128]{1,0:T(8,128)} %param.7) | copy-start | bytes 6291460
  120.4 26.6 %all-gather.5.cloned.1.call-start = ((), (), s32[]{:S(2)}) async-start(), calls=%async_computation.4 | async-start | bytes 1572864 | tf_op jit(solution)/shard_map/all_gather | solution.py:82
  136.6 106.5 %reduce-scatter.5.cloned.1.call-start = ((), (), s32[]{:S(2)}) async-start(), calls=%async_computation.5 | async-start | bytes 5242880 | tf_op jit(solution)/shard_map/reduce_scatter | solution.py:83
Sparse Core Ops, SparseCore 0:
  8.9 83.4 all-gather.2
  120.5 7.2 reduce-scatter.2
  136.8 10.1 all-gather.4
  165.1 77.9 reduce-scatter.4
where the time goes:
time: 250 us
  waiting for transfers between devices  182 us (73%)
  matrix products  48.5 us (19%)
  between operations  13.2 us (5%)
  blocking collectives  3.97 us (2%)
    all_gather x1, waiting for transfers between devices, on_device(): gathered = lax.all_gather(tokens, 'col', axis=0, tiled=True)  85.1 us
    reduce_scatter x1, waiting for transfers between devices, on_device(): lax.psum_scatter(jnp.dot(set_attended, w_out, preferred_element_type=jnp....  78.1 us
    dot_general x3, matrix products, product(): jnp.dot(gathered, weight, preferred_element_type=jnp.float32, precision=h...  26.8 us
    dot_general x1, matrix products, on_device(): jnp.dot(set_attended, w_out, preferred_element_type=jnp.float32, precisio...  18 us
    all_gather x1, waiting for transfers between devices, on_device(): set_attended = lax.all_gather(attention_output, 'row', axis=0, tiled=True)  10.3 us
    reduce_scatter x1, waiting for transfers between devices, on_device(): lax.psum_scatter(jnp.concatenate([product(w_query), product(w_key), produ...  7.42 us
  transfers between devices with their start and end apart: 4, of which 4 were waited for; matrix products, arithmetic and copies ran while one was open for 0% of the time, Pallas kernels for 0%

commit v1 on v0

v1 whole, which is shorter than its diff:
```python
import functools
import math

import jax
import jax.numpy as jnp
from jax import lax
from jax.experimental import pallas as pl
from jax.experimental.pallas import tpu as pltpu
from jax.sharding import PartitionSpec as P

QUERY_HEADS = 32
KEY_VALUE_HEADS = 4
HEAD_SIZE_DIM = 128
GROUP = QUERY_HEADS // KEY_VALUE_HEADS

VMEM_LIMIT = 40 * 1024 * 1024

ENDS_IN = [(1, 0), (2, 3)]
ENDS_OUT = [(0, 1), (3, 2)]
PAIRS = [(0, 1), (1, 0), (2, 3), (3, 2)]
MIDDLE = [(1, 2), (2, 1)]
CORES = [(0, 1), (1, 0)]


def split(a):
    high = a.astype(jnp.bfloat16)
    return high, (a - high.astype(jnp.float32)).astype(jnp.bfloat16)


def dot(a, b, dims=((1,), (0,))):
    return lax.dot_general(a, b, (dims, ((), ())), preferred_element_type=jnp.float32)


def dot3(a, b, dims=((1,), (0,))):
    rows = a[0].shape[0]
    both = dot(jnp.concatenate(a, axis=0), b[0], dims)
    return both[:rows] + (both[rows:] + dot(a[0], b[1], dims))


def project_kernel(terms, with_total, *refs):
    n_x = sum(terms)
    x_refs, (wq, wk, wv), rest = refs[:n_x], refs[n_x : n_x + 3], refs[n_x + 3 :]
    out = rest[-1]

    @pl.when(pl.program_id(0) == 0)
    def _():
        out[...] = rest[0][...] if with_total else jnp.zeros_like(out)

    blocks, at = [], 0
    for n in terms:
        block = x_refs[at][...]
        for r in x_refs[at + 1 : at + n]:
            block = block + r[...]
        blocks.append(block)
        at += n
    x = split(jnp.concatenate(blocks, axis=0) if len(blocks) > 1 else blocks[0])
    offset = 0
    for w in (wq, wk, wv):
        width = w.shape[1]
        out[:, offset : offset + width] += dot3(x, split(w[...]))
        offset += width


def project(blocks, weights, chunk, total=None, step=512):
    terms = tuple(len(b) for b in blocks)
    flat = [a for b in blocks for a in b]
    depth = flat[0].shape[1]
    rows = sum(b[0].shape[0] for b in blocks)
    steps = depth // step
    width = sum(w.shape[1] for w in weights)
    first = chunk * steps
    in_specs = [pl.BlockSpec((a.shape[0], step), lambda k: (0, k)) for a in flat]
    in_specs += [pl.BlockSpec((step, w.shape[1]), lambda k: (first + k, 0)) for w in weights]
    operands = flat + list(weights)
    if total is not None:
        in_specs.append(pl.BlockSpec((rows, width), lambda k: (0, 0)))
        operands.append(total)
    return pl.pallas_call(
        functools.partial(project_kernel, terms, total is not None),
        grid=(steps,),
        in_specs=in_specs,
        out_specs=pl.BlockSpec((rows, width), lambda k: (0, 0)),
        out_shape=jax.ShapeDtypeStruct((rows, width), jnp.float32),
        compiler_params=pltpu.CompilerParams(vmem_limit_bytes=VMEM_LIMIT),
        cost_estimate=pl.CostEstimate(
            flops=6 * rows * depth * width, bytes_accessed=4 * depth * (rows + width), transcendentals=0
        ),
        name="project",
    )(*operands)


def attend(parts, q_width, kv_width, store):
    groups = kv_width // HEAD_SIZE_DIM
    scale = 1.0 / math.sqrt(HEAD_SIZE_DIM)

    def columns(start, width):
        return jnp.concatenate([a[:, start : start + width] + b[:, start : start + width] for a, b in parts], axis=0)

    for g in range(groups):
        at = q_width + g * HEAD_SIZE_DIM
        keys = split(columns(at, HEAD_SIZE_DIM))
        values = split(columns(at + kv_width, HEAD_SIZE_DIM))
        for j in range(GROUP):
            head = (g * GROUP + j) * HEAD_SIZE_DIM
            queries = split(columns(head, HEAD_SIZE_DIM) * scale)
            scores = dot3(queries, keys, ((1,), (1,)))
            weights = jnp.exp(scores - jnp.max(scores, axis=-1, keepdims=True))
            total = jnp.sum(weights, axis=-1, keepdims=True)
            store(head, dot3(split(weights), values) / total)


def attend_out_kernel(n_parts, q_width, kv_width, *refs):
    part_refs, w_ref, rest = refs[: 2 * n_parts], refs[2 * n_parts], refs[2 * n_parts + 1 :]
    high, low, outs = rest[0], rest[1], rest[2:]

    @pl.when(pl.program_id(0) == 0)
    def _():
        def store(head, rows):
            h, l = split(rows)
            high[:, head : head + HEAD_SIZE_DIM] = h
            low[:, head : head + HEAD_SIZE_DIM] = l

        attend([(part_refs[2 * i], part_refs[2 * i + 1]) for i in range(n_parts)], q_width, kv_width, store)

    mix(high, low, w_ref, outs)


def mix(high, low, w_ref, outs):
    mixed = dot3((high[...], low[...]), split(w_ref[...]))
    at = 0
    for o in outs:
        o[...] = mixed[at : at + o.shape[0]]
        at += o.shape[0]


def mix_kernel(high, low, w_ref, *outs):
    mix(high, low, w_ref, outs)


def attend_out(parts, w_out, kv_width, slots, columns, step=512):
    rows = sum(a.shape[0] for a, _ in parts)
    q_width = w_out.shape[0]
    flat = [r for pair in parts for r in pair]
    whole = pl.BlockSpec((rows, q_width), lambda n: (0, 0))
    bf16 = jax.ShapeDtypeStruct((rows, q_width), jnp.bfloat16)
    res = pl.pallas_call(
        functools.partial(attend_out_kernel, len(parts), q_width, kv_width),
        grid=(columns // step,),
        in_specs=[pl.BlockSpec(a.shape, lambda n: (0, 0)) for a in flat]
        + [pl.BlockSpec((q_width, step), lambda n: (0, n))],
        out_specs=[whole, whole] + [pl.BlockSpec((s, step), lambda n: (0, n)) for s in slots],
        out_shape=[bf16, bf16] + [jax.ShapeDtypeStruct((s, columns), jnp.float32) for s in slots],
        compiler_params=pltpu.CompilerParams(vmem_limit_bytes=VMEM_LIMIT),
        cost_estimate=pl.CostEstimate(
            flops=6 * rows * q_width * columns + 24 * rows * rows * q_width,
            bytes_accessed=4 * columns * (q_width + rows),
            transcendentals=rows * rows * q_width // HEAD_SIZE_DIM,
        ),
        name="attend_out",
    )(*flat, w_out)
    return res[:2], res[2:]


def out_again(attended, w_out, slots, chunk, columns, step=512):
    high, low = attended
    rows, q_width = high.shape
    first = chunk * columns // step
    whole = pl.BlockSpec((rows, q_width), lambda n: (0, 0))
    return pl.pallas_call(
        mix_kernel,
        grid=(columns // step,),
        in_specs=[whole, whole, pl.BlockSpec((q_width, step), lambda n: (0, first + n))],
        out_specs=[pl.BlockSpec((s, step), lambda n: (0, n)) for s in slots],
        out_shape=[jax.ShapeDtypeStruct((s, columns), jnp.float32) for s in slots],
        compiler_params=pltpu.CompilerParams(vmem_limit_bytes=VMEM_LIMIT),
        cost_estimate=pl.CostEstimate(
            flops=6 * rows * q_width * columns, bytes_accessed=4 * columns * (q_width + rows), transcendentals=0
        ),
        name="out_again",
    )(high, low, w_out)


CHUNKS = 2


def on_line_of_four(tokens, w_query, w_key, w_value, w_out):
    rows, depth = tokens.shape
    weights = (w_query, w_key, w_value)
    kv_width = w_key.shape[1]
    step = depth // CHUNKS

    def hop(a, pairs):
        return lax.ppermute(a, "col", pairs)

    def swap(a):
        return lax.ppermute(a, "row", CORES)

    own = [tokens[:, c * step : (c + 1) * step] for c in range(CHUNKS)]
    near = [hop(a, PAIRS) for a in own]
    mid = [hop(a, MIDDLE) for a in own]
    end2 = [hop(a, ENDS_IN) for a in mid]
    mid2 = [hop(a, MIDDLE) for a in near]
    end3 = [hop(a, ENDS_IN) for a in mid2]

    def run(blocks):
        total = None
        for c in range(CHUNKS):
            total = project(blocks(c), weights, c, total)
        return total, swap(total)

    first = run(lambda c: [(own[c],), (near[c],)])
    second = run(lambda c: [(mid[c], end2[c])])
    third = run(lambda c: [(mid2[c], end3[c])])

    slots = [rows, rows, rows, rows]
    columns = w_out.shape[1] // CHUNKS
    attended, mixed = attend_out([first, second, third], w_out, kv_width, slots, columns)
    result = []
    for c in range(CHUNKS):
        if c > 0:
            mixed = out_again(attended, w_out, slots, c, columns)
        m_own, m_near, m_second, m_third = mixed
        r1 = hop(m_third, ENDS_OUT)
        r2e = hop(m_second, ENDS_OUT)
        r2m = hop(m_third + r1, MIDDLE)
        r3m = hop(m_second + r2e, MIDDLE)
        r3x = hop(m_near + r2m, PAIRS)
        result.append(m_own + (r3x + r3m))
    return jnp.concatenate(result, axis=1)


def on_device(tokens, w_query, w_key, w_value, w_out):
    highest = lax.Precision.HIGHEST
    gathered = lax.all_gather(tokens, "col", axis=0, tiled=True)
    q_width = w_query.shape[1]
    kv_width = w_key.shape[1]

    def product(weight):
        return jnp.dot(gathered, weight, preferred_element_type=jnp.float32, precision=highest)

    joined = lax.psum_scatter(
        jnp.concatenate([product(w_query), product(w_key), product(w_value)], axis=1),
        "row",
        scatter_dimension=0,
        tiled=True,
    )
    query_rows = joined[:, :q_width]
    keys = lax.all_gather(joined[:, q_width : q_width + kv_width], "row", axis=0, tiled=True)
    values = lax.all_gather(joined[:, q_width + kv_width :], "row", axis=0, tiled=True)
    count_of_rows, count_of_heads = query_rows.shape[0], kv_width // HEAD_SIZE_DIM
    query_rows = query_rows.reshape(count_of_rows, count_of_heads, GROUP, HEAD_SIZE_DIM)
    keys = keys.reshape(-1, count_of_heads, HEAD_SIZE_DIM)
    values = values.reshape(-1, count_of_heads, HEAD_SIZE_DIM)
    scores = jnp.einsum("rkgd,nkd->kgrn", query_rows, keys, precision=highest)
    weights = jax.nn.softmax(scores * (1.0 / math.sqrt(HEAD_SIZE_DIM)), axis=-1)
    attended = jnp.einsum("kgrn,nkd->rkgd", weights, values, precision=highest)
    attended = lax.all_gather(attended.reshape(count_of_rows, q_width), "row", axis=0, tiled=True)
    return lax.psum_scatter(
        jnp.dot(attended, w_out, preferred_element_type=jnp.float32, precision=highest),
        "col",
        scatter_dimension=0,
        tiled=True,
    )


def solution(mesh):
    placed = (
        P(("depth", "col"), "row"),
        P("row", "col"),
        P("row", "col"),
        P("row", "col"),
        P("col", "row"),
    )
    here = mesh.shape["row"] == 2 and mesh.shape["col"] == 4
    return jax.shard_map(
        on_line_of_four if here else on_device,
        mesh=mesh,
        in_specs=placed,
        out_specs=P(("depth", "col"), "row"),
        check_vma=False,
    )
```

time: 250 us -> 176 us (0.70)
  waiting for transfers between devices: 182 us -> 73.4 us
  matrix products: 48.5 us -> 0 us
  Pallas kernels: 0 us -> 48.5 us
  starting transfers between devices: 0.13 us -> 46.5 us
  between operations: 13.2 us -> 0.36 us
  blocking collectives: 3.97 us -> 0 us
  local copies, waits for them, and re-layouts: 0.89 us -> 4.63 us
    all_gather x2 -> x0, waiting for transfers between devices: 95.4 us -> none  [the longest x1 85.1 us: on_device(): gathered = lax.all_gather(tokens, 'col', axis=0, tiled=True)]
    reduce_scatter x2 -> x0, waiting for transfers between devices: 85.5 us -> none  [the longest x1 78.1 us: on_device(): lax.psum_scatter(jnp.dot(set_attended, w_out, preferred_element_type=jnp....]
    ppermute x0 -> x23, waiting for transfers between devices: none -> 73.4 us  [the longest x20 71.8 us: hop(): return lax.ppermute(a, 'col', pairs)]
    pallas_call x0 -> x8, Pallas kernels: none -> 48.5 us  [the longest x6 33.5 us: project(): pl.pallas_call(functools.partial(project_kernel, terms, total is not None...]
    dot_general x6 -> x0, matrix products: 48.5 us -> none  [the longest x3 26.8 us: product(): jnp.dot(gathered, weight, preferred_element_type=jnp.float32, precision=h...]
    ppermute x0 -> x23, starting transfers between devices: none -> 46.5 us  [the longest x20 46.2 us: hop(): return lax.ppermute(a, 'col', pairs)]
    all_gather x2 -> x0, blocking collectives: 3.97 us -> none  [the longest x1 2.07 us: on_device(): lax.all_gather(local_keys, 'row', axis=0, tiled=True)]
    unnamed x6 -> x8, local copies, waits for them, and re-layouts: 0.01 us -> 3.18 us
  transfers between devices with their start and end apart: 4 -> 23, of which waited for: 4 -> 12; matrix products, arithmetic and copies ran while one was open for 0% -> 0% of each run, Pallas kernels for 0% -> 23%
where the time goes in v1:
time: 176 us; the launch traced here: 175 us
  waiting for transfers between devices  73.4 us (42%)
  Pallas kernels  48.5 us (28%)
  starting transfers between devices  46.5 us (26%)
  local copies, waits for them, and re-layouts  4.63 us (3%)
    ppermute x20, waiting for transfers between devices, hop(): return lax.ppermute(a, 'col', pairs)  71.8 us
    ppermute x20, starting transfers between devices, hop(): return lax.ppermute(a, 'col', pairs)  46.2 us
    pallas_call x6, Pallas kernels, project(): pl.pallas_call(functools.partial(project_kernel, terms, total is not None...  33.5 us
    pallas_call x1, Pallas kernels, attend_out(): pl.pallas_call(functools.partial(attend_out_kernel, len(parts), q_width,...  8.64 us
    pallas_call x1, Pallas kernels, out_again(): pl.pallas_call(mix_kernel, grid=(columns // step,), in_specs=[whole, whol...  6.43 us
  transfers between devices with their start and end apart: 23, of which 12 were waited for; matrix products, arithmetic and copies ran while one was open for 0% of the time, Pallas kernels for 23%

profile of v1, /device:TPU:0, one launch (start us, length us, event | category | flops | bytes accessed | tf_op | source)
XLA Modules:
  0.0 175.0 jit_solution(6563469431689338606)
XLA Ops:
  0.0 1.4 fusion
  1.5 3.1 %collective-permute-start.1 = (f32[64,2048]{1,0:T(8,128)S(1)}, f32[64,2048]{1,0:T(8,128)S(1)}, u32[]{:S(2)}, u32[]{:S(2)}) collective-permute-start(f32[64,2048]{1,0:T(8,128)S(1)} %get-tuple-element.25.refs_0_), channel_id=1, source_target_pairs={{0,1},{1,0},{2,3},{3,2},{4,5},{5,4},{6,7},{7,6},{8,9},{9,8},{10,11... | collective-permute-start | bytes 1572872 | tf_op jit(solution)/shard_map/ppermute | solution.py:193
  4.5 0.1 collective-permute-start
  4.6 0.7 collective-permute-start.5
  5.3 0.7 collective-permute-start.3
  6.0 11.3 %collective-permute-done.1.refs_1_ = f32[64,2048]{1,0:T(8,128)S(1)} collective-permute-done((f32[64,2048]{1,0:T(8,128)S(1)}, f32[64,2048]{1,0:T(8,128)S(1)}, u32[]{:S(2)}, u32[]{:S(2)}) %collective-permute-start.1) | collective-permute-done | bytes 524320 | tf_op jit(solution)/shard_map/ppermute | solution.py:193
  17.3 0.7 collective-permute-start.10
  18.0 9.7 %collective-permute-done.refs_1_ = f32[64,2048]{1,0:T(8,128)S(1)} collective-permute-done((f32[64,2048]{1,0:T(8,128)S(1)}, f32[64,2048]{1,0:T(8,128)S(1)}, u32[]{:S(2)}, u32[]{:S(2)}) %collective-permute-start) | collective-permute-done | bytes 524320 | tf_op jit(solution)/shard_map/ppermute | solution.py:193
  27.7 0.7 collective-permute-start.8
  28.4 0.0 collective-permute-done.5.refs_0_
  28.4 1.3 collective-permute-start.6
  29.7 0.0 collective-permute-done.3.refs_0_
  29.7 1.3 collective-permute-start.4
  31.0 0.0 collective-permute-done.10.refs_0_
  31.0 1.3 collective-permute-start.11
  32.3 1.3 collective-permute-start.9
  33.6 0.0 copy-start
  33.6 1.6 copy-done
  35.2 1.6 copy-done.2
  36.8 6.1 %project.6.refs_5_ = f32[128,1280]{1,0:T(8,128)S(1)} custom-call(f32[64,2048]{1,0:T(8,128)S(1)} %get-tuple-element.25.refs_0_, f32[64,2048]{1,0:T(8,128)S(1)} %collective-permute-done.1.refs_1_, f32[4096,1024]{1,0:T(8,128)} %refs_2_.11, f32[4096,128]{1,0:T(8,128)S(1)} %copy-done, f32[4096,128]{1,0:T(8,128)S(1)} %copy-done.2), custom_call_target="tpu_custom_call" | custom-call | flops 2013265920 | bytes 11534336 | tf_op jit(solution)/shard_map/project/pallas_call | solution.py:78
  42.9 5.9 %project.7.refs_0_ = f32[128,1280]{1,0:T(8,128)S(1)} custom-call(f32[64,2048]{1,0:T(8,128)S(1)} %get-tuple-element.26.refs_0_, f32[64,2048]{1,0:T(8,128)S(1)} %collective-permute-done.refs_1_, f32[4096,1024]{1,0:T(8,128)} %refs_2_.11, f32[4096,128]{1,0:T(8,128)S(1)} %copy-done.1, f32[4096,128]{1,0:T(8,128)S(1)} %copy-done.3, f32[128,1280]{1,0:T(8,128)S(1)} %project.6.refs_5_), custom_call_target="tpu_custom_call" | custom-call | flops 2013265920 | bytes 11534336 | tf_op jit(solution)/shard_map/project/pallas_call | solution.py:78
  48.8 0.1 collective-permute-start.2
  48.9 5.4 %project.8.refs_5_ = f32[64,1280]{1,0:T(8,128)S(1)} custom-call(f32[64,2048]{1,0:T(8,128)S(1)} %collective-permute-done.5.refs_0_, f32[64,2048]{1,0:T(8,128)S(1)} %collective-permute-done.6.refs_1_, f32[4096,1024]{1,0:T(8,128)} %refs_2_.11, f32[4096,128]{1,0:T(8,128)S(1)} %copy-done.1, f32[4096,128]{1,0:T(8,128)S(1)} %copy-done.3), custom_call_target="tpu_custom_call" | custom-call | flops 1006632960 | bytes 11010048 | tf_op jit(solution)/shard_map/project/pallas_call | solution.py:78
  54.3 4.0 %collective-permute-done.4.refs_1_ = f32[64,2048]{1,0:T(8,128)S(1)} collective-permute-done((f32[64,2048]{1,0:T(8,128)S(1)}, f32[64,2048]{1,0:T(8,128)S(1)}, u32[]{:S(2)}, u32[]{:S(2)}) %collective-permute-start.4) | collective-permute-done | bytes 524320 | tf_op jit(solution)/shard_map/ppermute | solution.py:193
  58.3 5.4 %project.9.refs_2_ = f32[64,1280]{1,0:T(8,128)S(1)} custom-call(f32[64,2048]{1,0:T(8,128)S(1)} %collective-permute-done.3.refs_0_, f32[64,2048]{1,0:T(8,128)S(1)} %collective-permute-done.4.refs_1_, f32[4096,1024]{1,0:T(8,128)} %refs_2_.11, f32[4096,128]{1,0:T(8,128)S(1)} %copy-done.1, f32[4096,128]{1,0:T(8,128)S(1)} %copy-done.3, f32[64,1280]{1,0:T(8,128)S(1)} %project.8.refs_5_), custom_call_target="tpu_custom_call" | custom-call | flops 1006632960 | bytes 11010048 | tf_op jit(solution)/shard_map/project/pallas_call | solution.py:78
  63.7 0.1 collective-permute-start.7
  63.8 5.8 %collective-permute-done.11.refs_1_ = f32[64,2048]{1,0:T(8,128)S(1)} collective-permute-done((f32[64,2048]{1,0:T(8,128)S(1)}, f32[64,2048]{1,0:T(8,128)S(1)}, u32[]{:S(2)}, u32[]{:S(2)}) %collective-permute-start.11) | collective-permute-done | bytes 524320 | tf_op jit(solution)/shard_map/ppermute | solution.py:193
  69.5 5.4 %project.10.refs_5_ = f32[64,1280]{1,0:T(8,128)S(1)} custom-call(f32[64,2048]{1,0:T(8,128)S(1)} %collective-permute-done.10.refs_0_, f32[64,2048]{1,0:T(8,128)S(1)} %collective-permute-done.11.refs_1_, f32[4096,1024]{1,0:T(8,128)} %refs_2_.11, f32[4096,128]{1,0:T(8,128)S(1)} %copy-done.1, f32[4096,128]{1,0:T(8,128)S(1)} %copy-done.3), custom_call_target="tpu_custom_call" | custom-call | flops 1006632960 | bytes 11010048 | tf_op jit(solution)/shard_map/project/pallas_call | solution.py:78
  74.9 3.8 %collective-permute-done.9.refs_1_ = f32[64,2048]{1,0:T(8,128)S(1)} collective-permute-done((f32[64,2048]{1,0:T(8,128)S(1)}, f32[64,2048]{1,0:T(8,128)S(1)}, u32[]{:S(2)}, u32[]{:S(2)}) %collective-permute-start.9) | collective-permute-done | bytes 524320 | tf_op jit(solution)/shard_map/ppermute | solution.py:193
  78.7 5.4 %project.11.refs_4_ = f32[64,1280]{1,0:T(8,128)S(1)} custom-call(f32[64,2048]{1,0:T(8,128)S(1)} %collective-permute-done.8.refs_0_, f32[64,2048]{1,0:T(8,128)S(1)} %collective-permute-done.9.refs_1_, f32[4096,1024]{1,0:T(8,128)} %refs_2_.11, f32[4096,128]{1,0:T(8,128)S(1)} %copy-done.1, f32[4096,128]{1,0:T(8,128)S(1)} %copy-done.3, ...), custom_call_target="tpu_custom_call" | custom-call | flops 1006632960 | bytes 11010048 | tf_op jit(solution)/shard_map/project/pallas_call | solution.py:78
  84.1 0.1 collective-permute-start.12
  84.1 0.0 collective-permute-done.2.refs_1_
  84.2 0.0 collective-permute-done.7.refs_3_
  84.2 1.6 collective-permute-done.12.refs_5_
  85.8 8.6 %attend_out.1 = (bf16[256,1024]{1,0:T(8,128)(2,1)S(1)}, bf16[256,1024]{1,0:T(8,128)(2,1)S(1)}, f32[64,2048]{1,0:T(8,128)S(1)}, f32[64,2048]{1,0:T(8,128)S(1)}, f...) custom-call(f32[128,1280]{1,0:T(8,128)S(1)} %project.7.refs_0_, f32[128,1280]{1,0:T(8,128)S(1)} %collective-permute-done.2.refs_1_, ...), custom_call_target="tpu_custom_call" | custom-call | flops 4831838208 | bytes 10485760 | tf_op jit(solution)/shard_map/attend_out/pallas_call | solution.py:146
  94.4 11.9 %collective-permute-start.13 = (f32[64,2048]{1,0:T(8,128)S(1)}, f32[64,2048]{1,0:T(8,128)S(1)}, u32[]{:S(2)}, u32[]{:S(2)}) collective-permute-start(f32[64,2048]{1,0:T(8,128)S(1)} %get-tuple-element.17), channel_id=1, source_target_pairs={{0,1},{3,2},{4,5},{7,6},{8,9},{11,10},{12,13},{15,14},{16,17},{19,... | collective-permute-start | bytes 1572872 | tf_op jit(solution)/shard_map/ppermute | solution.py:193
  106.3 6.4 %out_again.1 = (f32[64,2048]{1,0:T(8,128)S(1)}, f32[64,2048]{1,0:T(8,128)S(1)}, f32[64,2048]{1,0:T(8,128)S(1)}, f32[64,2048]{1,0:T(8,128)S(1)}) custom-call(bf16[256,1024]{1,0:T(8,128)(2,1)S(1)} %get-tuple-element.19.high, bf16[256,1024]{1,0:T(8,128)(2,1)S(1)} %get-tuple-element.20.low, f32[1024,4096]{1,0:T(8,128)} %w_ref.1), custom_call_target="tpu_custom_call" | custom-call | flops 3221225472 | bytes 10485760 | tf_op jit(solution)/shard_map/out_again/pallas_call | solution.py:169
  112.7 1.3 collective-permute-start.18
  114.0 1.3 collective-permute-start.16
  115.4 3.1 %collective-permute-done.13 = f32[64,2048]{1,0:T(8,128)S(1)} collective-permute-done((f32[64,2048]{1,0:T(8,128)S(1)}, f32[64,2048]{1,0:T(8,128)S(1)}, u32[]{:S(2)}, u32[]{:S(2)}) %collective-permute-start.13) | collective-permute-done | bytes 524320 | tf_op jit(solution)/shard_map/ppermute | solution.py:193
  118.5 0.1 add.30
  118.6 0.7 collective-permute-start.14
  119.3 7.2 %collective-permute-start.21 = (f32[64,2048]{1,0:T(8,128)S(1)}, f32[64,2048]{1,0:T(8,128)S(1)}, u32[]{:S(2)}, u32[]{:S(2)}) collective-permute-start(f32[64,2048]{1,0:T(8,128)S(1)} %get-tuple-element.24), channel_id=1, source_target_pairs={{0,1},{3,2},{4,5},{7,6},{8,9},{11,10},{12,13},{15,14},{16,17},{19,... | collective-permute-start | bytes 1572872 | tf_op jit(solution)/shard_map/ppermute | solution.py:193
  126.5 3.3 %collective-permute-done.18 = f32[64,2048]{1,0:T(8,128)S(1)} collective-permute-done((f32[64,2048]{1,0:T(8,128)S(1)}, f32[64,2048]{1,0:T(8,128)S(1)}, u32[]{:S(2)}, u32[]{:S(2)}) %collective-permute-start.18) | collective-permute-done | bytes 524320 | tf_op jit(solution)/shard_map/ppermute | solution.py:193
  129.7 0.1 add.35
  129.8 0.7 collective-permute-start.19
  130.5 10.4 %collective-permute-done.16 = f32[64,2048]{1,0:T(8,128)S(1)} collective-permute-done((f32[64,2048]{1,0:T(8,128)S(1)}, f32[64,2048]{1,0:T(8,128)S(1)}, u32[]{:S(2)}, u32[]{:S(2)}) %collective-permute-start.16) | collective-permute-done | bytes 524320 | tf_op jit(solution)/shard_map/ppermute | solution.py:193
  141.0 0.1 add.32
  141.1 0.7 collective-permute-start.17
  141.8 0.0 collective-permute-done.14
  141.8 0.1 add.31
  141.9 5.3 %collective-permute-start.15 = (f32[64,2048]{1,0:T(8,128)S(1)}, f32[64,2048]{1,0:T(8,128)S(1)}, u32[]{:S(2)}, u32[]{:S(2)}) collective-permute-start(f32[64,2048]{1,0:T(8,128)S(1)} %add.31), channel_id=1, source_target_pairs={{0,1},{1,0},{2,3},{3,2},{4,5},{5,4},{6,7},{7,6},{8,9},{9,8},{10,11... | collective-permute-start | bytes 1572872 | tf_op jit(solution)/shard_map/ppermute | solution.py:193
  147.2 5.0 %collective-permute-done.21 = f32[64,2048]{1,0:T(8,128)S(1)} collective-permute-done((f32[64,2048]{1,0:T(8,128)S(1)}, f32[64,2048]{1,0:T(8,128)S(1)}, u32[]{:S(2)}, u32[]{:S(2)}) %collective-permute-start.21) | collective-permute-done | bytes 524320 | tf_op jit(solution)/shard_map/ppermute | solution.py:193
  152.2 0.1 add.37
  152.3 0.7 collective-permute-start.22
  153.0 0.1 add.36
  153.1 5.3 %collective-permute-start.20 = (f32[64,2048]{1,0:T(8,128)S(1)}, f32[64,2048]{1,0:T(8,128)S(1)}, u32[]{:S(2)}, u32[]{:S(2)}) collective-permute-start(f32[64,2048]{1,0:T(8,128)S(1)} %add.36), channel_id=1, source_target_pairs={{0,1},{1,0},{2,3},{3,2},{4,5},{5,4},{6,7},{7,6},{8,9},{9,8},{10,11... | collective-permute-start | bytes 1572872 | tf_op jit(solution)/shard_map/ppermute | solution.py:193
  158.4 0.0 collective-permute-done.17
  158.4 5.0 %collective-permute-done.15 = f32[64,2048]{1,0:T(8,128)S(1)} collective-permute-done((f32[64,2048]{1,0:T(8,128)S(1)}, f32[64,2048]{1,0:T(8,128)S(1)}, u32[]{:S(2)}, u32[]{:S(2)}) %collective-permute-start.15) | collective-permute-done | bytes 524320 | tf_op jit(solution)/shard_map/ppermute | solution.py:193
  163.5 0.1 add_add_fusion.1
  163.5 0.0 collective-permute-done.22
  163.5 10.3 %collective-permute-done.20 = f32[64,2048]{1,0:T(8,128)S(1)} collective-permute-done((f32[64,2048]{1,0:T(8,128)S(1)}, f32[64,2048]{1,0:T(8,128)S(1)}, u32[]{:S(2)}, u32[]{:S(2)}) %collective-permute-start.20) | collective-permute-done | bytes 524320 | tf_op jit(solution)/shard_map/ppermute | solution.py:193
  173.9 0.1 add_add_fusion
  174.0 1.0 pad_maximum_fusion
  (8 shorter events, 0.0 us)
Async XLA Ops:
  0.0 42.9 %copy-start.1 = (f32[4096,128]{1,0:T(8,128)S(1)}, f32[4096,128]{1,0:T(8,128)}, u32[]{:S(2)}) copy-start(f32[4096,128]{1,0:T(8,128)} %refs_3_.11) | copy-start | bytes 6291460
  1.5 15.8 %collective-permute-start.1 = (f32[64,2048]{1,0:T(8,128)S(1)}, f32[64,2048]{1,0:T(8,128)S(1)}, u32[]{:S(2)}, u32[]{:S(2)}) collective-permute-start(f32[64,2048]{1,0:T(8,128)S(1)} %get-tuple-element.25.refs_0_), channel_id=1, source_target_pairs={{0,1},{1,0},{2,3},{3,2},{4,5},{5,4},{6,7},{7,6},{8,9},{9,8},{10,11... | collective-permute-start | bytes 1572872 | tf_op jit(solution)/shard_map/ppermute | solution.py:193
  4.5 23.2 %collective-permute-start = (f32[64,2048]{1,0:T(8,128)S(1)}, f32[64,2048]{1,0:T(8,128)S(1)}, u32[]{:S(2)}, u32[]{:S(2)}) collective-permute-start(f32[64,2048]{1,0:T(8,128)S(1)} %get-tuple-element.26.refs_0_), channel_id=1, source_target_pairs={{0,1},{1,0},{2,3},{3,2},{4,5},{5,4},{6,7},{7,6},{8,9},{9,8},{10,11... | collective-permute-start | bytes 1572872 | tf_op jit(solution)/shard_map/ppermute | solution.py:193
  4.6 23.8 %collective-permute-start.5 = (f32[64,2048]{1,0:T(8,128)S(1)}, f32[64,2048]{1,0:T(8,128)S(1)}, u32[]{:S(2)}, u32[]{:S(2)}) collective-permute-start(f32[64,2048]{1,0:T(8,128)S(1)} %get-tuple-element.25.refs_0_), channel_id=1, source_target_pairs={{1,2},{2,1},{5,6},{6,5},{9,10},{10,9},{13,14},{14,13},{17,18},{18,... | collective-permute-start | bytes 1572872 | tf_op jit(solution)/shard_map/ppermute | solution.py:193
  5.3 24.4 %collective-permute-start.3 = (f32[64,2048]{1,0:T(8,128)S(1)}, f32[64,2048]{1,0:T(8,128)S(1)}, u32[]{:S(2)}, u32[]{:S(2)}) collective-permute-start(f32[64,2048]{1,0:T(8,128)S(1)} %get-tuple-element.26.refs_0_), channel_id=1, source_target_pairs={{1,2},{2,1},{5,6},{6,5},{9,10},{10,9},{13,14},{14,13},{17,18},{18,... | collective-permute-start | bytes 1572872 | tf_op jit(solution)/shard_map/ppermute | solution.py:193
  17.3 13.7 %collective-permute-start.10 = (f32[64,2048]{1,0:T(8,128)S(1)}, f32[64,2048]{1,0:T(8,128)S(1)}, u32[]{:S(2)}, u32[]{:S(2)}) collective-permute-start(f32[64,2048]{1,0:T(8,128)S(1)} %collective-permute-done.1.refs_1_), channel_id=1, source_target_pairs={{1,2},{2,1},{5,6},{6,5},{9,10},{10,9},{13,14},{14,13},{17,18},{18,... | collective-permute-start | bytes 1572872 | tf_op jit(solution)/shard_map/ppermute | solution.py:193
  27.7 4.6 %collective-permute-start.8 = (f32[64,2048]{1,0:T(8,128)S(1)}, f32[64,2048]{1,0:T(8,128)S(1)}, u32[]{:S(2)}, u32[]{:S(2)}) collective-permute-start(f32[64,2048]{1,0:T(8,128)S(1)} %collective-permute-done.refs_1_), channel_id=1, source_target_pairs={{1,2},{2,1},{5,6},{6,5},{9,10},{10,9},{13,14},{14,13},{17,18},{18,... | collective-permute-start | bytes 1572872 | tf_op jit(solution)/shard_map/ppermute | solution.py:193
  28.4 20.5 %collective-permute-start.6 = (f32[64,2048]{1,0:T(8,128)S(1)}, f32[64,2048]{1,0:T(8,128)S(1)}, u32[]{:S(2)}, u32[]{:S(2)}) collective-permute-start(f32[64,2048]{1,0:T(8,128)S(1)} %collective-permute-done.5.refs_0_), channel_id=1, source_target_pairs={{1,0},{2,3},{5,4},{6,7},{9,8},{10,11},{13,12},{14,15},{17,16},{18,... | collective-permute-start | bytes 1572872 | tf_op jit(solution)/shard_map/ppermute | solution.py:193
  29.7 28.6 %collective-permute-start.4 = (f32[64,2048]{1,0:T(8,128)S(1)}, f32[64,2048]{1,0:T(8,128)S(1)}, u32[]{:S(2)}, u32[]{:S(2)}) collective-permute-start(f32[64,2048]{1,0:T(8,128)S(1)} %collective-permute-done.3.refs_0_), channel_id=1, source_target_pairs={{1,0},{2,3},{5,4},{6,7},{9,8},{10,11},{13,12},{14,15},{17,16},{18,... | collective-permute-start | bytes 1572872 | tf_op jit(solution)/shard_map/ppermute | solution.py:193
  31.0 38.5 %collective-permute-start.11 = (f32[64,2048]{1,0:T(8,128)S(1)}, f32[64,2048]{1,0:T(8,128)S(1)}, u32[]{:S(2)}, u32[]{:S(2)}) collective-permute-start(f32[64,2048]{1,0:T(8,128)S(1)} %collective-permute-done.10.refs_0_), channel_id=1, source_target_pairs={{1,0},{2,3},{5,4},{6,7},{9,8},{10,11},{13,12},{14,15},{17,16},{18,... | collective-permute-start | bytes 1572872 | tf_op jit(solution)/shard_map/ppermute | solution.py:193
  32.3 46.4 %collective-permute-start.9 = (f32[64,2048]{1,0:T(8,128)S(1)}, f32[64,2048]{1,0:T(8,128)S(1)}, u32[]{:S(2)}, u32[]{:S(2)}) collective-permute-start(f32[64,2048]{1,0:T(8,128)S(1)} %collective-permute-done.8.refs_0_), channel_id=1, source_target_pairs={{1,0},{2,3},{5,4},{6,7},{9,8},{10,11},{13,12},{14,15},{17,16},{18,... | collective-permute-start | bytes 1572872 | tf_op jit(solution)/shard_map/ppermute | solution.py:193
  33.6 1.6 copy-start
  35.2 1.6 copy-start.2
  36.8 6.1 %copy-start.3 = (f32[4096,128]{1,0:T(8,128)S(1)}, f32[4096,128]{1,0:T(8,128)}, u32[]{:S(2)}) copy-start(f32[4096,128]{1,0:T(8,128)} %refs_4_.11) | copy-start | bytes 6291460
  48.8 35.3 %collective-permute-start.2 = (f32[128,1280]{1,0:T(8,128)S(1)}, f32[128,1280]{1,0:T(8,128)S(1)}, u32[]{:S(2)}, u32[]{:S(2)}) collective-permute-start(f32[128,1280]{1,0:T(8,128)S(1)} %project.7.refs_0_), channel_id=1, source_target_pairs={{0,4},{4,0},{1,5},{5,1},{2,6},{6,2},{3,7},{7,3},{8,12},{12,8},{9,1... | collective-permute-start | bytes 1966088 | tf_op jit(solution)/shard_map/ppermute | solution.py:196
  63.7 20.5 %collective-permute-start.7 = (f32[64,1280]{1,0:T(8,128)S(1)}, f32[64,1280]{1,0:T(8,128)S(1)}, u32[]{:S(2)}, u32[]{:S(2)}) collective-permute-start(f32[64,1280]{1,0:T(8,128)S(1)} %project.9.refs_2_), channel_id=1, source_target_pairs={{0,4},{4,0},{1,5},{5,1},{2,6},{6,2},{3,7},{7,3},{8,12},{12,8},{9,1... | collective-permute-start | bytes 983048 | tf_op jit(solution)/shard_map/ppermute | solution.py:196
  84.1 1.7 collective-permute-start.12
  94.4 24.1 %collective-permute-start.13 = (f32[64,2048]{1,0:T(8,128)S(1)}, f32[64,2048]{1,0:T(8,128)S(1)}, u32[]{:S(2)}, u32[]{:S(2)}) collective-permute-start(f32[64,2048]{1,0:T(8,128)S(1)} %get-tuple-element.17), channel_id=1, source_target_pairs={{0,1},{3,2},{4,5},{7,6},{8,9},{11,10},{12,13},{15,14},{16,17},{19,... | collective-permute-start | bytes 1572872 | tf_op jit(solution)/shard_map/ppermute | solution.py:193
  112.7 17.0 %collective-permute-start.18 = (f32[64,2048]{1,0:T(8,128)S(1)}, f32[64,2048]{1,0:T(8,128)S(1)}, u32[]{:S(2)}, u32[]{:S(2)}) collective-permute-start(f32[64,2048]{1,0:T(8,128)S(1)} %get-tuple-element.23), channel_id=1, source_target_pairs={{0,1},{3,2},{4,5},{7,6},{8,9},{11,10},{12,13},{15,14},{16,17},{19,... | collective-permute-start | bytes 1572872 | tf_op jit(solution)/shard_map/ppermute | solution.py:193
  114.0 26.9 %collective-permute-start.16 = (f32[64,2048]{1,0:T(8,128)S(1)}, f32[64,2048]{1,0:T(8,128)S(1)}, u32[]{:S(2)}, u32[]{:S(2)}) collective-permute-start(f32[64,2048]{1,0:T(8,128)S(1)} %get-tuple-element.18), channel_id=1, source_target_pairs={{0,1},{3,2},{4,5},{7,6},{8,9},{11,10},{12,13},{15,14},{16,17},{19,... | collective-permute-start | bytes 1572872 | tf_op jit(solution)/shard_map/ppermute | solution.py:193
  118.6 23.2 %collective-permute-start.14 = (f32[64,2048]{1,0:T(8,128)S(1)}, f32[64,2048]{1,0:T(8,128)S(1)}, u32[]{:S(2)}, u32[]{:S(2)}) collective-permute-start(f32[64,2048]{1,0:T(8,128)S(1)} %add.30), channel_id=1, source_target_pairs={{1,2},{2,1},{5,6},{6,5},{9,10},{10,9},{13,14},{14,13},{17,18},{18,... | collective-permute-start | bytes 1572872 | tf_op jit(solution)/shard_map/ppermute | solution.py:193
  119.3 32.9 %collective-permute-start.21 = (f32[64,2048]{1,0:T(8,128)S(1)}, f32[64,2048]{1,0:T(8,128)S(1)}, u32[]{:S(2)}, u32[]{:S(2)}) collective-permute-start(f32[64,2048]{1,0:T(8,128)S(1)} %get-tuple-element.24), channel_id=1, source_target_pairs={{0,1},{3,2},{4,5},{7,6},{8,9},{11,10},{12,13},{15,14},{16,17},{19,... | collective-permute-start | bytes 1572872 | tf_op jit(solution)/shard_map/ppermute | solution.py:193
  129.8 23.2 %collective-permute-start.19 = (f32[64,2048]{1,0:T(8,128)S(1)}, f32[64,2048]{1,0:T(8,128)S(1)}, u32[]{:S(2)}, u32[]{:S(2)}) collective-permute-start(f32[64,2048]{1,0:T(8,128)S(1)} %add.35), channel_id=1, source_target_pairs={{1,2},{2,1},{5,6},{6,5},{9,10},{10,9},{13,14},{14,13},{17,18},{18,... | collective-permute-start | bytes 1572872 | tf_op jit(solution)/shard_map/ppermute | solution.py:193
  141.1 17.4 %collective-permute-start.17 = (f32[64,2048]{1,0:T(8,128)S(1)}, f32[64,2048]{1,0:T(8,128)S(1)}, u32[]{:S(2)}, u32[]{:S(2)}) collective-permute-start(f32[64,2048]{1,0:T(8,128)S(1)} %add.32), channel_id=1, source_target_pairs={{1,2},{2,1},{5,6},{6,5},{9,10},{10,9},{13,14},{14,13},{17,18},{18,... | collective-permute-start | bytes 1572872 | tf_op jit(solution)/shard_map/ppermute | solution.py:193
  141.9 21.6 %collective-permute-start.15 = (f32[64,2048]{1,0:T(8,128)S(1)}, f32[64,2048]{1,0:T(8,128)S(1)}, u32[]{:S(2)}, u32[]{:S(2)}) collective-permute-start(f32[64,2048]{1,0:T(8,128)S(1)} %add.31), channel_id=1, source_target_pairs={{0,1},{1,0},{2,3},{3,2},{4,5},{5,4},{6,7},{7,6},{8,9},{9,8},{10,11... | collective-permute-start | bytes 1572872 | tf_op jit(solution)/shard_map/ppermute | solution.py:193
  152.3 11.2 %collective-permute-start.22 = (f32[64,2048]{1,0:T(8,128)S(1)}, f32[64,2048]{1,0:T(8,128)S(1)}, u32[]{:S(2)}, u32[]{:S(2)}) collective-permute-start(f32[64,2048]{1,0:T(8,128)S(1)} %add.37), channel_id=1, source_target_pairs={{1,2},{2,1},{5,6},{6,5},{9,10},{10,9},{13,14},{14,13},{17,18},{18,... | collective-permute-start | bytes 1572872 | tf_op jit(solution)/shard_map/ppermute | solution.py:193
  153.1 20.8 %collective-permute-start.20 = (f32[64,2048]{1,0:T(8,128)S(1)}, f32[64,2048]{1,0:T(8,128)S(1)}, u32[]{:S(2)}, u32[]{:S(2)}) collective-permute-start(f32[64,2048]{1,0:T(8,128)S(1)} %add.36), channel_id=1, source_target_pairs={{0,1},{1,0},{2,3},{3,2},{4,5},{5,4},{6,7},{7,6},{8,9},{9,8},{10,11... | collective-permute-start | bytes 1572872 | tf_op jit(solution)/shard_map/ppermute | solution.py:193

commit v2 on v1

--- a/solution.py
+++ b/solution.py
@@ -89,27 +89,46 @@
     )(*operands)
 
 
-def attend(parts, q_width, kv_width, store):
+def attend(keyed, asked, q_width, kv_width, store):
     groups = kv_width // HEAD_SIZE_DIM
     scale = 1.0 / math.sqrt(HEAD_SIZE_DIM)
 
-    def columns(start, width):
-        return jnp.concatenate([a[:, start : start + width] + b[:, start : start + width] for a, b in parts], axis=0)
-
+    def columns(pairs, start):
+        stop = start + HEAD_SIZE_DIM
+        return jnp.concatenate([a[:, start:stop] + b[:, start:stop] for a, b in pairs], axis=0)
+
+    rows = sum(a.shape[0] for a, _ in asked)
+    together = GROUP if rows <= 64 else 1
     for g in range(groups):
         at = q_width + g * HEAD_SIZE_DIM
-        keys = split(columns(at, HEAD_SIZE_DIM))
-        values = split(columns(at + kv_width, HEAD_SIZE_DIM))
-        for j in range(GROUP):
-            head = (g * GROUP + j) * HEAD_SIZE_DIM
-            queries = split(columns(head, HEAD_SIZE_DIM) * scale)
-            scores = dot3(queries, keys, ((1,), (1,)))
+        k_high, k_low = split(columns(keyed, at))
+        v_high, v_low = split(columns(keyed, at + kv_width))
+        k_both = jnp.concatenate([k_high, k_high], axis=1)
+        v_both = jnp.concatenate([v_high, v_low], axis=1)
+        for j in range(0, GROUP, together):
+            heads = [(g * GROUP + j + i) * HEAD_SIZE_DIM for i in range(together)]
+            q_high, q_low = split(jnp.concatenate([columns(asked, h) for h in heads], axis=0) * scale)
+            scores = dot(jnp.concatenate([q_high, q_low], axis=1), k_both, ((1,), (1,)))
+            scores = scores + dot(q_high, k_low, ((1,), (1,)))
             weights = jnp.exp(scores - jnp.max(scores, axis=-1, keepdims=True))
             total = jnp.sum(weights, axis=-1, keepdims=True)
-            store(head, dot3(split(weights), values) / total)
-
-
-def attend_out_kernel(n_parts, q_width, kv_width, *refs):
+            p_high, p_low = split(weights)
+            both = dot(p_high, v_both)
+            result = both[:, :HEAD_SIZE_DIM] + (both[:, HEAD_SIZE_DIM:] + dot(p_low, v_high))
+            result = result / total
+            for i, h in enumerate(heads):
+                store(h, result[i * rows : (i + 1) * rows])
+
+
+def mix(high, low, w_ref, outs):
+    mixed = dot3((high[...], low[...]), split(w_ref[...]))
+    at = 0
+    for o in outs:
+        o[...] = mixed[at : at + o.shape[0]]
+        at += o.shape[0]
+
+
+def attend_out_kernel(n_parts, first, last, q_width, kv_width, *refs):
     part_refs, w_ref, rest = refs[: 2 * n_parts], refs[2 * n_parts], refs[2 * n_parts + 1 :]
     high, low, outs = rest[0], rest[1], rest[2:]
 
@@ -120,31 +139,25 @@
             high[:, head : head + HEAD_SIZE_DIM] = h
             low[:, head : head + HEAD_SIZE_DIM] = l
 
-        attend([(part_refs[2 * i], part_refs[2 * i + 1]) for i in range(n_parts)], q_width, kv_width, store)
+        pairs = [(part_refs[2 * i], part_refs[2 * i + 1]) for i in range(n_parts)]
+        attend(pairs, pairs[first:last], q_width, kv_width, store)
 
     mix(high, low, w_ref, outs)
-
-
-def mix(high, low, w_ref, outs):
-    mixed = dot3((high[...], low[...]), split(w_ref[...]))
-    at = 0
-    for o in outs:
-        o[...] = mixed[at : at + o.shape[0]]
-        at += o.shape[0]
 
 
 def mix_kernel(high, low, w_ref, *outs):
     mix(high, low, w_ref, outs)
 
 
-def attend_out(parts, w_out, kv_width, slots, columns, step=512):
-    rows = sum(a.shape[0] for a, _ in parts)
+def attend_out(parts, first, last, w_out, kv_width, slots, columns, step=512):
+    rows = sum(a.shape[0] for a, _ in parts[first:last])
+    keyed = sum(a.shape[0] for a, _ in parts)
     q_width = w_out.shape[0]
     flat = [r for pair in parts for r in pair]
     whole = pl.BlockSpec((rows, q_width), lambda n: (0, 0))
     bf16 = jax.ShapeDtypeStruct((rows, q_width), jnp.bfloat16)
     res = pl.pallas_call(
-        functools.partial(attend_out_kernel, len(parts), q_width, kv_width),
+        functools.partial(attend_out_kernel, len(parts), first, last, q_width, kv_width),
         grid=(columns // step,),
         in_specs=[pl.BlockSpec(a.shape, lambda n: (0, 0)) for a in flat]
         + [pl.BlockSpec((q_width, step), lambda n: (0, n))],
@@ -152,19 +165,19 @@
         out_shape=[bf16, bf16] + [jax.ShapeDtypeStruct((s, columns), jnp.float32) for s in slots],
         compiler_params=pltpu.CompilerParams(vmem_limit_bytes=VMEM_LIMIT),
         cost_estimate=pl.CostEstimate(
-            flops=6 * rows * q_width * columns + 24 * rows * rows * q_width,
+            flops=6 * rows * q_width * columns + 24 * rows * keyed * q_width,
             bytes_accessed=4 * columns * (q_width + rows),
-            transcendentals=rows * rows * q_width // HEAD_SIZE_DIM,
+            transcendentals=rows * keyed * q_width // HEAD_SIZE_DIM,
         ),
         name="attend_out",
     )(*flat, w_out)
     return res[:2], res[2:]
 
 
-def out_again(attended, w_out, slots, chunk, columns, step=512):
+def out_again(attended, w_out, slots, start, columns, step=512):
     high, low = attended
     rows, q_width = high.shape
-    first = chunk * columns // step
+    first = start // step
     whole = pl.BlockSpec((rows, q_width), lambda n: (0, 0))
     return pl.pallas_call(
         mix_kernel,
@@ -180,6 +193,10 @@
     )(high, low, w_out)
 
 
+def after(a, *others):
+    return lax.optimization_barrier((a, *others))[0]
+
+
 CHUNKS = 2
 
 
@@ -195,34 +212,41 @@
     def swap(a):
         return lax.ppermute(a, "row", CORES)
 
+    def run(blocks, total=None):
+        for c in range(CHUNKS):
+            total = project(blocks(c), weights, c, total)
+        return total
+
     own = [tokens[:, c * step : (c + 1) * step] for c in range(CHUNKS)]
     near = [hop(a, PAIRS) for a in own]
     mid = [hop(a, MIDDLE) for a in own]
     end2 = [hop(a, ENDS_IN) for a in mid]
     mid2 = [hop(a, MIDDLE) for a in near]
+    first = run(lambda c: [(own[c],), (near[c],)])
+    mid2 = [after(a, first) for a in mid2]
+    first = (first, swap(first))
     end3 = [hop(a, ENDS_IN) for a in mid2]
-
-    def run(blocks):
-        total = None
-        for c in range(CHUNKS):
-            total = project(blocks(c), weights, c, total)
-        return total, swap(total)
-
-    first = run(lambda c: [(own[c],), (near[c],)])
     second = run(lambda c: [(mid[c], end2[c])])
+    second = (second, swap(second))
     third = run(lambda c: [(mid2[c], end3[c])])
-
-    slots = [rows, rows, rows, rows]
+    third = (third, swap(third))
+
     columns = w_out.shape[1] // CHUNKS
-    attended, mixed = attend_out([first, second, third], w_out, kv_width, slots, columns)
+    parts = [first, second, third]
+    a_third, m_third = attend_out(parts, 2, 3, w_out, kv_width, [rows], columns)
+    m_third = [m_third[0]] + [
+        out_again(a_third, w_out, [rows], c * columns, columns)[0] for c in range(1, CHUNKS)
+    ]
+    r1 = [hop(m, ENDS_OUT) for m in m_third]
+    others = [tuple(after(a, *m_third) for a in first), second, third]
+    a_rest, mixed = attend_out(others, 0, 2, w_out, kv_width, [rows] * 3, columns)
     result = []
     for c in range(CHUNKS):
         if c > 0:
-            mixed = out_again(attended, w_out, slots, c, columns)
-        m_own, m_near, m_second, m_third = mixed
-        r1 = hop(m_third, ENDS_OUT)
+            mixed = out_again(a_rest, w_out, [rows] * 3, c * columns, columns)
+        m_own, m_near, m_second = mixed
         r2e = hop(m_second, ENDS_OUT)
-        r2m = hop(m_third + r1, MIDDLE)
+        r2m = hop(m_third[c] + r1[c], MIDDLE)
         r3m = hop(m_second + r2e, MIDDLE)
         r3x = hop(m_near + r2m, PAIRS)
         result.append(m_own + (r3x + r3m))

time: 176 us -> 163 us (0.926)
  starting transfers between devices: 46.5 us -> 31 us
  Pallas kernels: 48.5 us -> 59.1 us
  waiting for transfers between devices: 73.4 us -> 65.2 us
    ppermute x20, starting transfers between devices: 46.2 us -> 30.7 us  [hop(): return lax.ppermute(a, 'col', pairs)]
    ppermute x20, waiting for transfers between devices: 71.8 us -> 63.6 us  [hop(): return lax.ppermute(a, 'col', pairs)]
    pallas_call x1 -> x2, Pallas kernels: 8.64 us -> 14.8 us  [attend_out(): pl.pallas_call(functools.partial(attend_out_kernel, len(parts), first, la...]
    pallas_call x1 -> x2, Pallas kernels: 6.43 us -> 10.8 us  [out_again(): pl.pallas_call(mix_kernel, grid=(columns // step,), in_specs=[whole, whol...]
  transfers between devices with their start and end apart: 23 -> 23, of which waited for: 12 -> 10; matrix products, arithmetic and copies ran while one was open for 0% -> 0% of each run, Pallas kernels for 23% -> 33%
where the time goes in v2:
time: 163 us; the launch traced here: 162 us
  waiting for transfers between devices  65.2 us (40%)
  Pallas kernels  59.1 us (36%)
  starting transfers between devices  31 us (19%)
  local copies, waits for them, and re-layouts  4.63 us (3%)
    ppermute x20, waiting for transfers between devices, hop(): return lax.ppermute(a, 'col', pairs)  63.6 us
    pallas_call x6, Pallas kernels, project(): pl.pallas_call(functools.partial(project_kernel, terms, total is not None...  33.5 us
    ppermute x20, starting transfers between devices, hop(): return lax.ppermute(a, 'col', pairs)  30.7 us
    pallas_call x2, Pallas kernels, attend_out(): pl.pallas_call(functools.partial(attend_out_kernel, len(parts), first, la...  14.8 us
    pallas_call x2, Pallas kernels, out_again(): pl.pallas_call(mix_kernel, grid=(columns // step,), in_specs=[whole, whol...  10.8 us
  transfers between devices with their start and end apart: 23, of which 10 were waited for; matrix products, arithmetic and copies ran while one was open for 0% of the time, Pallas kernels for 33%

profile of v2, /device:TPU:0, one launch (start us, length us, event | category | flops | bytes accessed | tf_op | source)
XLA Modules:
  0.0 161.9 jit_solution(8644741148177349028)
XLA Ops:
  0.0 1.4 fusion
  1.5 3.1 %collective-permute-start.1 = (f32[64,2048]{1,0:T(8,128)S(1)}, f32[64,2048]{1,0:T(8,128)S(1)}, u32[]{:S(2)}, u32[]{:S(2)}) collective-permute-start(f32[64,2048]{1,0:T(8,128)S(1)} %get-tuple-element.35.refs_0_), channel_id=1, source_target_pairs={{0,1},{1,0},{2,3},{3,2},{4,5},{5,4},{6,7},{7,6},{8,9},{9,8},{10,11... | collective-permute-start | bytes 1572872 | tf_op jit(solution)/shard_map/ppermute | solution.py:210
  4.5 0.1 collective-permute-start
  4.6 0.7 collective-permute-start.5
  5.3 0.7 collective-permute-start.3
  6.0 11.3 %collective-permute-done.1.refs_1_ = f32[64,2048]{1,0:T(8,128)S(1)} collective-permute-done((f32[64,2048]{1,0:T(8,128)S(1)}, f32[64,2048]{1,0:T(8,128)S(1)}, u32[]{:S(2)}, u32[]{:S(2)}) %collective-permute-start.1) | collective-permute-done | bytes 524320 | tf_op jit(solution)/shard_map/ppermute | solution.py:210
  17.3 0.7 collective-permute-start.10
  18.0 9.7 %collective-permute-done.refs_1_ = f32[64,2048]{1,0:T(8,128)S(1)} collective-permute-done((f32[64,2048]{1,0:T(8,128)S(1)}, f32[64,2048]{1,0:T(8,128)S(1)}, u32[]{:S(2)}, u32[]{:S(2)}) %collective-permute-start) | collective-permute-done | bytes 524320 | tf_op jit(solution)/shard_map/ppermute | solution.py:210
  27.7 0.7 collective-permute-start.8
  28.4 0.0 collective-permute-done.5.refs_0_
  28.4 1.3 collective-permute-start.6
  29.7 0.0 collective-permute-done.3.refs_0_
  29.7 1.3 collective-permute-start.4
  31.0 0.0 copy-start
  31.0 1.6 copy-done
  32.6 1.6 copy-done.2
  34.2 6.1 %project.6.refs_5_ = f32[128,1280]{1,0:T(8,128)S(1)} custom-call(f32[64,2048]{1,0:T(8,128)S(1)} %get-tuple-element.35.refs_0_, f32[64,2048]{1,0:T(8,128)S(1)} %collective-permute-done.1.refs_1_, f32[4096,1024]{1,0:T(8,128)} %refs_2_.11, f32[4096,128]{1,0:T(8,128)S(1)} %copy-done, f32[4096,128]{1,0:T(8,128)S(1)} %copy-done.2), custom_call_target="tpu_custom_call" | custom-call | flops 2013265920 | bytes 11534336 | tf_op jit(solution)/shard_map/project/pallas_call | solution.py:78
  40.3 5.9 %project.7.refs_0_ = f32[128,1280]{1,0:T(8,128)S(1)} custom-call(f32[64,2048]{1,0:T(8,128)S(1)} %get-tuple-element.36.refs_0_, f32[64,2048]{1,0:T(8,128)S(1)} %collective-permute-done.refs_1_, f32[4096,1024]{1,0:T(8,128)} %refs_2_.11, f32[4096,128]{1,0:T(8,128)S(1)} %copy-done.1, f32[4096,128]{1,0:T(8,128)S(1)} %copy-done.3, f32[128,1280]{1,0:T(8,128)S(1)} %project.6.refs_5_), custom_call_target="tpu_custom_call" | custom-call | flops 2013265920 | bytes 11534336 | tf_op jit(solution)/shard_map/project/pallas_call | solution.py:78
  46.2 0.0 collective-permute-done.10.refs_0_
  46.2 1.3 collective-permute-start.11
  47.5 1.3 collective-permute-start.9
  48.8 0.1 collective-permute-start.2
  48.9 5.4 %project.8.refs_5_ = f32[64,1280]{1,0:T(8,128)S(1)} custom-call(f32[64,2048]{1,0:T(8,128)S(1)} %collective-permute-done.5.refs_0_, f32[64,2048]{1,0:T(8,128)S(1)} %collective-permute-done.6.refs_1_, f32[4096,1024]{1,0:T(8,128)} %refs_2_.11, f32[4096,128]{1,0:T(8,128)S(1)} %copy-done.1, f32[4096,128]{1,0:T(8,128)S(1)} %copy-done.3), custom_call_target="tpu_custom_call" | custom-call | flops 1006632960 | bytes 11010048 | tf_op jit(solution)/shard_map/project/pallas_call | solution.py:78
  54.3 4.0 %collective-permute-done.4.refs_1_ = f32[64,2048]{1,0:T(8,128)S(1)} collective-permute-done((f32[64,2048]{1,0:T(8,128)S(1)}, f32[64,2048]{1,0:T(8,128)S(1)}, u32[]{:S(2)}, u32[]{:S(2)}) %collective-permute-start.4) | collective-permute-done | bytes 524320 | tf_op jit(solution)/shard_map/ppermute | solution.py:210
  58.3 5.4 %project.9.refs_2_ = f32[64,1280]{1,0:T(8,128)S(1)} custom-call(f32[64,2048]{1,0:T(8,128)S(1)} %collective-permute-done.3.refs_0_, f32[64,2048]{1,0:T(8,128)S(1)} %collective-permute-done.4.refs_1_, f32[4096,1024]{1,0:T(8,128)} %refs_2_.11, f32[4096,128]{1,0:T(8,128)S(1)} %copy-done.1, f32[4096,128]{1,0:T(8,128)S(1)} %copy-done.3, f32[64,1280]{1,0:T(8,128)S(1)} %project.8.refs_5_), custom_call_target="tpu_custom_call" | custom-call | flops 1006632960 | bytes 11010048 | tf_op jit(solution)/shard_map/project/pallas_call | solution.py:78
  63.7 0.1 collective-permute-start.7
  63.8 5.8 %collective-permute-done.11.refs_1_ = f32[64,2048]{1,0:T(8,128)S(1)} collective-permute-done((f32[64,2048]{1,0:T(8,128)S(1)}, f32[64,2048]{1,0:T(8,128)S(1)}, u32[]{:S(2)}, u32[]{:S(2)}) %collective-permute-start.11) | collective-permute-done | bytes 524320 | tf_op jit(solution)/shard_map/ppermute | solution.py:210
  69.5 5.4 %project.10.refs_5_ = f32[64,1280]{1,0:T(8,128)S(1)} custom-call(f32[64,2048]{1,0:T(8,128)S(1)} %collective-permute-done.10.refs_0_, f32[64,2048]{1,0:T(8,128)S(1)} %collective-permute-done.11.refs_1_, f32[4096,1024]{1,0:T(8,128)} %refs_2_.11, f32[4096,128]{1,0:T(8,128)S(1)} %copy-done.1, f32[4096,128]{1,0:T(8,128)S(1)} %copy-done.3), custom_call_target="tpu_custom_call" | custom-call | flops 1006632960 | bytes 11010048 | tf_op jit(solution)/shard_map/project/pallas_call | solution.py:78
  74.9 3.8 %collective-permute-done.9.refs_1_ = f32[64,2048]{1,0:T(8,128)S(1)} collective-permute-done((f32[64,2048]{1,0:T(8,128)S(1)}, f32[64,2048]{1,0:T(8,128)S(1)}, u32[]{:S(2)}, u32[]{:S(2)}) %collective-permute-start.9) | collective-permute-done | bytes 524320 | tf_op jit(solution)/shard_map/ppermute | solution.py:210
  78.7 5.4 %project.11.refs_4_ = f32[64,1280]{1,0:T(8,128)S(1)} custom-call(f32[64,2048]{1,0:T(8,128)S(1)} %collective-permute-done.8.refs_0_, f32[64,2048]{1,0:T(8,128)S(1)} %collective-permute-done.9.refs_1_, f32[4096,1024]{1,0:T(8,128)} %refs_2_.11, f32[4096,128]{1,0:T(8,128)S(1)} %copy-done.1, f32[4096,128]{1,0:T(8,128)S(1)} %copy-done.3, ...), custom_call_target="tpu_custom_call" | custom-call | flops 1006632960 | bytes 11010048 | tf_op jit(solution)/shard_map/project/pallas_call | solution.py:78
  84.1 0.1 collective-permute-start.12
  84.1 0.0 collective-permute-done.2.refs_1_
  84.2 1.6 collective-permute-done.12.refs_5_
  85.8 5.8 %attend_out.2 = (bf16[64,1024]{1,0:T(8,128)(2,1)S(1)}, bf16[64,1024]{1,0:T(8,128)(2,1)S(1)}, f32[64,2048]{1,0:T(8,128)S(1)}) custom-call(f32[128,1280]{1,0:T(8,128)S(1)} %project.7.refs_0_, f32[128,1280]{1,0:T(8,128)S(1)} %collective-permute-done.2.refs_1_, f32[64,1280]{1,0:T(8,128)S(1)} %project.9.refs_2_, f32[64,1280]{1,0:T(8,128)S(1)} %collective-permute-done.7.refs_3_, ...), custom_call_target="tpu_custom_call" | custom-call | flops 1207959552 | bytes 8912896 | tf_op jit(solution)/shard_map/attend_out/pallas_call | solution.py:159
  91.6 1.5 collective-permute-start.13
  93.1 5.0 %out_again.2 = f32[64,2048]{1,0:T(8,128)S(1)} custom-call(bf16[64,1024]{1,0:T(8,128)(2,1)S(1)} %get-tuple-element.23.high, bf16[64,1024]{1,0:T(8,128)(2,1)S(1)} %get-tuple-element.24.low, f32[1024,4096]{1,0:T(8,128)} %w_ref.3), custom_call_target="tpu_custom_call" | custom-call | flops 805306368 | bytes 8912896 | tf_op jit(solution)/shard_map/out_again/pallas_call | solution.py:182
  98.1 1.3 collective-permute-start.18
  99.4 9.0 %attend_out.3 = (bf16[192,1024]{1,0:T(8,128)(2,1)S(1)}, bf16[192,1024]{1,0:T(8,128)(2,1)S(1)}, f32[64,2048]{1,0:T(8,128)S(1)}, f32[64,2048]{1,0:T(8,128)S(1)}, f32[64,2048]{1,0:T(8,128)S(1)}) custom-call(f32[128,1280]{1,0:T(8,128)S(1)} %project.7.refs_0_, f32[128,1280]{1,0:T(8,128)S(1)} %collective-permute-done.2.refs_1_, f32[64,1280]{1,0:T(8,128)S(1)} %project.9.refs_2_, ...), custom_call_target="tpu_custom_call" | custom-call | flops 3623878656 | bytes 9961472 | tf_op jit(solution)/shard_map/attend_out/pallas_call | solution.py:159
  108.5 1.3 collective-permute-start.16
  109.8 0.1 add.30
  109.9 0.7 collective-permute-start.14
  110.6 5.8 %out_again.3 = (f32[64,2048]{1,0:T(8,128)S(1)}, f32[64,2048]{1,0:T(8,128)S(1)}, f32[64,2048]{1,0:T(8,128)S(1)}) custom-call(bf16[192,1024]{1,0:T(8,128)(2,1)S(1)} %get-tuple-element.30.high, bf16[192,1024]{1,0:T(8,128)(2,1)S(1)} %get-tuple-element.31.low, f32[1024,4096]{1,0:T(8,128)} %w_ref.3), custom_call_target="tpu_custom_call" | custom-call | flops 2415919104 | bytes 9961472 | tf_op jit(solution)/shard_map/out_again/pallas_call | solution.py:182
  116.4 3.4 %collective-permute-start.21 = (f32[64,2048]{1,0:T(8,128)S(1)}, f32[64,2048]{1,0:T(8,128)S(1)}, u32[]{:S(2)}, u32[]{:S(2)}) collective-permute-start(f32[64,2048]{1,0:T(8,128)S(1)} %get-tuple-element.34), channel_id=1, source_target_pairs={{0,1},{3,2},{4,5},{7,6},{8,9},{11,10},{12,13},{15,14},{16,17},{19,... | collective-permute-start | bytes 1572872 | tf_op jit(solution)/shard_map/ppermute | solution.py:210
  119.8 0.0 collective-permute-done.18
  119.8 0.1 add.35
  119.9 0.7 collective-permute-start.19
  120.6 7.2 %collective-permute-done.16 = f32[64,2048]{1,0:T(8,128)S(1)} collective-permute-done((f32[64,2048]{1,0:T(8,128)S(1)}, f32[64,2048]{1,0:T(8,128)S(1)}, u32[]{:S(2)}, u32[]{:S(2)}) %collective-permute-start.16) | collective-permute-done | bytes 524320 | tf_op jit(solution)/shard_map/ppermute | solution.py:210
  127.8 0.1 add.32
  127.8 0.7 collective-permute-start.17
  128.5 0.0 collective-permute-done.14
  128.5 0.1 add.31
  128.6 4.7 %collective-permute-start.15 = (f32[64,2048]{1,0:T(8,128)S(1)}, f32[64,2048]{1,0:T(8,128)S(1)}, u32[]{:S(2)}, u32[]{:S(2)}) collective-permute-start(f32[64,2048]{1,0:T(8,128)S(1)} %add.31), channel_id=1, source_target_pairs={{0,1},{1,0},{2,3},{3,2},{4,5},{5,4},{6,7},{7,6},{8,9},{9,8},{10,11... | collective-permute-start | bytes 1572872 | tf_op jit(solution)/shard_map/ppermute | solution.py:210
  133.3 5.7 %collective-permute-done.21 = f32[64,2048]{1,0:T(8,128)S(1)} collective-permute-done((f32[64,2048]{1,0:T(8,128)S(1)}, f32[64,2048]{1,0:T(8,128)S(1)}, u32[]{:S(2)}, u32[]{:S(2)}) %collective-permute-start.21) | collective-permute-done | bytes 524320 | tf_op jit(solution)/shard_map/ppermute | solution.py:210
  139.0 0.1 add.37
  139.1 0.7 collective-permute-start.22
  139.8 0.0 collective-permute-done.19
  139.8 0.1 add.36
  139.9 4.7 %collective-permute-start.20 = (f32[64,2048]{1,0:T(8,128)S(1)}, f32[64,2048]{1,0:T(8,128)S(1)}, u32[]{:S(2)}, u32[]{:S(2)}) collective-permute-start(f32[64,2048]{1,0:T(8,128)S(1)} %add.36), channel_id=1, source_target_pairs={{0,1},{1,0},{2,3},{3,2},{4,5},{5,4},{6,7},{7,6},{8,9},{9,8},{10,11... | collective-permute-start | bytes 1572872 | tf_op jit(solution)/shard_map/ppermute | solution.py:210
  144.5 0.0 collective-permute-done.17
  144.5 5.7 %collective-permute-done.15 = f32[64,2048]{1,0:T(8,128)S(1)} collective-permute-done((f32[64,2048]{1,0:T(8,128)S(1)}, f32[64,2048]{1,0:T(8,128)S(1)}, u32[]{:S(2)}, u32[]{:S(2)}) %collective-permute-start.15) | collective-permute-done | bytes 524320 | tf_op jit(solution)/shard_map/ppermute | solution.py:210
  150.2 0.1 add_add_fusion.1
  150.3 10.5 %collective-permute-done.20 = f32[64,2048]{1,0:T(8,128)S(1)} collective-permute-done((f32[64,2048]{1,0:T(8,128)S(1)}, f32[64,2048]{1,0:T(8,128)S(1)}, u32[]{:S(2)}, u32[]{:S(2)}) %collective-permute-start.20) | collective-permute-done | bytes 524320 | tf_op jit(solution)/shard_map/ppermute | solution.py:210
  160.8 0.1 add_add_fusion
  160.9 1.0 pad_maximum_fusion
  (10 shorter events, 0.0 us)
Async XLA Ops:
  0.0 40.3 %copy-start.1 = (f32[4096,128]{1,0:T(8,128)S(1)}, f32[4096,128]{1,0:T(8,128)}, u32[]{:S(2)}) copy-start(f32[4096,128]{1,0:T(8,128)} %refs_3_.11) | copy-start | bytes 6291460
  1.5 15.8 %collective-permute-start.1 = (f32[64,2048]{1,0:T(8,128)S(1)}, f32[64,2048]{1,0:T(8,128)S(1)}, u32[]{:S(2)}, u32[]{:S(2)}) collective-permute-start(f32[64,2048]{1,0:T(8,128)S(1)} %get-tuple-element.35.refs_0_), channel_id=1, source_target_pairs={{0,1},{1,0},{2,3},{3,2},{4,5},{5,4},{6,7},{7,6},{8,9},{9,8},{10,11... | collective-permute-start | bytes 1572872 | tf_op jit(solution)/shard_map/ppermute | solution.py:210
  4.5 23.2 %collective-permute-start = (f32[64,2048]{1,0:T(8,128)S(1)}, f32[64,2048]{1,0:T(8,128)S(1)}, u32[]{:S(2)}, u32[]{:S(2)}) collective-permute-start(f32[64,2048]{1,0:T(8,128)S(1)} %get-tuple-element.36.refs_0_), channel_id=1, source_target_pairs={{0,1},{1,0},{2,3},{3,2},{4,5},{5,4},{6,7},{7,6},{8,9},{9,8},{10,11... | collective-permute-start | bytes 1572872 | tf_op jit(solution)/shard_map/ppermute | solution.py:210
  4.6 23.8 %collective-permute-start.5 = (f32[64,2048]{1,0:T(8,128)S(1)}, f32[64,2048]{1,0:T(8,128)S(1)}, u32[]{:S(2)}, u32[]{:S(2)}) collective-permute-start(f32[64,2048]{1,0:T(8,128)S(1)} %get-tuple-element.35.refs_0_), channel_id=1, source_target_pairs={{1,2},{2,1},{5,6},{6,5},{9,10},{10,9},{13,14},{14,13},{17,18},{18,... | collective-permute-start | bytes 1572872 | tf_op jit(solution)/shard_map/ppermute | solution.py:210
  5.3 24.4 %collective-permute-start.3 = (f32[64,2048]{1,0:T(8,128)S(1)}, f32[64,2048]{1,0:T(8,128)S(1)}, u32[]{:S(2)}, u32[]{:S(2)}) collective-permute-start(f32[64,2048]{1,0:T(8,128)S(1)} %get-tuple-element.36.refs_0_), channel_id=1, source_target_pairs={{1,2},{2,1},{5,6},{6,5},{9,10},{10,9},{13,14},{14,13},{17,18},{18,... | collective-permute-start | bytes 1572872 | tf_op jit(solution)/shard_map/ppermute | solution.py:210
  17.3 28.9 %collective-permute-start.10 = (f32[64,2048]{1,0:T(8,128)S(1)}, f32[64,2048]{1,0:T(8,128)S(1)}, u32[]{:S(2)}, u32[]{:S(2)}) collective-permute-start(f32[64,2048]{1,0:T(8,128)S(1)} %collective-permute-done.1.refs_1_), channel_id=1, source_target_pairs={{1,2},{2,1},{5,6},{6,5},{9,10},{10,9},{13,14},{14,13},{17,18},{18,... | collective-permute-start | bytes 1572872 | tf_op jit(solution)/shard_map/ppermute | solution.py:210
  27.7 19.8 %collective-permute-start.8 = (f32[64,2048]{1,0:T(8,128)S(1)}, f32[64,2048]{1,0:T(8,128)S(1)}, u32[]{:S(2)}, u32[]{:S(2)}) collective-permute-start(f32[64,2048]{1,0:T(8,128)S(1)} %collective-permute-done.refs_1_), channel_id=1, source_target_pairs={{1,2},{2,1},{5,6},{6,5},{9,10},{10,9},{13,14},{14,13},{17,18},{18,... | collective-permute-start | bytes 1572872 | tf_op jit(solution)/shard_map/ppermute | solution.py:210
  28.4 20.5 %collective-permute-start.6 = (f32[64,2048]{1,0:T(8,128)S(1)}, f32[64,2048]{1,0:T(8,128)S(1)}, u32[]{:S(2)}, u32[]{:S(2)}) collective-permute-start(f32[64,2048]{1,0:T(8,128)S(1)} %collective-permute-done.5.refs_0_), channel_id=1, source_target_pairs={{1,0},{2,3},{5,4},{6,7},{9,8},{10,11},{13,12},{14,15},{17,16},{18,... | collective-permute-start | bytes 1572872 | tf_op jit(solution)/shard_map/ppermute | solution.py:210
  29.7 28.6 %collective-permute-start.4 = (f32[64,2048]{1,0:T(8,128)S(1)}, f32[64,2048]{1,0:T(8,128)S(1)}, u32[]{:S(2)}, u32[]{:S(2)}) collective-permute-start(f32[64,2048]{1,0:T(8,128)S(1)} %collective-permute-done.3.refs_0_), channel_id=1, source_target_pairs={{1,0},{2,3},{5,4},{6,7},{9,8},{10,11},{13,12},{14,15},{17,16},{18,... | collective-permute-start | bytes 1572872 | tf_op jit(solution)/shard_map/ppermute | solution.py:210
  31.0 1.6 copy-start
  32.6 1.6 copy-start.2
  34.2 6.1 %copy-start.3 = (f32[4096,128]{1,0:T(8,128)S(1)}, f32[4096,128]{1,0:T(8,128)}, u32[]{:S(2)}) copy-start(f32[4096,128]{1,0:T(8,128)} %refs_4_.11) | copy-start | bytes 6291460
  46.2 23.3 %collective-permute-start.11 = (f32[64,2048]{1,0:T(8,128)S(1)}, f32[64,2048]{1,0:T(8,128)S(1)}, u32[]{:S(2)}, u32[]{:S(2)}) collective-permute-start(f32[64,2048]{1,0:T(8,128)S(1)} %collective-permute-done.10.refs_0_), channel_id=1, source_target_pairs={{1,0},{2,3},{5,4},{6,7},{9,8},{10,11},{13,12},{14,15},{17,16},{18,... | collective-permute-start | bytes 1572872 | tf_op jit(solution)/shard_map/ppermute | solution.py:210
  47.5 31.1 %collective-permute-start.9 = (f32[64,2048]{1,0:T(8,128)S(1)}, f32[64,2048]{1,0:T(8,128)S(1)}, u32[]{:S(2)}, u32[]{:S(2)}) collective-permute-start(f32[64,2048]{1,0:T(8,128)S(1)} %collective-permute-done.8.refs_0_), channel_id=1, source_target_pairs={{1,0},{2,3},{5,4},{6,7},{9,8},{10,11},{13,12},{14,15},{17,16},{18,... | collective-permute-start | bytes 1572872 | tf_op jit(solution)/shard_map/ppermute | solution.py:210
  48.8 35.3 %collective-permute-start.2 = (f32[128,1280]{1,0:T(8,128)S(1)}, f32[128,1280]{1,0:T(8,128)S(1)}, u32[]{:S(2)}, u32[]{:S(2)}) collective-permute-start(f32[128,1280]{1,0:T(8,128)S(1)} %project.7.refs_0_), channel_id=1, source_target_pairs={{0,4},{4,0},{1,5},{5,1},{2,6},{6,2},{3,7},{7,3},{8,12},{12,8},{9,1... | collective-permute-start | bytes 1966088 | tf_op jit(solution)/shard_map/ppermute | solution.py:213
  63.7 20.5 %collective-permute-start.7 = (f32[64,1280]{1,0:T(8,128)S(1)}, f32[64,1280]{1,0:T(8,128)S(1)}, u32[]{:S(2)}, u32[]{:S(2)}) collective-permute-start(f32[64,1280]{1,0:T(8,128)S(1)} %project.9.refs_2_), channel_id=1, source_target_pairs={{0,4},{4,0},{1,5},{5,1},{2,6},{6,2},{3,7},{7,3},{8,12},{12,8},{9,1... | collective-permute-start | bytes 983048 | tf_op jit(solution)/shard_map/ppermute | solution.py:213
  84.1 1.7 %collective-permute-start.12 = (f32[64,1280]{1,0:T(8,128)S(1)}, f32[64,1280]{1,0:T(8,128)S(1)}, u32[]{:S(2)}, u32[]{:S(2)}) collective-permute-start(f32[64,1280]{1,0:T(8,128)S(1)} %project.11.refs_4_), channel_id=1, source_target_pairs={{0,4},{4,0},{1,5},{5,1},{2,6},{6,2},{3,7},{7,3},{8,12},{12,8},{9,1... | collective-permute-start | bytes 983048 | tf_op jit(solution)/shard_map/ppermute | solution.py:213
  91.6 18.3 %collective-permute-start.13 = (f32[64,2048]{1,0:T(8,128)S(1)}, f32[64,2048]{1,0:T(8,128)S(1)}, u32[]{:S(2)}, u32[]{:S(2)}) collective-permute-start(f32[64,2048]{1,0:T(8,128)S(1)} %get-tuple-element.22), channel_id=1, source_target_pairs={{0,1},{3,2},{4,5},{7,6},{8,9},{11,10},{12,13},{15,14},{16,17},{19,... | collective-permute-start | bytes 1572872 | tf_op jit(solution)/shard_map/ppermute | solution.py:210
  98.1 21.7 %collective-permute-start.18 = (f32[64,2048]{1,0:T(8,128)S(1)}, f32[64,2048]{1,0:T(8,128)S(1)}, u32[]{:S(2)}, u32[]{:S(2)}) collective-permute-start(f32[64,2048]{1,0:T(8,128)S(1)} %out_again.2), channel_id=1, source_target_pairs={{0,1},{3,2},{4,5},{7,6},{8,9},{11,10},{12,13},{15,14},{16,17},{19,... | collective-permute-start | bytes 1572872 | tf_op jit(solution)/shard_map/ppermute | solution.py:210
  108.5 19.3 %collective-permute-start.16 = (f32[64,2048]{1,0:T(8,128)S(1)}, f32[64,2048]{1,0:T(8,128)S(1)}, u32[]{:S(2)}, u32[]{:S(2)}) collective-permute-start(f32[64,2048]{1,0:T(8,128)S(1)} %get-tuple-element.29), channel_id=1, source_target_pairs={{0,1},{3,2},{4,5},{7,6},{8,9},{11,10},{12,13},{15,14},{16,17},{19,... | collective-permute-start | bytes 1572872 | tf_op jit(solution)/shard_map/ppermute | solution.py:210
  109.9 18.6 %collective-permute-start.14 = (f32[64,2048]{1,0:T(8,128)S(1)}, f32[64,2048]{1,0:T(8,128)S(1)}, u32[]{:S(2)}, u32[]{:S(2)}) collective-permute-start(f32[64,2048]{1,0:T(8,128)S(1)} %add.30), channel_id=1, source_target_pairs={{1,2},{2,1},{5,6},{6,5},{9,10},{10,9},{13,14},{14,13},{17,18},{18,... | collective-permute-start | bytes 1572872 | tf_op jit(solution)/shard_map/ppermute | solution.py:210
  116.4 22.6 %collective-permute-start.21 = (f32[64,2048]{1,0:T(8,128)S(1)}, f32[64,2048]{1,0:T(8,128)S(1)}, u32[]{:S(2)}, u32[]{:S(2)}) collective-permute-start(f32[64,2048]{1,0:T(8,128)S(1)} %get-tuple-element.34), channel_id=1, source_target_pairs={{0,1},{3,2},{4,5},{7,6},{8,9},{11,10},{12,13},{15,14},{16,17},{19,... | collective-permute-start | bytes 1572872 | tf_op jit(solution)/shard_map/ppermute | solution.py:210
  119.9 19.9 %collective-permute-start.19 = (f32[64,2048]{1,0:T(8,128)S(1)}, f32[64,2048]{1,0:T(8,128)S(1)}, u32[]{:S(2)}, u32[]{:S(2)}) collective-permute-start(f32[64,2048]{1,0:T(8,128)S(1)} %add.35), channel_id=1, source_target_pairs={{1,2},{2,1},{5,6},{6,5},{9,10},{10,9},{13,14},{14,13},{17,18},{18,... | collective-permute-start | bytes 1572872 | tf_op jit(solution)/shard_map/ppermute | solution.py:210
  127.8 16.7 %collective-permute-start.17 = (f32[64,2048]{1,0:T(8,128)S(1)}, f32[64,2048]{1,0:T(8,128)S(1)}, u32[]{:S(2)}, u32[]{:S(2)}) collective-permute-start(f32[64,2048]{1,0:T(8,128)S(1)} %add.32), channel_id=1, source_target_pairs={{1,2},{2,1},{5,6},{6,5},{9,10},{10,9},{13,14},{14,13},{17,18},{18,... | collective-permute-start | bytes 1572872 | tf_op jit(solution)/shard_map/ppermute | solution.py:210
  128.6 21.6 %collective-permute-start.15 = (f32[64,2048]{1,0:T(8,128)S(1)}, f32[64,2048]{1,0:T(8,128)S(1)}, u32[]{:S(2)}, u32[]{:S(2)}) collective-permute-start(f32[64,2048]{1,0:T(8,128)S(1)} %add.31), channel_id=1, source_target_pairs={{0,1},{1,0},{2,3},{3,2},{4,5},{5,4},{6,7},{7,6},{8,9},{9,8},{10,11... | collective-permute-start | bytes 1572872 | tf_op jit(solution)/shard_map/ppermute | solution.py:210
  139.1 11.3 %collective-permute-start.22 = (f32[64,2048]{1,0:T(8,128)S(1)}, f32[64,2048]{1,0:T(8,128)S(1)}, u32[]{:S(2)}, u32[]{:S(2)}) collective-permute-start(f32[64,2048]{1,0:T(8,128)S(1)} %add.37), channel_id=1, source_target_pairs={{1,2},{2,1},{5,6},{6,5},{9,10},{10,9},{13,14},{14,13},{17,18},{18,... | collective-permute-start | bytes 1572872 | tf_op jit(solution)/shard_map/ppermute | solution.py:210
  139.9 20.9 %collective-permute-start.20 = (f32[64,2048]{1,0:T(8,128)S(1)}, f32[64,2048]{1,0:T(8,128)S(1)}, u32[]{:S(2)}, u32[]{:S(2)}) collective-permute-start(f32[64,2048]{1,0:T(8,128)S(1)} %add.36), channel_id=1, source_target_pairs={{0,1},{1,0},{2,3},{3,2},{4,5},{5,4},{6,7},{7,6},{8,9},{9,8},{10,11... | collective-permute-start | bytes 1572872 | tf_op jit(solution)/shard_map/ppermute | solution.py:210

commit v3 on v2

--- a/solution.py
+++ b/solution.py
@@ -20,6 +20,8 @@
 PAIRS = [(0, 1), (1, 0), (2, 3), (3, 2)]
 MIDDLE = [(1, 2), (2, 1)]
 CORES = [(0, 1), (1, 0)]
+
+OUT_EIGHTHS = (4, 4)
 
 
 def split(a):
@@ -61,23 +63,25 @@
         offset += width
 
 
-def project(blocks, weights, chunk, total=None, step=512):
+def project(blocks, weights, start, depth, total=None, step=512):
     terms = tuple(len(b) for b in blocks)
-    flat = [a for b in blocks for a in b]
-    depth = flat[0].shape[1]
-    rows = sum(b[0].shape[0] for b in blocks)
-    steps = depth // step
+    flat = [t for b in blocks for t in b]
+    rows = sum(b[0][0].shape[0] for b in blocks)
     width = sum(w.shape[1] for w in weights)
-    first = chunk * steps
-    in_specs = [pl.BlockSpec((a.shape[0], step), lambda k: (0, k)) for a in flat]
+    first = start // step
+
+    def columns(a, at):
+        return pl.BlockSpec((a.shape[0], step), lambda k: (0, at // step + k))
+
+    in_specs = [columns(a, at) for a, at in flat]
     in_specs += [pl.BlockSpec((step, w.shape[1]), lambda k: (first + k, 0)) for w in weights]
-    operands = flat + list(weights)
+    operands = [a for a, _ in flat] + list(weights)
     if total is not None:
         in_specs.append(pl.BlockSpec((rows, width), lambda k: (0, 0)))
         operands.append(total)
     return pl.pallas_call(
         functools.partial(project_kernel, terms, total is not None),
-        grid=(steps,),
+        grid=(depth // step,),
         in_specs=in_specs,
         out_specs=pl.BlockSpec((rows, width), lambda k: (0, 0)),
         out_shape=jax.ShapeDtypeStruct((rows, width), jnp.float32),
@@ -197,14 +201,16 @@
     return lax.optimization_barrier((a, *others))[0]
 
 
-CHUNKS = 2
+def cut(sizes):
+    return [(sum(sizes[:i]), size) for i, size in enumerate(sizes)]
 
 
 def on_line_of_four(tokens, w_query, w_key, w_value, w_out):
     rows, depth = tokens.shape
     weights = (w_query, w_key, w_value)
     kv_width = w_key.shape[1]
-    step = depth // CHUNKS
+    halves = cut([depth // 2] * 2)
+    last = cut([depth // 2, depth // 4, depth // 4])
 
     def hop(a, pairs):
         return lax.ppermute(a, "col", pairs)
@@ -212,38 +218,41 @@
     def swap(a):
         return lax.ppermute(a, "row", CORES)
 
-    def run(blocks, total=None):
-        for c in range(CHUNKS):
-            total = project(blocks(c), weights, c, total)
-        return total
-
-    own = [tokens[:, c * step : (c + 1) * step] for c in range(CHUNKS)]
+    def columns(a, start, size):
+        return a[:, start : start + size]
+
+    own = [columns(tokens, *h) for h in halves]
     near = [hop(a, PAIRS) for a in own]
     mid = [hop(a, MIDDLE) for a in own]
+    mid2 = [hop(a, MIDDLE) for a in near]
     end2 = [hop(a, ENDS_IN) for a in mid]
-    mid2 = [hop(a, MIDDLE) for a in near]
-    first = run(lambda c: [(own[c],), (near[c],)])
-    mid2 = [after(a, first) for a in mid2]
-    first = (first, swap(first))
-    end3 = [hop(a, ENDS_IN) for a in mid2]
-    second = run(lambda c: [(mid[c], end2[c])])
-    second = (second, swap(second))
-    third = run(lambda c: [(mid2[c], end3[c])])
+    first = second = third = None
+    for h, o, n in zip(halves, own, near):
+        first = project([((o, 0),), ((n, 0),)], weights, *h, first)
+    mid2[0] = after(mid2[0], first)
+    second = project([((mid[0], 0), (end2[0], 0))], weights, *halves[0])
+    mid2[1] = after(mid2[1], second)
+    second = project([((mid[1], 0), (end2[1], 0))], weights, *halves[1], second)
+    first, second = [(a, swap(a)) for a in (first, second)]
+    for start, size in last:
+        half = start // halves[0][1]
+        at = start - halves[half][0]
+        end3 = hop(columns(mid2[half], at, size) if size < halves[0][1] else mid2[half], ENDS_IN)
+        third = project([((mid2[half], at), (end3, 0))], weights, start, size, third)
     third = (third, swap(third))
 
-    columns = w_out.shape[1] // CHUNKS
+    width = w_out.shape[1]
+    pieces = cut([width // 8 * n for n in OUT_EIGHTHS])
     parts = [first, second, third]
-    a_third, m_third = attend_out(parts, 2, 3, w_out, kv_width, [rows], columns)
-    m_third = [m_third[0]] + [
-        out_again(a_third, w_out, [rows], c * columns, columns)[0] for c in range(1, CHUNKS)
-    ]
+    a_third, m_third = attend_out(parts, 2, 3, w_out, kv_width, [rows], pieces[0][1])
+    m_third = list(m_third) + [out_again(a_third, w_out, [rows], *p)[0] for p in pieces[1:]]
     r1 = [hop(m, ENDS_OUT) for m in m_third]
     others = [tuple(after(a, *m_third) for a in first), second, third]
-    a_rest, mixed = attend_out(others, 0, 2, w_out, kv_width, [rows] * 3, columns)
+    a_rest, mixed = attend_out(others, 0, 2, w_out, kv_width, [rows] * 3, pieces[0][1])
     result = []
-    for c in range(CHUNKS):
+    for c, piece in enumerate(pieces):
         if c > 0:
-            mixed = out_again(a_rest, w_out, [rows] * 3, c * columns, columns)
+            mixed = out_again(a_rest, w_out, [rows] * 3, *piece)
         m_own, m_near, m_second = mixed
         r2e = hop(m_second, ENDS_OUT)
         r2m = hop(m_third[c] + r1[c], MIDDLE)

time: 163 us -> 156 us (0.957)
  waiting for transfers between devices: 65.2 us -> 46.8 us
  starting transfers between devices: 31 us -> 42 us
    ppermute x20 -> x21, waiting for transfers between devices: 63.6 us -> 45.2 us  [hop(): return lax.ppermute(a, 'col', pairs)]
    ppermute x20 -> x21, starting transfers between devices: 30.7 us -> 41.3 us  [hop(): return lax.ppermute(a, 'col', pairs)]
    pallas_call x6 -> x7, Pallas kernels: 33.5 us -> 34 us  [project(): pl.pallas_call(functools.partial(project_kernel, terms, total is not None...]
  transfers between devices with their start and end apart: 23 -> 24, of which waited for: 10 -> 9; matrix products, arithmetic and copies ran while one was open for 0% -> 0% of each run, Pallas kernels for 33% -> 35%
where the time goes in v3:
time: 156 us; the launch traced here: 155 us
  Pallas kernels  59.6 us (38%)
  waiting for transfers between devices  46.8 us (30%)
  starting transfers between devices  42 us (27%)
  local copies, waits for them, and re-layouts  4.67 us (3%)
  other arithmetic  1.57 us (1%)
    ppermute x21, waiting for transfers between devices, hop(): return lax.ppermute(a, 'col', pairs)  45.2 us
    ppermute x21, starting transfers between devices, hop(): return lax.ppermute(a, 'col', pairs)  41.3 us
    pallas_call x7, Pallas kernels, project(): pl.pallas_call(functools.partial(project_kernel, terms, total is not None...  34 us
    pallas_call x2, Pallas kernels, attend_out(): pl.pallas_call(functools.partial(attend_out_kernel, len(parts), first, la...  14.8 us
    pallas_call x2, Pallas kernels, out_again(): pl.pallas_call(mix_kernel, grid=(columns // step,), in_specs=[whole, whol...  10.8 us
    unnamed x8, local copies, waits for them, and re-layouts  3.18 us
  transfers between devices with their start and end apart: 24, of which 9 were waited for; matrix products, arithmetic and copies ran while one was open for 0% of the time, Pallas kernels for 35%

profile of v3, /device:TPU:0, one launch (start us, length us, event | category | flops | bytes accessed | tf_op | source)
XLA Modules:
  0.0 155.1 jit_solution(10433654056917255169)
XLA Ops:
  0.0 1.4 fusion
  1.5 3.1 %collective-permute-start.1 = (f32[64,2048]{1,0:T(8,128)S(1)}, f32[64,2048]{1,0:T(8,128)S(1)}, u32[]{:S(2)}, u32[]{:S(2)}) collective-permute-start(f32[64,2048]{1,0:T(8,128)S(1)} %get-tuple-element.35.refs_0_), channel_id=1, source_target_pairs={{0,1},{1,0},{2,3},{3,2},{4,5},{5,4},{6,7},{7,6},{8,9},{9,8},{10,11... | collective-permute-start | bytes 1572872 | tf_op jit(solution)/shard_map/ppermute | solution.py:216
  4.5 0.7 collective-permute-start.5
  5.2 4.4 %collective-permute-start = (f32[64,2048]{1,0:T(8,128)S(1)}, f32[64,2048]{1,0:T(8,128)S(1)}, u32[]{:S(2)}, u32[]{:S(2)}) collective-permute-start(f32[64,2048]{1,0:T(8,128)S(1)} %get-tuple-element.36.refs_0_), channel_id=1, source_target_pairs={{0,1},{1,0},{2,3},{3,2},{4,5},{5,4},{6,7},{7,6},{8,9},{9,8},{10,11... | collective-permute-start | bytes 1572872 | tf_op jit(solution)/shard_map/ppermute | solution.py:216
  9.7 0.7 collective-permute-start.3
  10.4 6.9 %collective-permute-done.1.refs_1_ = f32[64,2048]{1,0:T(8,128)S(1)} collective-permute-done((f32[64,2048]{1,0:T(8,128)S(1)}, f32[64,2048]{1,0:T(8,128)S(1)}, u32[]{:S(2)}, u32[]{:S(2)}) %collective-permute-start.1) | collective-permute-done | bytes 524320 | tf_op jit(solution)/shard_map/ppermute | solution.py:216
  17.3 0.7 collective-permute-start.11
  18.0 0.0 collective-permute-done.5.refs_0_
  18.0 1.3 collective-permute-start.6
  19.3 9.2 %collective-permute-done.refs_1_ = f32[64,2048]{1,0:T(8,128)S(1)} collective-permute-done((f32[64,2048]{1,0:T(8,128)S(1)}, f32[64,2048]{1,0:T(8,128)S(1)}, u32[]{:S(2)}, u32[]{:S(2)}) %collective-permute-start) | collective-permute-done | bytes 524320 | tf_op jit(solution)/shard_map/ppermute | solution.py:216
  28.5 0.7 collective-permute-start.8
  29.2 1.3 collective-permute-start.4
  30.5 0.0 copy-start
  30.5 1.6 %copy-done = f32[4096,128]{1,0:T(8,128)S(1)} copy-done((f32[4096,128]{1,0:T(8,128)S(1)}, f32[4096,128]{1,0:T(8,128)}, u32[]{:S(2)}) %copy-start) | copy-done | bytes 2097176
  32.1 1.6 %copy-done.2 = f32[4096,128]{1,0:T(8,128)S(1)} copy-done((f32[4096,128]{1,0:T(8,128)S(1)}, f32[4096,128]{1,0:T(8,128)}, u32[]{:S(2)}) %copy-start.2) | copy-done | bytes 2097176
  33.7 6.1 %project.7.refs_5_ = f32[128,1280]{1,0:T(8,128)S(1)} custom-call(f32[64,2048]{1,0:T(8,128)S(1)} %get-tuple-element.35.refs_0_, f32[64,2048]{1,0:T(8,128)S(1)} %collective-permute-done.1.refs_1_, f32[4096,1024]{1,0:T(8,128)} %refs_2_.13, f32[4096,128]{1,0:T(8,128)S(1)} %copy-done, f32[4096,128]{1,0:T(8,128)S(1)} %copy-done.2), custom_call_target="tpu_custom_call" | custom-call | flops 2013265920 | bytes 11534336 | tf_op jit(solution)/shard_map/project/pallas_call | solution.py:82
  39.8 5.9 %project.8.refs_0_ = f32[128,1280]{1,0:T(8,128)S(1)} custom-call(f32[64,2048]{1,0:T(8,128)S(1)} %get-tuple-element.36.refs_0_, f32[64,2048]{1,0:T(8,128)S(1)} %collective-permute-done.refs_1_, f32[4096,1024]{1,0:T(8,128)} %refs_2_.13, f32[4096,128]{1,0:T(8,128)S(1)} %copy-done.1, f32[4096,128]{1,0:T(8,128)S(1)} %copy-done.3, f32[128,1280]{1,0:T(8,128)S(1)} %project.7.refs_5_), custom_call_target="tpu_custom_call" | custom-call | flops 2013265920 | bytes 11534336 | tf_op jit(solution)/shard_map/project/pallas_call | solution.py:82
  45.7 1.3 collective-permute-start.12
  47.0 0.0 collective-permute-done.6.refs_1_
  47.1 5.4 %project.9.refs_5_ = f32[64,1280]{1,0:T(8,128)S(1)} custom-call(f32[64,2048]{1,0:T(8,128)S(1)} %collective-permute-done.5.refs_0_, f32[64,2048]{1,0:T(8,128)S(1)} %collective-permute-done.6.refs_1_, f32[4096,1024]{1,0:T(8,128)} %refs_2_.13, f32[4096,128]{1,0:T(8,128)S(1)} %copy-done.1, f32[4096,128]{1,0:T(8,128)S(1)} %copy-done.3), custom_call_target="tpu_custom_call" | custom-call | flops 1006632960 | bytes 11010048 | tf_op jit(solution)/shard_map/project/pallas_call | solution.py:82
  52.4 0.0 collective-permute-done.8.refs_0_
  52.5 1.3 collective-permute-start.10
  53.8 0.1 collective-permute-start.2
  53.9 1.3 collective-permute-start.9
  55.2 5.4 %project.10.refs_2_ = f32[64,1280]{1,0:T(8,128)S(1)} custom-call(f32[64,2048]{1,0:T(8,128)S(1)} %collective-permute-done.3.refs_0_, f32[64,2048]{1,0:T(8,128)S(1)} %collective-permute-done.4.refs_1_, f32[4096,1024]{1,0:T(8,128)} %refs_2_.13, f32[4096,128]{1,0:T(8,128)S(1)} %copy-done.1, f32[4096,128]{1,0:T(8,128)S(1)} %copy-done.3, ...), custom_call_target="tpu_custom_call" | custom-call | flops 1006632960 | bytes 11010048 | tf_op jit(solution)/shard_map/project/pallas_call | solution.py:82
  60.6 0.6 collective-permute-start.7
  61.1 3.1 %collective-permute-done.12.refs_1_ = f32[64,2048]{1,0:T(8,128)S(1)} collective-permute-done((f32[64,2048]{1,0:T(8,128)S(1)}, f32[64,2048]{1,0:T(8,128)S(1)}, u32[]{:S(2)}, u32[]{:S(2)}) %collective-permute-start.12) | collective-permute-done | bytes 524320 | tf_op jit(solution)/shard_map/ppermute | solution.py:216
  64.3 5.4 %project.11.refs_5_ = f32[64,1280]{1,0:T(8,128)S(1)} custom-call(f32[64,2048]{1,0:T(8,128)S(1)} %collective-permute-done.11.refs_0_, f32[64,2048]{1,0:T(8,128)S(1)} %collective-permute-done.12.refs_1_, f32[4096,1024]{1,0:T(8,128)} %refs_2_.13, f32[4096,128]{1,0:T(8,128)S(1)} %copy-done.1, f32[4096,128]{1,0:T(8,128)S(1)} %copy-done.3), custom_call_target="tpu_custom_call" | custom-call | flops 1006632960 | bytes 11010048 | tf_op jit(solution)/shard_map/project/pallas_call | solution.py:82
  69.6 0.2 collective-permute-done.10.refs_1_
  69.9 2.9 %project.12.refs_5_ = f32[64,1280]{1,0:T(8,128)S(1)} custom-call(f32[64,2048]{1,0:T(8,128)S(1)} %collective-permute-done.8.refs_0_, f32[64,1024]{1,0:T(8,128)S(1)} %collective-permute-done.10.refs_1_, f32[4096,1024]{1,0:T(8,128)} %refs_2_.13, f32[4096,128]{1,0:T(8,128)S(1)} %copy-done.1, f32[4096,128]{1,0:T(8,128)S(1)} %copy-done.3, ...), custom_call_target="tpu_custom_call" | custom-call | flops 503316480 | bytes 5505024 | tf_op jit(solution)/shard_map/project/pallas_call | solution.py:82
  72.8 0.0 collective-permute-done.9.refs_1_
  72.8 3.0 %project.13.refs_4_ = f32[64,1280]{1,0:T(8,128)S(1)} custom-call(f32[64,2048]{1,0:T(8,128)S(1)} %collective-permute-done.8.refs_0_, f32[64,1024]{1,0:T(8,128)S(1)} %collective-permute-done.9.refs_1_, f32[4096,1024]{1,0:T(8,128)} %refs_2_.13, f32[4096,128]{1,0:T(8,128)S(1)} %copy-done.1, f32[4096,128]{1,0:T(8,128)S(1)} %copy-done.3, ...), custom_call_target="tpu_custom_call" | custom-call | flops 503316480 | bytes 5505024 | tf_op jit(solution)/shard_map/project/pallas_call | solution.py:82
  75.8 0.1 collective-permute-start.13
  75.9 1.6 %collective-permute-done.13.refs_5_ = f32[64,1280]{1,0:T(8,128)S(1)} collective-permute-done((f32[64,1280]{1,0:T(8,128)S(1)}, f32[64,1280]{1,0:T(8,128)S(1)}, u32[]{:S(2)}, u32[]{:S(2)}) %collective-permute-start.13) | collective-permute-done | bytes 327712 | tf_op jit(solution)/shard_map/ppermute | solution.py:219
  77.5 5.8 %attend_out.2 = (bf16[64,1024]{1,0:T(8,128)(2,1)S(1)}, bf16[64,1024]{1,0:T(8,128)(2,1)S(1)}, f32[64,2048]{1,0:T(8,128)S(1)}) custom-call(f32[128,1280]{1,0:T(8,128)S(1)} %project.8.refs_0_, f32[128,1280]{1,0:T(8,128)S(1)} %collective-permute-done.2.refs_1_, f32[64,1280]{1,0:T(8,128)S(1)} %project.10.refs_2_, f32[64,1280]{1,0:T(8,128)S(1)} %collective-permute-done.7.refs_3_, ...), custom_call_target="tpu_custom_call" | custom-call | flops 1207959552 | bytes 8912896 | tf_op jit(solution)/shard_map/attend_out/pallas_call | solution.py:163
  83.3 3.0 %collective-permute-start.14 = (f32[64,2048]{1,0:T(8,128)S(1)}, f32[64,2048]{1,0:T(8,128)S(1)}, u32[]{:S(2)}, u32[]{:S(2)}) collective-permute-start(f32[64,2048]{1,0:T(8,128)S(1)} %get-tuple-element.22), channel_id=1, source_target_pairs={{0,1},{3,2},{4,5},{7,6},{8,9},{11,10},{12,13},{15,14},{16,17},{19,... | collective-permute-start | bytes 1572872 | tf_op jit(solution)/shard_map/ppermute | solution.py:216
  86.3 5.0 %out_again.2 = f32[64,2048]{1,0:T(8,128)S(1)} custom-call(bf16[64,1024]{1,0:T(8,128)(2,1)S(1)} %get-tuple-element.23.high, bf16[64,1024]{1,0:T(8,128)(2,1)S(1)} %get-tuple-element.24.low, f32[1024,4096]{1,0:T(8,128)} %w_ref.3), custom_call_target="tpu_custom_call" | custom-call | flops 805306368 | bytes 8912896 | tf_op jit(solution)/shard_map/out_again/pallas_call | solution.py:186
  91.4 1.3 collective-permute-start.19
  92.7 9.0 %attend_out.3 = (bf16[192,1024]{1,0:T(8,128)(2,1)S(1)}, bf16[192,1024]{1,0:T(8,128)(2,1)S(1)}, f32[64,2048]{1,0:T(8,128)S(1)}, f32[64,2048]{1,0:T(8,128)S(1)}, f32[64,2048]{1,0:T(8,128)S(1)}) custom-call(f32[128,1280]{1,0:T(8,128)S(1)} %project.8.refs_0_, f32[128,1280]{1,0:T(8,128)S(1)} %collective-permute-done.2.refs_1_, f32[64,1280]{1,0:T(8,128)S(1)} %project.10.refs_2_, ...), custom_call_target="tpu_custom_call" | custom-call | flops 3623878656 | bytes 9961472 | tf_op jit(solution)/shard_map/attend_out/pallas_call | solution.py:163
  101.7 1.3 collective-permute-start.17
  103.1 0.0 collective-permute-done.14
  103.1 0.1 add.30
  103.2 0.7 collective-permute-start.15
  103.9 5.8 %out_again.3 = (f32[64,2048]{1,0:T(8,128)S(1)}, f32[64,2048]{1,0:T(8,128)S(1)}, f32[64,2048]{1,0:T(8,128)S(1)}) custom-call(bf16[192,1024]{1,0:T(8,128)(2,1)S(1)} %get-tuple-element.30.high, bf16[192,1024]{1,0:T(8,128)(2,1)S(1)} %get-tuple-element.31.low, f32[1024,4096]{1,0:T(8,128)} %w_ref.3), custom_call_target="tpu_custom_call" | custom-call | flops 2415919104 | bytes 9961472 | tf_op jit(solution)/shard_map/out_again/pallas_call | solution.py:186
  109.7 4.5 %collective-permute-start.22 = (f32[64,2048]{1,0:T(8,128)S(1)}, f32[64,2048]{1,0:T(8,128)S(1)}, u32[]{:S(2)}, u32[]{:S(2)}) collective-permute-start(f32[64,2048]{1,0:T(8,128)S(1)} %get-tuple-element.34), channel_id=1, source_target_pairs={{0,1},{3,2},{4,5},{7,6},{8,9},{11,10},{12,13},{15,14},{16,17},{19,... | collective-permute-start | bytes 1572872 | tf_op jit(solution)/shard_map/ppermute | solution.py:216
  114.2 0.0 collective-permute-done.19
  114.2 0.1 add.35
  114.2 0.7 collective-permute-start.20
  114.9 6.1 %collective-permute-done.17 = f32[64,2048]{1,0:T(8,128)S(1)} collective-permute-done((f32[64,2048]{1,0:T(8,128)S(1)}, f32[64,2048]{1,0:T(8,128)S(1)}, u32[]{:S(2)}, u32[]{:S(2)}) %collective-permute-start.17) | collective-permute-done | bytes 524320 | tf_op jit(solution)/shard_map/ppermute | solution.py:216
  121.0 0.1 add.32
  121.1 0.7 collective-permute-start.18
  121.8 0.0 collective-permute-done.15
  121.8 0.1 add.31
  121.9 5.8 %collective-permute-start.16 = (f32[64,2048]{1,0:T(8,128)S(1)}, f32[64,2048]{1,0:T(8,128)S(1)}, u32[]{:S(2)}, u32[]{:S(2)}) collective-permute-start(f32[64,2048]{1,0:T(8,128)S(1)} %add.31), channel_id=1, source_target_pairs={{0,1},{1,0},{2,3},{3,2},{4,5},{5,4},{6,7},{7,6},{8,9},{9,8},{10,11... | collective-permute-start | bytes 1572872 | tf_op jit(solution)/shard_map/ppermute | solution.py:216
  127.7 4.6 %collective-permute-done.22 = f32[64,2048]{1,0:T(8,128)S(1)} collective-permute-done((f32[64,2048]{1,0:T(8,128)S(1)}, f32[64,2048]{1,0:T(8,128)S(1)}, u32[]{:S(2)}, u32[]{:S(2)}) %collective-permute-start.22) | collective-permute-done | bytes 524320 | tf_op jit(solution)/shard_map/ppermute | solution.py:216
  132.3 0.1 add.37
  132.4 0.7 collective-permute-start.23
  133.1 0.1 add.36
  133.1 5.8 %collective-permute-start.21 = (f32[64,2048]{1,0:T(8,128)S(1)}, f32[64,2048]{1,0:T(8,128)S(1)}, u32[]{:S(2)}, u32[]{:S(2)}) collective-permute-start(f32[64,2048]{1,0:T(8,128)S(1)} %add.36), channel_id=1, source_target_pairs={{0,1},{1,0},{2,3},{3,2},{4,5},{5,4},{6,7},{7,6},{8,9},{9,8},{10,11... | collective-permute-start | bytes 1572872 | tf_op jit(solution)/shard_map/ppermute | solution.py:216
  138.9 4.6 %collective-permute-done.16 = f32[64,2048]{1,0:T(8,128)S(1)} collective-permute-done((f32[64,2048]{1,0:T(8,128)S(1)}, f32[64,2048]{1,0:T(8,128)S(1)}, u32[]{:S(2)}, u32[]{:S(2)}) %collective-permute-start.16) | collective-permute-done | bytes 524320 | tf_op jit(solution)/shard_map/ppermute | solution.py:216
  143.5 0.1 add_add_fusion.1
  143.6 10.3 %collective-permute-done.21 = f32[64,2048]{1,0:T(8,128)S(1)} collective-permute-done((f32[64,2048]{1,0:T(8,128)S(1)}, f32[64,2048]{1,0:T(8,128)S(1)}, u32[]{:S(2)}, u32[]{:S(2)}) %collective-permute-start.21) | collective-permute-done | bytes 524320 | tf_op jit(solution)/shard_map/ppermute | solution.py:216
  153.9 0.1 add_add_fusion
  154.0 1.0 pad_maximum_fusion
  (14 shorter events, 0.1 us)
Async XLA Ops:
  0.0 39.8 %copy-start.1 = (f32[4096,128]{1,0:T(8,128)S(1)}, f32[4096,128]{1,0:T(8,128)}, u32[]{:S(2)}) copy-start(f32[4096,128]{1,0:T(8,128)} %refs_3_.13) | copy-start | bytes 6291460
  1.5 15.8 %collective-permute-start.1 = (f32[64,2048]{1,0:T(8,128)S(1)}, f32[64,2048]{1,0:T(8,128)S(1)}, u32[]{:S(2)}, u32[]{:S(2)}) collective-permute-start(f32[64,2048]{1,0:T(8,128)S(1)} %get-tuple-element.35.refs_0_), channel_id=1, source_target_pairs={{0,1},{1,0},{2,3},{3,2},{4,5},{5,4},{6,7},{7,6},{8,9},{9,8},{10,11... | collective-permute-start | bytes 1572872 | tf_op jit(solution)/shard_map/ppermute | solution.py:216
  4.5 13.4 %collective-permute-start.5 = (f32[64,2048]{1,0:T(8,128)S(1)}, f32[64,2048]{1,0:T(8,128)S(1)}, u32[]{:S(2)}, u32[]{:S(2)}) collective-permute-start(f32[64,2048]{1,0:T(8,128)S(1)} %get-tuple-element.35.refs_0_), channel_id=1, source_target_pairs={{1,2},{2,1},{5,6},{6,5},{9,10},{10,9},{13,14},{14,13},{17,18},{18,... | collective-permute-start | bytes 1572872 | tf_op jit(solution)/shard_map/ppermute | solution.py:216
  5.2 23.3 %collective-permute-start = (f32[64,2048]{1,0:T(8,128)S(1)}, f32[64,2048]{1,0:T(8,128)S(1)}, u32[]{:S(2)}, u32[]{:S(2)}) collective-permute-start(f32[64,2048]{1,0:T(8,128)S(1)} %get-tuple-element.36.refs_0_), channel_id=1, source_target_pairs={{0,1},{1,0},{2,3},{3,2},{4,5},{5,4},{6,7},{7,6},{8,9},{9,8},{10,11... | collective-permute-start | bytes 1572872 | tf_op jit(solution)/shard_map/ppermute | solution.py:216
  9.7 19.6 %collective-permute-start.3 = (f32[64,2048]{1,0:T(8,128)S(1)}, f32[64,2048]{1,0:T(8,128)S(1)}, u32[]{:S(2)}, u32[]{:S(2)}) collective-permute-start(f32[64,2048]{1,0:T(8,128)S(1)} %get-tuple-element.36.refs_0_), channel_id=1, source_target_pairs={{1,2},{2,1},{5,6},{6,5},{9,10},{10,9},{13,14},{14,13},{17,18},{18,... | collective-permute-start | bytes 1572872 | tf_op jit(solution)/shard_map/ppermute | solution.py:216
  17.3 28.4 %collective-permute-start.11 = (f32[64,2048]{1,0:T(8,128)S(1)}, f32[64,2048]{1,0:T(8,128)S(1)}, u32[]{:S(2)}, u32[]{:S(2)}) collective-permute-start(f32[64,2048]{1,0:T(8,128)S(1)} %collective-permute-done.1.refs_1_), channel_id=1, source_target_pairs={{1,2},{2,1},{5,6},{6,5},{9,10},{10,9},{13,14},{14,13},{17,18},{18,... | collective-permute-start | bytes 1572872 | tf_op jit(solution)/shard_map/ppermute | solution.py:216
  18.0 29.1 %collective-permute-start.6 = (f32[64,2048]{1,0:T(8,128)S(1)}, f32[64,2048]{1,0:T(8,128)S(1)}, u32[]{:S(2)}, u32[]{:S(2)}) collective-permute-start(f32[64,2048]{1,0:T(8,128)S(1)} %collective-permute-done.5.refs_0_), channel_id=1, source_target_pairs={{1,0},{2,3},{5,4},{6,7},{9,8},{10,11},{13,12},{14,15},{17,16},{18,... | collective-permute-start | bytes 1572872 | tf_op jit(solution)/shard_map/ppermute | solution.py:216
  28.5 23.9 %collective-permute-start.8 = (f32[64,2048]{1,0:T(8,128)S(1)}, f32[64,2048]{1,0:T(8,128)S(1)}, u32[]{:S(2)}, u32[]{:S(2)}) collective-permute-start(f32[64,2048]{1,0:T(8,128)S(1)} %collective-permute-done.refs_1_), channel_id=1, source_target_pairs={{1,2},{2,1},{5,6},{6,5},{9,10},{10,9},{13,14},{14,13},{17,18},{18,... | collective-permute-start | bytes 1572872 | tf_op jit(solution)/shard_map/ppermute | solution.py:216
  29.2 25.9 %collective-permute-start.4 = (f32[64,2048]{1,0:T(8,128)S(1)}, f32[64,2048]{1,0:T(8,128)S(1)}, u32[]{:S(2)}, u32[]{:S(2)}) collective-permute-start(f32[64,2048]{1,0:T(8,128)S(1)} %collective-permute-done.3.refs_0_), channel_id=1, source_target_pairs={{1,0},{2,3},{5,4},{6,7},{9,8},{10,11},{13,12},{14,15},{17,16},{18,... | collective-permute-start | bytes 1572872 | tf_op jit(solution)/shard_map/ppermute | solution.py:216
  30.5 1.6 %copy-start = (f32[4096,128]{1,0:T(8,128)S(1)}, f32[4096,128]{1,0:T(8,128)}, u32[]{:S(2)}) copy-start(f32[4096,128]{1,0:T(8,128)} %refs_3_.13) | copy-start | bytes 6291460
  32.1 1.6 %copy-start.2 = (f32[4096,128]{1,0:T(8,128)S(1)}, f32[4096,128]{1,0:T(8,128)}, u32[]{:S(2)}) copy-start(f32[4096,128]{1,0:T(8,128)} %refs_4_.13) | copy-start | bytes 6291460
  33.7 6.1 %copy-start.3 = (f32[4096,128]{1,0:T(8,128)S(1)}, f32[4096,128]{1,0:T(8,128)}, u32[]{:S(2)}) copy-start(f32[4096,128]{1,0:T(8,128)} %refs_4_.13) | copy-start | bytes 6291460
  45.7 18.5 %collective-permute-start.12 = (f32[64,2048]{1,0:T(8,128)S(1)}, f32[64,2048]{1,0:T(8,128)S(1)}, u32[]{:S(2)}, u32[]{:S(2)}) collective-permute-start(f32[64,2048]{1,0:T(8,128)S(1)} %collective-permute-done.11.refs_0_), channel_id=1, source_target_pairs={{1,0},{2,3},{5,4},{6,7},{9,8},{10,11},{13,12},{14,15},{17,16},{18,... | collective-permute-start | bytes 1572872 | tf_op jit(solution)/shard_map/ppermute | solution.py:216
  52.5 17.4 %collective-permute-start.10 = (f32[64,1024]{1,0:T(8,128)S(1)}, f32[64,1024]{1,0:T(8,128)S(1)}, u32[]{:S(2)}, u32[]{:S(2)}) collective-permute-start(f32[64,1024]{1,0:T(8,128)S(1)} %get-tuple-element.37), channel_id=1, source_target_pairs={{1,0},{2,3},{5,4},{6,7},{9,8},{10,11},{13,12},{14,15},{17,16},{18,... | collective-permute-start | bytes 786440 | tf_op jit(solution)/shard_map/ppermute | solution.py:216
  53.8 22.1 %collective-permute-start.2 = (f32[128,1280]{1,0:T(8,128)S(1)}, f32[128,1280]{1,0:T(8,128)S(1)}, u32[]{:S(2)}, u32[]{:S(2)}) collective-permute-start(f32[128,1280]{1,0:T(8,128)S(1)} %project.8.refs_0_), channel_id=1, source_target_pairs={{0,4},{4,0},{1,5},{5,1},{2,6},{6,2},{3,7},{7,3},{8,12},{12,8},{9,1... | collective-permute-start | bytes 1966088 | tf_op jit(solution)/shard_map/ppermute | solution.py:219
  53.9 19.0 %collective-permute-start.9 = (f32[64,1024]{1,0:T(8,128)S(1)}, f32[64,1024]{1,0:T(8,128)S(1)}, u32[]{:S(2)}, u32[]{:S(2)}) collective-permute-start(f32[64,1024]{1,0:T(8,128)S(1)} %get-tuple-element.38), channel_id=1, source_target_pairs={{1,0},{2,3},{5,4},{6,7},{9,8},{10,11},{13,12},{14,15},{17,16},{18,... | collective-permute-start | bytes 786440 | tf_op jit(solution)/shard_map/ppermute | solution.py:216
  60.6 15.3 %collective-permute-start.7 = (f32[64,1280]{1,0:T(8,128)S(1)}, f32[64,1280]{1,0:T(8,128)S(1)}, u32[]{:S(2)}, u32[]{:S(2)}) collective-permute-start(f32[64,1280]{1,0:T(8,128)S(1)} %project.10.refs_2_), channel_id=1, source_target_pairs={{0,4},{4,0},{1,5},{5,1},{2,6},{6,2},{3,7},{7,3},{8,12},{12,8},{9,1... | collective-permute-start | bytes 983048 | tf_op jit(solution)/shard_map/ppermute | solution.py:219
  75.8 1.7 %collective-permute-start.13 = (f32[64,1280]{1,0:T(8,128)S(1)}, f32[64,1280]{1,0:T(8,128)S(1)}, u32[]{:S(2)}, u32[]{:S(2)}) collective-permute-start(f32[64,1280]{1,0:T(8,128)S(1)} %project.13.refs_4_), channel_id=1, source_target_pairs={{0,4},{4,0},{1,5},{5,1},{2,6},{6,2},{3,7},{7,3},{8,12},{12,8},{9,1... | collective-permute-start | bytes 983048 | tf_op jit(solution)/shard_map/ppermute | solution.py:219
  83.3 19.8 %collective-permute-start.14 = (f32[64,2048]{1,0:T(8,128)S(1)}, f32[64,2048]{1,0:T(8,128)S(1)}, u32[]{:S(2)}, u32[]{:S(2)}) collective-permute-start(f32[64,2048]{1,0:T(8,128)S(1)} %get-tuple-element.22), channel_id=1, source_target_pairs={{0,1},{3,2},{4,5},{7,6},{8,9},{11,10},{12,13},{15,14},{16,17},{19,... | collective-permute-start | bytes 1572872 | tf_op jit(solution)/shard_map/ppermute | solution.py:216
  91.4 22.8 %collective-permute-start.19 = (f32[64,2048]{1,0:T(8,128)S(1)}, f32[64,2048]{1,0:T(8,128)S(1)}, u32[]{:S(2)}, u32[]{:S(2)}) collective-permute-start(f32[64,2048]{1,0:T(8,128)S(1)} %out_again.2), channel_id=1, source_target_pairs={{0,1},{3,2},{4,5},{7,6},{8,9},{11,10},{12,13},{15,14},{16,17},{19,... | collective-permute-start | bytes 1572872 | tf_op jit(solution)/shard_map/ppermute | solution.py:216
  101.7 19.3 %collective-permute-start.17 = (f32[64,2048]{1,0:T(8,128)S(1)}, f32[64,2048]{1,0:T(8,128)S(1)}, u32[]{:S(2)}, u32[]{:S(2)}) collective-permute-start(f32[64,2048]{1,0:T(8,128)S(1)} %get-tuple-element.29), channel_id=1, source_target_pairs={{0,1},{3,2},{4,5},{7,6},{8,9},{11,10},{12,13},{15,14},{16,17},{19,... | collective-permute-start | bytes 1572872 | tf_op jit(solution)/shard_map/ppermute | solution.py:216
  103.2 18.6 %collective-permute-start.15 = (f32[64,2048]{1,0:T(8,128)S(1)}, f32[64,2048]{1,0:T(8,128)S(1)}, u32[]{:S(2)}, u32[]{:S(2)}) collective-permute-start(f32[64,2048]{1,0:T(8,128)S(1)} %add.30), channel_id=1, source_target_pairs={{1,2},{2,1},{5,6},{6,5},{9,10},{10,9},{13,14},{14,13},{17,18},{18,... | collective-permute-start | bytes 1572872 | tf_op jit(solution)/shard_map/ppermute | solution.py:216
  109.7 22.6 %collective-permute-start.22 = (f32[64,2048]{1,0:T(8,128)S(1)}, f32[64,2048]{1,0:T(8,128)S(1)}, u32[]{:S(2)}, u32[]{:S(2)}) collective-permute-start(f32[64,2048]{1,0:T(8,128)S(1)} %get-tuple-element.34), channel_id=1, source_target_pairs={{0,1},{3,2},{4,5},{7,6},{8,9},{11,10},{12,13},{15,14},{16,17},{19,... | collective-permute-start | bytes 1572872 | tf_op jit(solution)/shard_map/ppermute | solution.py:216
  114.2 18.8 %collective-permute-start.20 = (f32[64,2048]{1,0:T(8,128)S(1)}, f32[64,2048]{1,0:T(8,128)S(1)}, u32[]{:S(2)}, u32[]{:S(2)}) collective-permute-start(f32[64,2048]{1,0:T(8,128)S(1)} %add.35), channel_id=1, source_target_pairs={{1,2},{2,1},{5,6},{6,5},{9,10},{10,9},{13,14},{14,13},{17,18},{18,... | collective-permute-start | bytes 1572872 | tf_op jit(solution)/shard_map/ppermute | solution.py:216
  121.1 17.8 %collective-permute-start.18 = (f32[64,2048]{1,0:T(8,128)S(1)}, f32[64,2048]{1,0:T(8,128)S(1)}, u32[]{:S(2)}, u32[]{:S(2)}) collective-permute-start(f32[64,2048]{1,0:T(8,128)S(1)} %add.32), channel_id=1, source_target_pairs={{1,2},{2,1},{5,6},{6,5},{9,10},{10,9},{13,14},{14,13},{17,18},{18,... | collective-permute-start | bytes 1572872 | tf_op jit(solution)/shard_map/ppermute | solution.py:216
  121.9 21.6 %collective-permute-start.16 = (f32[64,2048]{1,0:T(8,128)S(1)}, f32[64,2048]{1,0:T(8,128)S(1)}, u32[]{:S(2)}, u32[]{:S(2)}) collective-permute-start(f32[64,2048]{1,0:T(8,128)S(1)} %add.31), channel_id=1, source_target_pairs={{0,1},{1,0},{2,3},{3,2},{4,5},{5,4},{6,7},{7,6},{8,9},{9,8},{10,11... | collective-permute-start | bytes 1572872 | tf_op jit(solution)/shard_map/ppermute | solution.py:216
  132.4 11.2 %collective-permute-start.23 = (f32[64,2048]{1,0:T(8,128)S(1)}, f32[64,2048]{1,0:T(8,128)S(1)}, u32[]{:S(2)}, u32[]{:S(2)}) collective-permute-start(f32[64,2048]{1,0:T(8,128)S(1)} %add.37), channel_id=1, source_target_pairs={{1,2},{2,1},{5,6},{6,5},{9,10},{10,9},{13,14},{14,13},{17,18},{18,... | collective-permute-start | bytes 1572872 | tf_op jit(solution)/shard_map/ppermute | solution.py:216
  133.1 20.8 %collective-permute-start.21 = (f32[64,2048]{1,0:T(8,128)S(1)}, f32[64,2048]{1,0:T(8,128)S(1)}, u32[]{:S(2)}, u32[]{:S(2)}) collective-permute-start(f32[64,2048]{1,0:T(8,128)S(1)} %add.36), channel_id=1, source_target_pairs={{0,1},{1,0},{2,3},{3,2},{4,5},{5,4},{6,7},{7,6},{8,9},{9,8},{10,11... | collective-permute-start | bytes 1572872 | tf_op jit(solution)/shard_map/ppermute | solution.py:216

commit v4 on v3

v4 whole, which is shorter than its diff:
```python
import functools
import math

import jax
import jax.numpy as jnp
from jax import lax
from jax.experimental import pallas as pl
from jax.experimental.pallas import tpu as pltpu
from jax.sharding import PartitionSpec as P

QUERY_HEADS = 32
KEY_VALUE_HEADS = 4
HEAD_SIZE_DIM = 128
GROUP = QUERY_HEADS // KEY_VALUE_HEADS

VMEM_LIMIT = 38 * 1024 * 1024

ENDS_IN = [(1, 0), (2, 3)]
ENDS_OUT = [(0, 1), (3, 2)]
PAIRS = [(0, 1), (1, 0), (2, 3), (3, 2)]
MIDDLE = [(1, 2), (2, 1)]
CORES = [(0, 1), (1, 0)]


def split(a):
    high = a.astype(jnp.bfloat16)
    return high, (a - high.astype(jnp.float32)).astype(jnp.bfloat16)


def dot(a, b, dims=((1,), (0,))):
    return lax.dot_general(a, b, (dims, ((), ())), preferred_element_type=jnp.float32)


def dot3(a, b, dims=((1,), (0,))):
    rows = a[0].shape[0]
    both = dot(jnp.concatenate(a, axis=0), b[0], dims)
    return both[:rows] + (both[rows:] + dot(a[0], b[1], dims))


def project_kernel(terms, with_total, first, steps, step, n_before, *refs):
    n_x = sum(len(t) for t in terms)
    x_refs, w_refs, rest = refs[:n_x], refs[n_x : n_x + 3], refs[n_x + 3 :]
    total, rest = rest[0], rest[(1 if with_total else 0) + n_before :]
    out, kept, bufs, sems = rest[0], rest[1:-4], rest[-4:-1], rest[-1]

    def copies(k):
        rows = pl.ds(first + k * step, step)
        return [pltpu.make_async_copy(w.at[rows], b.at[k], sems.at[k, i]) for i, (w, b) in enumerate(zip(w_refs, bufs))]

    for k in range(bufs[0].shape[0]):
        for c in copies(k):
            c.start()
    for k in range(steps):
        blocks, i = [], 0
        for term in terms:
            block = None
            for at in term:
                piece = x_refs[i][:, at + k * step : at + (k + 1) * step]
                block = piece if block is None else block + piece
                i += 1
            blocks.append(block)
        x = split(jnp.concatenate(blocks, axis=0) if len(blocks) > 1 else blocks[0])
        for c in copies(k):
            c.wait()
        offset = 0
        for b in bufs:
            width = b.shape[2]
            columns = slice(offset, offset + width)
            product = dot3(x, split(b[k]))
            if k > 0:
                out[:, columns] += product
            elif with_total:
                out[:, columns] = total[:, columns] + product
            else:
                out[:, columns] = product
            offset += width
    for k in range(steps, bufs[0].shape[0]):
        for c in copies(k):
            c.wait()
        offset, rows = 0, slice((k - steps) * step, (k - steps + 1) * step)
        for b in bufs:
            columns = slice(offset, offset + b.shape[2])
            kept[0][rows, columns], kept[1][rows, columns] = split(b[k])
            offset += b.shape[2]


def project(blocks, weights, start, depth, total=None, keep=0, before=(), step=512):
    terms = tuple(tuple(at for _, at in b) for b in blocks)
    operands = [a for b in blocks for a, _ in b]
    rows = sum(b[0][0].shape[0] for b in blocks)
    width = sum(w.shape[1] for w in weights)
    steps = depth // step
    vmem, anywhere = pl.BlockSpec(memory_space=pltpu.VMEM), pl.BlockSpec(memory_space=pl.ANY)
    in_specs = [vmem] * len(operands) + [anywhere] * len(weights)
    operands += weights
    if total is not None:
        in_specs.append(vmem)
        operands.append(total)
    in_specs += [anywhere] * len(before)
    operands += before
    return pl.pallas_call(
        functools.partial(project_kernel, terms, total is not None, start, steps, step, len(before)),
        in_specs=in_specs,
        out_specs=[vmem] * 3 if keep else vmem,
        out_shape=[jax.ShapeDtypeStruct((rows, width), jnp.float32)]
        + [jax.ShapeDtypeStruct((keep, width), jnp.bfloat16)] * 2
        if keep
        else jax.ShapeDtypeStruct((rows, width), jnp.float32),
        scratch_shapes=[pltpu.VMEM((steps + keep // step, step, w.shape[1]), jnp.float32) for w in weights]
        + [pltpu.SemaphoreType.DMA((steps + keep // step, len(weights)))],
        compiler_params=pltpu.CompilerParams(vmem_limit_bytes=VMEM_LIMIT),
        cost_estimate=pl.CostEstimate(
            flops=6 * rows * depth * width, bytes_accessed=4 * depth * (rows + width), transcendentals=0
        ),
        name="project",
    )(*operands)


def project_last_kernel(at, x, y, high, low, total, out):
    size = y.shape[1]
    block = split(x[:, at : at + size] + y[...])
    out[...] = total[...] + dot3(block, (high[...], low[...]))


def project_last(block, kept, total):
    (x, at), (y, _) = block
    vmem = pl.BlockSpec(memory_space=pltpu.VMEM)
    return pl.pallas_call(
        functools.partial(project_last_kernel, at),
        in_specs=[vmem] * 5,
        out_specs=vmem,
        out_shape=jax.ShapeDtypeStruct(total.shape, jnp.float32),
        compiler_params=pltpu.CompilerParams(vmem_limit_bytes=VMEM_LIMIT),
        cost_estimate=pl.CostEstimate(
            flops=6 * y.shape[1] * total.size, bytes_accessed=4 * y.shape[1] * total.shape[1], transcendentals=0
        ),
        name="project_last",
    )(x, y, *kept, total)


def attend(keyed, asked, q_width, kv_width, store):
    groups = kv_width // HEAD_SIZE_DIM
    scale = 1.0 / math.sqrt(HEAD_SIZE_DIM)

    def columns(pairs, start):
        stop = start + HEAD_SIZE_DIM
        return jnp.concatenate([a[:, start:stop] + b[:, start:stop] for a, b in pairs], axis=0)

    rows = sum(a.shape[0] for a, _ in asked)
    together = GROUP if rows <= 64 else 1
    for g in range(groups):
        at = q_width + g * HEAD_SIZE_DIM
        k_high, k_low = split(columns(keyed, at))
        v_high, v_low = split(columns(keyed, at + kv_width))
        k_both = jnp.concatenate([k_high, k_high], axis=1)
        v_both = jnp.concatenate([v_high, v_low], axis=1)
        for j in range(0, GROUP, together):
            heads = [(g * GROUP + j + i) * HEAD_SIZE_DIM for i in range(together)]
            q_high, q_low = split(jnp.concatenate([columns(asked, h) for h in heads], axis=0) * scale)
            scores = dot(jnp.concatenate([q_high, q_low], axis=1), k_both, ((1,), (1,)))
            scores = scores + dot(q_high, k_low, ((1,), (1,)))
            weights = jnp.exp(scores - jnp.max(scores, axis=-1, keepdims=True))
            total = jnp.sum(weights, axis=-1, keepdims=True)
            p_high, p_low = split(weights)
            both = dot(p_high, v_both)
            result = both[:, :HEAD_SIZE_DIM] + (both[:, HEAD_SIZE_DIM:] + dot(p_low, v_high))
            result = result / total
            for i, h in enumerate(heads):
                store(h, result[i * rows : (i + 1) * rows])


def halve_kernel(start, w_ref, before, high, low, buf, sems):
    steps, step, size = buf.shape

    def copy(k):
        return pltpu.make_async_copy(w_ref.at[pl.ds(k * step, step), pl.ds(start, size)], buf.at[k], sems.at[k])

    for k in range(steps):
        copy(k).start()
    for k in range(steps):
        copy(k).wait()
        rows = slice(k * step, (k + 1) * step)
        high[rows], low[rows] = split(buf[k])


def halve(w, start, size, before, step=256):
    steps = w.shape[0] // step
    vmem, anywhere = pl.BlockSpec(memory_space=pltpu.VMEM), pl.BlockSpec(memory_space=pl.ANY)
    return pl.pallas_call(
        functools.partial(halve_kernel, start),
        in_specs=[anywhere] * 2,
        out_specs=[vmem] * 2,
        out_shape=[jax.ShapeDtypeStruct((w.shape[0], size), jnp.bfloat16)] * 2,
        scratch_shapes=[pltpu.VMEM((steps, step, size), jnp.float32), pltpu.SemaphoreType.DMA((steps,))],
        compiler_params=pltpu.CompilerParams(vmem_limit_bytes=VMEM_LIMIT),
        cost_estimate=pl.CostEstimate(flops=w.shape[0] * size, bytes_accessed=8 * w.shape[0] * size, transcendentals=0),
        name="halve",
    )(w, before)


def mix_kernel(n_parts, ask, q_width, kv_width, start, step, *refs):
    part_refs, rest = refs[:n_parts], refs[n_parts:]
    if start is None:
        (w_high, w_low), outs = rest[:2], rest[2:]
    else:
        w_ref, outs, (buf, sems) = rest[0], rest[1:-2], rest[-2:]

        def copy(k):
            return pltpu.make_async_copy(w_ref.at[:, pl.ds(start + k * step, step)], buf.at[k], sems.at[k])

        for k in range(buf.shape[0]):
            copy(k).start()
    if ask is None:
        high, low = part_refs
    else:
        high, low, outs = outs[0], outs[1], outs[2:]

        def store(head, rows):
            h, l = split(rows)
            high[:, head : head + HEAD_SIZE_DIM] = h
            low[:, head : head + HEAD_SIZE_DIM] = l

        pairs = [(part_refs[2 * i], part_refs[2 * i + 1]) for i in range(n_parts // 2)]
        attend(pairs, pairs[ask], q_width, kv_width, store)
    attended = (high[...], low[...])
    for k in range(outs[0].shape[1] // step):
        columns = slice(k * step, (k + 1) * step)
        if start is None:
            w = (w_high[:, columns], w_low[:, columns])
        else:
            copy(k).wait()
            w = split(buf[k])
        mixed = dot3(attended, w)
        at = 0
        for o in outs:
            o[:, columns] = mixed[at : at + o.shape[0]]
            at += o.shape[0]


def mix(operands, ask, rows, keyed, w, kv_width, slots, start, columns, name, step=512):
    q_width = w[0].shape[0]
    steps = columns // step
    attended = [jax.ShapeDtypeStruct((rows, q_width), jnp.bfloat16)] * (0 if ask is None else 2)
    out_shape = attended + [jax.ShapeDtypeStruct((s, columns), jnp.float32) for s in slots]
    vmem = pl.BlockSpec(memory_space=pltpu.VMEM)
    scratch = [pltpu.VMEM((steps, q_width, step), jnp.float32), pltpu.SemaphoreType.DMA((steps,))]
    return pl.pallas_call(
        functools.partial(mix_kernel, len(operands), ask, q_width, kv_width, start, step),
        in_specs=[vmem] * len(operands) + ([vmem] * 2 if start is None else [pl.BlockSpec(memory_space=pl.ANY)]),
        out_specs=[vmem] * len(out_shape),
        out_shape=out_shape,
        scratch_shapes=[] if start is None else scratch,
        compiler_params=pltpu.CompilerParams(vmem_limit_bytes=VMEM_LIMIT),
        cost_estimate=pl.CostEstimate(
            flops=6 * rows * q_width * columns + 24 * rows * keyed * q_width,
            bytes_accessed=4 * columns * (q_width + rows),
            transcendentals=rows * keyed * q_width // HEAD_SIZE_DIM,
        ),
        name=name,
    )(*operands, *w)


def attend_out(parts, first, last, w, kv_width, slots, columns):
    rows = sum(a.shape[0] for a, _ in parts[first:last])
    keyed = sum(a.shape[0] for a, _ in parts)
    flat = [r for pair in parts for r in pair]
    res = mix(flat, slice(first, last), rows, keyed, w, kv_width, slots, None, columns, "attend_out")
    return res[:2], res[2:]


def out_again(attended, w_out, slots, start, columns):
    rows = attended[0].shape[0]
    return mix(list(attended), None, rows, 0, [w_out], 0, slots, start, columns, "out_again")


def after(a, *others):
    return lax.optimization_barrier((a, *others))[0]


def cut(sizes):
    return [(sum(sizes[:i]), size) for i, size in enumerate(sizes)]


def on_line_of_four(tokens, w_query, w_key, w_value, w_out):
    rows, depth = tokens.shape
    weights = (w_query, w_key, w_value)
    kv_width = w_key.shape[1]
    halves = cut([depth // 2] * 2)
    last = cut([depth // 2, depth // 4, depth // 4])

    def hop(a, pairs):
        return lax.ppermute(a, "col", pairs)

    def swap(a):
        return lax.ppermute(a, "row", CORES)

    def columns(a, start, size):
        return a[:, start : start + size]

    own = [columns(tokens, *h) for h in halves]
    near = [hop(a, PAIRS) for a in own]
    mid = [hop(a, MIDDLE) for a in own]
    first = project([((own[0], 0),)], weights, *halves[0])
    near[1] = after(near[1], first)
    mid2 = [hop(a, MIDDLE) for a in near]
    end2 = [hop(a, ENDS_IN) for a in mid]
    first = project([((own[1], 0),)], weights, *halves[1], first)
    mid2[0] = after(mid2[0], first)
    pieces = cut([w_out.shape[1] // 2] * 2)
    w_split = halve(w_out, *pieces[0], first)
    second = third = None
    for c, h in enumerate(halves):
        block = [((near[c], 0),), ((mid[c], 0), (end2[c], 0))]
        second = project(block, weights, *h, second, before=w_split[:1])
        if c == 0:
            mid2[1] = after(mid2[1], second)
    first, second = [(a, swap(a)) for a in (first, second)]
    for i, (start, size) in enumerate(last):
        half = start // halves[0][1]
        at = start - halves[half][0]
        end3 = hop(columns(mid2[half], at, size) if size < halves[0][1] else mid2[half], ENDS_IN)
        block = ((mid2[half], at), (end3, 0))
        if i == len(last) - 1:
            third = project_last(block, kept, third)
        elif i == len(last) - 2:
            third, *kept = project([block], weights, start, size, third, last[-1][1])
        else:
            third = project([block], weights, start, size, third)
    third = (third, swap(third))

    parts = [first, second, third]
    a_third, m_third = attend_out(parts, 2, 3, w_split, kv_width, [rows], pieces[0][1])
    m_third = [m_third[0], out_again(a_third, w_out, [rows], *pieces[1])[0]]
    r1 = [hop(m, ENDS_OUT) for m in m_third]
    others = [tuple(after(a, *m_third) for a in first), second, third]
    a_rest, mixed = attend_out(others, 0, 2, w_split, kv_width, [rows] * 3, pieces[0][1])
    mixed = [mixed, out_again(a_rest, w_out, [rows] * 3, *pieces[1])]
    result = []
    for (m_own, m_near, m_second), m, r in zip(mixed, m_third, r1):
        r2e = hop(m_second, ENDS_OUT)
        r2m = hop(m + r, MIDDLE)
        r3m = hop(m_second + r2e, MIDDLE)
        r3x = hop(m_near + r2m, PAIRS)
        result.append(m_own + (r3x + r3m))
    return jnp.concatenate(result, axis=1)


def on_device(tokens, w_query, w_key, w_value, w_out):
    highest = lax.Precision.HIGHEST
    gathered = lax.all_gather(tokens, "col", axis=0, tiled=True)
    q_width = w_query.shape[1]
    kv_width = w_key.shape[1]

    def product(weight):
        return jnp.dot(gathered, weight, preferred_element_type=jnp.float32, precision=highest)

    joined = lax.psum_scatter(
        jnp.concatenate([product(w_query), product(w_key), product(w_value)], axis=1),
        "row",
        scatter_dimension=0,
        tiled=True,
    )
    query_rows = joined[:, :q_width]
    keys = lax.all_gather(joined[:, q_width : q_width + kv_width], "row", axis=0, tiled=True)
    values = lax.all_gather(joined[:, q_width + kv_width :], "row", axis=0, tiled=True)
    count_of_rows, count_of_heads = query_rows.shape[0], kv_width // HEAD_SIZE_DIM
    query_rows = query_rows.reshape(count_of_rows, count_of_heads, GROUP, HEAD_SIZE_DIM)
    keys = keys.reshape(-1, count_of_heads, HEAD_SIZE_DIM)
    values = values.reshape(-1, count_of_heads, HEAD_SIZE_DIM)
    scores = jnp.einsum("rkgd,nkd->kgrn", query_rows, keys, precision=highest)
    weights = jax.nn.softmax(scores * (1.0 / math.sqrt(HEAD_SIZE_DIM)), axis=-1)
    attended = jnp.einsum("kgrn,nkd->rkgd", weights, values, precision=highest)
    attended = lax.all_gather(attended.reshape(count_of_rows, q_width), "row", axis=0, tiled=True)
    return lax.psum_scatter(
        jnp.dot(attended, w_out, preferred_element_type=jnp.float32, precision=highest),
        "col",
        scatter_dimension=0,
        tiled=True,
    )


def solution(mesh):
    placed = (
        P(("depth", "col"), "row"),
        P("row", "col"),
        P("row", "col"),
        P("row", "col"),
        P("col", "row"),
    )
    here = mesh.shape["row"] == 2 and mesh.shape["col"] == 4
    return jax.shard_map(
        on_line_of_four if here else on_device,
        mesh=mesh,
        in_specs=placed,
        out_specs=P(("depth", "col"), "row"),
        check_vma=False,
    )
```

time: 156 us -> 149 us (0.955)
  Pallas kernels: 59.6 us -> 48.5 us
  starting transfers between devices: 42 us -> 46.1 us
    pallas_call x7 -> x6, Pallas kernels: 34 us -> 27.2 us  [project(): pl.pallas_call(functools.partial(project_kernel, terms, total is not None...]
    pallas_call x4 -> x6, Pallas kernels: 25.7 us -> 21.3 us  [the longest x4 16.6 us: mix(): pl.pallas_call(functools.partial(mix_kernel, len(operands), ask, q_width,...]
    ppermute x21, starting transfers between devices: 41.3 us -> 45.4 us  [hop(): return lax.ppermute(a, 'col', pairs)]
  transfers between devices with their start and end apart: 24 -> 24, of which waited for: 9 -> 11; matrix products, arithmetic and copies ran while one was open for 0% -> 0% of each run, Pallas kernels for 35% -> 31%
where the time goes in v4:
time: 149 us; the launch traced here: 148 us
  Pallas kernels  48.5 us (33%)
  waiting for transfers between devices  46.5 us (31%)
  starting transfers between devices  46.1 us (31%)
  local copies, waits for them, and re-layouts  4.67 us (3%)
  other arithmetic  1.55 us (1%)
    ppermute x21, starting transfers between devices, hop(): return lax.ppermute(a, 'col', pairs)  45.4 us
    ppermute x21, waiting for transfers between devices, hop(): return lax.ppermute(a, 'col', pairs)  44.9 us
    pallas_call x6, Pallas kernels, project(): pl.pallas_call(functools.partial(project_kernel, terms, total is not None...  27.2 us
    pallas_call x4, Pallas kernels, mix(): pl.pallas_call(functools.partial(mix_kernel, len(operands), ask, q_width,...  16.6 us
    pallas_call x1, Pallas kernels, halve(): pl.pallas_call(functools.partial(halve_kernel, start), in_specs=[anywhere...  3.8 us
    unnamed x8, local copies, waits for them, and re-layouts  3.18 us
  transfers between devices with their start and end apart: 24, of which 11 were waited for; matrix products, arithmetic and copies ran while one was open for 0% of the time, Pallas kernels for 31%

profile of v4, /device:TPU:0, one launch (start us, length us, event | category | flops | bytes accessed | tf_op | source)
XLA Modules:
  0.0 147.7 jit_solution(10660476142816216426)
XLA Ops:
  0.0 1.4 fusion
  1.5 3.1 %collective-permute-start.4 = (f32[64,2048]{1,0:T(8,128)S(1)}, f32[64,2048]{1,0:T(8,128)S(1)}, u32[]{:S(2)}, u32[]{:S(2)}) collective-permute-start(f32[64,2048]{1,0:T(8,128)S(1)} %get-tuple-element.47.refs_0_), channel_id=1, source_target_pairs={{0,1},{1,0},{2,3},{3,2},{4,5},{5,4},{6,7},{7,6},{8,9},{9,8},{10,11... | collective-permute-start | bytes 1572872 | tf_op jit(solution)/shard_map/ppermute | solution.py:292
  4.5 0.7 collective-permute-start.5
  5.2 4.4 %collective-permute-start.1 = (f32[64,2048]{1,0:T(8,128)S(1)}, f32[64,2048]{1,0:T(8,128)S(1)}, u32[]{:S(2)}, u32[]{:S(2)}) collective-permute-start(f32[64,2048]{1,0:T(8,128)S(1)} %get-tuple-element.48.refs_0_), channel_id=1, source_target_pairs={{0,1},{1,0},{2,3},{3,2},{4,5},{5,4},{6,7},{7,6},{8,9},{9,8},{10,11... | collective-permute-start | bytes 1572872 | tf_op jit(solution)/shard_map/ppermute | solution.py:292
  9.7 0.7 collective-permute-start.2
  10.4 6.9 %collective-permute-done.4.refs_0_ = f32[64,2048]{1,0:T(8,128)S(1)} collective-permute-done((f32[64,2048]{1,0:T(8,128)S(1)}, f32[64,2048]{1,0:T(8,128)S(1)}, u32[]{:S(2)}, u32[]{:S(2)}) %collective-permute-start.4) | collective-permute-done | bytes 524320 | tf_op jit(solution)/shard_map/ppermute | solution.py:292
  17.3 0.7 collective-permute-start.11
  18.0 1.3 collective-permute-start.6
  19.3 0.0 copy-start
  19.3 1.6 %copy-done = f32[4096,128]{1,0:T(8,128)S(1)} copy-done((f32[4096,128]{1,0:T(8,128)S(1)}, f32[4096,128]{1,0:T(8,128)}, u32[]{:S(2)}) %copy-start) | copy-done | bytes 2097176
  20.9 1.6 %copy-done.2 = f32[4096,128]{1,0:T(8,128)S(1)} copy-done((f32[4096,128]{1,0:T(8,128)S(1)}, f32[4096,128]{1,0:T(8,128)}, u32[]{:S(2)}) %copy-start.2) | copy-done | bytes 2097176
  22.5 4.4 %project.6.refs_4_ = f32[64,1280]{1,0:T(8,128)S(1)} custom-call(f32[64,2048]{1,0:T(8,128)S(1)} %get-tuple-element.47.refs_0_, f32[4096,1024]{1,0:T(8,128)} %refs_2_.9, f32[4096,128]{1,0:T(8,128)S(1)} %copy-done, f32[4096,128]{1,0:T(8,128)S(1)} %copy-done.2), custom_call_target="tpu_custom_call" | custom-call | flops 1006632960 | bytes 11010048 | tf_op jit(solution)/shard_map/project/pallas_call | solution.py:101
  26.9 1.6 %collective-permute-done.1.refs_0_ = f32[64,2048]{1,0:T(8,128)S(1)} collective-permute-done((f32[64,2048]{1,0:T(8,128)S(1)}, f32[64,2048]{1,0:T(8,128)S(1)}, u32[]{:S(2)}, u32[]{:S(2)}) %collective-permute-start.1) | collective-permute-done | bytes 524320 | tf_op jit(solution)/shard_map/ppermute | solution.py:292
  28.5 0.7 collective-permute-start.8
  29.2 1.3 collective-permute-start.3
  30.5 4.3 %project.7.before.refs_0_ = f32[64,1280]{1,0:T(8,128)S(1)} custom-call(f32[64,2048]{1,0:T(8,128)S(1)} %get-tuple-element.48.refs_0_, f32[4096,1024]{1,0:T(8,128)} %refs_2_.9, f32[4096,128]{1,0:T(8,128)S(1)} %copy-done.1, f32[4096,128]{1,0:T(8,128)S(1)} %copy-done.3, f32[64,1280]{1,0:T(8,128)S(1)} %project.6.refs_4_), custom_call_target="tpu_custom_call" | custom-call | flops 1006632960 | bytes 11010048 | tf_op jit(solution)/shard_map/project/pallas_call | solution.py:101
  34.9 3.8 %halve.1 = (bf16[1024,2048]{1,0:T(8,128)(2,1)S(1)}, bf16[1024,2048]{1,0:T(8,128)(2,1)S(1)}) custom-call(f32[1024,4096]{1,0:T(8,128)} %refs_2_.11, f32[64,1280]{1,0:T(8,128)S(1)} %project.7.before.refs_0_), custom_call_target="tpu_custom_call" | custom-call | flops 2097152 | bytes 16777216 | tf_op jit(solution)/shard_map/halve/pallas_call | solution.py:189
  38.7 0.0 collective-permute-done.11.refs_0_
  38.7 1.3 collective-permute-start.12
  40.0 0.0 collective-permute-done.6.refs_2_
  40.0 5.1 %project.8.refs_6_ = f32[128,1280]{1,0:T(8,128)S(1)} custom-call(f32[64,2048]{1,0:T(8,128)S(1)} %collective-permute-done.4.refs_0_, f32[64,2048]{1,0:T(8,128)S(1)} %collective-permute-done.5.refs_1_, f32[64,2048]{1,0:T(8,128)S(1)} %collective-permute-done.6.refs_2_, f32[4096,1024]{1,0:T(8,128)} %refs_2_.9, f32[4096,128]{1,0:T(8,128)S(1)} %copy-done.1, ...), custom_call_target="tpu_custom_call" | custom-call | flops 2013265920 | bytes 11534336 | tf_op jit(solution)/shard_map/project/pallas_call | solution.py:101
  45.1 1.5 collective-permute-start.10
  46.6 4.4 %collective-permute-done.3.refs_2_ = f32[64,2048]{1,0:T(8,128)S(1)} collective-permute-done((f32[64,2048]{1,0:T(8,128)S(1)}, f32[64,2048]{1,0:T(8,128)S(1)}, u32[]{:S(2)}, u32[]{:S(2)}) %collective-permute-start.3) | collective-permute-done | bytes 524320 | tf_op jit(solution)/shard_map/ppermute | solution.py:292
  51.0 5.1 %project.9.refs_2_ = f32[128,1280]{1,0:T(8,128)S(1)} custom-call(f32[64,2048]{1,0:T(8,128)S(1)} %collective-permute-done.1.refs_0_, f32[64,2048]{1,0:T(8,128)S(1)} %collective-permute-done.2.refs_1_, f32[64,2048]{1,0:T(8,128)S(1)} %collective-permute-done.3.refs_2_, f32[4096,1024]{1,0:T(8,128)} %refs_2_.9, f32[4096,128]{1,0:T(8,128)S(1)} %copy-done.1, ...), custom_call_target="tpu_custom_call" | custom-call | flops 2013265920 | bytes 11534336 | tf_op jit(solution)/shard_map/project/pallas_call | solution.py:101
  56.1 0.1 collective-permute-start.7
  56.2 1.3 collective-permute-start.9
  57.5 0.6 collective-permute-start
  58.0 4.2 %collective-permute-done.12.refs_1_ = f32[64,2048]{1,0:T(8,128)S(1)} collective-permute-done((f32[64,2048]{1,0:T(8,128)S(1)}, f32[64,2048]{1,0:T(8,128)S(1)}, u32[]{:S(2)}, u32[]{:S(2)}) %collective-permute-start.12) | collective-permute-done | bytes 524320 | tf_op jit(solution)/shard_map/ppermute | solution.py:292
  62.2 4.3 %project.10.refs_5_ = f32[64,1280]{1,0:T(8,128)S(1)} custom-call(f32[64,2048]{1,0:T(8,128)S(1)} %collective-permute-done.11.refs_0_, f32[64,2048]{1,0:T(8,128)S(1)} %collective-permute-done.12.refs_1_, f32[4096,1024]{1,0:T(8,128)} %refs_2_.9, f32[4096,128]{1,0:T(8,128)S(1)} %copy-done.1, f32[4096,128]{1,0:T(8,128)S(1)} %copy-done.3), custom_call_target="tpu_custom_call" | custom-call | flops 1006632960 | bytes 11010048 | tf_op jit(solution)/shard_map/project/pallas_call | solution.py:101
  66.6 1.3 collective-permute-done.10.refs_1_
  67.9 4.0 %project.11 = (f32[64,1280]{1,0:T(8,128)S(1)}, bf16[1024,1280]{1,0:T(8,128)(2,1)S(1)}, bf16[1024,1280]{1,0:T(8,128)(2,1)S(1)}) custom-call(f32[64,2048]{1,0:T(8,128)S(1)} %collective-permute-done.8.refs_0_.x, f32[64,1024]{1,0:T(8,128)S(1)} %collective-permute-done.10.refs_1_, f32[4096,1024]{1,0:T(8,128)} %refs_2_.9, f32[4096,128]{1,0:T(8,128)S(1)} %copy-done.1, ...), custom_call_target="tpu_custom_call" | custom-call | flops 503316480 | bytes 5505024 | tf_op jit(solution)/shard_map/project/pallas_call | solution.py:101
  71.9 0.8 collective-permute-done.9.y
  72.6 0.9 project_last.1.refs_4_
  73.6 0.1 collective-permute-start.13
  73.7 0.0 collective-permute-done.refs_1_
  73.7 0.0 collective-permute-done.7.refs_3_
  73.7 1.6 %collective-permute-done.13.refs_5_ = f32[64,1280]{1,0:T(8,128)S(1)} collective-permute-done((f32[64,1280]{1,0:T(8,128)S(1)}, f32[64,1280]{1,0:T(8,128)S(1)}, u32[]{:S(2)}, u32[]{:S(2)}) %collective-permute-start.13) | collective-permute-done | bytes 327712 | tf_op jit(solution)/shard_map/ppermute | solution.py:295
  75.3 2.1 %attend_out.2 = (bf16[64,1024]{1,0:T(8,128)(2,1)S(1)}, bf16[64,1024]{1,0:T(8,128)(2,1)S(1)}, f32[64,2048]{1,0:T(8,128)S(1)}) custom-call(f32[64,1280]{1,0:T(8,128)S(1)} %project.7.before.refs_0_, f32[64,1280]{1,0:T(8,128)S(1)} %collective-permute-done.refs_1_, f32[128,1280]{1,0:T(8,128)S(1)} %project.9.refs_2_, ...), custom_call_target="tpu_custom_call" | custom-call | flops 1207959552 | bytes 8912896 | tf_op jit(solution)/shard_map/attend_out/pallas_call | solution.py:247
  77.4 1.7 %collective-permute-start.14 = (f32[64,2048]{1,0:T(8,128)S(1)}, f32[64,2048]{1,0:T(8,128)S(1)}, u32[]{:S(2)}, u32[]{:S(2)}) collective-permute-start(f32[64,2048]{1,0:T(8,128)S(1)} %get-tuple-element.34), channel_id=1, source_target_pairs={{0,1},{3,2},{4,5},{7,6},{8,9},{11,10},{12,13},{15,14},{16,17},{19,... | collective-permute-start | bytes 1572872 | tf_op jit(solution)/shard_map/ppermute | solution.py:292
  79.1 4.0 %out_again.2 = f32[64,2048]{1,0:T(8,128)S(1)} custom-call(bf16[64,1024]{1,0:T(8,128)(2,1)S(1)} %get-tuple-element.35.refs_0_, bf16[64,1024]{1,0:T(8,128)(2,1)S(1)} %get-tuple-element.36.refs_1_, f32[1024,4096]{1,0:T(8,128)} %refs_2_.11), custom_call_target="tpu_custom_call" | custom-call | flops 805306368 | bytes 8912896 | tf_op jit(solution)/shard_map/out_again/pallas_call | solution.py:247
  83.1 1.3 collective-permute-start.19
  84.5 5.6 %attend_out.3 = (bf16[192,1024]{1,0:T(8,128)(2,1)S(1)}, bf16[192,1024]{1,0:T(8,128)(2,1)S(1)}, f32[64,2048]{1,0:T(8,128)S(1)}, f32[64,2048]{1,0:T(8,128)S(1)}, f32[64,2048]{1,0:T(8,128)S(1)}) custom-call(f32[64,1280]{1,0:T(8,128)S(1)} %project.7.before.refs_0_, f32[64,1280]{1,0:T(8,128)S(1)} %collective-permute-done.refs_1_, ...), custom_call_target="tpu_custom_call" | custom-call | flops 3623878656 | bytes 9961472 | tf_op jit(solution)/shard_map/attend_out/pallas_call | solution.py:247
  90.1 1.3 collective-permute-start.17
  91.5 0.1 add.30
  91.5 0.7 collective-permute-start.15
  92.2 4.8 %out_again.3 = (f32[64,2048]{1,0:T(8,128)S(1)}, f32[64,2048]{1,0:T(8,128)S(1)}, f32[64,2048]{1,0:T(8,128)S(1)}) custom-call(bf16[192,1024]{1,0:T(8,128)(2,1)S(1)} %get-tuple-element.42.refs_0_, bf16[192,1024]{1,0:T(8,128)(2,1)S(1)} %get-tuple-element.43.refs_1_, f32[1024,4096]{1,0:T(8,128)} %refs_2_.11), custom_call_target="tpu_custom_call" | custom-call | flops 2415919104 | bytes 9961472 | tf_op jit(solution)/shard_map/out_again/pallas_call | solution.py:247
  97.0 8.1 %collective-permute-start.22 = (f32[64,2048]{1,0:T(8,128)S(1)}, f32[64,2048]{1,0:T(8,128)S(1)}, u32[]{:S(2)}, u32[]{:S(2)}) collective-permute-start(f32[64,2048]{1,0:T(8,128)S(1)} %get-tuple-element.46), channel_id=1, source_target_pairs={{0,1},{3,2},{4,5},{7,6},{8,9},{11,10},{12,13},{15,14},{16,17},{19,... | collective-permute-start | bytes 1572872 | tf_op jit(solution)/shard_map/ppermute | solution.py:292
  105.2 0.1 add.35
  105.2 0.7 collective-permute-start.20
  105.9 7.7 %collective-permute-done.17 = f32[64,2048]{1,0:T(8,128)S(1)} collective-permute-done((f32[64,2048]{1,0:T(8,128)S(1)}, f32[64,2048]{1,0:T(8,128)S(1)}, u32[]{:S(2)}, u32[]{:S(2)}) %collective-permute-start.17) | collective-permute-done | bytes 524320 | tf_op jit(solution)/shard_map/ppermute | solution.py:292
  113.6 0.1 add.32
  113.6 0.7 collective-permute-start.18
  114.3 0.1 add.31
  114.4 6.6 %collective-permute-start.16 = (f32[64,2048]{1,0:T(8,128)S(1)}, f32[64,2048]{1,0:T(8,128)S(1)}, u32[]{:S(2)}, u32[]{:S(2)}) collective-permute-start(f32[64,2048]{1,0:T(8,128)S(1)} %add.31), channel_id=1, source_target_pairs={{0,1},{1,0},{2,3},{3,2},{4,5},{5,4},{6,7},{7,6},{8,9},{9,8},{10,11... | collective-permute-start | bytes 1572872 | tf_op jit(solution)/shard_map/ppermute | solution.py:292
  121.0 3.8 %collective-permute-done.22 = f32[64,2048]{1,0:T(8,128)S(1)} collective-permute-done((f32[64,2048]{1,0:T(8,128)S(1)}, f32[64,2048]{1,0:T(8,128)S(1)}, u32[]{:S(2)}, u32[]{:S(2)}) %collective-permute-start.22) | collective-permute-done | bytes 524320 | tf_op jit(solution)/shard_map/ppermute | solution.py:292
  124.8 0.1 add.37
  124.9 0.7 collective-permute-start.23
  125.6 0.1 add.36
  125.6 6.6 %collective-permute-start.21 = (f32[64,2048]{1,0:T(8,128)S(1)}, f32[64,2048]{1,0:T(8,128)S(1)}, u32[]{:S(2)}, u32[]{:S(2)}) collective-permute-start(f32[64,2048]{1,0:T(8,128)S(1)} %add.36), channel_id=1, source_target_pairs={{0,1},{1,0},{2,3},{3,2},{4,5},{5,4},{6,7},{7,6},{8,9},{9,8},{10,11... | collective-permute-start | bytes 1572872 | tf_op jit(solution)/shard_map/ppermute | solution.py:292
  132.3 3.8 %collective-permute-done.16 = f32[64,2048]{1,0:T(8,128)S(1)} collective-permute-done((f32[64,2048]{1,0:T(8,128)S(1)}, f32[64,2048]{1,0:T(8,128)S(1)}, u32[]{:S(2)}, u32[]{:S(2)}) %collective-permute-start.16) | collective-permute-done | bytes 524320 | tf_op jit(solution)/shard_map/ppermute | solution.py:292
  136.0 0.1 add_add_fusion.1
  136.1 10.5 %collective-permute-done.21 = f32[64,2048]{1,0:T(8,128)S(1)} collective-permute-done((f32[64,2048]{1,0:T(8,128)S(1)}, f32[64,2048]{1,0:T(8,128)S(1)}, u32[]{:S(2)}, u32[]{:S(2)}) %collective-permute-start.21) | collective-permute-done | bytes 524320 | tf_op jit(solution)/shard_map/ppermute | solution.py:292
  146.6 0.1 add_add_fusion
  146.7 1.0 pad_maximum_fusion
  (15 shorter events, 0.1 us)
Async XLA Ops:
  0.0 30.5 %copy-start.1 = (f32[4096,128]{1,0:T(8,128)S(1)}, f32[4096,128]{1,0:T(8,128)}, u32[]{:S(2)}) copy-start(f32[4096,128]{1,0:T(8,128)} %refs_3_.11) | copy-start | bytes 6291460
  1.5 15.8 %collective-permute-start.4 = (f32[64,2048]{1,0:T(8,128)S(1)}, f32[64,2048]{1,0:T(8,128)S(1)}, u32[]{:S(2)}, u32[]{:S(2)}) collective-permute-start(f32[64,2048]{1,0:T(8,128)S(1)} %get-tuple-element.47.refs_0_), channel_id=1, source_target_pairs={{0,1},{1,0},{2,3},{3,2},{4,5},{5,4},{6,7},{7,6},{8,9},{9,8},{10,11... | collective-permute-start | bytes 1572872 | tf_op jit(solution)/shard_map/ppermute | solution.py:292
  4.5 13.4 %collective-permute-start.5 = (f32[64,2048]{1,0:T(8,128)S(1)}, f32[64,2048]{1,0:T(8,128)S(1)}, u32[]{:S(2)}, u32[]{:S(2)}) collective-permute-start(f32[64,2048]{1,0:T(8,128)S(1)} %get-tuple-element.47.refs_0_), channel_id=1, source_target_pairs={{1,2},{2,1},{5,6},{6,5},{9,10},{10,9},{13,14},{14,13},{17,18},{18,... | collective-permute-start | bytes 1572872 | tf_op jit(solution)/shard_map/ppermute | solution.py:292
  5.2 23.3 %collective-permute-start.1 = (f32[64,2048]{1,0:T(8,128)S(1)}, f32[64,2048]{1,0:T(8,128)S(1)}, u32[]{:S(2)}, u32[]{:S(2)}) collective-permute-start(f32[64,2048]{1,0:T(8,128)S(1)} %get-tuple-element.48.refs_0_), channel_id=1, source_target_pairs={{0,1},{1,0},{2,3},{3,2},{4,5},{5,4},{6,7},{7,6},{8,9},{9,8},{10,11... | collective-permute-start | bytes 1572872 | tf_op jit(solution)/shard_map/ppermute | solution.py:292
  9.7 19.6 %collective-permute-start.2 = (f32[64,2048]{1,0:T(8,128)S(1)}, f32[64,2048]{1,0:T(8,128)S(1)}, u32[]{:S(2)}, u32[]{:S(2)}) collective-permute-start(f32[64,2048]{1,0:T(8,128)S(1)} %get-tuple-element.48.refs_0_), channel_id=1, source_target_pairs={{1,2},{2,1},{5,6},{6,5},{9,10},{10,9},{13,14},{14,13},{17,18},{18,... | collective-permute-start | bytes 1572872 | tf_op jit(solution)/shard_map/ppermute | solution.py:292
  17.3 21.4 %collective-permute-start.11 = (f32[64,2048]{1,0:T(8,128)S(1)}, f32[64,2048]{1,0:T(8,128)S(1)}, u32[]{:S(2)}, u32[]{:S(2)}) collective-permute-start(f32[64,2048]{1,0:T(8,128)S(1)} %collective-permute-done.4.refs_0_), channel_id=1, source_target_pairs={{1,2},{2,1},{5,6},{6,5},{9,10},{10,9},{13,14},{14,13},{17,18},{18,... | collective-permute-start | bytes 1572872 | tf_op jit(solution)/shard_map/ppermute | solution.py:292
  18.0 22.0 %collective-permute-start.6 = (f32[64,2048]{1,0:T(8,128)S(1)}, f32[64,2048]{1,0:T(8,128)S(1)}, u32[]{:S(2)}, u32[]{:S(2)}) collective-permute-start(f32[64,2048]{1,0:T(8,128)S(1)} %collective-permute-done.5.refs_1_), channel_id=1, source_target_pairs={{1,0},{2,3},{5,4},{6,7},{9,8},{10,11},{13,12},{14,15},{17,16},{18,... | collective-permute-start | bytes 1572872 | tf_op jit(solution)/shard_map/ppermute | solution.py:292
  19.3 1.6 %copy-start = (f32[4096,128]{1,0:T(8,128)S(1)}, f32[4096,128]{1,0:T(8,128)}, u32[]{:S(2)}) copy-start(f32[4096,128]{1,0:T(8,128)} %refs_3_.11) | copy-start | bytes 6291460
  20.9 1.6 %copy-start.2 = (f32[4096,128]{1,0:T(8,128)S(1)}, f32[4096,128]{1,0:T(8,128)}, u32[]{:S(2)}) copy-start(f32[4096,128]{1,0:T(8,128)} %refs_4_.7) | copy-start | bytes 6291460
  22.5 8.1 %copy-start.3 = (f32[4096,128]{1,0:T(8,128)S(1)}, f32[4096,128]{1,0:T(8,128)}, u32[]{:S(2)}) copy-start(f32[4096,128]{1,0:T(8,128)} %refs_4_.7) | copy-start | bytes 6291460
  28.5 16.5 %collective-permute-start.8 = (f32[64,2048]{1,0:T(8,128)S(1)}, f32[64,2048]{1,0:T(8,128)S(1)}, u32[]{:S(2)}, u32[]{:S(2)}) collective-permute-start(f32[64,2048]{1,0:T(8,128)S(1)} %collective-permute-done.1.refs_0_), channel_id=1, source_target_pairs={{1,2},{2,1},{5,6},{6,5},{9,10},{10,9},{13,14},{14,13},{17,18},{18,... | collective-permute-start | bytes 1572872 | tf_op jit(solution)/shard_map/ppermute | solution.py:292
  29.2 21.8 %collective-permute-start.3 = (f32[64,2048]{1,0:T(8,128)S(1)}, f32[64,2048]{1,0:T(8,128)S(1)}, u32[]{:S(2)}, u32[]{:S(2)}) collective-permute-start(f32[64,2048]{1,0:T(8,128)S(1)} %collective-permute-done.2.refs_1_), channel_id=1, source_target_pairs={{1,0},{2,3},{5,4},{6,7},{9,8},{10,11},{13,12},{14,15},{17,16},{18,... | collective-permute-start | bytes 1572872 | tf_op jit(solution)/shard_map/ppermute | solution.py:292
  38.7 23.6 %collective-permute-start.12 = (f32[64,2048]{1,0:T(8,128)S(1)}, f32[64,2048]{1,0:T(8,128)S(1)}, u32[]{:S(2)}, u32[]{:S(2)}) collective-permute-start(f32[64,2048]{1,0:T(8,128)S(1)} %collective-permute-done.11.refs_0_), channel_id=1, source_target_pairs={{1,0},{2,3},{5,4},{6,7},{9,8},{10,11},{13,12},{14,15},{17,16},{18,... | collective-permute-start | bytes 1572872 | tf_op jit(solution)/shard_map/ppermute | solution.py:292
  45.1 22.7 %collective-permute-start.10 = (f32[64,1024]{1,0:T(8,128)S(1)}, f32[64,1024]{1,0:T(8,128)S(1)}, u32[]{:S(2)}, u32[]{:S(2)}) collective-permute-start(f32[64,1024]{1,0:T(8,128)S(1)} %get-tuple-element.49), channel_id=1, source_target_pairs={{1,0},{2,3},{5,4},{6,7},{9,8},{10,11},{13,12},{14,15},{17,16},{18,... | collective-permute-start | bytes 786440 | tf_op jit(solution)/shard_map/ppermute | solution.py:292
  56.1 17.6 %collective-permute-start.7 = (f32[128,1280]{1,0:T(8,128)S(1)}, f32[128,1280]{1,0:T(8,128)S(1)}, u32[]{:S(2)}, u32[]{:S(2)}) collective-permute-start(f32[128,1280]{1,0:T(8,128)S(1)} %project.9.refs_2_), channel_id=1, source_target_pairs={{0,4},{4,0},{1,5},{5,1},{2,6},{6,2},{3,7},{7,3},{8,12},{12,8},{9,1... | collective-permute-start | bytes 1966088 | tf_op jit(solution)/shard_map/ppermute | solution.py:295
  56.2 16.5 %collective-permute-start.9 = (f32[64,1024]{1,0:T(8,128)S(1)}, f32[64,1024]{1,0:T(8,128)S(1)}, u32[]{:S(2)}, u32[]{:S(2)}) collective-permute-start(f32[64,1024]{1,0:T(8,128)S(1)} %get-tuple-element.50), channel_id=1, source_target_pairs={{1,0},{2,3},{5,4},{6,7},{9,8},{10,11},{13,12},{14,15},{17,16},{18,... | collective-permute-start | bytes 786440 | tf_op jit(solution)/shard_map/ppermute | solution.py:292
  57.5 16.2 %collective-permute-start = (f32[64,1280]{1,0:T(8,128)S(1)}, f32[64,1280]{1,0:T(8,128)S(1)}, u32[]{:S(2)}, u32[]{:S(2)}) collective-permute-start(f32[64,1280]{1,0:T(8,128)S(1)} %project.7.before.refs_0_), channel_id=1, source_target_pairs={{0,4},{4,0},{1,5},{5,1},{2,6},{6,2},{3,7},{7,3},{8,12},{12,8},{9,1... | collective-permute-start | bytes 983048 | tf_op jit(solution)/shard_map/ppermute | solution.py:295
  73.6 1.7 %collective-permute-start.13 = (f32[64,1280]{1,0:T(8,128)S(1)}, f32[64,1280]{1,0:T(8,128)S(1)}, u32[]{:S(2)}, u32[]{:S(2)}) collective-permute-start(f32[64,1280]{1,0:T(8,128)S(1)} %project_last.1.refs_4_), channel_id=1, source_target_pairs={{0,4},{4,0},{1,5},{5,1},{2,6},{6,2},{3,7},{7,3},{8,12},{12,8},{9,1... | collective-permute-start | bytes 983048 | tf_op jit(solution)/shard_map/ppermute | solution.py:295
  77.4 14.1 %collective-permute-start.14 = (f32[64,2048]{1,0:T(8,128)S(1)}, f32[64,2048]{1,0:T(8,128)S(1)}, u32[]{:S(2)}, u32[]{:S(2)}) collective-permute-start(f32[64,2048]{1,0:T(8,128)S(1)} %get-tuple-element.34), channel_id=1, source_target_pairs={{0,1},{3,2},{4,5},{7,6},{8,9},{11,10},{12,13},{15,14},{16,17},{19,... | collective-permute-start | bytes 1572872 | tf_op jit(solution)/shard_map/ppermute | solution.py:292
  83.1 22.0 %collective-permute-start.19 = (f32[64,2048]{1,0:T(8,128)S(1)}, f32[64,2048]{1,0:T(8,128)S(1)}, u32[]{:S(2)}, u32[]{:S(2)}) collective-permute-start(f32[64,2048]{1,0:T(8,128)S(1)} %out_again.2), channel_id=1, source_target_pairs={{0,1},{3,2},{4,5},{7,6},{8,9},{11,10},{12,13},{15,14},{16,17},{19,... | collective-permute-start | bytes 1572872 | tf_op jit(solution)/shard_map/ppermute | solution.py:292
  90.1 23.5 %collective-permute-start.17 = (f32[64,2048]{1,0:T(8,128)S(1)}, f32[64,2048]{1,0:T(8,128)S(1)}, u32[]{:S(2)}, u32[]{:S(2)}) collective-permute-start(f32[64,2048]{1,0:T(8,128)S(1)} %get-tuple-element.41), channel_id=1, source_target_pairs={{0,1},{3,2},{4,5},{7,6},{8,9},{11,10},{12,13},{15,14},{16,17},{19,... | collective-permute-start | bytes 1572872 | tf_op jit(solution)/shard_map/ppermute | solution.py:292
  91.5 22.8 %collective-permute-start.15 = (f32[64,2048]{1,0:T(8,128)S(1)}, f32[64,2048]{1,0:T(8,128)S(1)}, u32[]{:S(2)}, u32[]{:S(2)}) collective-permute-start(f32[64,2048]{1,0:T(8,128)S(1)} %add.30), channel_id=1, source_target_pairs={{1,2},{2,1},{5,6},{6,5},{9,10},{10,9},{13,14},{14,13},{17,18},{18,... | collective-permute-start | bytes 1572872 | tf_op jit(solution)/shard_map/ppermute | solution.py:292
  97.0 27.8 %collective-permute-start.22 = (f32[64,2048]{1,0:T(8,128)S(1)}, f32[64,2048]{1,0:T(8,128)S(1)}, u32[]{:S(2)}, u32[]{:S(2)}) collective-permute-start(f32[64,2048]{1,0:T(8,128)S(1)} %get-tuple-element.46), channel_id=1, source_target_pairs={{0,1},{3,2},{4,5},{7,6},{8,9},{11,10},{12,13},{15,14},{16,17},{19,... | collective-permute-start | bytes 1572872 | tf_op jit(solution)/shard_map/ppermute | solution.py:292
  105.2 20.4 %collective-permute-start.20 = (f32[64,2048]{1,0:T(8,128)S(1)}, f32[64,2048]{1,0:T(8,128)S(1)}, u32[]{:S(2)}, u32[]{:S(2)}) collective-permute-start(f32[64,2048]{1,0:T(8,128)S(1)} %add.35), channel_id=1, source_target_pairs={{1,2},{2,1},{5,6},{6,5},{9,10},{10,9},{13,14},{14,13},{17,18},{18,... | collective-permute-start | bytes 1572872 | tf_op jit(solution)/shard_map/ppermute | solution.py:292
  113.6 18.6 %collective-permute-start.18 = (f32[64,2048]{1,0:T(8,128)S(1)}, f32[64,2048]{1,0:T(8,128)S(1)}, u32[]{:S(2)}, u32[]{:S(2)}) collective-permute-start(f32[64,2048]{1,0:T(8,128)S(1)} %add.32), channel_id=1, source_target_pairs={{1,2},{2,1},{5,6},{6,5},{9,10},{10,9},{13,14},{14,13},{17,18},{18,... | collective-permute-start | bytes 1572872 | tf_op jit(solution)/shard_map/ppermute | solution.py:292
  114.4 21.6 %collective-permute-start.16 = (f32[64,2048]{1,0:T(8,128)S(1)}, f32[64,2048]{1,0:T(8,128)S(1)}, u32[]{:S(2)}, u32[]{:S(2)}) collective-permute-start(f32[64,2048]{1,0:T(8,128)S(1)} %add.31), channel_id=1, source_target_pairs={{0,1},{1,0},{2,3},{3,2},{4,5},{5,4},{6,7},{7,6},{8,9},{9,8},{10,11... | collective-permute-start | bytes 1572872 | tf_op jit(solution)/shard_map/ppermute | solution.py:292
  124.9 11.3 %collective-permute-start.23 = (f32[64,2048]{1,0:T(8,128)S(1)}, f32[64,2048]{1,0:T(8,128)S(1)}, u32[]{:S(2)}, u32[]{:S(2)}) collective-permute-start(f32[64,2048]{1,0:T(8,128)S(1)} %add.37), channel_id=1, source_target_pairs={{1,2},{2,1},{5,6},{6,5},{9,10},{10,9},{13,14},{14,13},{17,18},{18,... | collective-permute-start | bytes 1572872 | tf_op jit(solution)/shard_map/ppermute | solution.py:292
  125.6 21.0 %collective-permute-start.21 = (f32[64,2048]{1,0:T(8,128)S(1)}, f32[64,2048]{1,0:T(8,128)S(1)}, u32[]{:S(2)}, u32[]{:S(2)}) collective-permute-start(f32[64,2048]{1,0:T(8,128)S(1)} %add.36), channel_id=1, source_target_pairs={{0,1},{1,0},{2,3},{3,2},{4,5},{5,4},{6,7},{7,6},{8,9},{9,8},{10,11... | collective-permute-start | bytes 1572872 | tf_op jit(solution)/shard_map/ppermute | solution.py:292

commit v5 on v4

--- a/solution.py
+++ b/solution.py
@@ -31,10 +31,11 @@
     return lax.dot_general(a, b, (dims, ((), ())), preferred_element_type=jnp.float32)
 
 
-def dot3(a, b, dims=((1,), (0,))):
+def dot_split(a, b):
     rows = a[0].shape[0]
-    both = dot(jnp.concatenate(a, axis=0), b[0], dims)
-    return both[:rows] + (both[rows:] + dot(a[0], b[1], dims))
+    both = jnp.concatenate(a, axis=0)
+    high, low = dot(both, b[0]), dot(both, b[1])
+    return high[:rows] + ((high[rows:] + low[:rows]) + low[rows:])
 
 
 def project_kernel(terms, with_total, first, steps, step, n_before, *refs):
@@ -66,7 +67,7 @@
         for b in bufs:
             width = b.shape[2]
             columns = slice(offset, offset + width)
-            product = dot3(x, split(b[k]))
+            product = dot_split(x, split(b[k]))
             if k > 0:
                 out[:, columns] += product
             elif with_total:
@@ -110,7 +111,7 @@
         + [pltpu.SemaphoreType.DMA((steps + keep // step, len(weights)))],
         compiler_params=pltpu.CompilerParams(vmem_limit_bytes=VMEM_LIMIT),
         cost_estimate=pl.CostEstimate(
-            flops=6 * rows * depth * width, bytes_accessed=4 * depth * (rows + width), transcendentals=0
+            flops=8 * rows * depth * width, bytes_accessed=4 * depth * (rows + width), transcendentals=0
         ),
         name="project",
     )(*operands)
@@ -119,7 +120,7 @@
 def project_last_kernel(at, x, y, high, low, total, out):
     size = y.shape[1]
     block = split(x[:, at : at + size] + y[...])
-    out[...] = total[...] + dot3(block, (high[...], low[...]))
+    out[...] = total[...] + dot_split(block, (high[...], low[...]))
 
 
 def project_last(block, kept, total):
@@ -132,7 +133,7 @@
         out_shape=jax.ShapeDtypeStruct(total.shape, jnp.float32),
         compiler_params=pltpu.CompilerParams(vmem_limit_bytes=VMEM_LIMIT),
         cost_estimate=pl.CostEstimate(
-            flops=6 * y.shape[1] * total.size, bytes_accessed=4 * y.shape[1] * total.shape[1], transcendentals=0
+            flops=8 * y.shape[1] * total.size, bytes_accessed=4 * y.shape[1] * total.shape[1], transcendentals=0
         ),
         name="project_last",
     )(x, y, *kept, total)
@@ -152,18 +153,22 @@
         at = q_width + g * HEAD_SIZE_DIM
         k_high, k_low = split(columns(keyed, at))
         v_high, v_low = split(columns(keyed, at + kv_width))
-        k_both = jnp.concatenate([k_high, k_high], axis=1)
+        k_highs = jnp.concatenate([k_high, k_high], axis=1)
+        k_lows = jnp.concatenate([k_low, k_low], axis=1)
         v_both = jnp.concatenate([v_high, v_low], axis=1)
         for j in range(0, GROUP, together):
             heads = [(g * GROUP + j + i) * HEAD_SIZE_DIM for i in range(together)]
-            q_high, q_low = split(jnp.concatenate([columns(asked, h) for h in heads], axis=0) * scale)
-            scores = dot(jnp.concatenate([q_high, q_low], axis=1), k_both, ((1,), (1,)))
-            scores = scores + dot(q_high, k_low, ((1,), (1,)))
+            queries = split(jnp.concatenate([columns(asked, h) for h in heads], axis=0) * scale)
+            q_both = jnp.concatenate(queries, axis=1)
+            scores = dot(q_both, k_highs, ((1,), (1,))) + dot(q_both, k_lows, ((1,), (1,)))
             weights = jnp.exp(scores - jnp.max(scores, axis=-1, keepdims=True))
             total = jnp.sum(weights, axis=-1, keepdims=True)
             p_high, p_low = split(weights)
             both = dot(p_high, v_both)
-            result = both[:, :HEAD_SIZE_DIM] + (both[:, HEAD_SIZE_DIM:] + dot(p_low, v_high))
+            less = dot(p_low, v_both)
+            result = both[:, :HEAD_SIZE_DIM] + (
+                (both[:, HEAD_SIZE_DIM:] + less[:, :HEAD_SIZE_DIM]) + less[:, HEAD_SIZE_DIM:]
+            )
             result = result / total
             for i, h in enumerate(heads):
                 store(h, result[i * rows : (i + 1) * rows])
@@ -230,7 +235,7 @@
         else:
             copy(k).wait()
             w = split(buf[k])
-        mixed = dot3(attended, w)
+        mixed = dot_split(attended, w)
         at = 0
         for o in outs:
             o[:, columns] = mixed[at : at + o.shape[0]]
@@ -252,7 +257,7 @@
         scratch_shapes=[] if start is None else scratch,
         compiler_params=pltpu.CompilerParams(vmem_limit_bytes=VMEM_LIMIT),
         cost_estimate=pl.CostEstimate(
-            flops=6 * rows * q_width * columns + 24 * rows * keyed * q_width,
+            flops=8 * rows * q_width * columns + 32 * rows * keyed * q_width,
             bytes_accessed=4 * columns * (q_width + rows),
             transcendentals=rows * keyed * q_width // HEAD_SIZE_DIM,
         ),
@@ -297,7 +302,8 @@
     def columns(a, start, size):
         return a[:, start : start + size]
 
-    own = [columns(tokens, *h) for h in halves]
+    own = [columns(tokens, *halves[0])]
+    own.append(columns(after(tokens, own[0]), *halves[1]))
     near = [hop(a, PAIRS) for a in own]
     mid = [hop(a, MIDDLE) for a in own]
     first = project([((own[0], 0),)], weights, *halves[0])

time: 149 us -> 149 us (level)
  Pallas kernels: 48.5 us -> 51.4 us
  waiting for transfers between devices: 46.5 us -> 44.4 us
  starting transfers between devices: 46.1 us -> 44.4 us
    ppermute x21, waiting for transfers between devices: 44.9 us -> 42.8 us  [hop(): return lax.ppermute(a, 'col', pairs)]
    ppermute x21, starting transfers between devices: 45.4 us -> 43.7 us  [hop(): return lax.ppermute(a, 'col', pairs)]
    pallas_call x6, Pallas kernels: 27.2 us -> 28.8 us  [project(): pl.pallas_call(functools.partial(project_kernel, terms, total is not None...]
  transfers between devices with their start and end apart: 24 -> 24, of which waited for: 11 -> 11; matrix products, arithmetic and copies ran while one was open for 0% -> 1% of each run, Pallas kernels for 31% -> 33%
where the time goes in v5:
time: 149 us; the launch traced here: 148 us
  Pallas kernels  51.4 us (34%)
  starting transfers between devices  44.4 us (30%)
  waiting for transfers between devices  44.4 us (30%)
  local copies, waits for them, and re-layouts  5.38 us (4%)
  other arithmetic  1.55 us (1%)
    ppermute x21, starting transfers between devices, hop(): return lax.ppermute(a, 'col', pairs)  43.7 us
    ppermute x21, waiting for transfers between devices, hop(): return lax.ppermute(a, 'col', pairs)  42.8 us
    pallas_call x6, Pallas kernels, project(): pl.pallas_call(functools.partial(project_kernel, terms, total is not None...  28.8 us
    pallas_call x4, Pallas kernels, mix(): pl.pallas_call(functools.partial(mix_kernel, len(operands), ask, q_width,...  17.9 us
    pallas_call x1, Pallas kernels, halve(): pl.pallas_call(functools.partial(halve_kernel, start), in_specs=[anywhere...  3.8 us
    unnamed x8, local copies, waits for them, and re-layouts  3.18 us
  transfers between devices with their start and end apart: 24, of which 11 were waited for; matrix products, arithmetic and copies ran while one was open for 1% of the time, Pallas kernels for 33%

profile of v5, /device:TPU:0, one launch (start us, length us, event | category | flops | bytes accessed | tf_op | source)
XLA Modules:
  0.0 147.5 jit_solution(12475358214270136390)
XLA Ops:
  0.0 1.1 slice.12.refs_0_
  1.1 3.1 %collective-permute-start.4 = (f32[64,2048]{1,0:T(8,128)S(1)}, f32[64,2048]{1,0:T(8,128)S(1)}, u32[]{:S(2)}, u32[]{:S(2)}) collective-permute-start(f32[64,2048]{1,0:T(8,128)S(1)} %slice.12.refs_0_), channel_id=1, source_target_pairs={{0,1},{1,0},{2,3},{3,2},{4,5},{5,4},{6,7},{7,6},{8,9},{9,8},{10,11... | collective-permute-start | bytes 1572872 | tf_op jit(solution)/shard_map/ppermute | solution.py:297
  4.2 0.7 collective-permute-start.5
  4.9 1.1 slice.13.refs_0_
  5.9 4.4 %collective-permute-start.1 = (f32[64,2048]{1,0:T(8,128)S(1)}, f32[64,2048]{1,0:T(8,128)S(1)}, u32[]{:S(2)}, u32[]{:S(2)}) collective-permute-start(f32[64,2048]{1,0:T(8,128)S(1)} %slice.13.refs_0_), channel_id=1, source_target_pairs={{0,1},{1,0},{2,3},{3,2},{4,5},{5,4},{6,7},{7,6},{8,9},{9,8},{10,11... | collective-permute-start | bytes 1572872 | tf_op jit(solution)/shard_map/ppermute | solution.py:297
  10.4 0.7 collective-permute-start.2
  11.1 5.9 %collective-permute-done.4.refs_0_ = f32[64,2048]{1,0:T(8,128)S(1)} collective-permute-done((f32[64,2048]{1,0:T(8,128)S(1)}, f32[64,2048]{1,0:T(8,128)S(1)}, u32[]{:S(2)}, u32[]{:S(2)}) %collective-permute-start.4) | collective-permute-done | bytes 524320 | tf_op jit(solution)/shard_map/ppermute | solution.py:297
  16.9 0.7 collective-permute-start.11
  17.6 0.0 collective-permute-done.5.refs_1_
  17.6 1.3 collective-permute-start.6
  18.9 0.0 copy-start
  18.9 1.6 %copy-done = f32[4096,128]{1,0:T(8,128)S(1)} copy-done((f32[4096,128]{1,0:T(8,128)S(1)}, f32[4096,128]{1,0:T(8,128)}, u32[]{:S(2)}) %copy-start) | copy-done | bytes 2097176
  20.5 1.6 %copy-done.2 = f32[4096,128]{1,0:T(8,128)S(1)} copy-done((f32[4096,128]{1,0:T(8,128)S(1)}, f32[4096,128]{1,0:T(8,128)}, u32[]{:S(2)}) %copy-start.2) | copy-done | bytes 2097176
  22.1 4.5 %project.6.refs_4_ = f32[64,1280]{1,0:T(8,128)S(1)} custom-call(f32[64,2048]{1,0:T(8,128)S(1)} %slice.12.refs_0_, f32[4096,1024]{1,0:T(8,128)} %refs_2_.9, f32[4096,128]{1,0:T(8,128)S(1)} %copy-done, f32[4096,128]{1,0:T(8,128)S(1)} %copy-done.2), custom_call_target="tpu_custom_call" | custom-call | flops 1342177280 | bytes 11010048 | tf_op jit(solution)/shard_map/project/pallas_call | solution.py:102
  26.6 1.5 %collective-permute-done.1.refs_0_ = f32[64,2048]{1,0:T(8,128)S(1)} collective-permute-done((f32[64,2048]{1,0:T(8,128)S(1)}, f32[64,2048]{1,0:T(8,128)S(1)}, u32[]{:S(2)}, u32[]{:S(2)}) %collective-permute-start.1) | collective-permute-done | bytes 524320 | tf_op jit(solution)/shard_map/ppermute | solution.py:297
  28.2 0.7 collective-permute-start.8
  28.8 0.0 collective-permute-done.2.refs_1_
  28.9 1.3 collective-permute-start.3
  30.2 4.3 %project.7.before.refs_0_ = f32[64,1280]{1,0:T(8,128)S(1)} custom-call(f32[64,2048]{1,0:T(8,128)S(1)} %slice.13.refs_0_, f32[4096,1024]{1,0:T(8,128)} %refs_2_.9, f32[4096,128]{1,0:T(8,128)S(1)} %copy-done.1, f32[4096,128]{1,0:T(8,128)S(1)} %copy-done.3, f32[64,1280]{1,0:T(8,128)S(1)} %project.6.refs_4_), custom_call_target="tpu_custom_call" | custom-call | flops 1342177280 | bytes 11010048 | tf_op jit(solution)/shard_map/project/pallas_call | solution.py:102
  34.5 3.8 %halve.1 = (bf16[1024,2048]{1,0:T(8,128)(2,1)S(1)}, bf16[1024,2048]{1,0:T(8,128)(2,1)S(1)}) custom-call(f32[1024,4096]{1,0:T(8,128)} %refs_2_.11, f32[64,1280]{1,0:T(8,128)S(1)} %project.7.before.refs_0_), custom_call_target="tpu_custom_call" | custom-call | flops 2097152 | bytes 16777216 | tf_op jit(solution)/shard_map/halve/pallas_call | solution.py:194
  38.3 0.0 collective-permute-done.11.refs_0_
  38.3 1.3 collective-permute-start.12
  39.6 5.8 %project.8.refs_6_ = f32[128,1280]{1,0:T(8,128)S(1)} custom-call(f32[64,2048]{1,0:T(8,128)S(1)} %collective-permute-done.4.refs_0_, f32[64,2048]{1,0:T(8,128)S(1)} %collective-permute-done.5.refs_1_, f32[64,2048]{1,0:T(8,128)S(1)} %collective-permute-done.6.refs_2_, f32[4096,1024]{1,0:T(8,128)} %refs_2_.9, f32[4096,128]{1,0:T(8,128)S(1)} %copy-done.1, ...), custom_call_target="tpu_custom_call" | custom-call | flops 2684354560 | bytes 11534336 | tf_op jit(solution)/shard_map/project/pallas_call | solution.py:102
  45.5 1.5 collective-permute-start.10
  47.0 3.6 %collective-permute-done.3.refs_2_ = f32[64,2048]{1,0:T(8,128)S(1)} collective-permute-done((f32[64,2048]{1,0:T(8,128)S(1)}, f32[64,2048]{1,0:T(8,128)S(1)}, u32[]{:S(2)}, u32[]{:S(2)}) %collective-permute-start.3) | collective-permute-done | bytes 524320 | tf_op jit(solution)/shard_map/ppermute | solution.py:297
  50.6 5.8 %project.9.refs_2_ = f32[128,1280]{1,0:T(8,128)S(1)} custom-call(f32[64,2048]{1,0:T(8,128)S(1)} %collective-permute-done.1.refs_0_, f32[64,2048]{1,0:T(8,128)S(1)} %collective-permute-done.2.refs_1_, f32[64,2048]{1,0:T(8,128)S(1)} %collective-permute-done.3.refs_2_, f32[4096,1024]{1,0:T(8,128)} %refs_2_.9, f32[4096,128]{1,0:T(8,128)S(1)} %copy-done.1, ...), custom_call_target="tpu_custom_call" | custom-call | flops 2684354560 | bytes 11534336 | tf_op jit(solution)/shard_map/project/pallas_call | solution.py:102
  56.5 0.1 collective-permute-start.7
  56.5 1.3 collective-permute-start.9
  57.8 0.6 collective-permute-start
  58.4 3.5 %collective-permute-done.12.refs_1_ = f32[64,2048]{1,0:T(8,128)S(1)} collective-permute-done((f32[64,2048]{1,0:T(8,128)S(1)}, f32[64,2048]{1,0:T(8,128)S(1)}, u32[]{:S(2)}, u32[]{:S(2)}) %collective-permute-start.12) | collective-permute-done | bytes 524320 | tf_op jit(solution)/shard_map/ppermute | solution.py:297
  61.9 4.3 %project.10.refs_5_ = f32[64,1280]{1,0:T(8,128)S(1)} custom-call(f32[64,2048]{1,0:T(8,128)S(1)} %collective-permute-done.11.refs_0_, f32[64,2048]{1,0:T(8,128)S(1)} %collective-permute-done.12.refs_1_, f32[4096,1024]{1,0:T(8,128)} %refs_2_.9, f32[4096,128]{1,0:T(8,128)S(1)} %copy-done.1, f32[4096,128]{1,0:T(8,128)S(1)} %copy-done.3), custom_call_target="tpu_custom_call" | custom-call | flops 1342177280 | bytes 11010048 | tf_op jit(solution)/shard_map/project/pallas_call | solution.py:102
  66.2 1.3 collective-permute-done.10.refs_1_
  67.5 4.0 %project.11 = (f32[64,1280]{1,0:T(8,128)S(1)}, bf16[1024,1280]{1,0:T(8,128)(2,1)S(1)}, bf16[1024,1280]{1,0:T(8,128)(2,1)S(1)}) custom-call(f32[64,2048]{1,0:T(8,128)S(1)} %collective-permute-done.8.refs_0_.x, f32[64,1024]{1,0:T(8,128)S(1)} %collective-permute-done.10.refs_1_, f32[4096,1024]{1,0:T(8,128)} %refs_2_.9, f32[4096,128]{1,0:T(8,128)S(1)} %copy-done.1, ...), custom_call_target="tpu_custom_call" | custom-call | flops 671088640 | bytes 5505024 | tf_op jit(solution)/shard_map/project/pallas_call | solution.py:102
  71.5 0.8 collective-permute-done.9.y
  72.3 0.9 project_last.1.refs_4_
  73.1 0.1 collective-permute-start.13
  73.2 1.6 %collective-permute-done.13.refs_5_ = f32[64,1280]{1,0:T(8,128)S(1)} collective-permute-done((f32[64,1280]{1,0:T(8,128)S(1)}, f32[64,1280]{1,0:T(8,128)S(1)}, u32[]{:S(2)}, u32[]{:S(2)}) %collective-permute-start.13) | collective-permute-done | bytes 327712 | tf_op jit(solution)/shard_map/ppermute | solution.py:300
  74.8 2.0 %attend_out.2 = (bf16[64,1024]{1,0:T(8,128)(2,1)S(1)}, bf16[64,1024]{1,0:T(8,128)(2,1)S(1)}, f32[64,2048]{1,0:T(8,128)S(1)}) custom-call(f32[64,1280]{1,0:T(8,128)S(1)} %project.7.before.refs_0_, f32[64,1280]{1,0:T(8,128)S(1)} %collective-permute-done.refs_1_, f32[128,1280]{1,0:T(8,128)S(1)} %project.9.refs_2_, ...), custom_call_target="tpu_custom_call" | custom-call | flops 1610612736 | bytes 8912896 | tf_op jit(solution)/shard_map/attend_out/pallas_call | solution.py:252
  76.8 2.2 %collective-permute-start.14 = (f32[64,2048]{1,0:T(8,128)S(1)}, f32[64,2048]{1,0:T(8,128)S(1)}, u32[]{:S(2)}, u32[]{:S(2)}) collective-permute-start(f32[64,2048]{1,0:T(8,128)S(1)} %get-tuple-element.36), channel_id=1, source_target_pairs={{0,1},{3,2},{4,5},{7,6},{8,9},{11,10},{12,13},{15,14},{16,17},{19,... | collective-permute-start | bytes 1572872 | tf_op jit(solution)/shard_map/ppermute | solution.py:297
  79.0 4.0 %out_again.2 = f32[64,2048]{1,0:T(8,128)S(1)} custom-call(bf16[64,1024]{1,0:T(8,128)(2,1)S(1)} %get-tuple-element.37.refs_0_, bf16[64,1024]{1,0:T(8,128)(2,1)S(1)} %get-tuple-element.38.refs_1_, f32[1024,4096]{1,0:T(8,128)} %refs_2_.11), custom_call_target="tpu_custom_call" | custom-call | flops 1073741824 | bytes 8912896 | tf_op jit(solution)/shard_map/out_again/pallas_call | solution.py:252
  83.0 1.3 collective-permute-start.19
  84.3 6.4 %attend_out.3 = (bf16[192,1024]{1,0:T(8,128)(2,1)S(1)}, bf16[192,1024]{1,0:T(8,128)(2,1)S(1)}, f32[64,2048]{1,0:T(8,128)S(1)}, f32[64,2048]{1,0:T(8,128)S(1)}, f32[64,2048]{1,0:T(8,128)S(1)}) custom-call(f32[64,1280]{1,0:T(8,128)S(1)} %project.7.before.refs_0_, f32[64,1280]{1,0:T(8,128)S(1)} %collective-permute-done.refs_1_, ...), custom_call_target="tpu_custom_call" | custom-call | flops 4831838208 | bytes 9961472 | tf_op jit(solution)/shard_map/attend_out/pallas_call | solution.py:252
  90.7 1.3 collective-permute-start.17
  92.1 0.1 add.30
  92.1 0.7 collective-permute-start.15
  92.8 5.6 %out_again.3 = (f32[64,2048]{1,0:T(8,128)S(1)}, f32[64,2048]{1,0:T(8,128)S(1)}, f32[64,2048]{1,0:T(8,128)S(1)}) custom-call(bf16[192,1024]{1,0:T(8,128)(2,1)S(1)} %get-tuple-element.44.refs_0_, bf16[192,1024]{1,0:T(8,128)(2,1)S(1)} %get-tuple-element.45.refs_1_, f32[1024,4096]{1,0:T(8,128)} %refs_2_.11), custom_call_target="tpu_custom_call" | custom-call | flops 3221225472 | bytes 9961472 | tf_op jit(solution)/shard_map/out_again/pallas_call | solution.py:252
  98.4 6.9 %collective-permute-start.22 = (f32[64,2048]{1,0:T(8,128)S(1)}, f32[64,2048]{1,0:T(8,128)S(1)}, u32[]{:S(2)}, u32[]{:S(2)}) collective-permute-start(f32[64,2048]{1,0:T(8,128)S(1)} %get-tuple-element.48), channel_id=1, source_target_pairs={{0,1},{3,2},{4,5},{7,6},{8,9},{11,10},{12,13},{15,14},{16,17},{19,... | collective-permute-start | bytes 1572872 | tf_op jit(solution)/shard_map/ppermute | solution.py:297
  105.4 0.1 add.35
  105.4 0.7 collective-permute-start.20
  106.1 7.3 %collective-permute-done.17 = f32[64,2048]{1,0:T(8,128)S(1)} collective-permute-done((f32[64,2048]{1,0:T(8,128)S(1)}, f32[64,2048]{1,0:T(8,128)S(1)}, u32[]{:S(2)}, u32[]{:S(2)}) %collective-permute-start.17) | collective-permute-done | bytes 524320 | tf_op jit(solution)/shard_map/ppermute | solution.py:297
  113.5 0.1 add.32
  113.5 0.7 collective-permute-start.18
  114.3 0.1 add.31
  114.3 6.1 %collective-permute-start.16 = (f32[64,2048]{1,0:T(8,128)S(1)}, f32[64,2048]{1,0:T(8,128)S(1)}, u32[]{:S(2)}, u32[]{:S(2)}) collective-permute-start(f32[64,2048]{1,0:T(8,128)S(1)} %add.31), channel_id=1, source_target_pairs={{0,1},{1,0},{2,3},{3,2},{4,5},{5,4},{6,7},{7,6},{8,9},{9,8},{10,11... | collective-permute-start | bytes 1572872 | tf_op jit(solution)/shard_map/ppermute | solution.py:297
  120.4 4.3 %collective-permute-done.22 = f32[64,2048]{1,0:T(8,128)S(1)} collective-permute-done((f32[64,2048]{1,0:T(8,128)S(1)}, f32[64,2048]{1,0:T(8,128)S(1)}, u32[]{:S(2)}, u32[]{:S(2)}) %collective-permute-start.22) | collective-permute-done | bytes 524320 | tf_op jit(solution)/shard_map/ppermute | solution.py:297
  124.7 0.1 add.37
  124.8 0.7 collective-permute-start.23
  125.5 0.1 add.36
  125.6 6.1 %collective-permute-start.21 = (f32[64,2048]{1,0:T(8,128)S(1)}, f32[64,2048]{1,0:T(8,128)S(1)}, u32[]{:S(2)}, u32[]{:S(2)}) collective-permute-start(f32[64,2048]{1,0:T(8,128)S(1)} %add.36), channel_id=1, source_target_pairs={{0,1},{1,0},{2,3},{3,2},{4,5},{5,4},{6,7},{7,6},{8,9},{9,8},{10,11... | collective-permute-start | bytes 1572872 | tf_op jit(solution)/shard_map/ppermute | solution.py:297
  131.7 4.3 %collective-permute-done.16 = f32[64,2048]{1,0:T(8,128)S(1)} collective-permute-done((f32[64,2048]{1,0:T(8,128)S(1)}, f32[64,2048]{1,0:T(8,128)S(1)}, u32[]{:S(2)}, u32[]{:S(2)}) %collective-permute-start.16) | collective-permute-done | bytes 524320 | tf_op jit(solution)/shard_map/ppermute | solution.py:297
  136.0 0.1 add_add_fusion.1
  136.0 10.3 %collective-permute-done.21 = f32[64,2048]{1,0:T(8,128)S(1)} collective-permute-done((f32[64,2048]{1,0:T(8,128)S(1)}, f32[64,2048]{1,0:T(8,128)S(1)}, u32[]{:S(2)}, u32[]{:S(2)}) %collective-permute-start.21) | collective-permute-done | bytes 524320 | tf_op jit(solution)/shard_map/ppermute | solution.py:297
  146.4 0.1 add_add_fusion
  146.5 1.0 pad_maximum_fusion
  (16 shorter events, 0.1 us)
Async XLA Ops:
  1.1 15.8 %collective-permute-start.4 = (f32[64,2048]{1,0:T(8,128)S(1)}, f32[64,2048]{1,0:T(8,128)S(1)}, u32[]{:S(2)}, u32[]{:S(2)}) collective-permute-start(f32[64,2048]{1,0:T(8,128)S(1)} %slice.12.refs_0_), channel_id=1, source_target_pairs={{0,1},{1,0},{2,3},{3,2},{4,5},{5,4},{6,7},{7,6},{8,9},{9,8},{10,11... | collective-permute-start | bytes 1572872 | tf_op jit(solution)/shard_map/ppermute | solution.py:297
  4.2 13.4 %collective-permute-start.5 = (f32[64,2048]{1,0:T(8,128)S(1)}, f32[64,2048]{1,0:T(8,128)S(1)}, u32[]{:S(2)}, u32[]{:S(2)}) collective-permute-start(f32[64,2048]{1,0:T(8,128)S(1)} %slice.12.refs_0_), channel_id=1, source_target_pairs={{1,2},{2,1},{5,6},{6,5},{9,10},{10,9},{13,14},{14,13},{17,18},{18,... | collective-permute-start | bytes 1572872 | tf_op jit(solution)/shard_map/ppermute | solution.py:297
  5.9 22.2 %collective-permute-start.1 = (f32[64,2048]{1,0:T(8,128)S(1)}, f32[64,2048]{1,0:T(8,128)S(1)}, u32[]{:S(2)}, u32[]{:S(2)}) collective-permute-start(f32[64,2048]{1,0:T(8,128)S(1)} %slice.13.refs_0_), channel_id=1, source_target_pairs={{0,1},{1,0},{2,3},{3,2},{4,5},{5,4},{6,7},{7,6},{8,9},{9,8},{10,11... | collective-permute-start | bytes 1572872 | tf_op jit(solution)/shard_map/ppermute | solution.py:297
  10.4 18.5 %collective-permute-start.2 = (f32[64,2048]{1,0:T(8,128)S(1)}, f32[64,2048]{1,0:T(8,128)S(1)}, u32[]{:S(2)}, u32[]{:S(2)}) collective-permute-start(f32[64,2048]{1,0:T(8,128)S(1)} %slice.13.refs_0_), channel_id=1, source_target_pairs={{1,2},{2,1},{5,6},{6,5},{9,10},{10,9},{13,14},{14,13},{17,18},{18,... | collective-permute-start | bytes 1572872 | tf_op jit(solution)/shard_map/ppermute | solution.py:297
  16.9 21.4 %collective-permute-start.11 = (f32[64,2048]{1,0:T(8,128)S(1)}, f32[64,2048]{1,0:T(8,128)S(1)}, u32[]{:S(2)}, u32[]{:S(2)}) collective-permute-start(f32[64,2048]{1,0:T(8,128)S(1)} %collective-permute-done.4.refs_0_), channel_id=1, source_target_pairs={{1,2},{2,1},{5,6},{6,5},{9,10},{10,9},{13,14},{14,13},{17,18},{18,... | collective-permute-start | bytes 1572872 | tf_op jit(solution)/shard_map/ppermute | solution.py:297
  17.6 22.0 %collective-permute-start.6 = (f32[64,2048]{1,0:T(8,128)S(1)}, f32[64,2048]{1,0:T(8,128)S(1)}, u32[]{:S(2)}, u32[]{:S(2)}) collective-permute-start(f32[64,2048]{1,0:T(8,128)S(1)} %collective-permute-done.5.refs_1_), channel_id=1, source_target_pairs={{1,0},{2,3},{5,4},{6,7},{9,8},{10,11},{13,12},{14,15},{17,16},{18,... | collective-permute-start | bytes 1572872 | tf_op jit(solution)/shard_map/ppermute | solution.py:297
  18.9 1.6 %copy-start = (f32[4096,128]{1,0:T(8,128)S(1)}, f32[4096,128]{1,0:T(8,128)}, u32[]{:S(2)}) copy-start(f32[4096,128]{1,0:T(8,128)} %refs_3_.11) | copy-start | bytes 6291460
  20.5 1.6 %copy-start.2 = (f32[4096,128]{1,0:T(8,128)S(1)}, f32[4096,128]{1,0:T(8,128)}, u32[]{:S(2)}) copy-start(f32[4096,128]{1,0:T(8,128)} %refs_4_.7) | copy-start | bytes 6291460
  22.1 8.1 %copy-start.1 = (f32[4096,128]{1,0:T(8,128)S(1)}, f32[4096,128]{1,0:T(8,128)}, u32[]{:S(2)}) copy-start(f32[4096,128]{1,0:T(8,128)} %refs_3_.11) | copy-start | bytes 6291460
  22.1 8.1 %copy-start.3 = (f32[4096,128]{1,0:T(8,128)S(1)}, f32[4096,128]{1,0:T(8,128)}, u32[]{:S(2)}) copy-start(f32[4096,128]{1,0:T(8,128)} %refs_4_.7) | copy-start | bytes 6291460
  28.2 17.3 %collective-permute-start.8 = (f32[64,2048]{1,0:T(8,128)S(1)}, f32[64,2048]{1,0:T(8,128)S(1)}, u32[]{:S(2)}, u32[]{:S(2)}) collective-permute-start(f32[64,2048]{1,0:T(8,128)S(1)} %collective-permute-done.1.refs_0_), channel_id=1, source_target_pairs={{1,2},{2,1},{5,6},{6,5},{9,10},{10,9},{13,14},{14,13},{17,18},{18,... | collective-permute-start | bytes 1572872 | tf_op jit(solution)/shard_map/ppermute | solution.py:297
  28.9 21.8 %collective-permute-start.3 = (f32[64,2048]{1,0:T(8,128)S(1)}, f32[64,2048]{1,0:T(8,128)S(1)}, u32[]{:S(2)}, u32[]{:S(2)}) collective-permute-start(f32[64,2048]{1,0:T(8,128)S(1)} %collective-permute-done.2.refs_1_), channel_id=1, source_target_pairs={{1,0},{2,3},{5,4},{6,7},{9,8},{10,11},{13,12},{14,15},{17,16},{18,... | collective-permute-start | bytes 1572872 | tf_op jit(solution)/shard_map/ppermute | solution.py:297
  38.3 23.5 %collective-permute-start.12 = (f32[64,2048]{1,0:T(8,128)S(1)}, f32[64,2048]{1,0:T(8,128)S(1)}, u32[]{:S(2)}, u32[]{:S(2)}) collective-permute-start(f32[64,2048]{1,0:T(8,128)S(1)} %collective-permute-done.11.refs_0_), channel_id=1, source_target_pairs={{1,0},{2,3},{5,4},{6,7},{9,8},{10,11},{13,12},{14,15},{17,16},{18,... | collective-permute-start | bytes 1572872 | tf_op jit(solution)/shard_map/ppermute | solution.py:297
  45.5 22.0 %collective-permute-start.10 = (f32[64,1024]{1,0:T(8,128)S(1)}, f32[64,1024]{1,0:T(8,128)S(1)}, u32[]{:S(2)}, u32[]{:S(2)}) collective-permute-start(f32[64,1024]{1,0:T(8,128)S(1)} %get-tuple-element.49), channel_id=1, source_target_pairs={{1,0},{2,3},{5,4},{6,7},{9,8},{10,11},{13,12},{14,15},{17,16},{18,... | collective-permute-start | bytes 786440 | tf_op jit(solution)/shard_map/ppermute | solution.py:297
  56.5 16.8 %collective-permute-start.7 = (f32[128,1280]{1,0:T(8,128)S(1)}, f32[128,1280]{1,0:T(8,128)S(1)}, u32[]{:S(2)}, u32[]{:S(2)}) collective-permute-start(f32[128,1280]{1,0:T(8,128)S(1)} %project.9.refs_2_), channel_id=1, source_target_pairs={{0,4},{4,0},{1,5},{5,1},{2,6},{6,2},{3,7},{7,3},{8,12},{12,8},{9,1... | collective-permute-start | bytes 1966088 | tf_op jit(solution)/shard_map/ppermute | solution.py:300
  56.5 15.7 %collective-permute-start.9 = (f32[64,1024]{1,0:T(8,128)S(1)}, f32[64,1024]{1,0:T(8,128)S(1)}, u32[]{:S(2)}, u32[]{:S(2)}) collective-permute-start(f32[64,1024]{1,0:T(8,128)S(1)} %get-tuple-element.50), channel_id=1, source_target_pairs={{1,0},{2,3},{5,4},{6,7},{9,8},{10,11},{13,12},{14,15},{17,16},{18,... | collective-permute-start | bytes 786440 | tf_op jit(solution)/shard_map/ppermute | solution.py:297
  57.8 15.4 %collective-permute-start = (f32[64,1280]{1,0:T(8,128)S(1)}, f32[64,1280]{1,0:T(8,128)S(1)}, u32[]{:S(2)}, u32[]{:S(2)}) collective-permute-start(f32[64,1280]{1,0:T(8,128)S(1)} %project.7.before.refs_0_), channel_id=1, source_target_pairs={{0,4},{4,0},{1,5},{5,1},{2,6},{6,2},{3,7},{7,3},{8,12},{12,8},{9,1... | collective-permute-start | bytes 983048 | tf_op jit(solution)/shard_map/ppermute | solution.py:300
  73.1 1.7 %collective-permute-start.13 = (f32[64,1280]{1,0:T(8,128)S(1)}, f32[64,1280]{1,0:T(8,128)S(1)}, u32[]{:S(2)}, u32[]{:S(2)}) collective-permute-start(f32[64,1280]{1,0:T(8,128)S(1)} %project_last.1.refs_4_), channel_id=1, source_target_pairs={{0,4},{4,0},{1,5},{5,1},{2,6},{6,2},{3,7},{7,3},{8,12},{12,8},{9,1... | collective-permute-start | bytes 983048 | tf_op jit(solution)/shard_map/ppermute | solution.py:300
  76.8 15.3 %collective-permute-start.14 = (f32[64,2048]{1,0:T(8,128)S(1)}, f32[64,2048]{1,0:T(8,128)S(1)}, u32[]{:S(2)}, u32[]{:S(2)}) collective-permute-start(f32[64,2048]{1,0:T(8,128)S(1)} %get-tuple-element.36), channel_id=1, source_target_pairs={{0,1},{3,2},{4,5},{7,6},{8,9},{11,10},{12,13},{15,14},{16,17},{19,... | collective-permute-start | bytes 1572872 | tf_op jit(solution)/shard_map/ppermute | solution.py:297
  83.0 22.3 %collective-permute-start.19 = (f32[64,2048]{1,0:T(8,128)S(1)}, f32[64,2048]{1,0:T(8,128)S(1)}, u32[]{:S(2)}, u32[]{:S(2)}) collective-permute-start(f32[64,2048]{1,0:T(8,128)S(1)} %out_again.2), channel_id=1, source_target_pairs={{0,1},{3,2},{4,5},{7,6},{8,9},{11,10},{12,13},{15,14},{16,17},{19,... | collective-permute-start | bytes 1572872 | tf_op jit(solution)/shard_map/ppermute | solution.py:297
  90.7 22.8 %collective-permute-start.17 = (f32[64,2048]{1,0:T(8,128)S(1)}, f32[64,2048]{1,0:T(8,128)S(1)}, u32[]{:S(2)}, u32[]{:S(2)}) collective-permute-start(f32[64,2048]{1,0:T(8,128)S(1)} %get-tuple-element.43), channel_id=1, source_target_pairs={{0,1},{3,2},{4,5},{7,6},{8,9},{11,10},{12,13},{15,14},{16,17},{19,... | collective-permute-start | bytes 1572872 | tf_op jit(solution)/shard_map/ppermute | solution.py:297
  92.1 22.1 %collective-permute-start.15 = (f32[64,2048]{1,0:T(8,128)S(1)}, f32[64,2048]{1,0:T(8,128)S(1)}, u32[]{:S(2)}, u32[]{:S(2)}) collective-permute-start(f32[64,2048]{1,0:T(8,128)S(1)} %add.30), channel_id=1, source_target_pairs={{1,2},{2,1},{5,6},{6,5},{9,10},{10,9},{13,14},{14,13},{17,18},{18,... | collective-permute-start | bytes 1572872 | tf_op jit(solution)/shard_map/ppermute | solution.py:297
  98.4 26.3 %collective-permute-start.22 = (f32[64,2048]{1,0:T(8,128)S(1)}, f32[64,2048]{1,0:T(8,128)S(1)}, u32[]{:S(2)}, u32[]{:S(2)}) collective-permute-start(f32[64,2048]{1,0:T(8,128)S(1)} %get-tuple-element.48), channel_id=1, source_target_pairs={{0,1},{3,2},{4,5},{7,6},{8,9},{11,10},{12,13},{15,14},{16,17},{19,... | collective-permute-start | bytes 1572872 | tf_op jit(solution)/shard_map/ppermute | solution.py:297
  105.4 20.1 %collective-permute-start.20 = (f32[64,2048]{1,0:T(8,128)S(1)}, f32[64,2048]{1,0:T(8,128)S(1)}, u32[]{:S(2)}, u32[]{:S(2)}) collective-permute-start(f32[64,2048]{1,0:T(8,128)S(1)} %add.35), channel_id=1, source_target_pairs={{1,2},{2,1},{5,6},{6,5},{9,10},{10,9},{13,14},{14,13},{17,18},{18,... | collective-permute-start | bytes 1572872 | tf_op jit(solution)/shard_map/ppermute | solution.py:297
  113.5 18.1 %collective-permute-start.18 = (f32[64,2048]{1,0:T(8,128)S(1)}, f32[64,2048]{1,0:T(8,128)S(1)}, u32[]{:S(2)}, u32[]{:S(2)}) collective-permute-start(f32[64,2048]{1,0:T(8,128)S(1)} %add.32), channel_id=1, source_target_pairs={{1,2},{2,1},{5,6},{6,5},{9,10},{10,9},{13,14},{14,13},{17,18},{18,... | collective-permute-start | bytes 1572872 | tf_op jit(solution)/shard_map/ppermute | solution.py:297
  114.3 21.6 %collective-permute-start.16 = (f32[64,2048]{1,0:T(8,128)S(1)}, f32[64,2048]{1,0:T(8,128)S(1)}, u32[]{:S(2)}, u32[]{:S(2)}) collective-permute-start(f32[64,2048]{1,0:T(8,128)S(1)} %add.31), channel_id=1, source_target_pairs={{0,1},{1,0},{2,3},{3,2},{4,5},{5,4},{6,7},{7,6},{8,9},{9,8},{10,11... | collective-permute-start | bytes 1572872 | tf_op jit(solution)/shard_map/ppermute | solution.py:297
  124.8 11.3 %collective-permute-start.23 = (f32[64,2048]{1,0:T(8,128)S(1)}, f32[64,2048]{1,0:T(8,128)S(1)}, u32[]{:S(2)}, u32[]{:S(2)}) collective-permute-start(f32[64,2048]{1,0:T(8,128)S(1)} %add.37), channel_id=1, source_target_pairs={{1,2},{2,1},{5,6},{6,5},{9,10},{10,9},{13,14},{14,13},{17,18},{18,... | collective-permute-start | bytes 1572872 | tf_op jit(solution)/shard_map/ppermute | solution.py:297
  125.6 20.8 %collective-permute-start.21 = (f32[64,2048]{1,0:T(8,128)S(1)}, f32[64,2048]{1,0:T(8,128)S(1)}, u32[]{:S(2)}, u32[]{:S(2)}) collective-permute-start(f32[64,2048]{1,0:T(8,128)S(1)} %add.36), channel_id=1, source_target_pairs={{0,1},{1,0},{2,3},{3,2},{4,5},{5,4},{6,7},{7,6},{8,9},{9,8},{10,11... | collective-permute-start | bytes 1572872 | tf_op jit(solution)/shard_map/ppermute | solution.py:297

commit v6 on v5

--- a/solution.py
+++ b/solution.py
@@ -302,29 +302,31 @@
     def columns(a, start, size):
         return a[:, start : start + size]
 
-    own = [columns(tokens, *halves[0])]
-    own.append(columns(after(tokens, own[0]), *halves[1]))
-    near = [hop(a, PAIRS) for a in own]
-    mid = [hop(a, MIDDLE) for a in own]
-    first = project([((own[0], 0),)], weights, *halves[0])
-    near[1] = after(near[1], first)
-    mid2 = [hop(a, MIDDLE) for a in near]
+    near = hop(tokens, PAIRS)
+    mid = [hop(columns(tokens, *h), MIDDLE) for h in halves]
+    first = project([((tokens, 0),)], weights, *halves[0])
+    mid[0] = after(mid[0], first)
     end2 = [hop(a, ENDS_IN) for a in mid]
-    first = project([((own[1], 0),)], weights, *halves[1], first)
-    mid2[0] = after(mid2[0], first)
+    first = project([((tokens, halves[1][0]),)], weights, *halves[1], first, before=mid[:1])
+    near = after(near, first)
+    mid2 = [hop(columns(near, *halves[0]), MIDDLE)]
     pieces = cut([w_out.shape[1] // 2] * 2)
-    w_split = halve(w_out, *pieces[0], first)
+    w_split = halve(w_out, *pieces[0], near)
     second = third = None
-    for c, h in enumerate(halves):
-        block = [((near[c], 0),), ((mid[c], 0), (end2[c], 0))]
-        second = project(block, weights, *h, second, before=w_split[:1])
-        if c == 0:
-            mid2[1] = after(mid2[1], second)
+    for (start, size), m, e in zip(halves, mid, end2):
+        block = [((near, start),), ((m, 0), (e, 0))]
+        second = project(block, weights, start, size, second, before=[w_split[0], mid[1]])
+        if start == 0:
+            mid2.append(hop(columns(after(near, w_split[0]), *halves[1]), MIDDLE))
+            mid2[0] = after(mid2[0], second)
     first, second = [(a, swap(a)) for a in (first, second)]
     for i, (start, size) in enumerate(last):
         half = start // halves[0][1]
         at = start - halves[half][0]
-        end3 = hop(columns(mid2[half], at, size) if size < halves[0][1] else mid2[half], ENDS_IN)
+        far = columns(mid2[half], at, size) if size < halves[0][1] else mid2[half]
+        if i == 1:
+            far = after(far, second[0])
+        end3 = hop(far, ENDS_IN)
         block = ((mid2[half], at), (end3, 0))
         if i == len(last) - 1:
             third = project_last(block, kept, third)

time: 149 us -> 148 us (level)
  starting transfers between devices: 44.4 us -> 41.2 us
  waiting for transfers between devices: 44.4 us -> 46 us
    ppermute x21 -> x20, starting transfers between devices: 43.7 us -> 40.5 us  [hop(): return lax.ppermute(a, 'col', pairs)]
    ppermute x21 -> x20, waiting for transfers between devices: 42.8 us -> 44.4 us  [hop(): return lax.ppermute(a, 'col', pairs)]
    unnamed x8 -> x10, local copies, waits for them, and re-layouts: 3.18 us -> 4.41 us
  transfers between devices with their start and end apart: 24 -> 23, of which waited for: 11 -> 11; matrix products, arithmetic and copies ran while one was open for 1% -> 1% of each run, Pallas kernels for 33% -> 34%
where the time goes in v6:
time: 148 us; the launch traced here: 146 us
  Pallas kernels  51.2 us (35%)
  waiting for transfers between devices  46 us (31%)
  starting transfers between devices  41.2 us (28%)
  local copies, waits for them, and re-layouts  5.82 us (4%)
  other arithmetic  1.55 us (1%)
    ppermute x20, waiting for transfers between devices, hop(): return lax.ppermute(a, 'col', pairs)  44.4 us
    ppermute x20, starting transfers between devices, hop(): return lax.ppermute(a, 'col', pairs)  40.5 us
    pallas_call x6, Pallas kernels, project(): pl.pallas_call(functools.partial(project_kernel, terms, total is not None...  28.7 us
    pallas_call x4, Pallas kernels, mix(): pl.pallas_call(functools.partial(mix_kernel, len(operands), ask, q_width,...  17.9 us
    unnamed x10, local copies, waits for them, and re-layouts  4.41 us
    pallas_call x1, Pallas kernels, halve(): pl.pallas_call(functools.partial(halve_kernel, start), in_specs=[anywhere...  3.8 us
  transfers between devices with their start and end apart: 23, of which 11 were waited for; matrix products, arithmetic and copies ran while one was open for 1% of the time, Pallas kernels for 34%

profile of v6, /device:TPU:0, one launch (start us, length us, event | category | flops | bytes accessed | tf_op | source)
XLA Modules:
  0.0 146.2 jit_solution(3898928733586816547)
XLA Ops:
  0.0 3.0 %collective-permute-start.2 = (f32[64,4096]{1,0:T(8,128)}, f32[64,4096]{1,0:T(8,128)S(1)}, u32[]{:S(2)}, u32[]{:S(2)}) collective-permute-start(f32[64,4096]{1,0:T(8,128)} %refs_0_.3), channel_id=1, source_target_pairs={{0,1},{1,0},{2,3},{3,2},{4,5},{5,4},{6,7},{7,6},{8,9},{9,8},{10,11... | collective-permute-start | bytes 3145736 | tf_op jit(solution)/shard_map/ppermute | solution.py:297
  3.0 1.3 fusion
  4.3 0.7 collective-permute-start
  5.0 0.7 collective-permute-start.3
  5.7 0.0 copy-start
  5.7 1.6 %copy-done = f32[4096,128]{1,0:T(8,128)S(1)} copy-done((f32[4096,128]{1,0:T(8,128)S(1)}, f32[4096,128]{1,0:T(8,128)}, u32[]{:S(2)}) %copy-start) | copy-done | bytes 2097176
  7.3 1.6 %copy-done.2 = f32[4096,128]{1,0:T(8,128)S(1)} copy-done((f32[4096,128]{1,0:T(8,128)S(1)}, f32[4096,128]{1,0:T(8,128)}, u32[]{:S(2)}) %copy-start.2) | copy-done | bytes 2097176
  8.9 1.2 copy-done.4
  10.1 4.3 %project.6.refs_4_ = f32[64,1280]{1,0:T(8,128)S(1)} custom-call(f32[64,4096]{1,0:T(8,128)S(1)} %copy-done.4, f32[4096,1024]{1,0:T(8,128)} %refs_2_.9, f32[4096,128]{1,0:T(8,128)S(1)} %copy-done, f32[4096,128]{1,0:T(8,128)S(1)} %copy-done.2), custom_call_target="tpu_custom_call" | custom-call | flops 1342177280 | bytes 11010048 | tf_op jit(solution)/shard_map/project/pallas_call | solution.py:102
  14.5 0.0 collective-permute-done.refs_5_.refs_1_
  14.5 1.3 collective-permute-start.5
  15.8 4.3 %project.7.refs_0_ = f32[64,1280]{1,0:T(8,128)S(1)} custom-call(f32[64,4096]{1,0:T(8,128)S(1)} %copy-done.4, f32[4096,1024]{1,0:T(8,128)} %refs_2_.9, f32[4096,128]{1,0:T(8,128)S(1)} %copy-done, f32[4096,128]{1,0:T(8,128)S(1)} %copy-done.2, f32[64,1280]{1,0:T(8,128)S(1)} %project.6.refs_4_, f32[64,2048]{1,0:T(8,128)S(1)} %collective-permute-done.refs_5_.refs_1_), custom_call_target="tpu_custom_call" | custom-call | flops 1342177280 | bytes 11010048 | tf_op jit(solution)/shard_map/project/pallas_call | solution.py:102
  20.1 7.1 %collective-permute-done.2.before.refs_0_ = f32[64,4096]{1,0:T(8,128)S(1)} collective-permute-done((f32[64,4096]{1,0:T(8,128)}, f32[64,4096]{1,0:T(8,128)S(1)}, u32[]{:S(2)}, u32[]{:S(2)}) %collective-permute-start.2) | collective-permute-done | bytes 1048608 | tf_op jit(solution)/shard_map/ppermute | solution.py:297
  27.3 0.0 copy-start.1
  27.3 0.0 copy-start.3
  27.3 0.8 collective-permute-start.10
  28.1 0.0 collective-permute-done.3.refs_7_.refs_1_.refs_8_
  28.1 1.4 collective-permute-start.4
  29.6 3.8 %halve.1 = (bf16[1024,2048]{1,0:T(8,128)(2,1)S(1)}, bf16[1024,2048]{1,0:T(8,128)(2,1)S(1)}) custom-call(f32[1024,4096]{1,0:T(8,128)} %refs_2_.11, f32[64,4096]{1,0:T(8,128)S(1)} %collective-permute-done.2.before.refs_0_), custom_call_target="tpu_custom_call" | custom-call | flops 2097152 | bytes 16777216 | tf_op jit(solution)/shard_map/halve/pallas_call | solution.py:194
  33.4 0.7 collective-permute-start.7
  34.1 4.3 %collective-permute-done.5.refs_2_ = f32[64,2048]{1,0:T(8,128)S(1)} collective-permute-done((f32[64,2048]{1,0:T(8,128)S(1)}, f32[64,2048]{1,0:T(8,128)S(1)}, u32[]{:S(2)}, u32[]{:S(2)}) %collective-permute-start.5) | collective-permute-done | bytes 524320 | tf_op jit(solution)/shard_map/ppermute | solution.py:297
  38.5 5.8 %project.8.refs_6_ = f32[128,1280]{1,0:T(8,128)S(1)} custom-call(f32[64,4096]{1,0:T(8,128)S(1)} %collective-permute-done.2.before.refs_0_, f32[64,2048]{1,0:T(8,128)S(1)} %collective-permute-done.refs_5_.refs_1_, f32[64,2048]{1,0:T(8,128)S(1)} %collective-permute-done.5.refs_2_, f32[4096,1024]{1,0:T(8,128)} %refs_2_.9, f32[4096,128]{1,0:T(8,128)S(1)} %copy-done.1, ...), custom_call_target="tpu_custom_call" | custom-call | flops 2684354560 | bytes 11534336 | tf_op jit(solution)/shard_map/project/pallas_call | solution.py:102
  44.3 1.5 %collective-permute-start.11 = (f32[64,2048]{1,0:T(8,128)S(1)}, f32[64,2048]{1,0:T(8,128)S(1)}, u32[]{:S(2)}, u32[]{:S(2)}) collective-permute-start(f32[64,2048]{1,0:T(8,128)S(1)} %collective-permute-done.10.refs_0_), channel_id=1, source_target_pairs={{1,0},{2,3},{5,4},{6,7},{9,8},{10,11},{13,12},{14,15},{17,16},{18,... | collective-permute-start | bytes 1572872 | tf_op jit(solution)/shard_map/ppermute | solution.py:297
  45.8 3.9 %collective-permute-done.4.refs_2_ = f32[64,2048]{1,0:T(8,128)S(1)} collective-permute-done((f32[64,2048]{1,0:T(8,128)S(1)}, f32[64,2048]{1,0:T(8,128)S(1)}, u32[]{:S(2)}, u32[]{:S(2)}) %collective-permute-start.4) | collective-permute-done | bytes 524320 | tf_op jit(solution)/shard_map/ppermute | solution.py:297
  49.7 5.8 %project.9.refs_2_ = f32[128,1280]{1,0:T(8,128)S(1)} custom-call(f32[64,4096]{1,0:T(8,128)S(1)} %collective-permute-done.2.before.refs_0_, f32[64,2048]{1,0:T(8,128)S(1)} %collective-permute-done.3.refs_7_.refs_1_.refs_8_, f32[64,2048]{1,0:T(8,128)S(1)} %collective-permute-done.4.refs_2_, f32[4096,1024]{1,0:T(8,128)} %refs_2_.9, f32[4096,128]{1,0:T(8,128)S(1)} %copy-done.1, ...), custom_call_target="tpu_custom_call" | custom-call | flops 2684354560 | bytes 11534336 | tf_op jit(solution)/shard_map/project/pallas_call | solution.py:102
  55.6 1.3 collective-permute-start.9
  56.9 0.1 collective-permute-start.6
  57.0 1.3 collective-permute-start.8
  58.3 0.6 collective-permute-start.1
  58.8 2.7 %collective-permute-done.11.refs_1_ = f32[64,2048]{1,0:T(8,128)S(1)} collective-permute-done((f32[64,2048]{1,0:T(8,128)S(1)}, f32[64,2048]{1,0:T(8,128)S(1)}, u32[]{:S(2)}, u32[]{:S(2)}) %collective-permute-start.11) | collective-permute-done | bytes 524320 | tf_op jit(solution)/shard_map/ppermute | solution.py:297
  61.5 4.3 %project.10.refs_5_ = f32[64,1280]{1,0:T(8,128)S(1)} custom-call(f32[64,2048]{1,0:T(8,128)S(1)} %collective-permute-done.10.refs_0_, f32[64,2048]{1,0:T(8,128)S(1)} %collective-permute-done.11.refs_1_, f32[4096,1024]{1,0:T(8,128)} %refs_2_.9, f32[4096,128]{1,0:T(8,128)S(1)} %copy-done.1, f32[4096,128]{1,0:T(8,128)S(1)} %copy-done.3), custom_call_target="tpu_custom_call" | custom-call | flops 1342177280 | bytes 11010048 | tf_op jit(solution)/shard_map/project/pallas_call | solution.py:102
  65.8 1.3 collective-permute-done.9.refs_1_
  67.1 4.0 %project.11 = (f32[64,1280]{1,0:T(8,128)S(1)}, bf16[1024,1280]{1,0:T(8,128)(2,1)S(1)}, bf16[1024,1280]{1,0:T(8,128)(2,1)S(1)}) custom-call(f32[64,2048]{1,0:T(8,128)S(1)} %collective-permute-done.7.refs_0_.x, f32[64,1024]{1,0:T(8,128)S(1)} %collective-permute-done.9.refs_1_, f32[4096,1024]{1,0:T(8,128)} %refs_2_.9, f32[4096,128]{1,0:T(8,128)S(1)} %copy-done.1, ...), custom_call_target="tpu_custom_call" | custom-call | flops 671088640 | bytes 5505024 | tf_op jit(solution)/shard_map/project/pallas_call | solution.py:102
  71.1 0.2 collective-permute-done.8.y
  71.3 0.9 project_last.1.refs_4_
  72.2 0.1 collective-permute-start.12
  72.3 1.6 %collective-permute-done.12.refs_5_ = f32[64,1280]{1,0:T(8,128)S(1)} collective-permute-done((f32[64,1280]{1,0:T(8,128)S(1)}, f32[64,1280]{1,0:T(8,128)S(1)}, u32[]{:S(2)}, u32[]{:S(2)}) %collective-permute-start.12) | collective-permute-done | bytes 327712 | tf_op jit(solution)/shard_map/ppermute | solution.py:300
  73.9 2.0 %attend_out.2 = (bf16[64,1024]{1,0:T(8,128)(2,1)S(1)}, bf16[64,1024]{1,0:T(8,128)(2,1)S(1)}, f32[64,2048]{1,0:T(8,128)S(1)}) custom-call(f32[64,1280]{1,0:T(8,128)S(1)} %project.7.refs_0_, f32[64,1280]{1,0:T(8,128)S(1)} %collective-permute-done.1.refs_1_, f32[128,1280]{1,0:T(8,128)S(1)} %project.9.refs_2_, f32[128,1280]{1,0:T(8,128)S(1)} %collective-permute-done.6.refs_3_, ...), custom_call_target="tpu_custom_call" | custom-call | flops 1610612736 | bytes 8912896 | tf_op jit(solution)/shard_map/attend_out/pallas_call | solution.py:252
  75.9 1.7 %collective-permute-start.13 = (f32[64,2048]{1,0:T(8,128)S(1)}, f32[64,2048]{1,0:T(8,128)S(1)}, u32[]{:S(2)}, u32[]{:S(2)}) collective-permute-start(f32[64,2048]{1,0:T(8,128)S(1)} %get-tuple-element.38), channel_id=1, source_target_pairs={{0,1},{3,2},{4,5},{7,6},{8,9},{11,10},{12,13},{15,14},{16,17},{19,... | collective-permute-start | bytes 1572872 | tf_op jit(solution)/shard_map/ppermute | solution.py:297
  77.6 4.0 %out_again.2 = f32[64,2048]{1,0:T(8,128)S(1)} custom-call(bf16[64,1024]{1,0:T(8,128)(2,1)S(1)} %get-tuple-element.39.refs_0_, bf16[64,1024]{1,0:T(8,128)(2,1)S(1)} %get-tuple-element.40.refs_1_, f32[1024,4096]{1,0:T(8,128)} %refs_2_.11), custom_call_target="tpu_custom_call" | custom-call | flops 1073741824 | bytes 8912896 | tf_op jit(solution)/shard_map/out_again/pallas_call | solution.py:252
  81.6 1.3 collective-permute-start.18
  82.9 6.4 %attend_out.3 = (bf16[192,1024]{1,0:T(8,128)(2,1)S(1)}, bf16[192,1024]{1,0:T(8,128)(2,1)S(1)}, f32[64,2048]{1,0:T(8,128)S(1)}, f32[64,2048]{1,0:T(8,128)S(1)}, f32[64,2048]{1,0:T(8,128)S(1)}) custom-call(f32[64,1280]{1,0:T(8,128)S(1)} %project.7.refs_0_, f32[64,1280]{1,0:T(8,128)S(1)} %collective-permute-done.1.refs_1_, f32[128,1280]{1,0:T(8,128)S(1)} %project.9.refs_2_, ...), custom_call_target="tpu_custom_call" | custom-call | flops 4831838208 | bytes 9961472 | tf_op jit(solution)/shard_map/attend_out/pallas_call | solution.py:252
  89.3 1.3 collective-permute-start.16
  90.7 0.1 add.30
  90.7 0.7 collective-permute-start.14
  91.4 5.6 %out_again.3 = (f32[64,2048]{1,0:T(8,128)S(1)}, f32[64,2048]{1,0:T(8,128)S(1)}, f32[64,2048]{1,0:T(8,128)S(1)}) custom-call(bf16[192,1024]{1,0:T(8,128)(2,1)S(1)} %get-tuple-element.46.refs_0_, bf16[192,1024]{1,0:T(8,128)(2,1)S(1)} %get-tuple-element.47.refs_1_, f32[1024,4096]{1,0:T(8,128)} %refs_2_.11), custom_call_target="tpu_custom_call" | custom-call | flops 3221225472 | bytes 9961472 | tf_op jit(solution)/shard_map/out_again/pallas_call | solution.py:252
  97.0 7.4 %collective-permute-start.21 = (f32[64,2048]{1,0:T(8,128)S(1)}, f32[64,2048]{1,0:T(8,128)S(1)}, u32[]{:S(2)}, u32[]{:S(2)}) collective-permute-start(f32[64,2048]{1,0:T(8,128)S(1)} %get-tuple-element.50), channel_id=1, source_target_pairs={{0,1},{3,2},{4,5},{7,6},{8,9},{11,10},{12,13},{15,14},{16,17},{19,... | collective-permute-start | bytes 1572872 | tf_op jit(solution)/shard_map/ppermute | solution.py:297
  104.4 0.1 add.35
  104.5 0.7 collective-permute-start.19
  105.2 6.8 %collective-permute-done.16 = f32[64,2048]{1,0:T(8,128)S(1)} collective-permute-done((f32[64,2048]{1,0:T(8,128)S(1)}, f32[64,2048]{1,0:T(8,128)S(1)}, u32[]{:S(2)}, u32[]{:S(2)}) %collective-permute-start.16) | collective-permute-done | bytes 524320 | tf_op jit(solution)/shard_map/ppermute | solution.py:297
  112.0 0.1 add.32
  112.1 0.7 collective-permute-start.17
  112.8 0.1 add.31
  112.9 6.6 %collective-permute-start.15 = (f32[64,2048]{1,0:T(8,128)S(1)}, f32[64,2048]{1,0:T(8,128)S(1)}, u32[]{:S(2)}, u32[]{:S(2)}) collective-permute-start(f32[64,2048]{1,0:T(8,128)S(1)} %add.31), channel_id=1, source_target_pairs={{0,1},{1,0},{2,3},{3,2},{4,5},{5,4},{6,7},{7,6},{8,9},{9,8},{10,11... | collective-permute-start | bytes 1572872 | tf_op jit(solution)/shard_map/ppermute | solution.py:297
  119.5 3.8 %collective-permute-done.21 = f32[64,2048]{1,0:T(8,128)S(1)} collective-permute-done((f32[64,2048]{1,0:T(8,128)S(1)}, f32[64,2048]{1,0:T(8,128)S(1)}, u32[]{:S(2)}, u32[]{:S(2)}) %collective-permute-start.21) | collective-permute-done | bytes 524320 | tf_op jit(solution)/shard_map/ppermute | solution.py:297
  123.3 0.1 add.37
  123.3 0.7 collective-permute-start.22
  124.0 0.1 add.36
  124.1 6.6 %collective-permute-start.20 = (f32[64,2048]{1,0:T(8,128)S(1)}, f32[64,2048]{1,0:T(8,128)S(1)}, u32[]{:S(2)}, u32[]{:S(2)}) collective-permute-start(f32[64,2048]{1,0:T(8,128)S(1)} %add.36), channel_id=1, source_target_pairs={{0,1},{1,0},{2,3},{3,2},{4,5},{5,4},{6,7},{7,6},{8,9},{9,8},{10,11... | collective-permute-start | bytes 1572872 | tf_op jit(solution)/shard_map/ppermute | solution.py:297
  130.8 3.8 %collective-permute-done.15 = f32[64,2048]{1,0:T(8,128)S(1)} collective-permute-done((f32[64,2048]{1,0:T(8,128)S(1)}, f32[64,2048]{1,0:T(8,128)S(1)}, u32[]{:S(2)}, u32[]{:S(2)}) %collective-permute-start.15) | collective-permute-done | bytes 524320 | tf_op jit(solution)/shard_map/ppermute | solution.py:297
  134.5 0.1 add_add_fusion.1
  134.6 10.5 %collective-permute-done.20 = f32[64,2048]{1,0:T(8,128)S(1)} collective-permute-done((f32[64,2048]{1,0:T(8,128)S(1)}, f32[64,2048]{1,0:T(8,128)S(1)}, u32[]{:S(2)}, u32[]{:S(2)}) %collective-permute-start.20) | collective-permute-done | bytes 524320 | tf_op jit(solution)/shard_map/ppermute | solution.py:297
  145.1 0.1 add_add_fusion
  145.2 1.0 pad_maximum_fusion
  (17 shorter events, 0.1 us)
Async XLA Ops:
  0.0 27.2 %collective-permute-start.2 = (f32[64,4096]{1,0:T(8,128)}, f32[64,4096]{1,0:T(8,128)S(1)}, u32[]{:S(2)}, u32[]{:S(2)}) collective-permute-start(f32[64,4096]{1,0:T(8,128)} %refs_0_.3), channel_id=1, source_target_pairs={{0,1},{1,0},{2,3},{3,2},{4,5},{5,4},{6,7},{7,6},{8,9},{9,8},{10,11... | collective-permute-start | bytes 3145736 | tf_op jit(solution)/shard_map/ppermute | solution.py:297
  4.3 10.2 %collective-permute-start = (f32[64,2048]{1,0:T(8,128)S(1)}, f32[64,2048]{1,0:T(8,128)S(1)}, u32[]{:S(2)}, u32[]{:S(2)}) collective-permute-start(f32[64,2048]{1,0:T(8,128)S(1)} %get-tuple-element.52), channel_id=1, source_target_pairs={{1,2},{2,1},{5,6},{6,5},{9,10},{10,9},{13,14},{14,13},{17,18},{18,... | collective-permute-start | bytes 1572872 | tf_op jit(solution)/shard_map/ppermute | solution.py:297
  5.0 23.1 %collective-permute-start.3 = (f32[64,2048]{1,0:T(8,128)S(1)}, f32[64,2048]{1,0:T(8,128)S(1)}, u32[]{:S(2)}, u32[]{:S(2)}) collective-permute-start(f32[64,2048]{1,0:T(8,128)S(1)} %get-tuple-element.51), channel_id=1, source_target_pairs={{1,2},{2,1},{5,6},{6,5},{9,10},{10,9},{13,14},{14,13},{17,18},{18,... | collective-permute-start | bytes 1572872 | tf_op jit(solution)/shard_map/ppermute | solution.py:297
  5.7 1.6 %copy-start = (f32[4096,128]{1,0:T(8,128)S(1)}, f32[4096,128]{1,0:T(8,128)}, u32[]{:S(2)}) copy-start(f32[4096,128]{1,0:T(8,128)} %refs_3_.11) | copy-start | bytes 6291460
  7.3 1.6 %copy-start.2 = (f32[4096,128]{1,0:T(8,128)S(1)}, f32[4096,128]{1,0:T(8,128)}, u32[]{:S(2)}) copy-start(f32[4096,128]{1,0:T(8,128)} %refs_4_.7) | copy-start | bytes 6291460
  8.9 1.2 copy-start.4
  14.5 23.9 %collective-permute-start.5 = (f32[64,2048]{1,0:T(8,128)S(1)}, f32[64,2048]{1,0:T(8,128)S(1)}, u32[]{:S(2)}, u32[]{:S(2)}) collective-permute-start(f32[64,2048]{1,0:T(8,128)S(1)} %collective-permute-done.refs_5_.refs_1_), channel_id=1, source_target_pairs={{1,0},{2,3},{5,4},{6,7},{9,8},{10,11},{13,12},{14,15},{17,16},{18,... | collective-permute-start | bytes 1572872 | tf_op jit(solution)/shard_map/ppermute | solution.py:297
  27.3 11.2 %copy-start.1 = (f32[4096,128]{1,0:T(8,128)S(1)}, f32[4096,128]{1,0:T(8,128)}, u32[]{:S(2)}) copy-start(f32[4096,128]{1,0:T(8,128)} %refs_3_.11) | copy-start | bytes 6291460
  27.3 11.2 %copy-start.3 = (f32[4096,128]{1,0:T(8,128)S(1)}, f32[4096,128]{1,0:T(8,128)}, u32[]{:S(2)}) copy-start(f32[4096,128]{1,0:T(8,128)} %refs_4_.7) | copy-start | bytes 6291460
  27.3 17.0 %collective-permute-start.10 = (f32[64,2048]{1,0:T(8,128)S(1)}, f32[64,2048]{1,0:T(8,128)S(1)}, u32[]{:S(2)}, u32[]{:S(2)}) collective-permute-start(f32[64,2048]{1,0:T(8,128)S(1)} %slice.23), channel_id=1, source_target_pairs={{1,2},{2,1},{5,6},{6,5},{9,10},{10,9},{13,14},{14,13},{17,18},{18,... | collective-permute-start | bytes 1572872 | tf_op jit(solution)/shard_map/ppermute | solution.py:297
  28.1 21.6 %collective-permute-start.4 = (f32[64,2048]{1,0:T(8,128)S(1)}, f32[64,2048]{1,0:T(8,128)S(1)}, u32[]{:S(2)}, u32[]{:S(2)}) collective-permute-start(f32[64,2048]{1,0:T(8,128)S(1)} %collective-permute-done.3.refs_7_.refs_1_.refs_8_), channel_id=1, source_target_pairs={{1,0},{2,3},{5,4},{6,7},{9,8},{10,11},{13,12},{14,15},{17,16},{18,... | collective-permute-start | bytes 1572872 | tf_op jit(solution)/shard_map/ppermute | solution.py:297
  33.4 22.1 %collective-permute-start.7 = (f32[64,2048]{1,0:T(8,128)S(1)}, f32[64,2048]{1,0:T(8,128)S(1)}, u32[]{:S(2)}, u32[]{:S(2)}) collective-permute-start(f32[64,2048]{1,0:T(8,128)S(1)} %slice.20), channel_id=1, source_target_pairs={{1,2},{2,1},{5,6},{6,5},{9,10},{10,9},{13,14},{14,13},{17,18},{18,... | collective-permute-start | bytes 1572872 | tf_op jit(solution)/shard_map/ppermute | solution.py:297
  44.3 17.2 %collective-permute-start.11 = (f32[64,2048]{1,0:T(8,128)S(1)}, f32[64,2048]{1,0:T(8,128)S(1)}, u32[]{:S(2)}, u32[]{:S(2)}) collective-permute-start(f32[64,2048]{1,0:T(8,128)S(1)} %collective-permute-done.10.refs_0_), channel_id=1, source_target_pairs={{1,0},{2,3},{5,4},{6,7},{9,8},{10,11},{13,12},{14,15},{17,16},{18,... | collective-permute-start | bytes 1572872 | tf_op jit(solution)/shard_map/ppermute | solution.py:297
  55.6 11.5 %collective-permute-start.9 = (f32[64,1024]{1,0:T(8,128)S(1)}, f32[64,1024]{1,0:T(8,128)S(1)}, u32[]{:S(2)}, u32[]{:S(2)}) collective-permute-start(f32[64,1024]{1,0:T(8,128)S(1)} %get-tuple-element.32), channel_id=1, source_target_pairs={{1,0},{2,3},{5,4},{6,7},{9,8},{10,11},{13,12},{14,15},{17,16},{18,... | collective-permute-start | bytes 786440 | tf_op jit(solution)/shard_map/ppermute | solution.py:297
  56.9 15.4 %collective-permute-start.6 = (f32[128,1280]{1,0:T(8,128)S(1)}, f32[128,1280]{1,0:T(8,128)S(1)}, u32[]{:S(2)}, u32[]{:S(2)}) collective-permute-start(f32[128,1280]{1,0:T(8,128)S(1)} %project.9.refs_2_), channel_id=1, source_target_pairs={{0,4},{4,0},{1,5},{5,1},{2,6},{6,2},{3,7},{7,3},{8,12},{12,8},{9,1... | collective-permute-start | bytes 1966088 | tf_op jit(solution)/shard_map/ppermute | solution.py:300
  57.0 14.4 %collective-permute-start.8 = (f32[64,1024]{1,0:T(8,128)S(1)}, f32[64,1024]{1,0:T(8,128)S(1)}, u32[]{:S(2)}, u32[]{:S(2)}) collective-permute-start(f32[64,1024]{1,0:T(8,128)S(1)} %get-tuple-element.54), channel_id=1, source_target_pairs={{1,0},{2,3},{5,4},{6,7},{9,8},{10,11},{13,12},{14,15},{17,16},{18,... | collective-permute-start | bytes 786440 | tf_op jit(solution)/shard_map/ppermute | solution.py:297
  58.3 14.0 %collective-permute-start.1 = (f32[64,1280]{1,0:T(8,128)S(1)}, f32[64,1280]{1,0:T(8,128)S(1)}, u32[]{:S(2)}, u32[]{:S(2)}) collective-permute-start(f32[64,1280]{1,0:T(8,128)S(1)} %project.7.refs_0_), channel_id=1, source_target_pairs={{0,4},{4,0},{1,5},{5,1},{2,6},{6,2},{3,7},{7,3},{8,12},{12,8},{9,1... | collective-permute-start | bytes 983048 | tf_op jit(solution)/shard_map/ppermute | solution.py:300
  72.2 1.7 %collective-permute-start.12 = (f32[64,1280]{1,0:T(8,128)S(1)}, f32[64,1280]{1,0:T(8,128)S(1)}, u32[]{:S(2)}, u32[]{:S(2)}) collective-permute-start(f32[64,1280]{1,0:T(8,128)S(1)} %project_last.1.refs_4_), channel_id=1, source_target_pairs={{0,4},{4,0},{1,5},{5,1},{2,6},{6,2},{3,7},{7,3},{8,12},{12,8},{9,1... | collective-permute-start | bytes 983048 | tf_op jit(solution)/shard_map/ppermute | solution.py:300
  75.9 14.8 %collective-permute-start.13 = (f32[64,2048]{1,0:T(8,128)S(1)}, f32[64,2048]{1,0:T(8,128)S(1)}, u32[]{:S(2)}, u32[]{:S(2)}) collective-permute-start(f32[64,2048]{1,0:T(8,128)S(1)} %get-tuple-element.38), channel_id=1, source_target_pairs={{0,1},{3,2},{4,5},{7,6},{8,9},{11,10},{12,13},{15,14},{16,17},{19,... | collective-permute-start | bytes 1572872 | tf_op jit(solution)/shard_map/ppermute | solution.py:297
  81.6 22.8 %collective-permute-start.18 = (f32[64,2048]{1,0:T(8,128)S(1)}, f32[64,2048]{1,0:T(8,128)S(1)}, u32[]{:S(2)}, u32[]{:S(2)}) collective-permute-start(f32[64,2048]{1,0:T(8,128)S(1)} %out_again.2), channel_id=1, source_target_pairs={{0,1},{3,2},{4,5},{7,6},{8,9},{11,10},{12,13},{15,14},{16,17},{19,... | collective-permute-start | bytes 1572872 | tf_op jit(solution)/shard_map/ppermute | solution.py:297
  89.3 22.7 %collective-permute-start.16 = (f32[64,2048]{1,0:T(8,128)S(1)}, f32[64,2048]{1,0:T(8,128)S(1)}, u32[]{:S(2)}, u32[]{:S(2)}) collective-permute-start(f32[64,2048]{1,0:T(8,128)S(1)} %get-tuple-element.45), channel_id=1, source_target_pairs={{0,1},{3,2},{4,5},{7,6},{8,9},{11,10},{12,13},{15,14},{16,17},{19,... | collective-permute-start | bytes 1572872 | tf_op jit(solution)/shard_map/ppermute | solution.py:297
  90.7 22.1 %collective-permute-start.14 = (f32[64,2048]{1,0:T(8,128)S(1)}, f32[64,2048]{1,0:T(8,128)S(1)}, u32[]{:S(2)}, u32[]{:S(2)}) collective-permute-start(f32[64,2048]{1,0:T(8,128)S(1)} %add.30), channel_id=1, source_target_pairs={{1,2},{2,1},{5,6},{6,5},{9,10},{10,9},{13,14},{14,13},{17,18},{18,... | collective-permute-start | bytes 1572872 | tf_op jit(solution)/shard_map/ppermute | solution.py:297
  97.0 26.3 %collective-permute-start.21 = (f32[64,2048]{1,0:T(8,128)S(1)}, f32[64,2048]{1,0:T(8,128)S(1)}, u32[]{:S(2)}, u32[]{:S(2)}) collective-permute-start(f32[64,2048]{1,0:T(8,128)S(1)} %get-tuple-element.50), channel_id=1, source_target_pairs={{0,1},{3,2},{4,5},{7,6},{8,9},{11,10},{12,13},{15,14},{16,17},{19,... | collective-permute-start | bytes 1572872 | tf_op jit(solution)/shard_map/ppermute | solution.py:297
  104.5 19.5 %collective-permute-start.19 = (f32[64,2048]{1,0:T(8,128)S(1)}, f32[64,2048]{1,0:T(8,128)S(1)}, u32[]{:S(2)}, u32[]{:S(2)}) collective-permute-start(f32[64,2048]{1,0:T(8,128)S(1)} %add.35), channel_id=1, source_target_pairs={{1,2},{2,1},{5,6},{6,5},{9,10},{10,9},{13,14},{14,13},{17,18},{18,... | collective-permute-start | bytes 1572872 | tf_op jit(solution)/shard_map/ppermute | solution.py:297
  112.1 18.6 %collective-permute-start.17 = (f32[64,2048]{1,0:T(8,128)S(1)}, f32[64,2048]{1,0:T(8,128)S(1)}, u32[]{:S(2)}, u32[]{:S(2)}) collective-permute-start(f32[64,2048]{1,0:T(8,128)S(1)} %add.32), channel_id=1, source_target_pairs={{1,2},{2,1},{5,6},{6,5},{9,10},{10,9},{13,14},{14,13},{17,18},{18,... | collective-permute-start | bytes 1572872 | tf_op jit(solution)/shard_map/ppermute | solution.py:297
  112.9 21.6 %collective-permute-start.15 = (f32[64,2048]{1,0:T(8,128)S(1)}, f32[64,2048]{1,0:T(8,128)S(1)}, u32[]{:S(2)}, u32[]{:S(2)}) collective-permute-start(f32[64,2048]{1,0:T(8,128)S(1)} %add.31), channel_id=1, source_target_pairs={{0,1},{1,0},{2,3},{3,2},{4,5},{5,4},{6,7},{7,6},{8,9},{9,8},{10,11... | collective-permute-start | bytes 1572872 | tf_op jit(solution)/shard_map/ppermute | solution.py:297
  123.3 11.3 %collective-permute-start.22 = (f32[64,2048]{1,0:T(8,128)S(1)}, f32[64,2048]{1,0:T(8,128)S(1)}, u32[]{:S(2)}, u32[]{:S(2)}) collective-permute-start(f32[64,2048]{1,0:T(8,128)S(1)} %add.37), channel_id=1, source_target_pairs={{1,2},{2,1},{5,6},{6,5},{9,10},{10,9},{13,14},{14,13},{17,18},{18,... | collective-permute-start | bytes 1572872 | tf_op jit(solution)/shard_map/ppermute | solution.py:297
  124.1 21.0 %collective-permute-start.20 = (f32[64,2048]{1,0:T(8,128)S(1)}, f32[64,2048]{1,0:T(8,128)S(1)}, u32[]{:S(2)}, u32[]{:S(2)}) collective-permute-start(f32[64,2048]{1,0:T(8,128)S(1)} %add.36), channel_id=1, source_target_pairs={{0,1},{1,0},{2,3},{3,2},{4,5},{5,4},{6,7},{7,6},{8,9},{9,8},{10,11... | collective-permute-start | bytes 1572872 | tf_op jit(solution)/shard_map/ppermute | solution.py:297

commit v7 on v6

--- a/solution.py
+++ b/solution.py
@@ -203,9 +203,9 @@
     )(w, before)
 
 
-def mix_kernel(n_parts, ask, q_width, kv_width, start, step, *refs):
+def mix_kernel(n_parts, ask, q_width, kv_width, start, step, is_split, *refs):
     part_refs, rest = refs[:n_parts], refs[n_parts:]
-    if start is None:
+    if is_split:
         (w_high, w_low), outs = rest[:2], rest[2:]
     else:
         w_ref, outs, (buf, sems) = rest[0], rest[1:-2], rest[-2:]
@@ -230,8 +230,9 @@
     attended = (high[...], low[...])
     for k in range(outs[0].shape[1] // step):
         columns = slice(k * step, (k + 1) * step)
-        if start is None:
-            w = (w_high[:, columns], w_low[:, columns])
+        if is_split:
+            these = slice(start + k * step, start + (k + 1) * step)
+            w = (w_high[:, these], w_low[:, these])
         else:
             copy(k).wait()
             w = split(buf[k])
@@ -243,18 +244,18 @@
 
 
 def mix(operands, ask, rows, keyed, w, kv_width, slots, start, columns, name, step=512):
-    q_width = w[0].shape[0]
+    q_width, is_split = w[0].shape[0], len(w) == 2
     steps = columns // step
     attended = [jax.ShapeDtypeStruct((rows, q_width), jnp.bfloat16)] * (0 if ask is None else 2)
     out_shape = attended + [jax.ShapeDtypeStruct((s, columns), jnp.float32) for s in slots]
     vmem = pl.BlockSpec(memory_space=pltpu.VMEM)
     scratch = [pltpu.VMEM((steps, q_width, step), jnp.float32), pltpu.SemaphoreType.DMA((steps,))]
     return pl.pallas_call(
-        functools.partial(mix_kernel, len(operands), ask, q_width, kv_width, start, step),
-        in_specs=[vmem] * len(operands) + ([vmem] * 2 if start is None else [pl.BlockSpec(memory_space=pl.ANY)]),
+        functools.partial(mix_kernel, len(operands), ask, q_width, kv_width, start, step, is_split),
+        in_specs=[vmem] * len(operands) + ([vmem] * 2 if is_split else [pl.BlockSpec(memory_space=pl.ANY)]),
         out_specs=[vmem] * len(out_shape),
         out_shape=out_shape,
-        scratch_shapes=[] if start is None else scratch,
+        scratch_shapes=[] if is_split else scratch,
         compiler_params=pltpu.CompilerParams(vmem_limit_bytes=VMEM_LIMIT),
         cost_estimate=pl.CostEstimate(
             flops=8 * rows * q_width * columns + 32 * rows * keyed * q_width,
@@ -269,13 +270,13 @@
     rows = sum(a.shape[0] for a, _ in parts[first:last])
     keyed = sum(a.shape[0] for a, _ in parts)
     flat = [r for pair in parts for r in pair]
-    res = mix(flat, slice(first, last), rows, keyed, w, kv_width, slots, None, columns, "attend_out")
+    res = mix(flat, slice(first, last), rows, keyed, w, kv_width, slots, 0, columns, "attend_out")
     return res[:2], res[2:]
 
 
-def out_again(attended, w_out, slots, start, columns):
+def out_again(attended, w, slots, start, columns):
     rows = attended[0].shape[0]
-    return mix(list(attended), None, rows, 0, [w_out], 0, slots, start, columns, "out_again")
+    return mix(list(attended), None, rows, 0, w, 0, slots, start, columns, "out_again")
 
 
 def after(a, *others):
@@ -337,16 +338,21 @@
     third = (third, swap(third))
 
     parts = [first, second, third]
-    a_third, m_third = attend_out(parts, 2, 3, w_split, kv_width, [rows], pieces[0][1])
-    m_third = [m_third[0], out_again(a_third, w_out, [rows], *pieces[1])[0]]
+    early = cut([pieces[0][1] // 2] * 2 + [pieces[1][1]])
+    a_third, m_third = attend_out(parts, 2, 3, w_split, kv_width, [rows], early[0][1])
+    m_third = [m_third[0]] + [
+        out_again(a_third, w, [rows], *p)[0] for w, p in zip((w_split, [w_out]), early[1:])
+    ]
     r1 = [hop(m, ENDS_OUT) for m in m_third]
-    others = [tuple(after(a, *m_third) for a in first), second, third]
+    others = [tuple(after(a, r1[0], *m_third) for a in first), second, third]
     a_rest, mixed = attend_out(others, 0, 2, w_split, kv_width, [rows] * 3, pieces[0][1])
-    mixed = [mixed, out_again(a_rest, w_out, [rows] * 3, *pieces[1])]
+    r1[1] = after(r1[1], *a_rest)
+    mixed = [mixed, out_again(a_rest, [w_out], [rows] * 3, *pieces[1])]
+    far = [jnp.concatenate([m + r for m, r in zip(m_third[:2], r1[:2])], axis=1), m_third[2] + r1[2]]
     result = []
-    for (m_own, m_near, m_second), m, r in zip(mixed, m_third, r1):
+    for (m_own, m_near, m_second), f in zip(mixed, far):
         r2e = hop(m_second, ENDS_OUT)
-        r2m = hop(m + r, MIDDLE)
+        r2m = hop(f, MIDDLE)
         r3m = hop(m_second + r2e, MIDDLE)
         r3x = hop(m_near + r2m, PAIRS)
         result.append(m_own + (r3x + r3m))

time: 148 us -> 147 us (level)
  waiting for transfers between devices: 46 us -> 43.8 us
    ppermute x20 -> x21, waiting for transfers between devices: 44.4 us -> 42.2 us  [hop(): return lax.ppermute(a, 'col', pairs)]
    ppermute x20 -> x21, starting transfers between devices: 40.5 us -> 41.8 us  [hop(): return lax.ppermute(a, 'col', pairs)]
    pallas_call x4 -> x5, Pallas kernels: 17.9 us -> 18.1 us  [mix(): pl.pallas_call(functools.partial(mix_kernel, len(operands), ask, q_width,...]
  transfers between devices with their start and end apart: 23 -> 24, of which waited for: 11 -> 11; matrix products, arithmetic and copies ran while one was open for 1% -> 1% of each run, Pallas kernels for 34% -> 34%
where the time goes in v7:
time: 147 us; the launch traced here: 146 us
  Pallas kernels  51.4 us (35%)
  waiting for transfers between devices  43.8 us (30%)
  starting transfers between devices  42.5 us (29%)
  local copies, waits for them, and re-layouts  5.82 us (4%)
  other arithmetic  1.59 us (1%)
    ppermute x21, waiting for transfers between devices, hop(): return lax.ppermute(a, 'col', pairs)  42.2 us
    ppermute x21, starting transfers between devices, hop(): return lax.ppermute(a, 'col', pairs)  41.8 us
    pallas_call x6, Pallas kernels, project(): pl.pallas_call(functools.partial(project_kernel, terms, total is not None...  28.7 us
    pallas_call x5, Pallas kernels, mix(): pl.pallas_call(functools.partial(mix_kernel, len(operands), ask, q_width,...  18.1 us
    unnamed x10, local copies, waits for them, and re-layouts  4.41 us
    pallas_call x1, Pallas kernels, halve(): pl.pallas_call(functools.partial(halve_kernel, start), in_specs=[anywhere...  3.8 us
  transfers between devices with their start and end apart: 24, of which 11 were waited for; matrix products, arithmetic and copies ran while one was open for 1% of the time, Pallas kernels for 34%

profile of v7, /device:TPU:0, one launch (start us, length us, event | category | flops | bytes accessed | tf_op | source)
XLA Modules:
  0.0 145.7 jit_solution(15735114344486044249)
XLA Ops:
  0.0 3.0 %collective-permute-start.2 = (f32[64,4096]{1,0:T(8,128)}, f32[64,4096]{1,0:T(8,128)S(1)}, u32[]{:S(2)}, u32[]{:S(2)}) collective-permute-start(f32[64,4096]{1,0:T(8,128)} %refs_0_.3), channel_id=1, source_target_pairs={{0,1},{1,0},{2,3},{3,2},{4,5},{5,4},{6,7},{7,6},{8,9},{9,8},{10,11... | collective-permute-start | bytes 3145736 | tf_op jit(solution)/shard_map/ppermute | solution.py:298
  3.0 1.3 fusion
  4.3 0.7 collective-permute-start
  5.0 0.7 collective-permute-start.3
  5.7 0.0 copy-start
  5.7 1.6 %copy-done = f32[4096,128]{1,0:T(8,128)S(1)} copy-done((f32[4096,128]{1,0:T(8,128)S(1)}, f32[4096,128]{1,0:T(8,128)}, u32[]{:S(2)}) %copy-start) | copy-done | bytes 2097176
  7.3 1.6 %copy-done.2 = f32[4096,128]{1,0:T(8,128)S(1)} copy-done((f32[4096,128]{1,0:T(8,128)S(1)}, f32[4096,128]{1,0:T(8,128)}, u32[]{:S(2)}) %copy-start.2) | copy-done | bytes 2097176
  8.9 1.2 copy-done.4
  10.1 4.3 %project.6.refs_4_ = f32[64,1280]{1,0:T(8,128)S(1)} custom-call(f32[64,4096]{1,0:T(8,128)S(1)} %copy-done.4, f32[4096,1024]{1,0:T(8,128)} %refs_2_.9, f32[4096,128]{1,0:T(8,128)S(1)} %copy-done, f32[4096,128]{1,0:T(8,128)S(1)} %copy-done.2), custom_call_target="tpu_custom_call" | custom-call | flops 1342177280 | bytes 11010048 | tf_op jit(solution)/shard_map/project/pallas_call | solution.py:102
  14.5 0.0 collective-permute-done.refs_5_.refs_1_
  14.5 1.3 collective-permute-start.5
  15.8 4.3 %project.7.refs_0_ = f32[64,1280]{1,0:T(8,128)S(1)} custom-call(f32[64,4096]{1,0:T(8,128)S(1)} %copy-done.4, f32[4096,1024]{1,0:T(8,128)} %refs_2_.9, f32[4096,128]{1,0:T(8,128)S(1)} %copy-done, f32[4096,128]{1,0:T(8,128)S(1)} %copy-done.2, f32[64,1280]{1,0:T(8,128)S(1)} %project.6.refs_4_, f32[64,2048]{1,0:T(8,128)S(1)} %collective-permute-done.refs_5_.refs_1_), custom_call_target="tpu_custom_call" | custom-call | flops 1342177280 | bytes 11010048 | tf_op jit(solution)/shard_map/project/pallas_call | solution.py:102
  20.1 7.1 %collective-permute-done.2.before.refs_0_ = f32[64,4096]{1,0:T(8,128)S(1)} collective-permute-done((f32[64,4096]{1,0:T(8,128)}, f32[64,4096]{1,0:T(8,128)S(1)}, u32[]{:S(2)}, u32[]{:S(2)}) %collective-permute-start.2) | collective-permute-done | bytes 1048608 | tf_op jit(solution)/shard_map/ppermute | solution.py:298
  27.3 0.0 copy-start.1
  27.3 0.0 copy-start.3
  27.3 0.8 collective-permute-start.10
  28.1 1.4 collective-permute-start.4
  29.6 3.8 %halve.1 = (bf16[1024,2048]{1,0:T(8,128)(2,1)S(1)}, bf16[1024,2048]{1,0:T(8,128)(2,1)S(1)}) custom-call(f32[1024,4096]{1,0:T(8,128)} %refs_2_.11, f32[64,4096]{1,0:T(8,128)S(1)} %collective-permute-done.2.before.refs_0_), custom_call_target="tpu_custom_call" | custom-call | flops 2097152 | bytes 16777216 | tf_op jit(solution)/shard_map/halve/pallas_call | solution.py:194
  33.4 0.7 collective-permute-start.7
  34.1 4.3 %collective-permute-done.5.refs_2_ = f32[64,2048]{1,0:T(8,128)S(1)} collective-permute-done((f32[64,2048]{1,0:T(8,128)S(1)}, f32[64,2048]{1,0:T(8,128)S(1)}, u32[]{:S(2)}, u32[]{:S(2)}) %collective-permute-start.5) | collective-permute-done | bytes 524320 | tf_op jit(solution)/shard_map/ppermute | solution.py:298
  38.5 5.8 %project.8.refs_6_ = f32[128,1280]{1,0:T(8,128)S(1)} custom-call(f32[64,4096]{1,0:T(8,128)S(1)} %collective-permute-done.2.before.refs_0_, f32[64,2048]{1,0:T(8,128)S(1)} %collective-permute-done.refs_5_.refs_1_, f32[64,2048]{1,0:T(8,128)S(1)} %collective-permute-done.5.refs_2_, f32[4096,1024]{1,0:T(8,128)} %refs_2_.9, f32[4096,128]{1,0:T(8,128)S(1)} %copy-done.1, ...), custom_call_target="tpu_custom_call" | custom-call | flops 2684354560 | bytes 11534336 | tf_op jit(solution)/shard_map/project/pallas_call | solution.py:102
  44.3 1.5 %collective-permute-start.11 = (f32[64,2048]{1,0:T(8,128)S(1)}, f32[64,2048]{1,0:T(8,128)S(1)}, u32[]{:S(2)}, u32[]{:S(2)}) collective-permute-start(f32[64,2048]{1,0:T(8,128)S(1)} %collective-permute-done.10.refs_0_), channel_id=1, source_target_pairs={{1,0},{2,3},{5,4},{6,7},{9,8},{10,11},{13,12},{14,15},{17,16},{18,... | collective-permute-start | bytes 1572872 | tf_op jit(solution)/shard_map/ppermute | solution.py:298
  45.8 3.9 %collective-permute-done.4.refs_2_ = f32[64,2048]{1,0:T(8,128)S(1)} collective-permute-done((f32[64,2048]{1,0:T(8,128)S(1)}, f32[64,2048]{1,0:T(8,128)S(1)}, u32[]{:S(2)}, u32[]{:S(2)}) %collective-permute-start.4) | collective-permute-done | bytes 524320 | tf_op jit(solution)/shard_map/ppermute | solution.py:298
  49.7 5.8 %project.9.refs_2_ = f32[128,1280]{1,0:T(8,128)S(1)} custom-call(f32[64,4096]{1,0:T(8,128)S(1)} %collective-permute-done.2.before.refs_0_, f32[64,2048]{1,0:T(8,128)S(1)} %collective-permute-done.3.refs_7_.refs_1_.refs_8_, f32[64,2048]{1,0:T(8,128)S(1)} %collective-permute-done.4.refs_2_, f32[4096,1024]{1,0:T(8,128)} %refs_2_.9, f32[4096,128]{1,0:T(8,128)S(1)} %copy-done.1, ...), custom_call_target="tpu_custom_call" | custom-call | flops 2684354560 | bytes 11534336 | tf_op jit(solution)/shard_map/project/pallas_call | solution.py:102
  55.6 1.3 collective-permute-start.9
  56.9 0.1 collective-permute-start.6
  57.0 1.3 collective-permute-start.8
  58.3 0.6 collective-permute-start.1
  58.8 2.7 %collective-permute-done.11.refs_1_ = f32[64,2048]{1,0:T(8,128)S(1)} collective-permute-done((f32[64,2048]{1,0:T(8,128)S(1)}, f32[64,2048]{1,0:T(8,128)S(1)}, u32[]{:S(2)}, u32[]{:S(2)}) %collective-permute-start.11) | collective-permute-done | bytes 524320 | tf_op jit(solution)/shard_map/ppermute | solution.py:298
  61.5 4.3 %project.10.refs_5_ = f32[64,1280]{1,0:T(8,128)S(1)} custom-call(f32[64,2048]{1,0:T(8,128)S(1)} %collective-permute-done.10.refs_0_, f32[64,2048]{1,0:T(8,128)S(1)} %collective-permute-done.11.refs_1_, f32[4096,1024]{1,0:T(8,128)} %refs_2_.9, f32[4096,128]{1,0:T(8,128)S(1)} %copy-done.1, f32[4096,128]{1,0:T(8,128)S(1)} %copy-done.3), custom_call_target="tpu_custom_call" | custom-call | flops 1342177280 | bytes 11010048 | tf_op jit(solution)/shard_map/project/pallas_call | solution.py:102
  65.8 1.3 collective-permute-done.9.refs_1_
  67.1 4.0 %project.11 = (f32[64,1280]{1,0:T(8,128)S(1)}, bf16[1024,1280]{1,0:T(8,128)(2,1)S(1)}, bf16[1024,1280]{1,0:T(8,128)(2,1)S(1)}) custom-call(f32[64,2048]{1,0:T(8,128)S(1)} %collective-permute-done.7.refs_0_.x, f32[64,1024]{1,0:T(8,128)S(1)} %collective-permute-done.9.refs_1_, f32[4096,1024]{1,0:T(8,128)} %refs_2_.9, f32[4096,128]{1,0:T(8,128)S(1)} %copy-done.1, ...), custom_call_target="tpu_custom_call" | custom-call | flops 671088640 | bytes 5505024 | tf_op jit(solution)/shard_map/project/pallas_call | solution.py:102
  71.1 0.2 collective-permute-done.8.y
  71.3 0.9 project_last.1.refs_4_
  72.2 0.1 collective-permute-start.12
  72.3 1.6 %collective-permute-done.12.refs_5_ = f32[64,1280]{1,0:T(8,128)S(1)} collective-permute-done((f32[64,1280]{1,0:T(8,128)S(1)}, f32[64,1280]{1,0:T(8,128)S(1)}, u32[]{:S(2)}, u32[]{:S(2)}) %collective-permute-start.12) | collective-permute-done | bytes 327712 | tf_op jit(solution)/shard_map/ppermute | solution.py:301
  73.9 1.4 attend_out.2
  75.3 1.5 %collective-permute-start.13 = (f32[64,1024]{1,0:T(8,128)S(1)}, f32[64,1024]{1,0:T(8,128)S(1)}, u32[]{:S(2)}, u32[]{:S(2)}) collective-permute-start(f32[64,1024]{1,0:T(8,128)S(1)} %get-tuple-element.39), channel_id=1, source_target_pairs={{0,1},{3,2},{4,5},{7,6},{8,9},{11,10},{12,13},{15,14},{16,17},{19,... | collective-permute-start | bytes 786440 | tf_op jit(solution)/shard_map/ppermute | solution.py:298
  76.8 0.7 out_again.3
  77.5 1.5 %collective-permute-start.14 = (f32[64,1024]{1,0:T(8,128)S(1)}, f32[64,1024]{1,0:T(8,128)S(1)}, u32[]{:S(2)}, u32[]{:S(2)}) collective-permute-start(f32[64,1024]{1,0:T(8,128)S(1)} %out_again.3), channel_id=1, source_target_pairs={{0,1},{3,2},{4,5},{7,6},{8,9},{11,10},{12,13},{15,14},{16,17},{19,... | collective-permute-start | bytes 786440 | tf_op jit(solution)/shard_map/ppermute | solution.py:298
  79.0 4.0 %out_again.4 = f32[64,2048]{1,0:T(8,128)S(1)} custom-call(bf16[64,1024]{1,0:T(8,128)(2,1)S(1)} %get-tuple-element.40.refs_0_, bf16[64,1024]{1,0:T(8,128)(2,1)S(1)} %get-tuple-element.41.refs_1_, f32[1024,4096]{1,0:T(8,128)} %refs_2_.11), custom_call_target="tpu_custom_call" | custom-call | flops 1073741824 | bytes 8912896 | tf_op jit(solution)/shard_map/out_again/pallas_call | solution.py:253
  83.1 1.3 collective-permute-start.19
  84.4 6.4 %attend_out.3 = (bf16[192,1024]{1,0:T(8,128)(2,1)S(1)}, bf16[192,1024]{1,0:T(8,128)(2,1)S(1)}, f32[64,2048]{1,0:T(8,128)S(1)}, f32[64,2048]{1,0:T(8,128)S(1)}, f32[64,2048]{1,0:T(8,128)S(1)}) custom-call(f32[64,1280]{1,0:T(8,128)S(1)} %project.7.refs_0_, f32[64,1280]{1,0:T(8,128)S(1)} %collective-permute-done.1.refs_1_, f32[128,1280]{1,0:T(8,128)S(1)} %project.9.refs_2_, ...), custom_call_target="tpu_custom_call" | custom-call | flops 4831838208 | bytes 9961472 | tf_op jit(solution)/shard_map/attend_out/pallas_call | solution.py:253
  90.8 3.4 %collective-permute-start.17 = (f32[64,2048]{1,0:T(8,128)S(1)}, f32[64,2048]{1,0:T(8,128)S(1)}, u32[]{:S(2)}, u32[]{:S(2)}) collective-permute-start(f32[64,2048]{1,0:T(8,128)S(1)} %get-tuple-element.49), channel_id=1, source_target_pairs={{0,1},{3,2},{4,5},{7,6},{8,9},{11,10},{12,13},{15,14},{16,17},{19,... | collective-permute-start | bytes 1572872 | tf_op jit(solution)/shard_map/ppermute | solution.py:298
  94.3 0.7 collective-permute-start.15
  95.0 5.6 %out_again.5 = (f32[64,2048]{1,0:T(8,128)S(1)}, f32[64,2048]{1,0:T(8,128)S(1)}, f32[64,2048]{1,0:T(8,128)S(1)}) custom-call(bf16[192,1024]{1,0:T(8,128)(2,1)S(1)} %get-tuple-element.46.refs_0_, bf16[192,1024]{1,0:T(8,128)(2,1)S(1)} %get-tuple-element.47.refs_1_, f32[1024,4096]{1,0:T(8,128)} %refs_2_.11), custom_call_target="tpu_custom_call" | custom-call | flops 3221225472 | bytes 9961472 | tf_op jit(solution)/shard_map/out_again/pallas_call | solution.py:253
  100.6 5.4 %collective-permute-start.22 = (f32[64,2048]{1,0:T(8,128)S(1)}, f32[64,2048]{1,0:T(8,128)S(1)}, u32[]{:S(2)}, u32[]{:S(2)}) collective-permute-start(f32[64,2048]{1,0:T(8,128)S(1)} %get-tuple-element.52), channel_id=1, source_target_pairs={{0,1},{3,2},{4,5},{7,6},{8,9},{11,10},{12,13},{15,14},{16,17},{19,... | collective-permute-start | bytes 1572872 | tf_op jit(solution)/shard_map/ppermute | solution.py:298
  106.0 0.1 add.39
  106.1 0.7 collective-permute-start.20
  106.8 4.7 %collective-permute-done.17 = f32[64,2048]{1,0:T(8,128)S(1)} collective-permute-done((f32[64,2048]{1,0:T(8,128)S(1)}, f32[64,2048]{1,0:T(8,128)S(1)}, u32[]{:S(2)}, u32[]{:S(2)}) %collective-permute-start.17) | collective-permute-done | bytes 524320 | tf_op jit(solution)/shard_map/ppermute | solution.py:298
  111.5 0.1 add.36
  111.6 0.7 collective-permute-start.18
  112.3 0.1 add.35
  112.3 6.6 %collective-permute-start.16 = (f32[64,2048]{1,0:T(8,128)S(1)}, f32[64,2048]{1,0:T(8,128)S(1)}, u32[]{:S(2)}, u32[]{:S(2)}) collective-permute-start(f32[64,2048]{1,0:T(8,128)S(1)} %add.35), channel_id=1, source_target_pairs={{0,1},{1,0},{2,3},{3,2},{4,5},{5,4},{6,7},{7,6},{8,9},{9,8},{10,11... | collective-permute-start | bytes 1572872 | tf_op jit(solution)/shard_map/ppermute | solution.py:298
  119.0 3.8 %collective-permute-done.22 = f32[64,2048]{1,0:T(8,128)S(1)} collective-permute-done((f32[64,2048]{1,0:T(8,128)S(1)}, f32[64,2048]{1,0:T(8,128)S(1)}, u32[]{:S(2)}, u32[]{:S(2)}) %collective-permute-start.22) | collective-permute-done | bytes 524320 | tf_op jit(solution)/shard_map/ppermute | solution.py:298
  122.7 0.1 add.41
  122.8 0.7 collective-permute-start.23
  123.5 0.1 add.40
  123.6 6.6 %collective-permute-start.21 = (f32[64,2048]{1,0:T(8,128)S(1)}, f32[64,2048]{1,0:T(8,128)S(1)}, u32[]{:S(2)}, u32[]{:S(2)}) collective-permute-start(f32[64,2048]{1,0:T(8,128)S(1)} %add.40), channel_id=1, source_target_pairs={{0,1},{1,0},{2,3},{3,2},{4,5},{5,4},{6,7},{7,6},{8,9},{9,8},{10,11... | collective-permute-start | bytes 1572872 | tf_op jit(solution)/shard_map/ppermute | solution.py:298
  130.2 3.8 %collective-permute-done.16 = f32[64,2048]{1,0:T(8,128)S(1)} collective-permute-done((f32[64,2048]{1,0:T(8,128)S(1)}, f32[64,2048]{1,0:T(8,128)S(1)}, u32[]{:S(2)}, u32[]{:S(2)}) %collective-permute-start.16) | collective-permute-done | bytes 524320 | tf_op jit(solution)/shard_map/ppermute | solution.py:298
  134.0 0.1 add_add_fusion.1
  134.1 10.5 %collective-permute-done.21 = f32[64,2048]{1,0:T(8,128)S(1)} collective-permute-done((f32[64,2048]{1,0:T(8,128)S(1)}, f32[64,2048]{1,0:T(8,128)S(1)}, u32[]{:S(2)}, u32[]{:S(2)}) %collective-permute-start.21) | collective-permute-done | bytes 524320 | tf_op jit(solution)/shard_map/ppermute | solution.py:298
  144.5 0.1 add_add_fusion
  144.6 1.0 pad_maximum_fusion
  (22 shorter events, 0.2 us)
Async XLA Ops:
  0.0 27.2 %collective-permute-start.2 = (f32[64,4096]{1,0:T(8,128)}, f32[64,4096]{1,0:T(8,128)S(1)}, u32[]{:S(2)}, u32[]{:S(2)}) collective-permute-start(f32[64,4096]{1,0:T(8,128)} %refs_0_.3), channel_id=1, source_target_pairs={{0,1},{1,0},{2,3},{3,2},{4,5},{5,4},{6,7},{7,6},{8,9},{9,8},{10,11... | collective-permute-start | bytes 3145736 | tf_op jit(solution)/shard_map/ppermute | solution.py:298
  4.3 10.2 %collective-permute-start = (f32[64,2048]{1,0:T(8,128)S(1)}, f32[64,2048]{1,0:T(8,128)S(1)}, u32[]{:S(2)}, u32[]{:S(2)}) collective-permute-start(f32[64,2048]{1,0:T(8,128)S(1)} %get-tuple-element.54), channel_id=1, source_target_pairs={{1,2},{2,1},{5,6},{6,5},{9,10},{10,9},{13,14},{14,13},{17,18},{18,... | collective-permute-start | bytes 1572872 | tf_op jit(solution)/shard_map/ppermute | solution.py:298
  5.0 23.1 %collective-permute-start.3 = (f32[64,2048]{1,0:T(8,128)S(1)}, f32[64,2048]{1,0:T(8,128)S(1)}, u32[]{:S(2)}, u32[]{:S(2)}) collective-permute-start(f32[64,2048]{1,0:T(8,128)S(1)} %get-tuple-element.53), channel_id=1, source_target_pairs={{1,2},{2,1},{5,6},{6,5},{9,10},{10,9},{13,14},{14,13},{17,18},{18,... | collective-permute-start | bytes 1572872 | tf_op jit(solution)/shard_map/ppermute | solution.py:298
  5.7 1.6 %copy-start = (f32[4096,128]{1,0:T(8,128)S(1)}, f32[4096,128]{1,0:T(8,128)}, u32[]{:S(2)}) copy-start(f32[4096,128]{1,0:T(8,128)} %refs_3_.11) | copy-start | bytes 6291460
  7.3 1.6 %copy-start.2 = (f32[4096,128]{1,0:T(8,128)S(1)}, f32[4096,128]{1,0:T(8,128)}, u32[]{:S(2)}) copy-start(f32[4096,128]{1,0:T(8,128)} %refs_4_.7) | copy-start | bytes 6291460
  8.9 1.2 copy-start.4
  14.5 23.9 %collective-permute-start.5 = (f32[64,2048]{1,0:T(8,128)S(1)}, f32[64,2048]{1,0:T(8,128)S(1)}, u32[]{:S(2)}, u32[]{:S(2)}) collective-permute-start(f32[64,2048]{1,0:T(8,128)S(1)} %collective-permute-done.refs_5_.refs_1_), channel_id=1, source_target_pairs={{1,0},{2,3},{5,4},{6,7},{9,8},{10,11},{13,12},{14,15},{17,16},{18,... | collective-permute-start | bytes 1572872 | tf_op jit(solution)/shard_map/ppermute | solution.py:298
  27.3 11.2 %copy-start.1 = (f32[4096,128]{1,0:T(8,128)S(1)}, f32[4096,128]{1,0:T(8,128)}, u32[]{:S(2)}) copy-start(f32[4096,128]{1,0:T(8,128)} %refs_3_.11) | copy-start | bytes 6291460
  27.3 11.2 %copy-start.3 = (f32[4096,128]{1,0:T(8,128)S(1)}, f32[4096,128]{1,0:T(8,128)}, u32[]{:S(2)}) copy-start(f32[4096,128]{1,0:T(8,128)} %refs_4_.7) | copy-start | bytes 6291460
  27.3 17.0 %collective-permute-start.10 = (f32[64,2048]{1,0:T(8,128)S(1)}, f32[64,2048]{1,0:T(8,128)S(1)}, u32[]{:S(2)}, u32[]{:S(2)}) collective-permute-start(f32[64,2048]{1,0:T(8,128)S(1)} %slice.23), channel_id=1, source_target_pairs={{1,2},{2,1},{5,6},{6,5},{9,10},{10,9},{13,14},{14,13},{17,18},{18,... | collective-permute-start | bytes 1572872 | tf_op jit(solution)/shard_map/ppermute | solution.py:298
  28.1 21.6 %collective-permute-start.4 = (f32[64,2048]{1,0:T(8,128)S(1)}, f32[64,2048]{1,0:T(8,128)S(1)}, u32[]{:S(2)}, u32[]{:S(2)}) collective-permute-start(f32[64,2048]{1,0:T(8,128)S(1)} %collective-permute-done.3.refs_7_.refs_1_.refs_8_), channel_id=1, source_target_pairs={{1,0},{2,3},{5,4},{6,7},{9,8},{10,11},{13,12},{14,15},{17,16},{18,... | collective-permute-start | bytes 1572872 | tf_op jit(solution)/shard_map/ppermute | solution.py:298
  33.4 22.1 %collective-permute-start.7 = (f32[64,2048]{1,0:T(8,128)S(1)}, f32[64,2048]{1,0:T(8,128)S(1)}, u32[]{:S(2)}, u32[]{:S(2)}) collective-permute-start(f32[64,2048]{1,0:T(8,128)S(1)} %slice.20), channel_id=1, source_target_pairs={{1,2},{2,1},{5,6},{6,5},{9,10},{10,9},{13,14},{14,13},{17,18},{18,... | collective-permute-start | bytes 1572872 | tf_op jit(solution)/shard_map/ppermute | solution.py:298
  44.3 17.2 %collective-permute-start.11 = (f32[64,2048]{1,0:T(8,128)S(1)}, f32[64,2048]{1,0:T(8,128)S(1)}, u32[]{:S(2)}, u32[]{:S(2)}) collective-permute-start(f32[64,2048]{1,0:T(8,128)S(1)} %collective-permute-done.10.refs_0_), channel_id=1, source_target_pairs={{1,0},{2,3},{5,4},{6,7},{9,8},{10,11},{13,12},{14,15},{17,16},{18,... | collective-permute-start | bytes 1572872 | tf_op jit(solution)/shard_map/ppermute | solution.py:298
  55.6 11.5 %collective-permute-start.9 = (f32[64,1024]{1,0:T(8,128)S(1)}, f32[64,1024]{1,0:T(8,128)S(1)}, u32[]{:S(2)}, u32[]{:S(2)}) collective-permute-start(f32[64,1024]{1,0:T(8,128)S(1)} %get-tuple-element.33), channel_id=1, source_target_pairs={{1,0},{2,3},{5,4},{6,7},{9,8},{10,11},{13,12},{14,15},{17,16},{18,... | collective-permute-start | bytes 786440 | tf_op jit(solution)/shard_map/ppermute | solution.py:298
  56.9 15.4 %collective-permute-start.6 = (f32[128,1280]{1,0:T(8,128)S(1)}, f32[128,1280]{1,0:T(8,128)S(1)}, u32[]{:S(2)}, u32[]{:S(2)}) collective-permute-start(f32[128,1280]{1,0:T(8,128)S(1)} %project.9.refs_2_), channel_id=1, source_target_pairs={{0,4},{4,0},{1,5},{5,1},{2,6},{6,2},{3,7},{7,3},{8,12},{12,8},{9,1... | collective-permute-start | bytes 1966088 | tf_op jit(solution)/shard_map/ppermute | solution.py:301
  57.0 14.4 %collective-permute-start.8 = (f32[64,1024]{1,0:T(8,128)S(1)}, f32[64,1024]{1,0:T(8,128)S(1)}, u32[]{:S(2)}, u32[]{:S(2)}) collective-permute-start(f32[64,1024]{1,0:T(8,128)S(1)} %get-tuple-element.56), channel_id=1, source_target_pairs={{1,0},{2,3},{5,4},{6,7},{9,8},{10,11},{13,12},{14,15},{17,16},{18,... | collective-permute-start | bytes 786440 | tf_op jit(solution)/shard_map/ppermute | solution.py:298
  58.3 14.0 %collective-permute-start.1 = (f32[64,1280]{1,0:T(8,128)S(1)}, f32[64,1280]{1,0:T(8,128)S(1)}, u32[]{:S(2)}, u32[]{:S(2)}) collective-permute-start(f32[64,1280]{1,0:T(8,128)S(1)} %project.7.refs_0_), channel_id=1, source_target_pairs={{0,4},{4,0},{1,5},{5,1},{2,6},{6,2},{3,7},{7,3},{8,12},{12,8},{9,1... | collective-permute-start | bytes 983048 | tf_op jit(solution)/shard_map/ppermute | solution.py:301
  72.2 1.7 %collective-permute-start.12 = (f32[64,1280]{1,0:T(8,128)S(1)}, f32[64,1280]{1,0:T(8,128)S(1)}, u32[]{:S(2)}, u32[]{:S(2)}) collective-permute-start(f32[64,1280]{1,0:T(8,128)S(1)} %project_last.1.refs_4_), channel_id=1, source_target_pairs={{0,4},{4,0},{1,5},{5,1},{2,6},{6,2},{3,7},{7,3},{8,12},{12,8},{9,1... | collective-permute-start | bytes 983048 | tf_op jit(solution)/shard_map/ppermute | solution.py:301
  75.3 9.1 %collective-permute-start.13 = (f32[64,1024]{1,0:T(8,128)S(1)}, f32[64,1024]{1,0:T(8,128)S(1)}, u32[]{:S(2)}, u32[]{:S(2)}) collective-permute-start(f32[64,1024]{1,0:T(8,128)S(1)} %get-tuple-element.39), channel_id=1, source_target_pairs={{0,1},{3,2},{4,5},{7,6},{8,9},{11,10},{12,13},{15,14},{16,17},{19,... | collective-permute-start | bytes 786440 | tf_op jit(solution)/shard_map/ppermute | solution.py:298
  77.5 16.7 %collective-permute-start.14 = (f32[64,1024]{1,0:T(8,128)S(1)}, f32[64,1024]{1,0:T(8,128)S(1)}, u32[]{:S(2)}, u32[]{:S(2)}) collective-permute-start(f32[64,1024]{1,0:T(8,128)S(1)} %out_again.3), channel_id=1, source_target_pairs={{0,1},{3,2},{4,5},{7,6},{8,9},{11,10},{12,13},{15,14},{16,17},{19,... | collective-permute-start | bytes 786440 | tf_op jit(solution)/shard_map/ppermute | solution.py:298
  83.1 22.9 %collective-permute-start.19 = (f32[64,2048]{1,0:T(8,128)S(1)}, f32[64,2048]{1,0:T(8,128)S(1)}, u32[]{:S(2)}, u32[]{:S(2)}) collective-permute-start(f32[64,2048]{1,0:T(8,128)S(1)} %out_again.4), channel_id=1, source_target_pairs={{0,1},{3,2},{4,5},{7,6},{8,9},{11,10},{12,13},{15,14},{16,17},{19,... | collective-permute-start | bytes 1572872 | tf_op jit(solution)/shard_map/ppermute | solution.py:298
  90.8 20.7 %collective-permute-start.17 = (f32[64,2048]{1,0:T(8,128)S(1)}, f32[64,2048]{1,0:T(8,128)S(1)}, u32[]{:S(2)}, u32[]{:S(2)}) collective-permute-start(f32[64,2048]{1,0:T(8,128)S(1)} %get-tuple-element.49), channel_id=1, source_target_pairs={{0,1},{3,2},{4,5},{7,6},{8,9},{11,10},{12,13},{15,14},{16,17},{19,... | collective-permute-start | bytes 1572872 | tf_op jit(solution)/shard_map/ppermute | solution.py:298
  94.3 17.9 %collective-permute-start.15 = (f32[64,2048]{1,0:T(8,128)S(1)}, f32[64,2048]{1,0:T(8,128)S(1)}, u32[]{:S(2)}, u32[]{:S(2)}) collective-permute-start(f32[64,2048]{1,0:T(8,128)S(1)} %pad_maximum_fusion.1), channel_id=1, source_target_pairs={{1,2},{2,1},{5,6},{6,5},{9,10},{10,9},{13,14},{14,13},{17,18},{18,... | collective-permute-start | bytes 1572872 | tf_op jit(solution)/shard_map/ppermute | solution.py:298
  100.6 22.1 %collective-permute-start.22 = (f32[64,2048]{1,0:T(8,128)S(1)}, f32[64,2048]{1,0:T(8,128)S(1)}, u32[]{:S(2)}, u32[]{:S(2)}) collective-permute-start(f32[64,2048]{1,0:T(8,128)S(1)} %get-tuple-element.52), channel_id=1, source_target_pairs={{0,1},{3,2},{4,5},{7,6},{8,9},{11,10},{12,13},{15,14},{16,17},{19,... | collective-permute-start | bytes 1572872 | tf_op jit(solution)/shard_map/ppermute | solution.py:298
  106.1 17.4 %collective-permute-start.20 = (f32[64,2048]{1,0:T(8,128)S(1)}, f32[64,2048]{1,0:T(8,128)S(1)}, u32[]{:S(2)}, u32[]{:S(2)}) collective-permute-start(f32[64,2048]{1,0:T(8,128)S(1)} %add.39), channel_id=1, source_target_pairs={{1,2},{2,1},{5,6},{6,5},{9,10},{10,9},{13,14},{14,13},{17,18},{18,... | collective-permute-start | bytes 1572872 | tf_op jit(solution)/shard_map/ppermute | solution.py:298
  111.6 18.6 %collective-permute-start.18 = (f32[64,2048]{1,0:T(8,128)S(1)}, f32[64,2048]{1,0:T(8,128)S(1)}, u32[]{:S(2)}, u32[]{:S(2)}) collective-permute-start(f32[64,2048]{1,0:T(8,128)S(1)} %add.36), channel_id=1, source_target_pairs={{1,2},{2,1},{5,6},{6,5},{9,10},{10,9},{13,14},{14,13},{17,18},{18,... | collective-permute-start | bytes 1572872 | tf_op jit(solution)/shard_map/ppermute | solution.py:298
  112.3 21.6 %collective-permute-start.16 = (f32[64,2048]{1,0:T(8,128)S(1)}, f32[64,2048]{1,0:T(8,128)S(1)}, u32[]{:S(2)}, u32[]{:S(2)}) collective-permute-start(f32[64,2048]{1,0:T(8,128)S(1)} %add.35), channel_id=1, source_target_pairs={{0,1},{1,0},{2,3},{3,2},{4,5},{5,4},{6,7},{7,6},{8,9},{9,8},{10,11... | collective-permute-start | bytes 1572872 | tf_op jit(solution)/shard_map/ppermute | solution.py:298
  122.8 11.3 %collective-permute-start.23 = (f32[64,2048]{1,0:T(8,128)S(1)}, f32[64,2048]{1,0:T(8,128)S(1)}, u32[]{:S(2)}, u32[]{:S(2)}) collective-permute-start(f32[64,2048]{1,0:T(8,128)S(1)} %add.41), channel_id=1, source_target_pairs={{1,2},{2,1},{5,6},{6,5},{9,10},{10,9},{13,14},{14,13},{17,18},{18,... | collective-permute-start | bytes 1572872 | tf_op jit(solution)/shard_map/ppermute | solution.py:298
  123.6 21.0 %collective-permute-start.21 = (f32[64,2048]{1,0:T(8,128)S(1)}, f32[64,2048]{1,0:T(8,128)S(1)}, u32[]{:S(2)}, u32[]{:S(2)}) collective-permute-start(f32[64,2048]{1,0:T(8,128)S(1)} %add.40), channel_id=1, source_target_pairs={{0,1},{1,0},{2,3},{3,2},{4,5},{5,4},{6,7},{7,6},{8,9},{9,8},{10,11... | collective-permute-start | bytes 1572872 | tf_op jit(solution)/shard_map/ppermute | solution.py:298

commit v8 on v7

--- a/solution.py
+++ b/solution.py
@@ -38,14 +38,15 @@
     return high[:rows] + ((high[rows:] + low[:rows]) + low[rows:])
 
 
-def project_kernel(terms, with_total, first, steps, step, n_before, *refs):
+def project_kernel(terms, with_total, first, steps, step, keep, n_before, *refs):
     n_x = sum(len(t) for t in terms)
     x_refs, w_refs, rest = refs[:n_x], refs[n_x : n_x + 3], refs[n_x + 3 :]
     total, rest = rest[0], rest[(1 if with_total else 0) + n_before :]
     out, kept, bufs, sems = rest[0], rest[1:-4], rest[-4:-1], rest[-1]
 
     def copies(k):
-        rows = pl.ds(first + k * step, step)
+        start = first + k * step if k < steps else keep + (k - steps) * step
+        rows = pl.ds(start, step)
         return [pltpu.make_async_copy(w.at[rows], b.at[k], sems.at[k, i]) for i, (w, b) in enumerate(zip(w_refs, bufs))]
 
     for k in range(bufs[0].shape[0]):
@@ -85,7 +86,7 @@
             offset += b.shape[2]
 
 
-def project(blocks, weights, start, depth, total=None, keep=0, before=(), step=512):
+def project(blocks, weights, start, depth, total=None, keep=(0, 0), before=(), step=512):
     terms = tuple(tuple(at for _, at in b) for b in blocks)
     operands = [a for b in blocks for a, _ in b]
     rows = sum(b[0][0].shape[0] for b in blocks)
@@ -100,15 +101,15 @@
     in_specs += [anywhere] * len(before)
     operands += before
     return pl.pallas_call(
-        functools.partial(project_kernel, terms, total is not None, start, steps, step, len(before)),
+        functools.partial(project_kernel, terms, total is not None, start, steps, step, keep[0], len(before)),
         in_specs=in_specs,
-        out_specs=[vmem] * 3 if keep else vmem,
+        out_specs=[vmem] * 3 if keep[1] else vmem,
         out_shape=[jax.ShapeDtypeStruct((rows, width), jnp.float32)]
-        + [jax.ShapeDtypeStruct((keep, width), jnp.bfloat16)] * 2
-        if keep
+        + [jax.ShapeDtypeStruct((keep[1], width), jnp.bfloat16)] * 2
+        if keep[1]
         else jax.ShapeDtypeStruct((rows, width), jnp.float32),
-        scratch_shapes=[pltpu.VMEM((steps + keep // step, step, w.shape[1]), jnp.float32) for w in weights]
-        + [pltpu.SemaphoreType.DMA((steps + keep // step, len(weights)))],
+        scratch_shapes=[pltpu.VMEM((steps + keep[1] // step, step, w.shape[1]), jnp.float32) for w in weights]
+        + [pltpu.SemaphoreType.DMA((steps + keep[1] // step, len(weights)))],
         compiler_params=pltpu.CompilerParams(vmem_limit_bytes=VMEM_LIMIT),
         cost_estimate=pl.CostEstimate(
             flops=8 * rows * depth * width, bytes_accessed=4 * depth * (rows + width), transcendentals=0
@@ -117,17 +118,18 @@
     )(*operands)
 
 
-def project_last_kernel(at, x, y, high, low, total, out):
+def project_last_kernel(at, start, x, y, high, low, total, out):
     size = y.shape[1]
     block = split(x[:, at : at + size] + y[...])
-    out[...] = total[...] + dot_split(block, (high[...], low[...]))
-
-
-def project_last(block, kept, total):
+    rows = slice(start, start + size)
+    out[...] = total[...] + dot_split(block, (high[rows], low[rows]))
+
+
+def project_last(block, kept, start, total):
     (x, at), (y, _) = block
     vmem = pl.BlockSpec(memory_space=pltpu.VMEM)
     return pl.pallas_call(
-        functools.partial(project_last_kernel, at),
+        functools.partial(project_last_kernel, at, start),
         in_specs=[vmem] * 5,
         out_specs=vmem,
         out_shape=jax.ShapeDtypeStruct(total.shape, jnp.float32),
@@ -293,6 +295,7 @@
     kv_width = w_key.shape[1]
     halves = cut([depth // 2] * 2)
     last = cut([depth // 2, depth // 4, depth // 4])
+    later = (3 * depth // 4, depth // 4)
 
     def hop(a, pairs):
         return lax.ppermute(a, "col", pairs)
@@ -329,26 +332,26 @@
             far = after(far, second[0])
         end3 = hop(far, ENDS_IN)
         block = ((mid2[half], at), (end3, 0))
-        if i == len(last) - 1:
-            third = project_last(block, kept, third)
-        elif i == len(last) - 2:
-            third, *kept = project([block], weights, start, size, third, last[-1][1])
+        if i > 1:
+            third = project_last(block, kept, start - later[0], third)
+        elif i == 1:
+            third = project([block], weights, start, size, third)
         else:
-            third = project([block], weights, start, size, third)
+            third, *kept = project([block], weights, start, size, third, later)
     third = (third, swap(third))
 
     parts = [first, second, third]
-    early = cut([pieces[0][1] // 2] * 2 + [pieces[1][1]])
+    early = cut([pieces[0][1] // 4] * 2 + [pieces[0][1] // 2, pieces[1][1]])
     a_third, m_third = attend_out(parts, 2, 3, w_split, kv_width, [rows], early[0][1])
     m_third = [m_third[0]] + [
-        out_again(a_third, w, [rows], *p)[0] for w, p in zip((w_split, [w_out]), early[1:])
+        out_again(a_third, w, [rows], *p)[0] for w, p in zip((w_split, w_split, [w_out]), early[1:])
     ]
     r1 = [hop(m, ENDS_OUT) for m in m_third]
     others = [tuple(after(a, r1[0], *m_third) for a in first), second, third]
     a_rest, mixed = attend_out(others, 0, 2, w_split, kv_width, [rows] * 3, pieces[0][1])
-    r1[1] = after(r1[1], *a_rest)
+    r1[1:3] = [after(r, *a_rest) for r in r1[1:3]]
     mixed = [mixed, out_again(a_rest, [w_out], [rows] * 3, *pieces[1])]
-    far = [jnp.concatenate([m + r for m, r in zip(m_third[:2], r1[:2])], axis=1), m_third[2] + r1[2]]
+    far = [jnp.concatenate([m + r for m, r in zip(m_third[:3], r1[:3])], axis=1), m_third[3] + r1[3]]
     result = []
     for (m_own, m_near, m_second), f in zip(mixed, far):
         r2e = hop(m_second, ENDS_OUT)

time: 147 us -> 147 us (level)
    ppermute x21 -> x22, starting transfers between devices: 41.8 us -> 41 us  [hop(): return lax.ppermute(a, 'col', pairs)]
    ppermute x21 -> x22, waiting for transfers between devices: 42.2 us -> 42.7 us  [hop(): return lax.ppermute(a, 'col', pairs)]
    pallas_call x5 -> x6, Pallas kernels: 18.1 us -> 18.3 us  [mix(): pl.pallas_call(functools.partial(mix_kernel, len(operands), ask, q_width,...]
  transfers between devices with their start and end apart: 24 -> 25, of which waited for: 11 -> 11; matrix products, arithmetic and copies ran while one was open for 1% -> 1% of each run, Pallas kernels for 34% -> 35%
where the time goes in v8:
time: 147 us; the launch traced here: 145 us
  Pallas kernels  51.5 us (35%)
  waiting for transfers between devices  44.3 us (30%)
  starting transfers between devices  41.7 us (28%)
  local copies, waits for them, and re-layouts  5.82 us (4%)
  other arithmetic  1.6 us (1%)
    ppermute x22, waiting for transfers between devices, hop(): return lax.ppermute(a, 'col', pairs)  42.7 us
    ppermute x22, starting transfers between devices, hop(): return lax.ppermute(a, 'col', pairs)  41 us
    pallas_call x6, Pallas kernels, project(): pl.pallas_call(functools.partial(project_kernel, terms, total is not None...  28.5 us
    pallas_call x6, Pallas kernels, mix(): pl.pallas_call(functools.partial(mix_kernel, len(operands), ask, q_width,...  18.3 us
    unnamed x10, local copies, waits for them, and re-layouts  4.41 us
    pallas_call x1, Pallas kernels, halve(): pl.pallas_call(functools.partial(halve_kernel, start), in_specs=[anywhere...  3.8 us
  transfers between devices with their start and end apart: 25, of which 11 were waited for; matrix products, arithmetic and copies ran while one was open for 1% of the time, Pallas kernels for 35%

profile of v8, /device:TPU:0, one launch (start us, length us, event | category | flops | bytes accessed | tf_op | source)
XLA Modules:
  0.0 145.4 jit_solution(2202908978886671992)
XLA Ops:
  0.0 3.0 %collective-permute-start.2 = (f32[64,4096]{1,0:T(8,128)}, f32[64,4096]{1,0:T(8,128)S(1)}, u32[]{:S(2)}, u32[]{:S(2)}) collective-permute-start(f32[64,4096]{1,0:T(8,128)} %refs_0_.3), channel_id=1, source_target_pairs={{0,1},{1,0},{2,3},{3,2},{4,5},{5,4},{6,7},{7,6},{8,9},{9,8},{10,11... | collective-permute-start | bytes 3145736 | tf_op jit(solution)/shard_map/ppermute | solution.py:301
  3.0 1.3 fusion
  4.3 0.7 collective-permute-start
  5.0 0.7 collective-permute-start.3
  5.7 0.0 copy-start
  5.7 1.6 %copy-done = f32[4096,128]{1,0:T(8,128)S(1)} copy-done((f32[4096,128]{1,0:T(8,128)S(1)}, f32[4096,128]{1,0:T(8,128)}, u32[]{:S(2)}) %copy-start) | copy-done | bytes 2097176
  7.3 1.6 %copy-done.2 = f32[4096,128]{1,0:T(8,128)S(1)} copy-done((f32[4096,128]{1,0:T(8,128)S(1)}, f32[4096,128]{1,0:T(8,128)}, u32[]{:S(2)}) %copy-start.2) | copy-done | bytes 2097176
  8.9 1.2 copy-done.4
  10.1 4.3 %project.6.refs_4_ = f32[64,1280]{1,0:T(8,128)S(1)} custom-call(f32[64,4096]{1,0:T(8,128)S(1)} %copy-done.4, f32[4096,1024]{1,0:T(8,128)} %refs_2_.9, f32[4096,128]{1,0:T(8,128)S(1)} %copy-done, f32[4096,128]{1,0:T(8,128)S(1)} %copy-done.2), custom_call_target="tpu_custom_call" | custom-call | flops 1342177280 | bytes 11010048 | tf_op jit(solution)/shard_map/project/pallas_call | solution.py:103
  14.5 1.3 collective-permute-start.5
  15.8 4.3 %project.7.refs_0_ = f32[64,1280]{1,0:T(8,128)S(1)} custom-call(f32[64,4096]{1,0:T(8,128)S(1)} %copy-done.4, f32[4096,1024]{1,0:T(8,128)} %refs_2_.9, f32[4096,128]{1,0:T(8,128)S(1)} %copy-done, f32[4096,128]{1,0:T(8,128)S(1)} %copy-done.2, f32[64,1280]{1,0:T(8,128)S(1)} %project.6.refs_4_, f32[64,2048]{1,0:T(8,128)S(1)} %collective-permute-done.refs_5_.refs_1_), custom_call_target="tpu_custom_call" | custom-call | flops 1342177280 | bytes 11010048 | tf_op jit(solution)/shard_map/project/pallas_call | solution.py:103
  20.1 7.1 %collective-permute-done.2.before.refs_0_ = f32[64,4096]{1,0:T(8,128)S(1)} collective-permute-done((f32[64,4096]{1,0:T(8,128)}, f32[64,4096]{1,0:T(8,128)S(1)}, u32[]{:S(2)}, u32[]{:S(2)}) %collective-permute-start.2) | collective-permute-done | bytes 1048608 | tf_op jit(solution)/shard_map/ppermute | solution.py:301
  27.3 0.0 copy-start.1
  27.3 0.8 collective-permute-start.9
  28.1 1.4 collective-permute-start.4
  29.6 3.8 %halve.1 = (bf16[1024,2048]{1,0:T(8,128)(2,1)S(1)}, bf16[1024,2048]{1,0:T(8,128)(2,1)S(1)}) custom-call(f32[1024,4096]{1,0:T(8,128)} %refs_2_.11, f32[64,4096]{1,0:T(8,128)S(1)} %collective-permute-done.2.before.refs_0_), custom_call_target="tpu_custom_call" | custom-call | flops 2097152 | bytes 16777216 | tf_op jit(solution)/shard_map/halve/pallas_call | solution.py:196
  33.4 0.7 collective-permute-start.7
  34.1 4.3 %collective-permute-done.5.refs_2_ = f32[64,2048]{1,0:T(8,128)S(1)} collective-permute-done((f32[64,2048]{1,0:T(8,128)S(1)}, f32[64,2048]{1,0:T(8,128)S(1)}, u32[]{:S(2)}, u32[]{:S(2)}) %collective-permute-start.5) | collective-permute-done | bytes 524320 | tf_op jit(solution)/shard_map/ppermute | solution.py:301
  38.5 5.8 %project.8.refs_6_ = f32[128,1280]{1,0:T(8,128)S(1)} custom-call(f32[64,4096]{1,0:T(8,128)S(1)} %collective-permute-done.2.before.refs_0_, f32[64,2048]{1,0:T(8,128)S(1)} %collective-permute-done.refs_5_.refs_1_, f32[64,2048]{1,0:T(8,128)S(1)} %collective-permute-done.5.refs_2_, f32[4096,1024]{1,0:T(8,128)} %refs_2_.9, f32[4096,128]{1,0:T(8,128)S(1)} %copy-done.1, ...), custom_call_target="tpu_custom_call" | custom-call | flops 2684354560 | bytes 11534336 | tf_op jit(solution)/shard_map/project/pallas_call | solution.py:103
  44.3 1.5 %collective-permute-start.10 = (f32[64,2048]{1,0:T(8,128)S(1)}, f32[64,2048]{1,0:T(8,128)S(1)}, u32[]{:S(2)}, u32[]{:S(2)}) collective-permute-start(f32[64,2048]{1,0:T(8,128)S(1)} %collective-permute-done.9.refs_0_), channel_id=1, source_target_pairs={{1,0},{2,3},{5,4},{6,7},{9,8},{10,11},{13,12},{14,15},{17,16},{18,... | collective-permute-start | bytes 1572872 | tf_op jit(solution)/shard_map/ppermute | solution.py:301
  45.8 3.9 %collective-permute-done.4.refs_2_ = f32[64,2048]{1,0:T(8,128)S(1)} collective-permute-done((f32[64,2048]{1,0:T(8,128)S(1)}, f32[64,2048]{1,0:T(8,128)S(1)}, u32[]{:S(2)}, u32[]{:S(2)}) %collective-permute-start.4) | collective-permute-done | bytes 524320 | tf_op jit(solution)/shard_map/ppermute | solution.py:301
  49.7 5.8 %project.9.refs_2_ = f32[128,1280]{1,0:T(8,128)S(1)} custom-call(f32[64,4096]{1,0:T(8,128)S(1)} %collective-permute-done.2.before.refs_0_, f32[64,2048]{1,0:T(8,128)S(1)} %collective-permute-done.3.refs_7_.refs_1_.refs_8_, f32[64,2048]{1,0:T(8,128)S(1)} %collective-permute-done.4.refs_2_, f32[4096,1024]{1,0:T(8,128)} %refs_2_.9, f32[4096,128]{1,0:T(8,128)S(1)} %copy-done.1, ...), custom_call_target="tpu_custom_call" | custom-call | flops 2684354560 | bytes 11534336 | tf_op jit(solution)/shard_map/project/pallas_call | solution.py:103
  55.6 1.3 collective-permute-start.11
  56.9 0.1 collective-permute-start.6
  57.0 1.3 collective-permute-start.8
  58.3 0.6 collective-permute-start.1
  58.8 2.7 %collective-permute-done.10.refs_1_ = f32[64,2048]{1,0:T(8,128)S(1)} collective-permute-done((f32[64,2048]{1,0:T(8,128)S(1)}, f32[64,2048]{1,0:T(8,128)S(1)}, u32[]{:S(2)}, u32[]{:S(2)}) %collective-permute-start.10) | collective-permute-done | bytes 524320 | tf_op jit(solution)/shard_map/ppermute | solution.py:301
  61.5 5.3 %project.10 = (f32[64,1280]{1,0:T(8,128)S(1)}, bf16[1024,1280]{1,0:T(8,128)(2,1)S(1)}, bf16[1024,1280]{1,0:T(8,128)(2,1)S(1)}) custom-call(f32[64,2048]{1,0:T(8,128)S(1)} %collective-permute-done.9.refs_0_, f32[64,2048]{1,0:T(8,128)S(1)} %collective-permute-done.10.refs_1_, f32[4096,1024]{1,0:T(8,128)} %refs_2_.9, f32[4096,128]{1,0:T(8,128)S(1)} %copy-done.1, ...), custom_call_target="tpu_custom_call" | custom-call | flops 1342177280 | bytes 11010048 | tf_op jit(solution)/shard_map/project/pallas_call | solution.py:103
  66.7 0.3 collective-permute-done.11.refs_1_
  67.1 3.0 %project.11.total = f32[64,1280]{1,0:T(8,128)S(1)} custom-call(f32[64,2048]{1,0:T(8,128)S(1)} %collective-permute-done.7.refs_0_.x, f32[64,1024]{1,0:T(8,128)S(1)} %collective-permute-done.11.refs_1_, f32[4096,1024]{1,0:T(8,128)} %refs_2_.9, f32[4096,128]{1,0:T(8,128)S(1)} %copy-done.1, f32[4096,128]{1,0:T(8,128)S(1)} %copy-done.3, ...), custom_call_target="tpu_custom_call" | custom-call | flops 671088640 | bytes 5505024 | tf_op jit(solution)/shard_map/project/pallas_call | solution.py:103
  70.1 1.3 collective-permute-done.8.y
  71.3 0.9 project_last.1.refs_4_
  72.2 0.1 collective-permute-start.12
  72.3 1.6 %collective-permute-done.12.refs_5_ = f32[64,1280]{1,0:T(8,128)S(1)} collective-permute-done((f32[64,1280]{1,0:T(8,128)S(1)}, f32[64,1280]{1,0:T(8,128)S(1)}, u32[]{:S(2)}, u32[]{:S(2)}) %collective-permute-start.12) | collective-permute-done | bytes 327712 | tf_op jit(solution)/shard_map/ppermute | solution.py:304
  73.9 1.1 attend_out.2
  75.0 1.5 collective-permute-start.13
  76.5 0.4 out_again.4
  77.0 1.3 collective-permute-start.14
  78.3 0.7 out_again.5
  79.0 1.5 %collective-permute-start.15 = (f32[64,1024]{1,0:T(8,128)S(1)}, f32[64,1024]{1,0:T(8,128)S(1)}, u32[]{:S(2)}, u32[]{:S(2)}) collective-permute-start(f32[64,1024]{1,0:T(8,128)S(1)} %out_again.5), channel_id=1, source_target_pairs={{0,1},{3,2},{4,5},{7,6},{8,9},{11,10},{12,13},{15,14},{16,17},{19,... | collective-permute-start | bytes 786440 | tf_op jit(solution)/shard_map/ppermute | solution.py:301
  80.5 4.0 %out_again.6 = f32[64,2048]{1,0:T(8,128)S(1)} custom-call(bf16[64,1024]{1,0:T(8,128)(2,1)S(1)} %get-tuple-element.41.refs_0_, bf16[64,1024]{1,0:T(8,128)(2,1)S(1)} %get-tuple-element.42.refs_1_, f32[1024,4096]{1,0:T(8,128)} %refs_2_.11), custom_call_target="tpu_custom_call" | custom-call | flops 1073741824 | bytes 8912896 | tf_op jit(solution)/shard_map/out_again/pallas_call | solution.py:255
  84.6 1.3 collective-permute-start.20
  85.9 6.4 %attend_out.3 = (bf16[192,1024]{1,0:T(8,128)(2,1)S(1)}, bf16[192,1024]{1,0:T(8,128)(2,1)S(1)}, f32[64,2048]{1,0:T(8,128)S(1)}, f32[64,2048]{1,0:T(8,128)S(1)}, f32[64,2048]{1,0:T(8,128)S(1)}) custom-call(f32[64,1280]{1,0:T(8,128)S(1)} %project.7.refs_0_, f32[64,1280]{1,0:T(8,128)S(1)} %collective-permute-done.1.refs_1_, f32[128,1280]{1,0:T(8,128)S(1)} %project.9.refs_2_, ...), custom_call_target="tpu_custom_call" | custom-call | flops 4831838208 | bytes 9961472 | tf_op jit(solution)/shard_map/attend_out/pallas_call | solution.py:255
  92.3 1.3 collective-permute-start.18
  93.8 0.7 collective-permute-start.16
  94.5 5.6 %out_again.7 = (f32[64,2048]{1,0:T(8,128)S(1)}, f32[64,2048]{1,0:T(8,128)S(1)}, f32[64,2048]{1,0:T(8,128)S(1)}) custom-call(bf16[192,1024]{1,0:T(8,128)(2,1)S(1)} %get-tuple-element.47.refs_0_, bf16[192,1024]{1,0:T(8,128)(2,1)S(1)} %get-tuple-element.48.refs_1_, f32[1024,4096]{1,0:T(8,128)} %refs_2_.11), custom_call_target="tpu_custom_call" | custom-call | flops 3221225472 | bytes 9961472 | tf_op jit(solution)/shard_map/out_again/pallas_call | solution.py:255
  100.0 5.3 %collective-permute-start.23 = (f32[64,2048]{1,0:T(8,128)S(1)}, f32[64,2048]{1,0:T(8,128)S(1)}, u32[]{:S(2)}, u32[]{:S(2)}) collective-permute-start(f32[64,2048]{1,0:T(8,128)S(1)} %get-tuple-element.54), channel_id=1, source_target_pairs={{0,1},{3,2},{4,5},{7,6},{8,9},{11,10},{12,13},{15,14},{16,17},{19,... | collective-permute-start | bytes 1572872 | tf_op jit(solution)/shard_map/ppermute | solution.py:301
  105.4 0.1 add.43
  105.5 0.7 collective-permute-start.21
  106.2 5.1 %collective-permute-done.18 = f32[64,2048]{1,0:T(8,128)S(1)} collective-permute-done((f32[64,2048]{1,0:T(8,128)S(1)}, f32[64,2048]{1,0:T(8,128)S(1)}, u32[]{:S(2)}, u32[]{:S(2)}) %collective-permute-start.18) | collective-permute-done | bytes 524320 | tf_op jit(solution)/shard_map/ppermute | solution.py:301
  111.2 0.1 add.40
  111.3 0.7 collective-permute-start.19
  112.0 0.1 add.39
  112.1 6.6 %collective-permute-start.17 = (f32[64,2048]{1,0:T(8,128)S(1)}, f32[64,2048]{1,0:T(8,128)S(1)}, u32[]{:S(2)}, u32[]{:S(2)}) collective-permute-start(f32[64,2048]{1,0:T(8,128)S(1)} %add.39), channel_id=1, source_target_pairs={{0,1},{1,0},{2,3},{3,2},{4,5},{5,4},{6,7},{7,6},{8,9},{9,8},{10,11... | collective-permute-start | bytes 1572872 | tf_op jit(solution)/shard_map/ppermute | solution.py:301
  118.7 3.8 %collective-permute-done.23 = f32[64,2048]{1,0:T(8,128)S(1)} collective-permute-done((f32[64,2048]{1,0:T(8,128)S(1)}, f32[64,2048]{1,0:T(8,128)S(1)}, u32[]{:S(2)}, u32[]{:S(2)}) %collective-permute-start.23) | collective-permute-done | bytes 524320 | tf_op jit(solution)/shard_map/ppermute | solution.py:301
  122.4 0.1 add.45
  122.5 0.7 collective-permute-start.24
  123.2 0.1 add.44
  123.3 6.6 %collective-permute-start.22 = (f32[64,2048]{1,0:T(8,128)S(1)}, f32[64,2048]{1,0:T(8,128)S(1)}, u32[]{:S(2)}, u32[]{:S(2)}) collective-permute-start(f32[64,2048]{1,0:T(8,128)S(1)} %add.44), channel_id=1, source_target_pairs={{0,1},{1,0},{2,3},{3,2},{4,5},{5,4},{6,7},{7,6},{8,9},{9,8},{10,11... | collective-permute-start | bytes 1572872 | tf_op jit(solution)/shard_map/ppermute | solution.py:301
  129.9 3.8 %collective-permute-done.17 = f32[64,2048]{1,0:T(8,128)S(1)} collective-permute-done((f32[64,2048]{1,0:T(8,128)S(1)}, f32[64,2048]{1,0:T(8,128)S(1)}, u32[]{:S(2)}, u32[]{:S(2)}) %collective-permute-start.17) | collective-permute-done | bytes 524320 | tf_op jit(solution)/shard_map/ppermute | solution.py:301
  133.7 0.1 add_add_fusion.1
  133.8 10.5 %collective-permute-done.22 = f32[64,2048]{1,0:T(8,128)S(1)} collective-permute-done((f32[64,2048]{1,0:T(8,128)S(1)}, f32[64,2048]{1,0:T(8,128)S(1)}, u32[]{:S(2)}, u32[]{:S(2)}) %collective-permute-start.22) | collective-permute-done | bytes 524320 | tf_op jit(solution)/shard_map/ppermute | solution.py:301
  144.3 0.1 add_add_fusion
  144.3 1.0 pad_maximum_fusion
  (26 shorter events, 0.3 us)
Async XLA Ops:
  0.0 27.2 %collective-permute-start.2 = (f32[64,4096]{1,0:T(8,128)}, f32[64,4096]{1,0:T(8,128)S(1)}, u32[]{:S(2)}, u32[]{:S(2)}) collective-permute-start(f32[64,4096]{1,0:T(8,128)} %refs_0_.3), channel_id=1, source_target_pairs={{0,1},{1,0},{2,3},{3,2},{4,5},{5,4},{6,7},{7,6},{8,9},{9,8},{10,11... | collective-permute-start | bytes 3145736 | tf_op jit(solution)/shard_map/ppermute | solution.py:301
  4.3 10.2 %collective-permute-start = (f32[64,2048]{1,0:T(8,128)S(1)}, f32[64,2048]{1,0:T(8,128)S(1)}, u32[]{:S(2)}, u32[]{:S(2)}) collective-permute-start(f32[64,2048]{1,0:T(8,128)S(1)} %get-tuple-element.56), channel_id=1, source_target_pairs={{1,2},{2,1},{5,6},{6,5},{9,10},{10,9},{13,14},{14,13},{17,18},{18,... | collective-permute-start | bytes 1572872 | tf_op jit(solution)/shard_map/ppermute | solution.py:301
  5.0 23.1 %collective-permute-start.3 = (f32[64,2048]{1,0:T(8,128)S(1)}, f32[64,2048]{1,0:T(8,128)S(1)}, u32[]{:S(2)}, u32[]{:S(2)}) collective-permute-start(f32[64,2048]{1,0:T(8,128)S(1)} %get-tuple-element.55), channel_id=1, source_target_pairs={{1,2},{2,1},{5,6},{6,5},{9,10},{10,9},{13,14},{14,13},{17,18},{18,... | collective-permute-start | bytes 1572872 | tf_op jit(solution)/shard_map/ppermute | solution.py:301
  5.7 1.6 %copy-start = (f32[4096,128]{1,0:T(8,128)S(1)}, f32[4096,128]{1,0:T(8,128)}, u32[]{:S(2)}) copy-start(f32[4096,128]{1,0:T(8,128)} %refs_3_.11) | copy-start | bytes 6291460
  7.3 1.6 %copy-start.2 = (f32[4096,128]{1,0:T(8,128)S(1)}, f32[4096,128]{1,0:T(8,128)}, u32[]{:S(2)}) copy-start(f32[4096,128]{1,0:T(8,128)} %refs_4_.7) | copy-start | bytes 6291460
  8.9 1.2 copy-start.4
  14.5 23.9 %collective-permute-start.5 = (f32[64,2048]{1,0:T(8,128)S(1)}, f32[64,2048]{1,0:T(8,128)S(1)}, u32[]{:S(2)}, u32[]{:S(2)}) collective-permute-start(f32[64,2048]{1,0:T(8,128)S(1)} %collective-permute-done.refs_5_.refs_1_), channel_id=1, source_target_pairs={{1,0},{2,3},{5,4},{6,7},{9,8},{10,11},{13,12},{14,15},{17,16},{18,... | collective-permute-start | bytes 1572872 | tf_op jit(solution)/shard_map/ppermute | solution.py:301
  27.3 11.2 %copy-start.1 = (f32[4096,128]{1,0:T(8,128)S(1)}, f32[4096,128]{1,0:T(8,128)}, u32[]{:S(2)}) copy-start(f32[4096,128]{1,0:T(8,128)} %refs_3_.11) | copy-start | bytes 6291460
  27.3 11.2 %copy-start.3 = (f32[4096,128]{1,0:T(8,128)S(1)}, f32[4096,128]{1,0:T(8,128)}, u32[]{:S(2)}) copy-start(f32[4096,128]{1,0:T(8,128)} %refs_4_.7) | copy-start | bytes 6291460
  27.3 17.0 %collective-permute-start.9 = (f32[64,2048]{1,0:T(8,128)S(1)}, f32[64,2048]{1,0:T(8,128)S(1)}, u32[]{:S(2)}, u32[]{:S(2)}) collective-permute-start(f32[64,2048]{1,0:T(8,128)S(1)} %slice.22), channel_id=1, source_target_pairs={{1,2},{2,1},{5,6},{6,5},{9,10},{10,9},{13,14},{14,13},{17,18},{18,... | collective-permute-start | bytes 1572872 | tf_op jit(solution)/shard_map/ppermute | solution.py:301
  28.1 21.6 %collective-permute-start.4 = (f32[64,2048]{1,0:T(8,128)S(1)}, f32[64,2048]{1,0:T(8,128)S(1)}, u32[]{:S(2)}, u32[]{:S(2)}) collective-permute-start(f32[64,2048]{1,0:T(8,128)S(1)} %collective-permute-done.3.refs_7_.refs_1_.refs_8_), channel_id=1, source_target_pairs={{1,0},{2,3},{5,4},{6,7},{9,8},{10,11},{13,12},{14,15},{17,16},{18,... | collective-permute-start | bytes 1572872 | tf_op jit(solution)/shard_map/ppermute | solution.py:301
  33.4 22.1 %collective-permute-start.7 = (f32[64,2048]{1,0:T(8,128)S(1)}, f32[64,2048]{1,0:T(8,128)S(1)}, u32[]{:S(2)}, u32[]{:S(2)}) collective-permute-start(f32[64,2048]{1,0:T(8,128)S(1)} %slice.20), channel_id=1, source_target_pairs={{1,2},{2,1},{5,6},{6,5},{9,10},{10,9},{13,14},{14,13},{17,18},{18,... | collective-permute-start | bytes 1572872 | tf_op jit(solution)/shard_map/ppermute | solution.py:301
  44.3 17.2 %collective-permute-start.10 = (f32[64,2048]{1,0:T(8,128)S(1)}, f32[64,2048]{1,0:T(8,128)S(1)}, u32[]{:S(2)}, u32[]{:S(2)}) collective-permute-start(f32[64,2048]{1,0:T(8,128)S(1)} %collective-permute-done.9.refs_0_), channel_id=1, source_target_pairs={{1,0},{2,3},{5,4},{6,7},{9,8},{10,11},{13,12},{14,15},{17,16},{18,... | collective-permute-start | bytes 1572872 | tf_op jit(solution)/shard_map/ppermute | solution.py:301
  55.6 11.5 %collective-permute-start.11 = (f32[64,1024]{1,0:T(8,128)S(1)}, f32[64,1024]{1,0:T(8,128)S(1)}, u32[]{:S(2)}, u32[]{:S(2)}) collective-permute-start(f32[64,1024]{1,0:T(8,128)S(1)} %get-tuple-element.37), channel_id=1, source_target_pairs={{1,0},{2,3},{5,4},{6,7},{9,8},{10,11},{13,12},{14,15},{17,16},{18,... | collective-permute-start | bytes 786440 | tf_op jit(solution)/shard_map/ppermute | solution.py:301
  56.9 15.4 %collective-permute-start.6 = (f32[128,1280]{1,0:T(8,128)S(1)}, f32[128,1280]{1,0:T(8,128)S(1)}, u32[]{:S(2)}, u32[]{:S(2)}) collective-permute-start(f32[128,1280]{1,0:T(8,128)S(1)} %project.9.refs_2_), channel_id=1, source_target_pairs={{0,4},{4,0},{1,5},{5,1},{2,6},{6,2},{3,7},{7,3},{8,12},{12,8},{9,1... | collective-permute-start | bytes 1966088 | tf_op jit(solution)/shard_map/ppermute | solution.py:304
  57.0 14.4 %collective-permute-start.8 = (f32[64,1024]{1,0:T(8,128)S(1)}, f32[64,1024]{1,0:T(8,128)S(1)}, u32[]{:S(2)}, u32[]{:S(2)}) collective-permute-start(f32[64,1024]{1,0:T(8,128)S(1)} %get-tuple-element.58), channel_id=1, source_target_pairs={{1,0},{2,3},{5,4},{6,7},{9,8},{10,11},{13,12},{14,15},{17,16},{18,... | collective-permute-start | bytes 786440 | tf_op jit(solution)/shard_map/ppermute | solution.py:301
  58.3 14.0 %collective-permute-start.1 = (f32[64,1280]{1,0:T(8,128)S(1)}, f32[64,1280]{1,0:T(8,128)S(1)}, u32[]{:S(2)}, u32[]{:S(2)}) collective-permute-start(f32[64,1280]{1,0:T(8,128)S(1)} %project.7.refs_0_), channel_id=1, source_target_pairs={{0,4},{4,0},{1,5},{5,1},{2,6},{6,2},{3,7},{7,3},{8,12},{12,8},{9,1... | collective-permute-start | bytes 983048 | tf_op jit(solution)/shard_map/ppermute | solution.py:304
  72.2 1.7 %collective-permute-start.12 = (f32[64,1280]{1,0:T(8,128)S(1)}, f32[64,1280]{1,0:T(8,128)S(1)}, u32[]{:S(2)}, u32[]{:S(2)}) collective-permute-start(f32[64,1280]{1,0:T(8,128)S(1)} %project_last.1.refs_4_), channel_id=1, source_target_pairs={{0,4},{4,0},{1,5},{5,1},{2,6},{6,2},{3,7},{7,3},{8,12},{12,8},{9,1... | collective-permute-start | bytes 983048 | tf_op jit(solution)/shard_map/ppermute | solution.py:304
  75.0 10.9 %collective-permute-start.13 = (f32[64,512]{1,0:T(8,128)S(1)}, f32[64,512]{1,0:T(8,128)S(1)}, u32[]{:S(2)}, u32[]{:S(2)}) collective-permute-start(f32[64,512]{1,0:T(8,128)S(1)} %get-tuple-element.40), channel_id=1, source_target_pairs={{0,1},{3,2},{4,5},{7,6},{8,9},{11,10},{12,13},{15,14},{16,17},{19,... | collective-permute-start | bytes 393224 | tf_op jit(solution)/shard_map/ppermute | solution.py:301
  77.0 16.7 %collective-permute-start.14 = (f32[64,512]{1,0:T(8,128)S(1)}, f32[64,512]{1,0:T(8,128)S(1)}, u32[]{:S(2)}, u32[]{:S(2)}) collective-permute-start(f32[64,512]{1,0:T(8,128)S(1)} %out_again.4), channel_id=1, source_target_pairs={{0,1},{3,2},{4,5},{7,6},{8,9},{11,10},{12,13},{15,14},{16,17},{19,... | collective-permute-start | bytes 393224 | tf_op jit(solution)/shard_map/ppermute | solution.py:301
  79.0 14.7 %collective-permute-start.15 = (f32[64,1024]{1,0:T(8,128)S(1)}, f32[64,1024]{1,0:T(8,128)S(1)}, u32[]{:S(2)}, u32[]{:S(2)}) collective-permute-start(f32[64,1024]{1,0:T(8,128)S(1)} %out_again.5), channel_id=1, source_target_pairs={{0,1},{3,2},{4,5},{7,6},{8,9},{11,10},{12,13},{15,14},{16,17},{19,... | collective-permute-start | bytes 786440 | tf_op jit(solution)/shard_map/ppermute | solution.py:301
  84.6 20.8 %collective-permute-start.20 = (f32[64,2048]{1,0:T(8,128)S(1)}, f32[64,2048]{1,0:T(8,128)S(1)}, u32[]{:S(2)}, u32[]{:S(2)}) collective-permute-start(f32[64,2048]{1,0:T(8,128)S(1)} %out_again.6), channel_id=1, source_target_pairs={{0,1},{3,2},{4,5},{7,6},{8,9},{11,10},{12,13},{15,14},{16,17},{19,... | collective-permute-start | bytes 1572872 | tf_op jit(solution)/shard_map/ppermute | solution.py:301
  92.3 18.9 %collective-permute-start.18 = (f32[64,2048]{1,0:T(8,128)S(1)}, f32[64,2048]{1,0:T(8,128)S(1)}, u32[]{:S(2)}, u32[]{:S(2)}) collective-permute-start(f32[64,2048]{1,0:T(8,128)S(1)} %get-tuple-element.51), channel_id=1, source_target_pairs={{0,1},{3,2},{4,5},{7,6},{8,9},{11,10},{12,13},{15,14},{16,17},{19,... | collective-permute-start | bytes 1572872 | tf_op jit(solution)/shard_map/ppermute | solution.py:301
  93.8 18.2 %collective-permute-start.16 = (f32[64,2048]{1,0:T(8,128)S(1)}, f32[64,2048]{1,0:T(8,128)S(1)}, u32[]{:S(2)}, u32[]{:S(2)}) collective-permute-start(f32[64,2048]{1,0:T(8,128)S(1)} %pad_maximum_fusion.1), channel_id=1, source_target_pairs={{1,2},{2,1},{5,6},{6,5},{9,10},{10,9},{13,14},{14,13},{17,18},{18,... | collective-permute-start | bytes 1572872 | tf_op jit(solution)/shard_map/ppermute | solution.py:301
  100.0 22.4 %collective-permute-start.23 = (f32[64,2048]{1,0:T(8,128)S(1)}, f32[64,2048]{1,0:T(8,128)S(1)}, u32[]{:S(2)}, u32[]{:S(2)}) collective-permute-start(f32[64,2048]{1,0:T(8,128)S(1)} %get-tuple-element.54), channel_id=1, source_target_pairs={{0,1},{3,2},{4,5},{7,6},{8,9},{11,10},{12,13},{15,14},{16,17},{19,... | collective-permute-start | bytes 1572872 | tf_op jit(solution)/shard_map/ppermute | solution.py:301
  105.5 17.8 %collective-permute-start.21 = (f32[64,2048]{1,0:T(8,128)S(1)}, f32[64,2048]{1,0:T(8,128)S(1)}, u32[]{:S(2)}, u32[]{:S(2)}) collective-permute-start(f32[64,2048]{1,0:T(8,128)S(1)} %add.43), channel_id=1, source_target_pairs={{1,2},{2,1},{5,6},{6,5},{9,10},{10,9},{13,14},{14,13},{17,18},{18,... | collective-permute-start | bytes 1572872 | tf_op jit(solution)/shard_map/ppermute | solution.py:301
  111.3 18.7 %collective-permute-start.19 = (f32[64,2048]{1,0:T(8,128)S(1)}, f32[64,2048]{1,0:T(8,128)S(1)}, u32[]{:S(2)}, u32[]{:S(2)}) collective-permute-start(f32[64,2048]{1,0:T(8,128)S(1)} %add.40), channel_id=1, source_target_pairs={{1,2},{2,1},{5,6},{6,5},{9,10},{10,9},{13,14},{14,13},{17,18},{18,... | collective-permute-start | bytes 1572872 | tf_op jit(solution)/shard_map/ppermute | solution.py:301
  112.1 21.6 %collective-permute-start.17 = (f32[64,2048]{1,0:T(8,128)S(1)}, f32[64,2048]{1,0:T(8,128)S(1)}, u32[]{:S(2)}, u32[]{:S(2)}) collective-permute-start(f32[64,2048]{1,0:T(8,128)S(1)} %add.39), channel_id=1, source_target_pairs={{0,1},{1,0},{2,3},{3,2},{4,5},{5,4},{6,7},{7,6},{8,9},{9,8},{10,11... | collective-permute-start | bytes 1572872 | tf_op jit(solution)/shard_map/ppermute | solution.py:301
  122.5 11.3 %collective-permute-start.24 = (f32[64,2048]{1,0:T(8,128)S(1)}, f32[64,2048]{1,0:T(8,128)S(1)}, u32[]{:S(2)}, u32[]{:S(2)}) collective-permute-start(f32[64,2048]{1,0:T(8,128)S(1)} %add.45), channel_id=1, source_target_pairs={{1,2},{2,1},{5,6},{6,5},{9,10},{10,9},{13,14},{14,13},{17,18},{18,... | collective-permute-start | bytes 1572872 | tf_op jit(solution)/shard_map/ppermute | solution.py:301
  123.3 21.0 %collective-permute-start.22 = (f32[64,2048]{1,0:T(8,128)S(1)}, f32[64,2048]{1,0:T(8,128)S(1)}, u32[]{:S(2)}, u32[]{:S(2)}) collective-permute-start(f32[64,2048]{1,0:T(8,128)S(1)} %add.44), channel_id=1, source_target_pairs={{0,1},{1,0},{2,3},{3,2},{4,5},{5,4},{6,7},{7,6},{8,9},{9,8},{10,11... | collective-permute-start | bytes 1572872 | tf_op jit(solution)/shard_map/ppermute | solution.py:301

commit v9 on v8

--- a/solution.py
+++ b/solution.py
@@ -359,7 +359,9 @@
         r3m = hop(m_second + r2e, MIDDLE)
         r3x = hop(m_near + r2m, PAIRS)
         result.append(m_own + (r3x + r3m))
-    return jnp.concatenate(result, axis=1)
+    size = pieces[0][1]
+    left = jnp.pad(result[0], ((0, 0), (0, size)))
+    return left + jnp.pad(result[1], ((0, 0), (size, 0)))
 
 
 def on_device(tokens, w_query, w_key, w_value, w_out):

time: 147 us -> 147 us (level)
  no operation moved by 1% of the time
where the time goes in v9:
time: 147 us; the launch traced here: 145 us
  Pallas kernels  51.5 us (35%)
  waiting for transfers between devices  44.3 us (30%)
  starting transfers between devices  41.7 us (28%)
  local copies, waits for them, and re-layouts  5.82 us (4%)
  other arithmetic  1.6 us (1%)
    ppermute x22, waiting for transfers between devices, hop(): return lax.ppermute(a, 'col', pairs)  42.7 us
    ppermute x22, starting transfers between devices, hop(): return lax.ppermute(a, 'col', pairs)  41 us
    pallas_call x6, Pallas kernels, project(): pl.pallas_call(functools.partial(project_kernel, terms, total is not None...  28.5 us
    pallas_call x6, Pallas kernels, mix(): pl.pallas_call(functools.partial(mix_kernel, len(operands), ask, q_width,...  18.3 us
    unnamed x10, local copies, waits for them, and re-layouts  4.41 us
    pallas_call x1, Pallas kernels, halve(): pl.pallas_call(functools.partial(halve_kernel, start), in_specs=[anywhere...  3.8 us
  transfers between devices with their start and end apart: 25, of which 11 were waited for; matrix products, arithmetic and copies ran while one was open for 1% of the time, Pallas kernels for 35%

profile of v9, /device:TPU:0, one launch (start us, length us, event | category | flops | bytes accessed | tf_op | source)
XLA Modules:
  0.0 145.4 jit_solution(2202908978886671992)
XLA Ops:
  0.0 3.0 %collective-permute-start.2 = (f32[64,4096]{1,0:T(8,128)}, f32[64,4096]{1,0:T(8,128)S(1)}, u32[]{:S(2)}, u32[]{:S(2)}) collective-permute-start(f32[64,4096]{1,0:T(8,128)} %refs_0_.3), channel_id=1, source_target_pairs={{0,1},{1,0},{2,3},{3,2},{4,5},{5,4},{6,7},{7,6},{8,9},{9,8},{10,11... | collective-permute-start | bytes 3145736 | tf_op jit(solution)/shard_map/ppermute | solution.py:301
  3.0 1.3 fusion
  4.3 0.7 collective-permute-start
  5.0 0.7 collective-permute-start.3
  5.7 0.0 copy-start
  5.7 1.6 %copy-done = f32[4096,128]{1,0:T(8,128)S(1)} copy-done((f32[4096,128]{1,0:T(8,128)S(1)}, f32[4096,128]{1,0:T(8,128)}, u32[]{:S(2)}) %copy-start) | copy-done | bytes 2097176
  7.3 1.6 %copy-done.2 = f32[4096,128]{1,0:T(8,128)S(1)} copy-done((f32[4096,128]{1,0:T(8,128)S(1)}, f32[4096,128]{1,0:T(8,128)}, u32[]{:S(2)}) %copy-start.2) | copy-done | bytes 2097176
  8.9 1.2 copy-done.4
  10.1 4.3 %project.6.refs_4_ = f32[64,1280]{1,0:T(8,128)S(1)} custom-call(f32[64,4096]{1,0:T(8,128)S(1)} %copy-done.4, f32[4096,1024]{1,0:T(8,128)} %refs_2_.9, f32[4096,128]{1,0:T(8,128)S(1)} %copy-done, f32[4096,128]{1,0:T(8,128)S(1)} %copy-done.2), custom_call_target="tpu_custom_call" | custom-call | flops 1342177280 | bytes 11010048 | tf_op jit(solution)/shard_map/project/pallas_call | solution.py:103
  14.5 1.3 collective-permute-start.5
  15.8 4.3 %project.7.refs_0_ = f32[64,1280]{1,0:T(8,128)S(1)} custom-call(f32[64,4096]{1,0:T(8,128)S(1)} %copy-done.4, f32[4096,1024]{1,0:T(8,128)} %refs_2_.9, f32[4096,128]{1,0:T(8,128)S(1)} %copy-done, f32[4096,128]{1,0:T(8,128)S(1)} %copy-done.2, f32[64,1280]{1,0:T(8,128)S(1)} %project.6.refs_4_, f32[64,2048]{1,0:T(8,128)S(1)} %collective-permute-done.refs_5_.refs_1_), custom_call_target="tpu_custom_call" | custom-call | flops 1342177280 | bytes 11010048 | tf_op jit(solution)/shard_map/project/pallas_call | solution.py:103
  20.1 7.1 %collective-permute-done.2.before.refs_0_ = f32[64,4096]{1,0:T(8,128)S(1)} collective-permute-done((f32[64,4096]{1,0:T(8,128)}, f32[64,4096]{1,0:T(8,128)S(1)}, u32[]{:S(2)}, u32[]{:S(2)}) %collective-permute-start.2) | collective-permute-done | bytes 1048608 | tf_op jit(solution)/shard_map/ppermute | solution.py:301
  27.3 0.0 copy-start.1
  27.3 0.8 collective-permute-start.9
  28.1 1.4 collective-permute-start.4
  29.6 3.8 %halve.1 = (bf16[1024,2048]{1,0:T(8,128)(2,1)S(1)}, bf16[1024,2048]{1,0:T(8,128)(2,1)S(1)}) custom-call(f32[1024,4096]{1,0:T(8,128)} %refs_2_.11, f32[64,4096]{1,0:T(8,128)S(1)} %collective-permute-done.2.before.refs_0_), custom_call_target="tpu_custom_call" | custom-call | flops 2097152 | bytes 16777216 | tf_op jit(solution)/shard_map/halve/pallas_call | solution.py:196
  33.4 0.7 collective-permute-start.7
  34.1 4.3 %collective-permute-done.5.refs_2_ = f32[64,2048]{1,0:T(8,128)S(1)} collective-permute-done((f32[64,2048]{1,0:T(8,128)S(1)}, f32[64,2048]{1,0:T(8,128)S(1)}, u32[]{:S(2)}, u32[]{:S(2)}) %collective-permute-start.5) | collective-permute-done | bytes 524320 | tf_op jit(solution)/shard_map/ppermute | solution.py:301
  38.5 5.8 %project.8.refs_6_ = f32[128,1280]{1,0:T(8,128)S(1)} custom-call(f32[64,4096]{1,0:T(8,128)S(1)} %collective-permute-done.2.before.refs_0_, f32[64,2048]{1,0:T(8,128)S(1)} %collective-permute-done.refs_5_.refs_1_, f32[64,2048]{1,0:T(8,128)S(1)} %collective-permute-done.5.refs_2_, f32[4096,1024]{1,0:T(8,128)} %refs_2_.9, f32[4096,128]{1,0:T(8,128)S(1)} %copy-done.1, ...), custom_call_target="tpu_custom_call" | custom-call | flops 2684354560 | bytes 11534336 | tf_op jit(solution)/shard_map/project/pallas_call | solution.py:103
  44.3 1.5 %collective-permute-start.10 = (f32[64,2048]{1,0:T(8,128)S(1)}, f32[64,2048]{1,0:T(8,128)S(1)}, u32[]{:S(2)}, u32[]{:S(2)}) collective-permute-start(f32[64,2048]{1,0:T(8,128)S(1)} %collective-permute-done.9.refs_0_), channel_id=1, source_target_pairs={{1,0},{2,3},{5,4},{6,7},{9,8},{10,11},{13,12},{14,15},{17,16},{18,... | collective-permute-start | bytes 1572872 | tf_op jit(solution)/shard_map/ppermute | solution.py:301
  45.8 3.9 %collective-permute-done.4.refs_2_ = f32[64,2048]{1,0:T(8,128)S(1)} collective-permute-done((f32[64,2048]{1,0:T(8,128)S(1)}, f32[64,2048]{1,0:T(8,128)S(1)}, u32[]{:S(2)}, u32[]{:S(2)}) %collective-permute-start.4) | collective-permute-done | bytes 524320 | tf_op jit(solution)/shard_map/ppermute | solution.py:301
  49.7 5.8 %project.9.refs_2_ = f32[128,1280]{1,0:T(8,128)S(1)} custom-call(f32[64,4096]{1,0:T(8,128)S(1)} %collective-permute-done.2.before.refs_0_, f32[64,2048]{1,0:T(8,128)S(1)} %collective-permute-done.3.refs_7_.refs_1_.refs_8_, f32[64,2048]{1,0:T(8,128)S(1)} %collective-permute-done.4.refs_2_, f32[4096,1024]{1,0:T(8,128)} %refs_2_.9, f32[4096,128]{1,0:T(8,128)S(1)} %copy-done.1, ...), custom_call_target="tpu_custom_call" | custom-call | flops 2684354560 | bytes 11534336 | tf_op jit(solution)/shard_map/project/pallas_call | solution.py:103
  55.6 1.3 collective-permute-start.11
  56.9 0.1 collective-permute-start.6
  57.0 1.3 collective-permute-start.8
  58.3 0.6 collective-permute-start.1
  58.8 2.7 %collective-permute-done.10.refs_1_ = f32[64,2048]{1,0:T(8,128)S(1)} collective-permute-done((f32[64,2048]{1,0:T(8,128)S(1)}, f32[64,2048]{1,0:T(8,128)S(1)}, u32[]{:S(2)}, u32[]{:S(2)}) %collective-permute-start.10) | collective-permute-done | bytes 524320 | tf_op jit(solution)/shard_map/ppermute | solution.py:301
  61.5 5.3 %project.10 = (f32[64,1280]{1,0:T(8,128)S(1)}, bf16[1024,1280]{1,0:T(8,128)(2,1)S(1)}, bf16[1024,1280]{1,0:T(8,128)(2,1)S(1)}) custom-call(f32[64,2048]{1,0:T(8,128)S(1)} %collective-permute-done.9.refs_0_, f32[64,2048]{1,0:T(8,128)S(1)} %collective-permute-done.10.refs_1_, f32[4096,1024]{1,0:T(8,128)} %refs_2_.9, f32[4096,128]{1,0:T(8,128)S(1)} %copy-done.1, ...), custom_call_target="tpu_custom_call" | custom-call | flops 1342177280 | bytes 11010048 | tf_op jit(solution)/shard_map/project/pallas_call | solution.py:103
  66.7 0.3 collective-permute-done.11.refs_1_
  67.1 3.0 %project.11.total = f32[64,1280]{1,0:T(8,128)S(1)} custom-call(f32[64,2048]{1,0:T(8,128)S(1)} %collective-permute-done.7.refs_0_.x, f32[64,1024]{1,0:T(8,128)S(1)} %collective-permute-done.11.refs_1_, f32[4096,1024]{1,0:T(8,128)} %refs_2_.9, f32[4096,128]{1,0:T(8,128)S(1)} %copy-done.1, f32[4096,128]{1,0:T(8,128)S(1)} %copy-done.3, ...), custom_call_target="tpu_custom_call" | custom-call | flops 671088640 | bytes 5505024 | tf_op jit(solution)/shard_map/project/pallas_call | solution.py:103
  70.1 1.3 collective-permute-done.8.y
  71.3 0.9 project_last.1.refs_4_
  72.2 0.1 collective-permute-start.12
  72.3 1.6 %collective-permute-done.12.refs_5_ = f32[64,1280]{1,0:T(8,128)S(1)} collective-permute-done((f32[64,1280]{1,0:T(8,128)S(1)}, f32[64,1280]{1,0:T(8,128)S(1)}, u32[]{:S(2)}, u32[]{:S(2)}) %collective-permute-start.12) | collective-permute-done | bytes 327712 | tf_op jit(solution)/shard_map/ppermute | solution.py:304
  73.9 1.1 attend_out.2
  75.0 1.5 collective-permute-start.13
  76.5 0.4 out_again.4
  77.0 1.3 collective-permute-start.14
  78.3 0.7 out_again.5
  79.0 1.5 %collective-permute-start.15 = (f32[64,1024]{1,0:T(8,128)S(1)}, f32[64,1024]{1,0:T(8,128)S(1)}, u32[]{:S(2)}, u32[]{:S(2)}) collective-permute-start(f32[64,1024]{1,0:T(8,128)S(1)} %out_again.5), channel_id=1, source_target_pairs={{0,1},{3,2},{4,5},{7,6},{8,9},{11,10},{12,13},{15,14},{16,17},{19,... | collective-permute-start | bytes 786440 | tf_op jit(solution)/shard_map/ppermute | solution.py:301
  80.5 4.0 %out_again.6 = f32[64,2048]{1,0:T(8,128)S(1)} custom-call(bf16[64,1024]{1,0:T(8,128)(2,1)S(1)} %get-tuple-element.41.refs_0_, bf16[64,1024]{1,0:T(8,128)(2,1)S(1)} %get-tuple-element.42.refs_1_, f32[1024,4096]{1,0:T(8,128)} %refs_2_.11), custom_call_target="tpu_custom_call" | custom-call | flops 1073741824 | bytes 8912896 | tf_op jit(solution)/shard_map/out_again/pallas_call | solution.py:255
  84.6 1.3 collective-permute-start.20
  85.9 6.4 %attend_out.3 = (bf16[192,1024]{1,0:T(8,128)(2,1)S(1)}, bf16[192,1024]{1,0:T(8,128)(2,1)S(1)}, f32[64,2048]{1,0:T(8,128)S(1)}, f32[64,2048]{1,0:T(8,128)S(1)}, f32[64,2048]{1,0:T(8,128)S(1)}) custom-call(f32[64,1280]{1,0:T(8,128)S(1)} %project.7.refs_0_, f32[64,1280]{1,0:T(8,128)S(1)} %collective-permute-done.1.refs_1_, f32[128,1280]{1,0:T(8,128)S(1)} %project.9.refs_2_, ...), custom_call_target="tpu_custom_call" | custom-call | flops 4831838208 | bytes 9961472 | tf_op jit(solution)/shard_map/attend_out/pallas_call | solution.py:255
  92.3 1.3 collective-permute-start.18
  93.8 0.7 collective-permute-start.16
  94.5 5.6 %out_again.7 = (f32[64,2048]{1,0:T(8,128)S(1)}, f32[64,2048]{1,0:T(8,128)S(1)}, f32[64,2048]{1,0:T(8,128)S(1)}) custom-call(bf16[192,1024]{1,0:T(8,128)(2,1)S(1)} %get-tuple-element.47.refs_0_, bf16[192,1024]{1,0:T(8,128)(2,1)S(1)} %get-tuple-element.48.refs_1_, f32[1024,4096]{1,0:T(8,128)} %refs_2_.11), custom_call_target="tpu_custom_call" | custom-call | flops 3221225472 | bytes 9961472 | tf_op jit(solution)/shard_map/out_again/pallas_call | solution.py:255
  100.0 5.3 %collective-permute-start.23 = (f32[64,2048]{1,0:T(8,128)S(1)}, f32[64,2048]{1,0:T(8,128)S(1)}, u32[]{:S(2)}, u32[]{:S(2)}) collective-permute-start(f32[64,2048]{1,0:T(8,128)S(1)} %get-tuple-element.54), channel_id=1, source_target_pairs={{0,1},{3,2},{4,5},{7,6},{8,9},{11,10},{12,13},{15,14},{16,17},{19,... | collective-permute-start | bytes 1572872 | tf_op jit(solution)/shard_map/ppermute | solution.py:301
  105.4 0.1 add.50
  105.5 0.7 collective-permute-start.21
  106.2 5.1 %collective-permute-done.18 = f32[64,2048]{1,0:T(8,128)S(1)} collective-permute-done((f32[64,2048]{1,0:T(8,128)S(1)}, f32[64,2048]{1,0:T(8,128)S(1)}, u32[]{:S(2)}, u32[]{:S(2)}) %collective-permute-start.18) | collective-permute-done | bytes 524320 | tf_op jit(solution)/shard_map/ppermute | solution.py:301
  111.2 0.1 add.47
  111.3 0.7 collective-permute-start.19
  112.0 0.1 add.46
  112.1 6.6 %collective-permute-start.17 = (f32[64,2048]{1,0:T(8,128)S(1)}, f32[64,2048]{1,0:T(8,128)S(1)}, u32[]{:S(2)}, u32[]{:S(2)}) collective-permute-start(f32[64,2048]{1,0:T(8,128)S(1)} %add.46), channel_id=1, source_target_pairs={{0,1},{1,0},{2,3},{3,2},{4,5},{5,4},{6,7},{7,6},{8,9},{9,8},{10,11... | collective-permute-start | bytes 1572872 | tf_op jit(solution)/shard_map/ppermute | solution.py:301
  118.7 3.8 %collective-permute-done.23 = f32[64,2048]{1,0:T(8,128)S(1)} collective-permute-done((f32[64,2048]{1,0:T(8,128)S(1)}, f32[64,2048]{1,0:T(8,128)S(1)}, u32[]{:S(2)}, u32[]{:S(2)}) %collective-permute-start.23) | collective-permute-done | bytes 524320 | tf_op jit(solution)/shard_map/ppermute | solution.py:301
  122.4 0.1 add.52
  122.5 0.7 collective-permute-start.24
  123.2 0.1 add.51
  123.3 6.6 %collective-permute-start.22 = (f32[64,2048]{1,0:T(8,128)S(1)}, f32[64,2048]{1,0:T(8,128)S(1)}, u32[]{:S(2)}, u32[]{:S(2)}) collective-permute-start(f32[64,2048]{1,0:T(8,128)S(1)} %add.51), channel_id=1, source_target_pairs={{0,1},{1,0},{2,3},{3,2},{4,5},{5,4},{6,7},{7,6},{8,9},{9,8},{10,11... | collective-permute-start | bytes 1572872 | tf_op jit(solution)/shard_map/ppermute | solution.py:301
  129.9 3.8 %collective-permute-done.17 = f32[64,2048]{1,0:T(8,128)S(1)} collective-permute-done((f32[64,2048]{1,0:T(8,128)S(1)}, f32[64,2048]{1,0:T(8,128)S(1)}, u32[]{:S(2)}, u32[]{:S(2)}) %collective-permute-start.17) | collective-permute-done | bytes 524320 | tf_op jit(solution)/shard_map/ppermute | solution.py:301
  133.7 0.1 add_add_fusion.1
  133.8 10.5 %collective-permute-done.22 = f32[64,2048]{1,0:T(8,128)S(1)} collective-permute-done((f32[64,2048]{1,0:T(8,128)S(1)}, f32[64,2048]{1,0:T(8,128)S(1)}, u32[]{:S(2)}, u32[]{:S(2)}) %collective-permute-start.22) | collective-permute-done | bytes 524320 | tf_op jit(solution)/shard_map/ppermute | solution.py:301
  144.3 0.1 add_add_fusion
  144.3 1.0 pad_add_fusion
  (26 shorter events, 0.3 us)
Async XLA Ops:
  0.0 27.2 %collective-permute-start.2 = (f32[64,4096]{1,0:T(8,128)}, f32[64,4096]{1,0:T(8,128)S(1)}, u32[]{:S(2)}, u32[]{:S(2)}) collective-permute-start(f32[64,4096]{1,0:T(8,128)} %refs_0_.3), channel_id=1, source_target_pairs={{0,1},{1,0},{2,3},{3,2},{4,5},{5,4},{6,7},{7,6},{8,9},{9,8},{10,11... | collective-permute-start | bytes 3145736 | tf_op jit(solution)/shard_map/ppermute | solution.py:301
  4.3 10.2 %collective-permute-start = (f32[64,2048]{1,0:T(8,128)S(1)}, f32[64,2048]{1,0:T(8,128)S(1)}, u32[]{:S(2)}, u32[]{:S(2)}) collective-permute-start(f32[64,2048]{1,0:T(8,128)S(1)} %get-tuple-element.56), channel_id=1, source_target_pairs={{1,2},{2,1},{5,6},{6,5},{9,10},{10,9},{13,14},{14,13},{17,18},{18,... | collective-permute-start | bytes 1572872 | tf_op jit(solution)/shard_map/ppermute | solution.py:301
  5.0 23.1 %collective-permute-start.3 = (f32[64,2048]{1,0:T(8,128)S(1)}, f32[64,2048]{1,0:T(8,128)S(1)}, u32[]{:S(2)}, u32[]{:S(2)}) collective-permute-start(f32[64,2048]{1,0:T(8,128)S(1)} %get-tuple-element.55), channel_id=1, source_target_pairs={{1,2},{2,1},{5,6},{6,5},{9,10},{10,9},{13,14},{14,13},{17,18},{18,... | collective-permute-start | bytes 1572872 | tf_op jit(solution)/shard_map/ppermute | solution.py:301
  5.7 1.6 %copy-start = (f32[4096,128]{1,0:T(8,128)S(1)}, f32[4096,128]{1,0:T(8,128)}, u32[]{:S(2)}) copy-start(f32[4096,128]{1,0:T(8,128)} %refs_3_.11) | copy-start | bytes 6291460
  7.3 1.6 %copy-start.2 = (f32[4096,128]{1,0:T(8,128)S(1)}, f32[4096,128]{1,0:T(8,128)}, u32[]{:S(2)}) copy-start(f32[4096,128]{1,0:T(8,128)} %refs_4_.7) | copy-start | bytes 6291460
  8.9 1.2 copy-start.4
  14.5 23.9 %collective-permute-start.5 = (f32[64,2048]{1,0:T(8,128)S(1)}, f32[64,2048]{1,0:T(8,128)S(1)}, u32[]{:S(2)}, u32[]{:S(2)}) collective-permute-start(f32[64,2048]{1,0:T(8,128)S(1)} %collective-permute-done.refs_5_.refs_1_), channel_id=1, source_target_pairs={{1,0},{2,3},{5,4},{6,7},{9,8},{10,11},{13,12},{14,15},{17,16},{18,... | collective-permute-start | bytes 1572872 | tf_op jit(solution)/shard_map/ppermute | solution.py:301
  27.3 11.2 %copy-start.1 = (f32[4096,128]{1,0:T(8,128)S(1)}, f32[4096,128]{1,0:T(8,128)}, u32[]{:S(2)}) copy-start(f32[4096,128]{1,0:T(8,128)} %refs_3_.11) | copy-start | bytes 6291460
  27.3 11.2 %copy-start.3 = (f32[4096,128]{1,0:T(8,128)S(1)}, f32[4096,128]{1,0:T(8,128)}, u32[]{:S(2)}) copy-start(f32[4096,128]{1,0:T(8,128)} %refs_4_.7) | copy-start | bytes 6291460
  27.3 17.0 %collective-permute-start.9 = (f32[64,2048]{1,0:T(8,128)S(1)}, f32[64,2048]{1,0:T(8,128)S(1)}, u32[]{:S(2)}, u32[]{:S(2)}) collective-permute-start(f32[64,2048]{1,0:T(8,128)S(1)} %slice.22), channel_id=1, source_target_pairs={{1,2},{2,1},{5,6},{6,5},{9,10},{10,9},{13,14},{14,13},{17,18},{18,... | collective-permute-start | bytes 1572872 | tf_op jit(solution)/shard_map/ppermute | solution.py:301
  28.1 21.6 %collective-permute-start.4 = (f32[64,2048]{1,0:T(8,128)S(1)}, f32[64,2048]{1,0:T(8,128)S(1)}, u32[]{:S(2)}, u32[]{:S(2)}) collective-permute-start(f32[64,2048]{1,0:T(8,128)S(1)} %collective-permute-done.3.refs_7_.refs_1_.refs_8_), channel_id=1, source_target_pairs={{1,0},{2,3},{5,4},{6,7},{9,8},{10,11},{13,12},{14,15},{17,16},{18,... | collective-permute-start | bytes 1572872 | tf_op jit(solution)/shard_map/ppermute | solution.py:301
  33.4 22.1 %collective-permute-start.7 = (f32[64,2048]{1,0:T(8,128)S(1)}, f32[64,2048]{1,0:T(8,128)S(1)}, u32[]{:S(2)}, u32[]{:S(2)}) collective-permute-start(f32[64,2048]{1,0:T(8,128)S(1)} %slice.20), channel_id=1, source_target_pairs={{1,2},{2,1},{5,6},{6,5},{9,10},{10,9},{13,14},{14,13},{17,18},{18,... | collective-permute-start | bytes 1572872 | tf_op jit(solution)/shard_map/ppermute | solution.py:301
  44.3 17.2 %collective-permute-start.10 = (f32[64,2048]{1,0:T(8,128)S(1)}, f32[64,2048]{1,0:T(8,128)S(1)}, u32[]{:S(2)}, u32[]{:S(2)}) collective-permute-start(f32[64,2048]{1,0:T(8,128)S(1)} %collective-permute-done.9.refs_0_), channel_id=1, source_target_pairs={{1,0},{2,3},{5,4},{6,7},{9,8},{10,11},{13,12},{14,15},{17,16},{18,... | collective-permute-start | bytes 1572872 | tf_op jit(solution)/shard_map/ppermute | solution.py:301
  55.6 11.5 %collective-permute-start.11 = (f32[64,1024]{1,0:T(8,128)S(1)}, f32[64,1024]{1,0:T(8,128)S(1)}, u32[]{:S(2)}, u32[]{:S(2)}) collective-permute-start(f32[64,1024]{1,0:T(8,128)S(1)} %get-tuple-element.37), channel_id=1, source_target_pairs={{1,0},{2,3},{5,4},{6,7},{9,8},{10,11},{13,12},{14,15},{17,16},{18,... | collective-permute-start | bytes 786440 | tf_op jit(solution)/shard_map/ppermute | solution.py:301
  56.9 15.4 %collective-permute-start.6 = (f32[128,1280]{1,0:T(8,128)S(1)}, f32[128,1280]{1,0:T(8,128)S(1)}, u32[]{:S(2)}, u32[]{:S(2)}) collective-permute-start(f32[128,1280]{1,0:T(8,128)S(1)} %project.9.refs_2_), channel_id=1, source_target_pairs={{0,4},{4,0},{1,5},{5,1},{2,6},{6,2},{3,7},{7,3},{8,12},{12,8},{9,1... | collective-permute-start | bytes 1966088 | tf_op jit(solution)/shard_map/ppermute | solution.py:304
  57.0 14.4 %collective-permute-start.8 = (f32[64,1024]{1,0:T(8,128)S(1)}, f32[64,1024]{1,0:T(8,128)S(1)}, u32[]{:S(2)}, u32[]{:S(2)}) collective-permute-start(f32[64,1024]{1,0:T(8,128)S(1)} %get-tuple-element.58), channel_id=1, source_target_pairs={{1,0},{2,3},{5,4},{6,7},{9,8},{10,11},{13,12},{14,15},{17,16},{18,... | collective-permute-start | bytes 786440 | tf_op jit(solution)/shard_map/ppermute | solution.py:301
  58.3 14.0 %collective-permute-start.1 = (f32[64,1280]{1,0:T(8,128)S(1)}, f32[64,1280]{1,0:T(8,128)S(1)}, u32[]{:S(2)}, u32[]{:S(2)}) collective-permute-start(f32[64,1280]{1,0:T(8,128)S(1)} %project.7.refs_0_), channel_id=1, source_target_pairs={{0,4},{4,0},{1,5},{5,1},{2,6},{6,2},{3,7},{7,3},{8,12},{12,8},{9,1... | collective-permute-start | bytes 983048 | tf_op jit(solution)/shard_map/ppermute | solution.py:304
  72.2 1.7 %collective-permute-start.12 = (f32[64,1280]{1,0:T(8,128)S(1)}, f32[64,1280]{1,0:T(8,128)S(1)}, u32[]{:S(2)}, u32[]{:S(2)}) collective-permute-start(f32[64,1280]{1,0:T(8,128)S(1)} %project_last.1.refs_4_), channel_id=1, source_target_pairs={{0,4},{4,0},{1,5},{5,1},{2,6},{6,2},{3,7},{7,3},{8,12},{12,8},{9,1... | collective-permute-start | bytes 983048 | tf_op jit(solution)/shard_map/ppermute | solution.py:304
  75.0 10.9 %collective-permute-start.13 = (f32[64,512]{1,0:T(8,128)S(1)}, f32[64,512]{1,0:T(8,128)S(1)}, u32[]{:S(2)}, u32[]{:S(2)}) collective-permute-start(f32[64,512]{1,0:T(8,128)S(1)} %get-tuple-element.40), channel_id=1, source_target_pairs={{0,1},{3,2},{4,5},{7,6},{8,9},{11,10},{12,13},{15,14},{16,17},{19,... | collective-permute-start | bytes 393224 | tf_op jit(solution)/shard_map/ppermute | solution.py:301
  77.0 16.7 %collective-permute-start.14 = (f32[64,512]{1,0:T(8,128)S(1)}, f32[64,512]{1,0:T(8,128)S(1)}, u32[]{:S(2)}, u32[]{:S(2)}) collective-permute-start(f32[64,512]{1,0:T(8,128)S(1)} %out_again.4), channel_id=1, source_target_pairs={{0,1},{3,2},{4,5},{7,6},{8,9},{11,10},{12,13},{15,14},{16,17},{19,... | collective-permute-start | bytes 393224 | tf_op jit(solution)/shard_map/ppermute | solution.py:301
  79.0 14.7 %collective-permute-start.15 = (f32[64,1024]{1,0:T(8,128)S(1)}, f32[64,1024]{1,0:T(8,128)S(1)}, u32[]{:S(2)}, u32[]{:S(2)}) collective-permute-start(f32[64,1024]{1,0:T(8,128)S(1)} %out_again.5), channel_id=1, source_target_pairs={{0,1},{3,2},{4,5},{7,6},{8,9},{11,10},{12,13},{15,14},{16,17},{19,... | collective-permute-start | bytes 786440 | tf_op jit(solution)/shard_map/ppermute | solution.py:301
  84.6 20.8 %collective-permute-start.20 = (f32[64,2048]{1,0:T(8,128)S(1)}, f32[64,2048]{1,0:T(8,128)S(1)}, u32[]{:S(2)}, u32[]{:S(2)}) collective-permute-start(f32[64,2048]{1,0:T(8,128)S(1)} %out_again.6), channel_id=1, source_target_pairs={{0,1},{3,2},{4,5},{7,6},{8,9},{11,10},{12,13},{15,14},{16,17},{19,... | collective-permute-start | bytes 1572872 | tf_op jit(solution)/shard_map/ppermute | solution.py:301
  92.3 18.9 %collective-permute-start.18 = (f32[64,2048]{1,0:T(8,128)S(1)}, f32[64,2048]{1,0:T(8,128)S(1)}, u32[]{:S(2)}, u32[]{:S(2)}) collective-permute-start(f32[64,2048]{1,0:T(8,128)S(1)} %get-tuple-element.51), channel_id=1, source_target_pairs={{0,1},{3,2},{4,5},{7,6},{8,9},{11,10},{12,13},{15,14},{16,17},{19,... | collective-permute-start | bytes 1572872 | tf_op jit(solution)/shard_map/ppermute | solution.py:301
  93.8 18.2 %collective-permute-start.16 = (f32[64,2048]{1,0:T(8,128)S(1)}, f32[64,2048]{1,0:T(8,128)S(1)}, u32[]{:S(2)}, u32[]{:S(2)}) collective-permute-start(f32[64,2048]{1,0:T(8,128)S(1)} %pad_maximum_fusion), channel_id=1, source_target_pairs={{1,2},{2,1},{5,6},{6,5},{9,10},{10,9},{13,14},{14,13},{17,18},{18,... | collective-permute-start | bytes 1572872 | tf_op jit(solution)/shard_map/ppermute | solution.py:301
  100.0 22.4 %collective-permute-start.23 = (f32[64,2048]{1,0:T(8,128)S(1)}, f32[64,2048]{1,0:T(8,128)S(1)}, u32[]{:S(2)}, u32[]{:S(2)}) collective-permute-start(f32[64,2048]{1,0:T(8,128)S(1)} %get-tuple-element.54), channel_id=1, source_target_pairs={{0,1},{3,2},{4,5},{7,6},{8,9},{11,10},{12,13},{15,14},{16,17},{19,... | collective-permute-start | bytes 1572872 | tf_op jit(solution)/shard_map/ppermute | solution.py:301
  105.5 17.8 %collective-permute-start.21 = (f32[64,2048]{1,0:T(8,128)S(1)}, f32[64,2048]{1,0:T(8,128)S(1)}, u32[]{:S(2)}, u32[]{:S(2)}) collective-permute-start(f32[64,2048]{1,0:T(8,128)S(1)} %add.50), channel_id=1, source_target_pairs={{1,2},{2,1},{5,6},{6,5},{9,10},{10,9},{13,14},{14,13},{17,18},{18,... | collective-permute-start | bytes 1572872 | tf_op jit(solution)/shard_map/ppermute | solution.py:301
  111.3 18.7 %collective-permute-start.19 = (f32[64,2048]{1,0:T(8,128)S(1)}, f32[64,2048]{1,0:T(8,128)S(1)}, u32[]{:S(2)}, u32[]{:S(2)}) collective-permute-start(f32[64,2048]{1,0:T(8,128)S(1)} %add.47), channel_id=1, source_target_pairs={{1,2},{2,1},{5,6},{6,5},{9,10},{10,9},{13,14},{14,13},{17,18},{18,... | collective-permute-start | bytes 1572872 | tf_op jit(solution)/shard_map/ppermute | solution.py:301
  112.1 21.6 %collective-permute-start.17 = (f32[64,2048]{1,0:T(8,128)S(1)}, f32[64,2048]{1,0:T(8,128)S(1)}, u32[]{:S(2)}, u32[]{:S(2)}) collective-permute-start(f32[64,2048]{1,0:T(8,128)S(1)} %add.46), channel_id=1, source_target_pairs={{0,1},{1,0},{2,3},{3,2},{4,5},{5,4},{6,7},{7,6},{8,9},{9,8},{10,11... | collective-permute-start | bytes 1572872 | tf_op jit(solution)/shard_map/ppermute | solution.py:301
  122.5 11.3 %collective-permute-start.24 = (f32[64,2048]{1,0:T(8,128)S(1)}, f32[64,2048]{1,0:T(8,128)S(1)}, u32[]{:S(2)}, u32[]{:S(2)}) collective-permute-start(f32[64,2048]{1,0:T(8,128)S(1)} %add.52), channel_id=1, source_target_pairs={{1,2},{2,1},{5,6},{6,5},{9,10},{10,9},{13,14},{14,13},{17,18},{18,... | collective-permute-start | bytes 1572872 | tf_op jit(solution)/shard_map/ppermute | solution.py:301
  123.3 21.0 %collective-permute-start.22 = (f32[64,2048]{1,0:T(8,128)S(1)}, f32[64,2048]{1,0:T(8,128)S(1)}, u32[]{:S(2)}, u32[]{:S(2)}) collective-permute-start(f32[64,2048]{1,0:T(8,128)S(1)} %add.51), channel_id=1, source_target_pairs={{0,1},{1,0},{2,3},{3,2},{4,5},{5,4},{6,7},{7,6},{8,9},{9,8},{10,11... | collective-permute-start | bytes 1572872 | tf_op jit(solution)/shard_map/ppermute | solution.py:301

commit v10 on v8

--- a/solution.py
+++ b/solution.py
@@ -341,17 +341,17 @@
     third = (third, swap(third))
 
     parts = [first, second, third]
-    early = cut([pieces[0][1] // 4] * 2 + [pieces[0][1] // 2, pieces[1][1]])
+    early = cut([pieces[0][1] // 4, 3 * pieces[0][1] // 4, pieces[1][1]])
     a_third, m_third = attend_out(parts, 2, 3, w_split, kv_width, [rows], early[0][1])
     m_third = [m_third[0]] + [
-        out_again(a_third, w, [rows], *p)[0] for w, p in zip((w_split, w_split, [w_out]), early[1:])
+        out_again(a_third, w, [rows], *p)[0] for w, p in zip((w_split, [w_out]), early[1:])
     ]
     r1 = [hop(m, ENDS_OUT) for m in m_third]
     others = [tuple(after(a, r1[0], *m_third) for a in first), second, third]
     a_rest, mixed = attend_out(others, 0, 2, w_split, kv_width, [rows] * 3, pieces[0][1])
-    r1[1:3] = [after(r, *a_rest) for r in r1[1:3]]
+    r1[1] = after(r1[1], *a_rest)
     mixed = [mixed, out_again(a_rest, [w_out], [rows] * 3, *pieces[1])]
-    far = [jnp.concatenate([m + r for m, r in zip(m_third[:3], r1[:3])], axis=1), m_third[3] + r1[3]]
+    far = [jnp.concatenate([m + r for m, r in zip(m_third[:2], r1[:2])], axis=1), m_third[2] + r1[2]]
     result = []
     for (m_own, m_near, m_second), f in zip(mixed, far):
         r2e = hop(m_second, ENDS_OUT)

time: 147 us -> 147 us (level)
  waiting for transfers between devices: 44.3 us -> 45.8 us
    ppermute x22 -> x21, waiting for transfers between devices: 42.7 us -> 44.2 us  [hop(): return lax.ppermute(a, 'col', pairs)]
    ppermute x22 -> x21, starting transfers between devices: 41 us -> 39.7 us  [hop(): return lax.ppermute(a, 'col', pairs)]
    pallas_call x6 -> x5, Pallas kernels: 18.3 us -> 18.1 us  [mix(): pl.pallas_call(functools.partial(mix_kernel, len(operands), ask, q_width,...]
  transfers between devices with their start and end apart: 25 -> 24, of which waited for: 11 -> 11; matrix products, arithmetic and copies ran while one was open for 1% -> 1% of each run, Pallas kernels for 35% -> 35%
where the time goes in v10:
time: 147 us; the launch traced here: 145 us
  Pallas kernels  51.3 us (35%)
  waiting for transfers between devices  45.8 us (31%)
  starting transfers between devices  40.4 us (27%)
  local copies, waits for them, and re-layouts  5.82 us (4%)
  other arithmetic  1.59 us (1%)
    ppermute x21, waiting for transfers between devices, hop(): return lax.ppermute(a, 'col', pairs)  44.2 us
    ppermute x21, starting transfers between devices, hop(): return lax.ppermute(a, 'col', pairs)  39.7 us
    pallas_call x6, Pallas kernels, project(): pl.pallas_call(functools.partial(project_kernel, terms, total is not None...  28.5 us
    pallas_call x5, Pallas kernels, mix(): pl.pallas_call(functools.partial(mix_kernel, len(operands), ask, q_width,...  18.1 us
    unnamed x10, local copies, waits for them, and re-layouts  4.41 us
    pallas_call x1, Pallas kernels, halve(): pl.pallas_call(functools.partial(halve_kernel, start), in_specs=[anywhere...  3.8 us
  transfers between devices with their start and end apart: 24, of which 11 were waited for; matrix products, arithmetic and copies ran while one was open for 1% of the time, Pallas kernels for 35%

profile of v10, /device:TPU:0, one launch (start us, length us, event | category | flops | bytes accessed | tf_op | source)
XLA Modules:
  0.0 145.4 jit_solution(11991842400843506769)
XLA Ops:
  0.0 3.0 %collective-permute-start.2 = (f32[64,4096]{1,0:T(8,128)}, f32[64,4096]{1,0:T(8,128)S(1)}, u32[]{:S(2)}, u32[]{:S(2)}) collective-permute-start(f32[64,4096]{1,0:T(8,128)} %refs_0_.3), channel_id=1, source_target_pairs={{0,1},{1,0},{2,3},{3,2},{4,5},{5,4},{6,7},{7,6},{8,9},{9,8},{10,11... | collective-permute-start | bytes 3145736 | tf_op jit(solution)/shard_map/ppermute | solution.py:301
  3.0 1.3 fusion
  4.3 0.7 collective-permute-start
  5.0 0.7 collective-permute-start.3
  5.7 0.0 copy-start
  5.7 1.6 %copy-done = f32[4096,128]{1,0:T(8,128)S(1)} copy-done((f32[4096,128]{1,0:T(8,128)S(1)}, f32[4096,128]{1,0:T(8,128)}, u32[]{:S(2)}) %copy-start) | copy-done | bytes 2097176
  7.3 1.6 %copy-done.2 = f32[4096,128]{1,0:T(8,128)S(1)} copy-done((f32[4096,128]{1,0:T(8,128)S(1)}, f32[4096,128]{1,0:T(8,128)}, u32[]{:S(2)}) %copy-start.2) | copy-done | bytes 2097176
  8.9 1.2 copy-done.4
  10.1 4.3 %project.6.refs_4_ = f32[64,1280]{1,0:T(8,128)S(1)} custom-call(f32[64,4096]{1,0:T(8,128)S(1)} %copy-done.4, f32[4096,1024]{1,0:T(8,128)} %refs_2_.9, f32[4096,128]{1,0:T(8,128)S(1)} %copy-done, f32[4096,128]{1,0:T(8,128)S(1)} %copy-done.2), custom_call_target="tpu_custom_call" | custom-call | flops 1342177280 | bytes 11010048 | tf_op jit(solution)/shard_map/project/pallas_call | solution.py:103
  14.5 0.0 collective-permute-done.refs_5_.refs_1_
  14.5 1.3 collective-permute-start.5
  15.8 4.3 %project.7.refs_0_ = f32[64,1280]{1,0:T(8,128)S(1)} custom-call(f32[64,4096]{1,0:T(8,128)S(1)} %copy-done.4, f32[4096,1024]{1,0:T(8,128)} %refs_2_.9, f32[4096,128]{1,0:T(8,128)S(1)} %copy-done, f32[4096,128]{1,0:T(8,128)S(1)} %copy-done.2, f32[64,1280]{1,0:T(8,128)S(1)} %project.6.refs_4_, f32[64,2048]{1,0:T(8,128)S(1)} %collective-permute-done.refs_5_.refs_1_), custom_call_target="tpu_custom_call" | custom-call | flops 1342177280 | bytes 11010048 | tf_op jit(solution)/shard_map/project/pallas_call | solution.py:103
  20.1 7.1 %collective-permute-done.2.before.refs_0_ = f32[64,4096]{1,0:T(8,128)S(1)} collective-permute-done((f32[64,4096]{1,0:T(8,128)}, f32[64,4096]{1,0:T(8,128)S(1)}, u32[]{:S(2)}, u32[]{:S(2)}) %collective-permute-start.2) | collective-permute-done | bytes 1048608 | tf_op jit(solution)/shard_map/ppermute | solution.py:301
  27.3 0.0 copy-start.1
  27.3 0.0 copy-start.3
  27.3 0.8 collective-permute-start.9
  28.1 1.4 collective-permute-start.4
  29.6 3.8 %halve.1 = (bf16[1024,2048]{1,0:T(8,128)(2,1)S(1)}, bf16[1024,2048]{1,0:T(8,128)(2,1)S(1)}) custom-call(f32[1024,4096]{1,0:T(8,128)} %refs_2_.11, f32[64,4096]{1,0:T(8,128)S(1)} %collective-permute-done.2.before.refs_0_), custom_call_target="tpu_custom_call" | custom-call | flops 2097152 | bytes 16777216 | tf_op jit(solution)/shard_map/halve/pallas_call | solution.py:196
  33.4 0.7 collective-permute-start.7
  34.1 4.3 %collective-permute-done.5.refs_2_ = f32[64,2048]{1,0:T(8,128)S(1)} collective-permute-done((f32[64,2048]{1,0:T(8,128)S(1)}, f32[64,2048]{1,0:T(8,128)S(1)}, u32[]{:S(2)}, u32[]{:S(2)}) %collective-permute-start.5) | collective-permute-done | bytes 524320 | tf_op jit(solution)/shard_map/ppermute | solution.py:301
  38.5 5.8 %project.8.refs_6_ = f32[128,1280]{1,0:T(8,128)S(1)} custom-call(f32[64,4096]{1,0:T(8,128)S(1)} %collective-permute-done.2.before.refs_0_, f32[64,2048]{1,0:T(8,128)S(1)} %collective-permute-done.refs_5_.refs_1_, f32[64,2048]{1,0:T(8,128)S(1)} %collective-permute-done.5.refs_2_, f32[4096,1024]{1,0:T(8,128)} %refs_2_.9, f32[4096,128]{1,0:T(8,128)S(1)} %copy-done.1, ...), custom_call_target="tpu_custom_call" | custom-call | flops 2684354560 | bytes 11534336 | tf_op jit(solution)/shard_map/project/pallas_call | solution.py:103
  44.3 1.5 %collective-permute-start.10 = (f32[64,2048]{1,0:T(8,128)S(1)}, f32[64,2048]{1,0:T(8,128)S(1)}, u32[]{:S(2)}, u32[]{:S(2)}) collective-permute-start(f32[64,2048]{1,0:T(8,128)S(1)} %collective-permute-done.9.refs_0_), channel_id=1, source_target_pairs={{1,0},{2,3},{5,4},{6,7},{9,8},{10,11},{13,12},{14,15},{17,16},{18,... | collective-permute-start | bytes 1572872 | tf_op jit(solution)/shard_map/ppermute | solution.py:301
  45.8 3.9 %collective-permute-done.4.refs_2_ = f32[64,2048]{1,0:T(8,128)S(1)} collective-permute-done((f32[64,2048]{1,0:T(8,128)S(1)}, f32[64,2048]{1,0:T(8,128)S(1)}, u32[]{:S(2)}, u32[]{:S(2)}) %collective-permute-start.4) | collective-permute-done | bytes 524320 | tf_op jit(solution)/shard_map/ppermute | solution.py:301
  49.7 5.8 %project.9.refs_2_ = f32[128,1280]{1,0:T(8,128)S(1)} custom-call(f32[64,4096]{1,0:T(8,128)S(1)} %collective-permute-done.2.before.refs_0_, f32[64,2048]{1,0:T(8,128)S(1)} %collective-permute-done.3.refs_7_.refs_1_.refs_8_, f32[64,2048]{1,0:T(8,128)S(1)} %collective-permute-done.4.refs_2_, f32[4096,1024]{1,0:T(8,128)} %refs_2_.9, f32[4096,128]{1,0:T(8,128)S(1)} %copy-done.1, ...), custom_call_target="tpu_custom_call" | custom-call | flops 2684354560 | bytes 11534336 | tf_op jit(solution)/shard_map/project/pallas_call | solution.py:103
  55.6 1.3 collective-permute-start.11
  56.9 0.1 collective-permute-start.6
  57.0 1.3 collective-permute-start.8
  58.3 0.6 collective-permute-start.1
  58.8 2.7 %collective-permute-done.10.refs_1_ = f32[64,2048]{1,0:T(8,128)S(1)} collective-permute-done((f32[64,2048]{1,0:T(8,128)S(1)}, f32[64,2048]{1,0:T(8,128)S(1)}, u32[]{:S(2)}, u32[]{:S(2)}) %collective-permute-start.10) | collective-permute-done | bytes 524320 | tf_op jit(solution)/shard_map/ppermute | solution.py:301
  61.5 5.3 %project.10 = (f32[64,1280]{1,0:T(8,128)S(1)}, bf16[1024,1280]{1,0:T(8,128)(2,1)S(1)}, bf16[1024,1280]{1,0:T(8,128)(2,1)S(1)}) custom-call(f32[64,2048]{1,0:T(8,128)S(1)} %collective-permute-done.9.refs_0_, f32[64,2048]{1,0:T(8,128)S(1)} %collective-permute-done.10.refs_1_, f32[4096,1024]{1,0:T(8,128)} %refs_2_.9, f32[4096,128]{1,0:T(8,128)S(1)} %copy-done.1, ...), custom_call_target="tpu_custom_call" | custom-call | flops 1342177280 | bytes 11010048 | tf_op jit(solution)/shard_map/project/pallas_call | solution.py:103
  66.7 0.3 collective-permute-done.11.refs_1_
  67.1 3.0 %project.11.total = f32[64,1280]{1,0:T(8,128)S(1)} custom-call(f32[64,2048]{1,0:T(8,128)S(1)} %collective-permute-done.7.refs_0_.x, f32[64,1024]{1,0:T(8,128)S(1)} %collective-permute-done.11.refs_1_, f32[4096,1024]{1,0:T(8,128)} %refs_2_.9, f32[4096,128]{1,0:T(8,128)S(1)} %copy-done.1, f32[4096,128]{1,0:T(8,128)S(1)} %copy-done.3, ...), custom_call_target="tpu_custom_call" | custom-call | flops 671088640 | bytes 5505024 | tf_op jit(solution)/shard_map/project/pallas_call | solution.py:103
  70.1 1.3 collective-permute-done.8.y
  71.3 0.9 project_last.1.refs_4_
  72.2 0.1 collective-permute-start.12
  72.3 1.6 %collective-permute-done.12.refs_5_ = f32[64,1280]{1,0:T(8,128)S(1)} collective-permute-done((f32[64,1280]{1,0:T(8,128)S(1)}, f32[64,1280]{1,0:T(8,128)S(1)}, u32[]{:S(2)}, u32[]{:S(2)}) %collective-permute-start.12) | collective-permute-done | bytes 327712 | tf_op jit(solution)/shard_map/ppermute | solution.py:304
  73.9 1.1 attend_out.2
  75.0 1.5 collective-permute-start.13
  76.5 1.0 out_again.3
  77.5 1.5 %collective-permute-start.14 = (f32[64,1536]{1,0:T(8,128)S(1)}, f32[64,1536]{1,0:T(8,128)S(1)}, u32[]{:S(2)}, u32[]{:S(2)}) collective-permute-start(f32[64,1536]{1,0:T(8,128)S(1)} %out_again.3), channel_id=1, source_target_pairs={{0,1},{3,2},{4,5},{7,6},{8,9},{11,10},{12,13},{15,14},{16,17},{19,... | collective-permute-start | bytes 1179656 | tf_op jit(solution)/shard_map/ppermute | solution.py:301
  79.0 4.0 %out_again.4 = f32[64,2048]{1,0:T(8,128)S(1)} custom-call(bf16[64,1024]{1,0:T(8,128)(2,1)S(1)} %get-tuple-element.40.refs_0_, bf16[64,1024]{1,0:T(8,128)(2,1)S(1)} %get-tuple-element.41.refs_1_, f32[1024,4096]{1,0:T(8,128)} %refs_2_.11), custom_call_target="tpu_custom_call" | custom-call | flops 1073741824 | bytes 8912896 | tf_op jit(solution)/shard_map/out_again/pallas_call | solution.py:255
  83.1 1.3 collective-permute-start.19
  84.4 6.4 %attend_out.3 = (bf16[192,1024]{1,0:T(8,128)(2,1)S(1)}, bf16[192,1024]{1,0:T(8,128)(2,1)S(1)}, f32[64,2048]{1,0:T(8,128)S(1)}, f32[64,2048]{1,0:T(8,128)S(1)}, f32[64,2048]{1,0:T(8,128)S(1)}) custom-call(f32[64,1280]{1,0:T(8,128)S(1)} %project.7.refs_0_, f32[64,1280]{1,0:T(8,128)S(1)} %collective-permute-done.1.refs_1_, f32[128,1280]{1,0:T(8,128)S(1)} %project.9.refs_2_, ...), custom_call_target="tpu_custom_call" | custom-call | flops 4831838208 | bytes 9961472 | tf_op jit(solution)/shard_map/attend_out/pallas_call | solution.py:255
  90.8 1.3 collective-permute-start.17
  92.3 0.7 collective-permute-start.15
  93.0 5.6 %out_again.5 = (f32[64,2048]{1,0:T(8,128)S(1)}, f32[64,2048]{1,0:T(8,128)S(1)}, f32[64,2048]{1,0:T(8,128)S(1)}) custom-call(bf16[192,1024]{1,0:T(8,128)(2,1)S(1)} %get-tuple-element.46.refs_0_, bf16[192,1024]{1,0:T(8,128)(2,1)S(1)} %get-tuple-element.47.refs_1_, f32[1024,4096]{1,0:T(8,128)} %refs_2_.11), custom_call_target="tpu_custom_call" | custom-call | flops 3221225472 | bytes 9961472 | tf_op jit(solution)/shard_map/out_again/pallas_call | solution.py:255
  98.5 5.3 %collective-permute-start.22 = (f32[64,2048]{1,0:T(8,128)S(1)}, f32[64,2048]{1,0:T(8,128)S(1)}, u32[]{:S(2)}, u32[]{:S(2)}) collective-permute-start(f32[64,2048]{1,0:T(8,128)S(1)} %get-tuple-element.52), channel_id=1, source_target_pairs={{0,1},{3,2},{4,5},{7,6},{8,9},{11,10},{12,13},{15,14},{16,17},{19,... | collective-permute-start | bytes 1572872 | tf_op jit(solution)/shard_map/ppermute | solution.py:301
  103.9 0.1 add.39
  103.9 0.7 collective-permute-start.20
  104.7 6.3 %collective-permute-done.17 = f32[64,2048]{1,0:T(8,128)S(1)} collective-permute-done((f32[64,2048]{1,0:T(8,128)S(1)}, f32[64,2048]{1,0:T(8,128)S(1)}, u32[]{:S(2)}, u32[]{:S(2)}) %collective-permute-start.17) | collective-permute-done | bytes 524320 | tf_op jit(solution)/shard_map/ppermute | solution.py:301
  111.0 0.1 add.36
  111.0 0.7 collective-permute-start.18
  111.8 0.1 add.35
  111.8 6.6 %collective-permute-start.16 = (f32[64,2048]{1,0:T(8,128)S(1)}, f32[64,2048]{1,0:T(8,128)S(1)}, u32[]{:S(2)}, u32[]{:S(2)}) collective-permute-start(f32[64,2048]{1,0:T(8,128)S(1)} %add.35), channel_id=1, source_target_pairs={{0,1},{1,0},{2,3},{3,2},{4,5},{5,4},{6,7},{7,6},{8,9},{9,8},{10,11... | collective-permute-start | bytes 1572872 | tf_op jit(solution)/shard_map/ppermute | solution.py:301
  118.5 3.8 %collective-permute-done.22 = f32[64,2048]{1,0:T(8,128)S(1)} collective-permute-done((f32[64,2048]{1,0:T(8,128)S(1)}, f32[64,2048]{1,0:T(8,128)S(1)}, u32[]{:S(2)}, u32[]{:S(2)}) %collective-permute-start.22) | collective-permute-done | bytes 524320 | tf_op jit(solution)/shard_map/ppermute | solution.py:301
  122.2 0.1 add.41
  122.3 0.7 collective-permute-start.23
  123.0 0.1 add.40
  123.1 6.6 %collective-permute-start.21 = (f32[64,2048]{1,0:T(8,128)S(1)}, f32[64,2048]{1,0:T(8,128)S(1)}, u32[]{:S(2)}, u32[]{:S(2)}) collective-permute-start(f32[64,2048]{1,0:T(8,128)S(1)} %add.40), channel_id=1, source_target_pairs={{0,1},{1,0},{2,3},{3,2},{4,5},{5,4},{6,7},{7,6},{8,9},{9,8},{10,11... | collective-permute-start | bytes 1572872 | tf_op jit(solution)/shard_map/ppermute | solution.py:301
  129.7 3.8 %collective-permute-done.16 = f32[64,2048]{1,0:T(8,128)S(1)} collective-permute-done((f32[64,2048]{1,0:T(8,128)S(1)}, f32[64,2048]{1,0:T(8,128)S(1)}, u32[]{:S(2)}, u32[]{:S(2)}) %collective-permute-start.16) | collective-permute-done | bytes 524320 | tf_op jit(solution)/shard_map/ppermute | solution.py:301
  133.5 0.1 add_add_fusion.1
  133.6 10.7 %collective-permute-done.21 = f32[64,2048]{1,0:T(8,128)S(1)} collective-permute-done((f32[64,2048]{1,0:T(8,128)S(1)}, f32[64,2048]{1,0:T(8,128)S(1)}, u32[]{:S(2)}, u32[]{:S(2)}) %collective-permute-start.21) | collective-permute-done | bytes 524320 | tf_op jit(solution)/shard_map/ppermute | solution.py:301
  144.3 0.1 add_add_fusion
  144.3 1.0 pad_maximum_fusion
  (22 shorter events, 0.3 us)
Async XLA Ops:
  0.0 27.2 %collective-permute-start.2 = (f32[64,4096]{1,0:T(8,128)}, f32[64,4096]{1,0:T(8,128)S(1)}, u32[]{:S(2)}, u32[]{:S(2)}) collective-permute-start(f32[64,4096]{1,0:T(8,128)} %refs_0_.3), channel_id=1, source_target_pairs={{0,1},{1,0},{2,3},{3,2},{4,5},{5,4},{6,7},{7,6},{8,9},{9,8},{10,11... | collective-permute-start | bytes 3145736 | tf_op jit(solution)/shard_map/ppermute | solution.py:301
  4.3 10.2 %collective-permute-start = (f32[64,2048]{1,0:T(8,128)S(1)}, f32[64,2048]{1,0:T(8,128)S(1)}, u32[]{:S(2)}, u32[]{:S(2)}) collective-permute-start(f32[64,2048]{1,0:T(8,128)S(1)} %get-tuple-element.54), channel_id=1, source_target_pairs={{1,2},{2,1},{5,6},{6,5},{9,10},{10,9},{13,14},{14,13},{17,18},{18,... | collective-permute-start | bytes 1572872 | tf_op jit(solution)/shard_map/ppermute | solution.py:301
  5.0 23.1 %collective-permute-start.3 = (f32[64,2048]{1,0:T(8,128)S(1)}, f32[64,2048]{1,0:T(8,128)S(1)}, u32[]{:S(2)}, u32[]{:S(2)}) collective-permute-start(f32[64,2048]{1,0:T(8,128)S(1)} %get-tuple-element.53), channel_id=1, source_target_pairs={{1,2},{2,1},{5,6},{6,5},{9,10},{10,9},{13,14},{14,13},{17,18},{18,... | collective-permute-start | bytes 1572872 | tf_op jit(solution)/shard_map/ppermute | solution.py:301
  5.7 1.6 %copy-start = (f32[4096,128]{1,0:T(8,128)S(1)}, f32[4096,128]{1,0:T(8,128)}, u32[]{:S(2)}) copy-start(f32[4096,128]{1,0:T(8,128)} %refs_3_.11) | copy-start | bytes 6291460
  7.3 1.6 %copy-start.2 = (f32[4096,128]{1,0:T(8,128)S(1)}, f32[4096,128]{1,0:T(8,128)}, u32[]{:S(2)}) copy-start(f32[4096,128]{1,0:T(8,128)} %refs_4_.7) | copy-start | bytes 6291460
  8.9 1.2 copy-start.4
  14.5 23.9 %collective-permute-start.5 = (f32[64,2048]{1,0:T(8,128)S(1)}, f32[64,2048]{1,0:T(8,128)S(1)}, u32[]{:S(2)}, u32[]{:S(2)}) collective-permute-start(f32[64,2048]{1,0:T(8,128)S(1)} %collective-permute-done.refs_5_.refs_1_), channel_id=1, source_target_pairs={{1,0},{2,3},{5,4},{6,7},{9,8},{10,11},{13,12},{14,15},{17,16},{18,... | collective-permute-start | bytes 1572872 | tf_op jit(solution)/shard_map/ppermute | solution.py:301
  27.3 11.2 %copy-start.1 = (f32[4096,128]{1,0:T(8,128)S(1)}, f32[4096,128]{1,0:T(8,128)}, u32[]{:S(2)}) copy-start(f32[4096,128]{1,0:T(8,128)} %refs_3_.11) | copy-start | bytes 6291460
  27.3 11.2 %copy-start.3 = (f32[4096,128]{1,0:T(8,128)S(1)}, f32[4096,128]{1,0:T(8,128)}, u32[]{:S(2)}) copy-start(f32[4096,128]{1,0:T(8,128)} %refs_4_.7) | copy-start | bytes 6291460
  27.3 17.0 %collective-permute-start.9 = (f32[64,2048]{1,0:T(8,128)S(1)}, f32[64,2048]{1,0:T(8,128)S(1)}, u32[]{:S(2)}, u32[]{:S(2)}) collective-permute-start(f32[64,2048]{1,0:T(8,128)S(1)} %slice.22), channel_id=1, source_target_pairs={{1,2},{2,1},{5,6},{6,5},{9,10},{10,9},{13,14},{14,13},{17,18},{18,... | collective-permute-start | bytes 1572872 | tf_op jit(solution)/shard_map/ppermute | solution.py:301
  28.1 21.6 %collective-permute-start.4 = (f32[64,2048]{1,0:T(8,128)S(1)}, f32[64,2048]{1,0:T(8,128)S(1)}, u32[]{:S(2)}, u32[]{:S(2)}) collective-permute-start(f32[64,2048]{1,0:T(8,128)S(1)} %collective-permute-done.3.refs_7_.refs_1_.refs_8_), channel_id=1, source_target_pairs={{1,0},{2,3},{5,4},{6,7},{9,8},{10,11},{13,12},{14,15},{17,16},{18,... | collective-permute-start | bytes 1572872 | tf_op jit(solution)/shard_map/ppermute | solution.py:301
  33.4 22.1 %collective-permute-start.7 = (f32[64,2048]{1,0:T(8,128)S(1)}, f32[64,2048]{1,0:T(8,128)S(1)}, u32[]{:S(2)}, u32[]{:S(2)}) collective-permute-start(f32[64,2048]{1,0:T(8,128)S(1)} %slice.20), channel_id=1, source_target_pairs={{1,2},{2,1},{5,6},{6,5},{9,10},{10,9},{13,14},{14,13},{17,18},{18,... | collective-permute-start | bytes 1572872 | tf_op jit(solution)/shard_map/ppermute | solution.py:301
  44.3 17.2 %collective-permute-start.10 = (f32[64,2048]{1,0:T(8,128)S(1)}, f32[64,2048]{1,0:T(8,128)S(1)}, u32[]{:S(2)}, u32[]{:S(2)}) collective-permute-start(f32[64,2048]{1,0:T(8,128)S(1)} %collective-permute-done.9.refs_0_), channel_id=1, source_target_pairs={{1,0},{2,3},{5,4},{6,7},{9,8},{10,11},{13,12},{14,15},{17,16},{18,... | collective-permute-start | bytes 1572872 | tf_op jit(solution)/shard_map/ppermute | solution.py:301
  55.6 11.5 %collective-permute-start.11 = (f32[64,1024]{1,0:T(8,128)S(1)}, f32[64,1024]{1,0:T(8,128)S(1)}, u32[]{:S(2)}, u32[]{:S(2)}) collective-permute-start(f32[64,1024]{1,0:T(8,128)S(1)} %get-tuple-element.36), channel_id=1, source_target_pairs={{1,0},{2,3},{5,4},{6,7},{9,8},{10,11},{13,12},{14,15},{17,16},{18,... | collective-permute-start | bytes 786440 | tf_op jit(solution)/shard_map/ppermute | solution.py:301
  56.9 15.4 %collective-permute-start.6 = (f32[128,1280]{1,0:T(8,128)S(1)}, f32[128,1280]{1,0:T(8,128)S(1)}, u32[]{:S(2)}, u32[]{:S(2)}) collective-permute-start(f32[128,1280]{1,0:T(8,128)S(1)} %project.9.refs_2_), channel_id=1, source_target_pairs={{0,4},{4,0},{1,5},{5,1},{2,6},{6,2},{3,7},{7,3},{8,12},{12,8},{9,1... | collective-permute-start | bytes 1966088 | tf_op jit(solution)/shard_map/ppermute | solution.py:304
  57.0 14.4 %collective-permute-start.8 = (f32[64,1024]{1,0:T(8,128)S(1)}, f32[64,1024]{1,0:T(8,128)S(1)}, u32[]{:S(2)}, u32[]{:S(2)}) collective-permute-start(f32[64,1024]{1,0:T(8,128)S(1)} %get-tuple-element.56), channel_id=1, source_target_pairs={{1,0},{2,3},{5,4},{6,7},{9,8},{10,11},{13,12},{14,15},{17,16},{18,... | collective-permute-start | bytes 786440 | tf_op jit(solution)/shard_map/ppermute | solution.py:301
  58.3 14.0 %collective-permute-start.1 = (f32[64,1280]{1,0:T(8,128)S(1)}, f32[64,1280]{1,0:T(8,128)S(1)}, u32[]{:S(2)}, u32[]{:S(2)}) collective-permute-start(f32[64,1280]{1,0:T(8,128)S(1)} %project.7.refs_0_), channel_id=1, source_target_pairs={{0,4},{4,0},{1,5},{5,1},{2,6},{6,2},{3,7},{7,3},{8,12},{12,8},{9,1... | collective-permute-start | bytes 983048 | tf_op jit(solution)/shard_map/ppermute | solution.py:304
  72.2 1.7 %collective-permute-start.12 = (f32[64,1280]{1,0:T(8,128)S(1)}, f32[64,1280]{1,0:T(8,128)S(1)}, u32[]{:S(2)}, u32[]{:S(2)}) collective-permute-start(f32[64,1280]{1,0:T(8,128)S(1)} %project_last.1.refs_4_), channel_id=1, source_target_pairs={{0,4},{4,0},{1,5},{5,1},{2,6},{6,2},{3,7},{7,3},{8,12},{12,8},{9,1... | collective-permute-start | bytes 983048 | tf_op jit(solution)/shard_map/ppermute | solution.py:304
  75.0 9.4 %collective-permute-start.13 = (f32[64,512]{1,0:T(8,128)S(1)}, f32[64,512]{1,0:T(8,128)S(1)}, u32[]{:S(2)}, u32[]{:S(2)}) collective-permute-start(f32[64,512]{1,0:T(8,128)S(1)} %get-tuple-element.39), channel_id=1, source_target_pairs={{0,1},{3,2},{4,5},{7,6},{8,9},{11,10},{12,13},{15,14},{16,17},{19,... | collective-permute-start | bytes 393224 | tf_op jit(solution)/shard_map/ppermute | solution.py:301
  77.5 14.7 %collective-permute-start.14 = (f32[64,1536]{1,0:T(8,128)S(1)}, f32[64,1536]{1,0:T(8,128)S(1)}, u32[]{:S(2)}, u32[]{:S(2)}) collective-permute-start(f32[64,1536]{1,0:T(8,128)S(1)} %out_again.3), channel_id=1, source_target_pairs={{0,1},{3,2},{4,5},{7,6},{8,9},{11,10},{12,13},{15,14},{16,17},{19,... | collective-permute-start | bytes 1179656 | tf_op jit(solution)/shard_map/ppermute | solution.py:301
  83.1 20.8 %collective-permute-start.19 = (f32[64,2048]{1,0:T(8,128)S(1)}, f32[64,2048]{1,0:T(8,128)S(1)}, u32[]{:S(2)}, u32[]{:S(2)}) collective-permute-start(f32[64,2048]{1,0:T(8,128)S(1)} %out_again.4), channel_id=1, source_target_pairs={{0,1},{3,2},{4,5},{7,6},{8,9},{11,10},{12,13},{15,14},{16,17},{19,... | collective-permute-start | bytes 1572872 | tf_op jit(solution)/shard_map/ppermute | solution.py:301
  90.8 20.2 %collective-permute-start.17 = (f32[64,2048]{1,0:T(8,128)S(1)}, f32[64,2048]{1,0:T(8,128)S(1)}, u32[]{:S(2)}, u32[]{:S(2)}) collective-permute-start(f32[64,2048]{1,0:T(8,128)S(1)} %get-tuple-element.49), channel_id=1, source_target_pairs={{0,1},{3,2},{4,5},{7,6},{8,9},{11,10},{12,13},{15,14},{16,17},{19,... | collective-permute-start | bytes 1572872 | tf_op jit(solution)/shard_map/ppermute | solution.py:301
  92.3 19.5 %collective-permute-start.15 = (f32[64,2048]{1,0:T(8,128)S(1)}, f32[64,2048]{1,0:T(8,128)S(1)}, u32[]{:S(2)}, u32[]{:S(2)}) collective-permute-start(f32[64,2048]{1,0:T(8,128)S(1)} %pad_maximum_fusion.1), channel_id=1, source_target_pairs={{1,2},{2,1},{5,6},{6,5},{9,10},{10,9},{13,14},{14,13},{17,18},{18,... | collective-permute-start | bytes 1572872 | tf_op jit(solution)/shard_map/ppermute | solution.py:301
  98.5 23.7 %collective-permute-start.22 = (f32[64,2048]{1,0:T(8,128)S(1)}, f32[64,2048]{1,0:T(8,128)S(1)}, u32[]{:S(2)}, u32[]{:S(2)}) collective-permute-start(f32[64,2048]{1,0:T(8,128)S(1)} %get-tuple-element.52), channel_id=1, source_target_pairs={{0,1},{3,2},{4,5},{7,6},{8,9},{11,10},{12,13},{15,14},{16,17},{19,... | collective-permute-start | bytes 1572872 | tf_op jit(solution)/shard_map/ppermute | solution.py:301
  103.9 19.0 %collective-permute-start.20 = (f32[64,2048]{1,0:T(8,128)S(1)}, f32[64,2048]{1,0:T(8,128)S(1)}, u32[]{:S(2)}, u32[]{:S(2)}) collective-permute-start(f32[64,2048]{1,0:T(8,128)S(1)} %add.39), channel_id=1, source_target_pairs={{1,2},{2,1},{5,6},{6,5},{9,10},{10,9},{13,14},{14,13},{17,18},{18,... | collective-permute-start | bytes 1572872 | tf_op jit(solution)/shard_map/ppermute | solution.py:301
  111.0 18.6 %collective-permute-start.18 = (f32[64,2048]{1,0:T(8,128)S(1)}, f32[64,2048]{1,0:T(8,128)S(1)}, u32[]{:S(2)}, u32[]{:S(2)}) collective-permute-start(f32[64,2048]{1,0:T(8,128)S(1)} %add.36), channel_id=1, source_target_pairs={{1,2},{2,1},{5,6},{6,5},{9,10},{10,9},{13,14},{14,13},{17,18},{18,... | collective-permute-start | bytes 1572872 | tf_op jit(solution)/shard_map/ppermute | solution.py:301
  111.8 21.6 %collective-permute-start.16 = (f32[64,2048]{1,0:T(8,128)S(1)}, f32[64,2048]{1,0:T(8,128)S(1)}, u32[]{:S(2)}, u32[]{:S(2)}) collective-permute-start(f32[64,2048]{1,0:T(8,128)S(1)} %add.35), channel_id=1, source_target_pairs={{0,1},{1,0},{2,3},{3,2},{4,5},{5,4},{6,7},{7,6},{8,9},{9,8},{10,11... | collective-permute-start | bytes 1572872 | tf_op jit(solution)/shard_map/ppermute | solution.py:301
  122.3 11.3 %collective-permute-start.23 = (f32[64,2048]{1,0:T(8,128)S(1)}, f32[64,2048]{1,0:T(8,128)S(1)}, u32[]{:S(2)}, u32[]{:S(2)}) collective-permute-start(f32[64,2048]{1,0:T(8,128)S(1)} %add.41), channel_id=1, source_target_pairs={{1,2},{2,1},{5,6},{6,5},{9,10},{10,9},{13,14},{14,13},{17,18},{18,... | collective-permute-start | bytes 1572872 | tf_op jit(solution)/shard_map/ppermute | solution.py:301
  123.1 21.2 %collective-permute-start.21 = (f32[64,2048]{1,0:T(8,128)S(1)}, f32[64,2048]{1,0:T(8,128)S(1)}, u32[]{:S(2)}, u32[]{:S(2)}) collective-permute-start(f32[64,2048]{1,0:T(8,128)S(1)} %add.40), channel_id=1, source_target_pairs={{0,1},{1,0},{2,3},{3,2},{4,5},{5,4},{6,7},{7,6},{8,9},{9,8},{10,11... | collective-permute-start | bytes 1572872 | tf_op jit(solution)/shard_map/ppermute | solution.py:301
